TPU v7x, 32 devices: a whole 2x2x4 slice. The times are simulated.
32 devices in a mesh: gx: 2 (over y), gy: 4 (over x, core), gz: 4 (over z).
Axes of the slice: x: 2, y: 2, z: 4, core: 2. Of those that a mesh axis runs over, the one named last changes fastest.
Arguments:
- bold_data: bfloat16 [16, 64, 128, 512], P('gx', 'gy', 'gz'), may hold values from -6 to 6
- spatial_maps: float32 [64, 16, 64, 128], P(None, 'gx', 'gy', 'gz'), may hold values from -6 to 6
- live_blocks: int32 [2, 4, 4], P('gx', 'gy', 'gz'), may hold values from 16 to 128, as said below
Outputs:
- new_maps: float32 [64, 16, 64, 128], P(None, 'gx', 'gy', 'gz')
- time_courses: bfloat16 [64, 512], replicated
Inputs may be any that keep to these rules, and one draw needn't show every extreme that they name: live_blocks counts live rows of a device's block; rows are numbered (x mod 8) * 16 + (y mod 16) and the live ones come first.
All inputs are finite; a program needn't handle non-finite values.
Results may differ from a plain program's by a relative error of at most 0.011.
Values may be sent and summed in bfloat16 or wider, within the bound.
No kernel may reach another device: no remote copies, remote signals or barrier semaphores. Data moves between devices by JAX's collectives and lax.ppermute only.
A program may use at most 192 MiB of HBM per device.

v0:
```python
import math

import jax
import jax.numpy as jnp
from jax import lax
from jax.sharding import PartitionSpec as P

RADIUS = 8
ITERS = 2


def extended(x, sides, width):
    for axis, dim in sides:
        peers, length = (lax.axis_size(axis), x.shape[dim])
        up = [(i, (i + 1) % peers) for i in range(peers - 1)]
        down = [(j, i) for i, j in up]
        last = lax.slice_in_dim(x, length - width, length, axis=dim)
        leading = lax.slice_in_dim(x, 0, width, axis=dim)
        before = lax.ppermute(last, axis, up)
        after = lax.ppermute(leading, axis, down)
        x = jnp.concatenate([before, x, after], axis=dim)
    return x


def band_matrix(length, dtype):
    total = sum((math.exp(-float(d * d) / 32.0) for d in range(-RADIUS, RADIUS + 1)))
    count = length - 2 * RADIUS
    rows = lax.broadcasted_iota(jnp.int32, (length, count), 0)
    cols = lax.broadcasted_iota(jnp.int32, (length, count), 1)
    offset = (rows - cols - RADIUS).astype(dtype)
    inside = jnp.logical_and(rows - cols >= 0, rows - cols <= 2 * RADIUS)
    return jnp.where(inside, jnp.exp(-offset * offset / 32.0) / total, jnp.zeros_like(offset))


def filter_along(field, axis):
    band = band_matrix(field.shape[axis], field.dtype)
    result = jnp.tensordot(field, band, axes=((axis,), (0,)), precision=lax.Precision.HIGHEST)
    return jnp.moveaxis(result, -1, axis)


def smooth_maps(plain):
    first_pad = extended(plain, (("gx", 1),), RADIUS).astype(jnp.float32)
    along_first = filter_along(first_pad, 1)
    second_pad = extended(along_first.astype(jnp.bfloat16), (("gy", 2),), RADIUS).astype(
        along_first.dtype
    )
    along_second = filter_along(second_pad, 2)
    third_pad = extended(along_second.astype(jnp.bfloat16), (("gz", 3),), RADIUS).astype(
        along_second.dtype
    )
    return filter_along(third_pad, 3)


def smooth_grad(plain):
    first_pad = extended(plain, (("gx", 1),), RADIUS).astype(jnp.float32)
    along_first = filter_along(first_pad, 1)
    second_pad = extended(along_first.astype(jnp.bfloat16), (("gy", 2),), RADIUS).astype(
        along_first.dtype
    )
    along_second = filter_along(second_pad, 2)
    third_pad = extended(along_second.astype(jnp.bfloat16), (("gz", 3),), RADIUS).astype(
        along_second.dtype
    )
    return filter_along(third_pad, 3)


def per_device(bold_data, spatial_maps, live_blocks):
    chans, size_x, size_y, size_z = spatial_maps.shape
    frame_count = bold_data.shape[3]
    count = live_blocks[0, 0, 0]
    row_ids = lax.broadcasted_iota(jnp.int32, (size_x, size_y), 0) * size_y + lax.broadcasted_iota(
        jnp.int32, (size_x, size_y), 1
    )
    live = jnp.broadcast_to((row_ids < count)[:, :, None], (size_x, size_y, size_z))
    live_half = live.astype(jnp.bfloat16)[None]
    live_flat = live.reshape(1, -1).astype(jnp.float32)
    flat_frames = bold_data.reshape(size_x * size_y * size_z, frame_count)
    all_cells = float(chans * size_x * size_y * size_z * lax.axis_size(("gx", "gy", "gz")))
    weights = spatial_maps.reshape(chans, -1)
    rounded = None
    for step in range(ITERS):
        plain = weights.reshape(chans, size_x, size_y, size_z).astype(jnp.bfloat16)
        filtered = smooth_maps(plain)
        smoothed = filtered.astype(jnp.bfloat16) * live_half
        partial_courses = jnp.dot(
            smoothed.reshape(chans, -1), flat_frames, preferred_element_type=jnp.float32
        )
        courses = lax.psum(partial_courses, ("gx", "gy", "gz"))
        gram = jnp.dot(courses, courses.T, precision=lax.Precision.HIGHEST)
        rounded = courses.astype(jnp.bfloat16)
        trace_value = jnp.trace(gram)
        raw_grad = (
            jnp.dot(rounded, flat_frames.T, preferred_element_type=jnp.float32) * live_flat
        ).astype(jnp.bfloat16)
        grad = smooth_grad(raw_grad.reshape(chans, size_x, size_y, size_z)).reshape(chans, -1)
        energy = lax.psum(jnp.sum(grad * grad), ("gx", "gy", "gz")) / all_cells
        scale = 1.0 / jnp.sqrt(energy + 1e-06)
        decay = jnp.dot(gram, weights, precision=lax.Precision.HIGHEST)
        weights = weights + 0.5 * (grad * scale - float(chans) / trace_value * decay)
    return (weights.reshape(chans, size_x, size_y, size_z), rounded)


def solution(mesh):
    return jax.shard_map(
        per_device,
        mesh=mesh,
        in_specs=(P("gx", "gy", "gz", None), P(None, "gx", "gy", "gz"), P("gx", "gy", "gz")),
        out_specs=(P(None, "gx", "gy", "gz"), P()),
        check_vma=False,
    )
```

profile of v0, /device:TPU:0, one launch (start us, length us, event | category | flops | bytes accessed | tf_op | source)
XLA Modules:
  0.0 621.1 jit_solution(5084006788904016541)
XLA Ops:
  7.2 3.2 copy.96
  10.5 1.3 collective-permute-start.1
  11.8 5.0 collective-permute-start
  16.8 21.1 %collective-permute-done.1 = bf16[64,8,16,32]{0,1,3,2:T(8,128)(2,1)S(1)} collective-permute-done((bf16[64,8,16,32]{0,1,3,2:T(8,128)(2,1)S(1)}, bf16[64,8,16,32]{0,1,3,2:T(8,128)(2,1)S(1)}, u32[]{:S(2)}, u32[]{:S(2)}) %collective-permute-start.1) | collective-permute-done | bytes 524320 | tf_op jit(solution)/shard_map/ppermute | solution.py:20
  39.1 1.6 fusion.84
  40.8 1.3 collective-permute-start.2
  42.1 1.3 collective-permute-start.3
  44.1 4.4 collective-permute-done.3
  48.9 3.0 fusion.105
  51.9 3.5 collective-permute-start.4
  55.4 1.3 collective-permute-start.5
  56.8 2.5 collective-permute-done.4
  59.3 4.4 collective-permute-done.5
  65.9 1.5 convolution_bitcast_fusion.1
  67.7 129.0 %all-reduce.3.cloned.1.call-done = f32[64,512]{1,0:T(8,128)} async-done(((f32[64,512]{1,0:T(8,128)}), f32[64,512]{1,0:T(8,128)}) %all-reduce.3.cloned.1.call-update) | async-done | bytes 131088 | tf_op jit(solution)/shard_map/psum | solution.py:88
  196.6 3.6 fusion.6
  201.5 1.5 collective-permute-start.7
  203.0 4.7 collective-permute-start.6
  207.7 19.9 %collective-permute-done.7 = bf16[64,8,16,32]{0,1,3,2:T(8,128)(2,1)S(1)} collective-permute-done((bf16[64,8,16,32]{0,1,3,2:T(8,128)(2,1)S(1)}, bf16[64,8,16,32]{0,1,3,2:T(8,128)(2,1)S(1)}, u32[]{:S(2)}, u32[]{:S(2)}) %collective-permute-start.7) | collective-permute-done | bytes 524320 | tf_op jit(solution)/shard_map/ppermute | solution.py:20
  227.6 1.5 collective-permute-done.6
  229.0 1.6 fusion.87
  231.6 2.1 collective-permute-start.8
  235.0 1.6 copy.34
  236.6 2.1 collective-permute-done.9
  238.8 1.7 pad_maximum_fusion.1
  240.4 3.0 fusion.102
  244.2 2.1 collective-permute-start.10
  246.4 1.3 collective-permute-start.11
  249.2 1.3 collective-permute-done.10
  250.5 4.4 collective-permute-done.11
  254.9 1.3 pad_maximum_fusion.5
  256.2 2.9 multiply_reduce_fusion.1
  259.2 46.9 %psum.29 = f32[]{:T(128)} all-reduce(f32[]{:T(128)} %get-tuple-element.22), channel_id=1, replica_groups=mesh['gx'=2,'gy'=4,'gz'=4] {'gx','gy','gz'}, use_global_device_ids=true, to_apply=%region_2.3 | all-reduce | flops 1 | bytes 8 | tf_op jit(solution)/shard_map/psum | solution.py:96
  306.7 3.2 broadcast_multiply_fusion.1
  310.0 3.2 copy.33
  313.2 4.7 fusion.291
  317.9 1.5 copy.35
  320.1 1.3 collective-permute-start.13
  321.4 4.7 collective-permute-start.12
  326.1 20.2 %collective-permute-done.13 = bf16[64,8,16,32]{0,1,3,2:T(8,128)(2,1)S(1)} collective-permute-done((bf16[64,8,16,32]{0,1,3,2:T(8,128)(2,1)S(1)}, bf16[64,8,16,32]{0,1,3,2:T(8,128)(2,1)S(1)}, u32[]{:S(2)}, u32[]{:S(2)}) %collective-permute-start.13) | collective-permute-done | bytes 524320 | tf_op jit(solution)/shard_map/ppermute | solution.py:20
  347.5 1.6 fusion.90
  349.2 1.3 collective-permute-start.14
  352.0 3.4 collective-permute-done.15
  355.9 3.0 fusion.99
  358.9 2.8 collective-permute-start.16
  361.7 1.5 collective-permute-start.17
  363.2 2.4 collective-permute-done.16
  365.6 4.4 collective-permute-done.17
  372.2 1.5 convolution_bitcast_fusion
  373.7 128.4 %all-reduce.5.cloned.1.call-done = f32[64,512]{1,0:T(8,128)} async-done(((f32[64,512]{1,0:T(8,128)}), f32[64,512]{1,0:T(8,128)}) %all-reduce.5.cloned.1.call-update) | async-done | bytes 131088 | tf_op jit(solution)/shard_map/psum | solution.py:88
  503.0 3.6 fusion.7
  509.1 4.7 collective-permute-start.18
  513.8 20.1 %collective-permute-done.19 = bf16[64,8,16,32]{0,1,3,2:T(8,128)(2,1)S(1)} collective-permute-done((bf16[64,8,16,32]{0,1,3,2:T(8,128)(2,1)S(1)}, bf16[64,8,16,32]{0,1,3,2:T(8,128)(2,1)S(1)}, u32[]{:S(2)}, u32[]{:S(2)}) %collective-permute-start.19) | collective-permute-done | bytes 524320 | tf_op jit(solution)/shard_map/ppermute | solution.py:20
  535.1 1.6 fusion.93
  536.8 1.3 collective-permute-start.20
  539.6 4.0 collective-permute-done.21
  544.1 3.0 fusion.96
  547.1 2.1 collective-permute-start.22
  553.1 4.4 collective-permute-done.23
  557.8 1.9 multiply_reduce_fusion
  559.7 46.7 %psum.31 = f32[]{:T(128)} all-reduce(f32[]{:T(128)} %get-tuple-element.28), channel_id=1, replica_groups=mesh['gx'=2,'gy'=4,'gz'=4] {'gx','gy','gz'}, use_global_device_ids=true, to_apply=%region_6.7 | all-reduce | flops 1 | bytes 8 | tf_op jit(solution)/shard_map/psum | solution.py:96
  607.1 1.6 broadcast_multiply_fusion
  608.7 2.3 copy.46
  612.1 1.9 copy.47
  (62 shorter events, 27.0 us)
Async XLA Ops:
  7.2 189.5 %all-reduce.3.cloned.1.call-start = ((), (), s32[]{:S(2)}) async-start(), calls=%async_computation | async-start | bytes 262144 | tf_op jit(solution)/shard_map/psum | solution.py:88
  10.5 27.4 %collective-permute-start.1 = (bf16[64,8,16,32]{0,1,3,2:T(8,128)(2,1)S(1)}, bf16[64,8,16,32]{0,1,3,2:T(8,128)(2,1)S(1)}, u32[]{:S(2)}, u32[]{:S(2)}) collective-permute-start(bf16[64,8,16,32]{0,1,3,2:T(8,128)(2,1)S(1)} %copy.96), channel_id=1, source_target_pairs={{16,0},{17,1},{18,2},{19,3},{20,4},{21,5},{22,6},{23,7},{24,8},{25... | collective-permute-start | bytes 1572872 | tf_op jit(solution)/shard_map/ppermute | solution.py:20
  11.8 27.4 %collective-permute-start = (bf16[64,8,16,32]{0,1,3,2:T(8,128)(2,1)S(1)}, bf16[64,8,16,32]{0,1,3,2:T(8,128)(2,1)S(1)}, u32[]{:S(2)}, u32[]{:S(2)}) collective-permute-start(bf16[64,8,16,32]{0,1,3,2:T(8,128)(2,1)S(1)} %copy.96), channel_id=1, source_target_pairs={{0,16},{1,17},{2,18},{3,19},{4,20},{5,21},{6,22},{7,23},{8,24},{9,... | collective-permute-start | bytes 1572872 | tf_op jit(solution)/shard_map/ppermute | solution.py:19
  40.8 3.3 collective-permute-start.2
  42.1 6.3 %collective-permute-start.3 = (bf16[64,8,8,32]{0,1,3,2:T(8,128)(2,1)S(1)}, bf16[64,8,8,32]{0,1,3,2:T(8,128)(2,1)S(1)}, u32[]{:S(2)}, u32[]{:S(2)}) collective-permute-start(bf16[64,8,8,32]{0,1,3,2:T(8,128)(2,1)S(1)} %get-tuple-element.19), channel_id=1, source_target_pairs={{4,0},{8,4},{12,8},{5,1},{9,5},{13,9},{6,2},{10,6},{14,10},{7,3},{... | collective-permute-start | bytes 786440 | tf_op jit(solution)/shard_map/ppermute | solution.py:20
  51.9 7.4 %collective-permute-start.4 = (bf16[64,8,16,8]{0,2,3,1:T(8,128)(2,1)S(1)}, bf16[64,8,16,8]{0,2,3,1:T(8,128)(2,1)S(1)}, u32[]{:S(2)}, u32[]{:S(2)}) collective-permute-start(bf16[64,8,16,8]{0,2,3,1:T(8,128)(2,1)S(1)} %get-tuple-element.16), channel_id=1, source_target_pairs={{0,1},{1,2},{2,3},{4,5},{5,6},{6,7},{8,9},{9,10},{10,11},{12,13},{... | collective-permute-start | bytes 393224 | tf_op jit(solution)/shard_map/ppermute | solution.py:19
  55.4 8.3 %collective-permute-start.5 = (bf16[64,8,16,8]{0,2,3,1:T(8,128)(2,1)S(1)}, bf16[64,8,16,8]{0,2,3,1:T(8,128)(2,1)S(1)}, u32[]{:S(2)}, u32[]{:S(2)}) collective-permute-start(bf16[64,8,16,8]{0,2,3,1:T(8,128)(2,1)S(1)} %get-tuple-element.17), channel_id=1, source_target_pairs={{1,0},{2,1},{3,2},{5,4},{6,5},{7,6},{9,8},{10,9},{11,10},{13,12},{... | collective-permute-start | bytes 393224 | tf_op jit(solution)/shard_map/ppermute | solution.py:20
  63.7 2.2 copy-start
  67.5 434.6 %all-reduce.5.cloned.1.call-start = ((), (), s32[]{:S(2)}) async-start(), calls=%async_computation.1 | async-start | bytes 262144 | tf_op jit(solution)/shard_map/psum | solution.py:88
  201.5 26.1 %collective-permute-start.7 = (bf16[64,8,16,32]{0,1,3,2:T(8,128)(2,1)S(1)}, bf16[64,8,16,32]{0,1,3,2:T(8,128)(2,1)S(1)}, u32[]{:S(2)}, u32[]{:S(2)}) collective-permute-start(bf16[64,8,16,32]{0,1,3,2:T(8,128)(2,1)S(1)} %copy.28), channel_id=1, source_target_pairs={{16,0},{17,1},{18,2},{19,3},{20,4},{21,5},{22,6},{23,7},{24,8},{25... | collective-permute-start | bytes 1572872 | tf_op jit(solution)/shard_map/ppermute | solution.py:20
  203.0 26.0 %collective-permute-start.6 = (bf16[64,8,16,32]{0,1,3,2:T(8,128)(2,1)S(1)}, bf16[64,8,16,32]{0,1,3,2:T(8,128)(2,1)S(1)}, u32[]{:S(2)}, u32[]{:S(2)}) collective-permute-start(bf16[64,8,16,32]{0,1,3,2:T(8,128)(2,1)S(1)} %copy.28), channel_id=1, source_target_pairs={{0,16},{1,17},{2,18},{3,19},{4,20},{5,21},{6,22},{7,23},{8,24},{9,... | collective-permute-start | bytes 1572872 | tf_op jit(solution)/shard_map/ppermute | solution.py:19
  230.6 4.4 copy-start.2
  231.6 5.0 collective-permute-start.8
  233.7 5.0 collective-permute-start.9
  240.4 7.2 %copy-start.5 = (f32[64,512]{1,0:T(8,128)S(1)}, f32[64,512]{1,0:T(8,128)}, u32[]{:S(2)}) copy-start(f32[64,512]{1,0:T(8,128)} %all-reduce.3.cloned.1.call-done) | copy-start | bytes 393220
  244.2 6.3 %collective-permute-start.10 = (bf16[64,8,16,8]{0,2,3,1:T(8,128)(2,1)}, bf16[64,8,16,8]{0,2,3,1:T(8,128)(2,1)S(1)}, u32[]{:S(2)}, u32[]{:S(2)}) collective-permute-start(bf16[64,8,16,8]{0,2,3,1:T(8,128)(2,1)} %get-tuple-element.12), channel_id=1, source_target_pairs={{0,1},{1,2},{2,3},{4,5},{5,6},{6,7},{8,9},{9,10},{10,11},{12,13},{... | collective-permute-start | bytes 393224 | tf_op jit(solution)/shard_map/ppermute | solution.py:19
  246.4 8.6 %collective-permute-start.11 = (bf16[64,8,16,8]{0,2,3,1:T(8,128)(2,1)}, bf16[64,8,16,8]{0,2,3,1:T(8,128)(2,1)}, u32[]{:S(2)}, u32[]{:S(2)}) collective-permute-start(bf16[64,8,16,8]{0,2,3,1:T(8,128)(2,1)} %get-tuple-element.13), channel_id=1, source_target_pairs={{1,0},{2,1},{3,2},{5,4},{6,5},{7,6},{9,8},{10,9},{11,10},{13,12},{... | collective-permute-start | bytes 393224 | tf_op jit(solution)/shard_map/ppermute | solution.py:20
  310.0 3.2 copy-start.3
  320.1 26.2 %collective-permute-start.13 = (bf16[64,8,16,32]{0,1,3,2:T(8,128)(2,1)S(1)}, bf16[64,8,16,32]{0,1,3,2:T(8,128)(2,1)S(1)}, u32[]{:S(2)}, u32[]{:S(2)}) collective-permute-start(bf16[64,8,16,32]{0,1,3,2:T(8,128)(2,1)S(1)} %copy.36), channel_id=1, source_target_pairs={{16,0},{17,1},{18,2},{19,3},{20,4},{21,5},{22,6},{23,7},{24,8},{25... | collective-permute-start | bytes 1572872 | tf_op jit(solution)/shard_map/ppermute | solution.py:20
  321.4 26.1 %collective-permute-start.12 = (bf16[64,8,16,32]{0,1,3,2:T(8,128)(2,1)S(1)}, bf16[64,8,16,32]{0,1,3,2:T(8,128)(2,1)S(1)}, u32[]{:S(2)}, u32[]{:S(2)}) collective-permute-start(bf16[64,8,16,32]{0,1,3,2:T(8,128)(2,1)S(1)} %copy.36), channel_id=1, source_target_pairs={{0,16},{1,17},{2,18},{3,19},{4,20},{5,21},{6,22},{7,23},{8,24},{9,... | collective-permute-start | bytes 1572872 | tf_op jit(solution)/shard_map/ppermute | solution.py:19
  349.2 2.8 collective-permute-start.14
  350.5 4.9 collective-permute-start.15
  358.9 6.7 %collective-permute-start.16 = (bf16[64,8,16,8]{0,2,3,1:T(8,128)(2,1)S(1)}, bf16[64,8,16,8]{0,2,3,1:T(8,128)(2,1)S(1)}, u32[]{:S(2)}, u32[]{:S(2)}) collective-permute-start(bf16[64,8,16,8]{0,2,3,1:T(8,128)(2,1)S(1)} %get-tuple-element.8), channel_id=1, source_target_pairs={{0,1},{1,2},{2,3},{4,5},{5,6},{6,7},{8,9},{9,10},{10,11},{12,13},{... | collective-permute-start | bytes 393224 | tf_op jit(solution)/shard_map/ppermute | solution.py:19
  361.7 8.3 %collective-permute-start.17 = (bf16[64,8,16,8]{0,2,3,1:T(8,128)(2,1)S(1)}, bf16[64,8,16,8]{0,2,3,1:T(8,128)(2,1)S(1)}, u32[]{:S(2)}, u32[]{:S(2)}) collective-permute-start(bf16[64,8,16,8]{0,2,3,1:T(8,128)(2,1)S(1)} %get-tuple-element.9), channel_id=1, source_target_pairs={{1,0},{2,1},{3,2},{5,4},{6,5},{7,6},{9,8},{10,9},{11,10},{13,12},{... | collective-permute-start | bytes 393224 | tf_op jit(solution)/shard_map/ppermute | solution.py:20
  370.0 2.2 copy-start.1
  503.0 3.6 copy-start.7
  507.8 26.1 %collective-permute-start.19 = (bf16[64,8,16,32]{0,1,3,2:T(8,128)(2,1)S(1)}, bf16[64,8,16,32]{0,1,3,2:T(8,128)(2,1)S(1)}, u32[]{:S(2)}, u32[]{:S(2)}) collective-permute-start(bf16[64,8,16,32]{0,1,3,2:T(8,128)(2,1)S(1)} %copy.41), channel_id=1, source_target_pairs={{16,0},{17,1},{18,2},{19,3},{20,4},{21,5},{22,6},{23,7},{24,8},{25... | collective-permute-start | bytes 1572872 | tf_op jit(solution)/shard_map/ppermute | solution.py:20
  509.1 26.0 %collective-permute-start.18 = (bf16[64,8,16,32]{0,1,3,2:T(8,128)(2,1)S(1)}, bf16[64,8,16,32]{0,1,3,2:T(8,128)(2,1)S(1)}, u32[]{:S(2)}, u32[]{:S(2)}) collective-permute-start(bf16[64,8,16,32]{0,1,3,2:T(8,128)(2,1)S(1)} %copy.41), channel_id=1, source_target_pairs={{0,16},{1,17},{2,18},{3,19},{4,20},{5,21},{6,22},{7,23},{8,24},{9,... | collective-permute-start | bytes 1572872 | tf_op jit(solution)/shard_map/ppermute | solution.py:19
  536.8 2.8 collective-permute-start.20
  538.1 5.5 collective-permute-start.21
  544.0 6.5 %copy-start.6 = (f32[64,512]{1,0:T(8,128)S(1)}, f32[64,512]{1,0:T(8,128)}, u32[]{:S(2)}) copy-start(f32[64,512]{1,0:T(8,128)} %all-reduce.5.cloned.1.call-done) | copy-start | bytes 393220
  547.1 6.0 collective-permute-start.22
  549.2 8.3 %collective-permute-start.23 = (bf16[64,8,16,8]{0,2,3,1:T(8,128)(2,1)S(1)}, bf16[64,8,16,8]{0,2,3,1:T(8,128)(2,1)S(1)}, u32[]{:S(2)}, u32[]{:S(2)}) collective-permute-start(bf16[64,8,16,8]{0,2,3,1:T(8,128)(2,1)S(1)} %get-tuple-element.5), channel_id=1, source_target_pairs={{1,0},{2,1},{3,2},{5,4},{6,5},{7,6},{9,8},{10,9},{11,10},{13,12},{... | collective-permute-start | bytes 393224 | tf_op jit(solution)/shard_map/ppermute | solution.py:20
  608.7 2.3 copy-start.4
Sparse Core Ops, SparseCore 0:
  67.6 129.0 all-reduce.2
  373.8 128.1 all-reduce.4
where the time goes:
time: 631 us; the launch traced here: 621 us
  waiting for transfers between devices  383 us (61%)
  blocking collectives  93.6 us (15%)
  starting transfers between devices  51.6 us (8%)
  matrix products  42.8 us (7%)
  local copies, waits for them, and re-layouts  20.9 us (3%)
  between operations  18.2 us (3%)
  other arithmetic  11.2 us (2%)
    psum x2, waiting for transfers between devices, per_device(): courses = lax.psum(partial_courses, ('gx', 'gy', 'gz'))  257 us
    ppermute x12, waiting for transfers between devices, extended(): after = lax.ppermute(leading, axis, down)  113 us
    psum x2, blocking collectives, per_device(): energy = lax.psum(jnp.sum(grad * grad), ('gx', 'gy', 'gz')) / all_cells  93.6 us
    ppermute x12, starting transfers between devices, extended(): before = lax.ppermute(last, axis, up)  35.6 us
    dot_general x12, matrix products, filter_along(): jnp.tensordot(field, band, axes=((axis,), (0,)), precision=lax.Precision....  24.9 us
    ppermute x12, starting transfers between devices, extended(): after = lax.ppermute(leading, axis, down)  15.9 us
    ppermute x12, waiting for transfers between devices, extended(): before = lax.ppermute(last, axis, up)  12.7 us
  transfers between devices with their start and end apart: 26, of which 24 were waited for; matrix products, arithmetic and copies ran while one was open for 1% of the time, Pallas kernels for 0%

commit v1 on v0

v1 whole, which is shorter than its diff:
```python
import functools
import math

import jax
import jax.numpy as jnp
import ml_dtypes
import numpy as np
from jax import lax
from jax.experimental import pallas as pl
from jax.experimental.pallas import tpu as pltpu
from jax.sharding import PartitionSpec as P

RADIUS = 8
F32 = jnp.float32
BF16 = jnp.bfloat16
AXES = ("gx", "gy", "gz")


def band(length):
    total = sum(math.exp(-float(d * d) / 32.0) for d in range(-RADIUS, RADIUS + 1))
    gap = np.abs(np.arange(length)[:, None] - np.arange(length)[None, :])
    return np.where(gap <= RADIUS, np.exp(-(gap.astype(np.float64) ** 2) / 32.0) / total, 0.0)


def windows(matrix, size, parts, reach):
    padded = np.pad(matrix, ((0, 0), (reach, reach)))
    return np.stack(
        [padded[p * size : (p + 1) * size, p * size : (p + 1) * size + 2 * reach] for p in range(parts)]
    )


def half(array):
    return np.asarray(array, dtype=ml_dtypes.bfloat16)


def inner_window(size):
    return windows(band(3 * size), size, 3, RADIUS)[1]


def vmem(count):
    return [pl.BlockSpec(memory_space=pltpu.VMEM)] * count


def call(body, shapes, smem, arrays, flops=10**8, name=None):
    total = sum(a.size * a.dtype.itemsize for a in arrays)
    return pl.pallas_call(
        body,
        out_shape=shapes,
        in_specs=[pl.BlockSpec(memory_space=pltpu.SMEM)] * len(smem) + vmem(len(arrays)),
        out_specs=jax.tree.map(lambda _: pl.BlockSpec(memory_space=pltpu.VMEM), shapes),
        compiler_params=pltpu.CompilerParams(vmem_limit_bytes=40 * 1024 * 1024),
        cost_estimate=pl.CostEstimate(flops=flops, bytes_accessed=total, transcendentals=0),
        name=name,
    )(*smem, *arrays)


def dot(a, b):
    return jnp.dot(a, b, preferred_element_type=F32)


def pack_maps(voxel_maps, layers, chans, plane):
    def body(src, out):
        unit = (
            lax.broadcasted_iota(jnp.int32, (chans, chans), 0)
            == lax.broadcasted_iota(jnp.int32, (chans, chans), 1)
        ).astype(F32).astype(BF16)
        for x in range(layers):
            turned = lax.dot_general(
                unit, src[x].astype(BF16), (((1,), (1,)), ((), ())), preferred_element_type=F32
            )
            out[x * chans : (x + 1) * chans, :] = turned.astype(BF16)

    return call(body, jax.ShapeDtypeStruct((layers * chans, plane), BF16), [], [voxel_maps], name="pack_maps")


def mix_layers(place, coefs, chans, sources, sums, out_types):
    rows, plane = sources[0].shape
    outs = len(out_types)
    base = len(sources)
    tall, wide = 16, 128

    def body(place_ref, *refs):
        ins, adds, results = refs[:base], refs[base : base + len(sums)], refs[base + len(sums) :]

        def run(tables):
            layers = tables[0][0].shape[0]
            for r in range(0, chans, tall):
                for c in range(0, plane, wide):
                    tiles = [
                        [
                            src[s * chans + r : s * chans + r + tall, c : c + wide].astype(F32)
                            for s in range(layers)
                        ]
                        for src in ins
                    ]
                    for o in range(outs):
                        for x in range(layers):
                            at = slice(x * chans + r, x * chans + r + tall)
                            total = adds[o][at, c : c + wide] if adds else None
                            for tile, table in zip(tiles, tables[o]):
                                for s in range(layers):
                                    weight = float(table[x, s])
                                    if weight != 0.0:
                                        term = tile[s] * weight
                                        total = term if total is None else total + term
                            if total is None:
                                total = jnp.zeros((tall, wide), F32)
                            results[o][at, c : c + wide] = total.astype(results[o].dtype)

        if len(coefs) == 1:
            run(coefs[0])
        else:
            for v in range(len(coefs)):
                pl.when(place_ref[0] == v)(functools.partial(run, coefs[v]))

    shapes = tuple(jax.ShapeDtypeStruct((rows, plane), t) for t in out_types)
    return call(body, shapes, [place], [*sources, *sums], name="mix_layers")


def blocks_dot(pieces, table, out_type, name):
    rows, plane = (pieces[0].shape[0], table.shape[1])

    def body(*refs):
        ins, weights, out = refs[:-2], refs[-2], refs[-1]
        at, total = 0, None
        for piece in ins:
            width = piece.shape[1]
            term = dot(piece[...], weights[at : at + width, :])
            total = term if total is None else total + term
            at += width
        out[...] = total.astype(out.dtype)

    return call(body, jax.ShapeDtypeStruct((rows, plane), out_type), [], [*pieces, table], name=name)


def live_lanes(count, layer, shape, size_y, size_z):
    row = layer * size_y + lax.broadcasted_iota(jnp.int32, shape, 1) // size_z
    return row < count


def courses_of(count, acc, pieces, table, bold, chans, size_y, size_z):
    frames = bold.shape[1]
    plane = size_y * size_z
    layers = bold.shape[0] // plane

    def body(count_ref, *refs):
        ins = refs[: len(pieces)]
        rest = refs[len(pieces) :]
        weights, frames_ref, out = rest[0], rest[1], rest[-1]
        start = rest[2] if acc is not None else None
        total = jnp.zeros((chans, frames), F32)
        for x in range(layers):
            rows = slice(x * chans, (x + 1) * chans)
            value = start[rows, :] if start is not None else None
            at = 0
            for piece in ins:
                width = piece.shape[1]
                term = dot(piece[rows, :], weights[at : at + width, :])
                value = term if value is None else value + term
                at += width
            keep = live_lanes(count_ref[0], x, value.shape, size_y, size_z)
            value = jnp.where(keep, value, 0.0).astype(BF16)
            total = total + dot(value, frames_ref[x * plane : (x + 1) * plane, :])
        out[...] = total

    arrays = [*pieces, table, bold] + ([acc] if acc is not None else [])
    return call(
        body, jax.ShapeDtypeStruct((chans, frames), F32), [count], arrays, flops=10**9, name="courses_of"
    )


def raw_gradient(count, courses, bold, size_y, size_z):
    chans, frames = courses.shape
    plane = size_y * size_z
    layers = bold.shape[0] // plane

    def body(count_ref, courses_ref, frames_ref, out):
        for x in range(layers):
            value = lax.dot_general(
                courses_ref[...],
                frames_ref[x * plane : (x + 1) * plane, :],
                (((1,), (1,)), ((), ())),
                preferred_element_type=F32,
            )
            keep = live_lanes(count_ref[0], x, value.shape, size_y, size_z)
            out[x * chans : (x + 1) * chans, :] = jnp.where(keep, value, 0.0).astype(BF16)

    return call(
        body,
        jax.ShapeDtypeStruct((layers * chans, plane), BF16),
        [count],
        [courses, bold],
        flops=10**9,
        name="raw_gradient",
    )


def gradient_of(acc, pieces, table, chans):
    rows, plane = acc.shape
    layers = rows // chans

    def body(start, *refs):
        ins, weights, out, energy = refs[:-3], refs[-3], refs[-2], refs[-1]
        total = jnp.zeros((chans, plane), F32)
        for x in range(layers):
            at, value = 0, start[x * chans : (x + 1) * chans, :]
            for piece in ins:
                width = piece.shape[1]
                value = value + dot(piece[x * chans : (x + 1) * chans, :], weights[at : at + width, :])
                at += width
            total = total + value * value
            out[x] = value.T
        energy[...] = jnp.sum(total).reshape(1, 1)

    shapes = (jax.ShapeDtypeStruct((layers, plane, chans), F32), jax.ShapeDtypeStruct((1, 1), F32))
    return call(body, shapes, [], [acc, *pieces, table], name="gradient_of")


def base_maps(voxel_maps, grad, first, second):
    layers, plane, chans = voxel_maps.shape

    def body(maps_ref, grad_ref, first_ref, second_ref, out):
        for x in range(layers):
            out[x] = lax.dot_general(
                maps_ref[x],
                first_ref[...],
                (((1,), (1,)), ((), ())),
                precision=lax.Precision.HIGHEST,
                preferred_element_type=F32,
            ) + lax.dot_general(
                grad_ref[x],
                second_ref[...],
                (((1,), (1,)), ((), ())),
                precision=lax.Precision.HIGHEST,
                preferred_element_type=F32,
            )

    return call(
        body,
        jax.ShapeDtypeStruct((layers, plane, chans), F32),
        [],
        [voxel_maps, grad, first, second],
        flops=10**9,
        name="base_maps",
    )


def final_maps(scale, base, grad):
    layers, plane, chans = base.shape

    def body(scale_ref, base_ref, grad_ref, out):
        out[...] = base_ref[...] + scale_ref[0] * grad_ref[...]

    return call(
        body, jax.ShapeDtypeStruct((layers, plane, chans), F32), [scale], [base, grad], name="final_maps"
    )


def shifted(lower, upper, axis):
    peers = lax.axis_size(axis)
    up = [(i, i + 1) for i in range(peers - 1)]
    down = [(j, i) for i, j in up]
    return lax.ppermute(upper, axis, up), lax.ppermute(lower, axis, down)


def hypercube_sum(value, narrow):
    steps = []
    for axis in AXES:
        peers = lax.axis_size(axis)
        if peers & (peers - 1):
            return lax.psum(value, AXES)
        steps += [(axis, 1 << b) for b in range(peers.bit_length() - 1)]
    for axis, bit in steps:
        pairs = [(i, i ^ bit) for i in range(lax.axis_size(axis))]
        if narrow:
            value = lax.reduce_precision(value, 8, 7)
            value = value + lax.ppermute(value.astype(BF16), axis, pairs).astype(F32)
        else:
            value = value + lax.ppermute(value, axis, pairs)
    return value


def per_device(bold_data, spatial_maps, live_blocks):
    chans, size_x, size_y, size_z = spatial_maps.shape
    frames = bold_data.shape[3]
    plane = size_y * size_z
    parts_x, parts_y, parts_z = (lax.axis_size(a) for a in AXES)
    place_x = lax.axis_index("gx").astype(jnp.int32).reshape(1)
    count = live_blocks.reshape(1)
    bold = bold_data.reshape(size_x * plane, frames)
    voxel_maps = jnp.transpose(spatial_maps, (1, 2, 3, 0)).reshape(size_x, plane, chans)
    all_cells = float(chans * size_x * plane * parts_x * parts_y * parts_z)

    win_x, win_y, win_z = (inner_window(s) for s in (size_x, size_y, size_z))
    unit_z = np.eye(size_z)
    ends = np.concatenate([np.kron(win_y.T, unit_z[:, :RADIUS]), np.kron(win_y.T, unit_z[:, -RADIUS:])], 1)
    table_ends = jnp.asarray(half(ends))
    table_own = jnp.asarray(half(np.kron(win_y.T, win_z[:, RADIUS:-RADIUS].T)))
    unit_y = np.eye(size_y)
    table_z = jnp.asarray(
        half(np.concatenate([np.kron(unit_y, win_z[:, :RADIUS].T), np.kron(unit_y, win_z[:, -RADIUS:].T)]))
    )
    face_y, face_z = RADIUS * size_z, RADIUS * size_y

    reach = 2 * RADIUS
    twice = parts_x == 2 and size_y == reach and size_z == 2 * reach
    pair_x = parts_x == 2
    full_x = band(size_x * parts_x)
    own_x = [slice(p * size_x, (p + 1) * size_x) for p in range(parts_x)]

    def coefs_x(matrices):
        mine = [[[m[own_x[p], own_x[p]]] for m in matrices] for p in range(2)]
        other = [[[m[own_x[p], own_x[1 - p]]] for m in matrices] for p in range(2)]
        return mine, other

    def along_x(block, matrices):
        if pair_x:
            mine, other = coefs_x(matrices)
            got = lax.ppermute(block, "gx", [(0, 1), (1, 0)])
            sums = mix_layers(place_x, mine, chans, [block], [], [F32] * len(matrices))
            return mix_layers(place_x, other, chans, [got], list(sums), [BF16] * len(matrices))
        depth = RADIUS * chans
        before, after = shifted(block[:depth], block[-depth:], "gx")
        rest = jnp.zeros((block.shape[0] - depth, plane), BF16)
        before, after = jnp.concatenate([rest, before]), jnp.concatenate([after, rest])
        tables = []
        for lo in (-size_x, 0, size_x):
            columns = np.arange(size_x) + lo + RADIUS
            inside = (columns >= 0) & (columns < win_x.shape[1])
            tables.append(np.where(inside[None], win_x[:, np.clip(columns, 0, win_x.shape[1] - 1)], 0.0))
        return mix_layers(place_x, [[tables]], chans, [before, block, after], [], [BF16])

    def along_rest(first):
        before, after = shifted(first[:, :face_y], first[:, -face_y:], "gy")
        pieces = [before, first, after]
        faces = blocks_dot(pieces, table_ends, BF16, "faces_z")
        below, above = shifted(faces[:, :face_z], faces[:, face_z:], "gz")
        acc = blocks_dot(pieces, table_own, F32, "filter_own")
        return acc, [below, above]

    def all_courses(acc, pieces, table):
        return hypercube_sum(
            courses_of(count, acc, pieces, table, bold, chans, size_y, size_z), narrow=True
        )

    plain = pack_maps(voxel_maps, size_x, chans, plane)
    (first,) = along_x(plain, [full_x])
    acc, pieces = along_rest(first)
    courses1 = all_courses(acc, pieces, table_z)
    half1 = courses1.astype(BF16)
    raw1 = raw_gradient(count, half1, bold, size_y, size_z)
    if twice:
        first, second = along_x(raw1, [full_x, full_x @ full_x])
        square_y = windows(np.linalg.matrix_power(band(size_y * parts_y), 2), size_y, parts_y, reach)
        square_z = windows(np.linalg.matrix_power(band(size_z * parts_z), 2), size_z, parts_z, reach)
        ordered = np.concatenate([unit_z[:, :reach], unit_z[:, reach:]], 1).reshape(size_z, 2, reach)
        tables_y = np.stack([
            np.concatenate([np.kron(w.T, ordered[:, h]) for h in range(2)], 1) for w in square_y
        ])
        tables_z = np.stack([
            np.concatenate([np.kron(unit_y, w[:, h * reach : (h + 1) * reach].T) for h in range(4)])
            for w in square_z
        ])
        table_y2 = lax.dynamic_index_in_dim(jnp.asarray(half(tables_y)), lax.axis_index("gy"), 0, False)
        table_z2 = lax.dynamic_index_in_dim(jnp.asarray(half(tables_z)), lax.axis_index("gz"), 0, False)
        before, after = shifted(second, second, "gy")
        both = blocks_dot([before, second, after], table_y2, BF16, "filter_y2")
        wide = reach * size_y
        lower, upper = both[:, :wide], both[:, wide:]
        below, above = shifted(lower, upper, "gz")
        change = all_courses(None, [below, lower, upper, above], table_z2)
        acc1, pieces1 = along_rest(first)
        grad1, _ = gradient_of(acc1, pieces1, table_z, chans)
    else:
        (first,) = along_x(raw1, [full_x])
        acc1, pieces1 = along_rest(first)
        grad1, _ = gradient_of(acc1, pieces1, table_z, chans)
        again = pack_maps(grad1, size_x, chans, plane)
        (second,) = along_x(again, [full_x])
        acc2, pieces2 = along_rest(second)
        change = all_courses(acc2, pieces2, table_z)

    def gram_of(courses):
        gram = jnp.dot(courses, courses.T, precision=lax.Precision.HIGHEST)
        return 0.5 * (float(chans) / jnp.trace(gram)) * gram

    unit = jnp.eye(chans, dtype=F32)
    gram1 = gram_of(courses1)
    energy1 = jnp.maximum(jnp.sum(half1.astype(F32) * change), 0.0) / all_cells
    scale1 = 0.5 / jnp.sqrt(energy1 + 1e-06)
    kept = courses1 - jnp.dot(gram1, courses1, precision=lax.Precision.HIGHEST)

    courses2 = kept + scale1 * change
    half2 = courses2.astype(BF16)
    raw2 = raw_gradient(count, half2, bold, size_y, size_z)
    (first,) = along_x(raw2, [full_x])
    acc, pieces = along_rest(first)
    grad2, squares = gradient_of(acc, pieces, table_z, chans)
    energy2 = hypercube_sum(squares, narrow=False) / all_cells
    scale2 = (0.5 / jnp.sqrt(energy2 + 1e-06)).reshape(1)

    fade2 = unit - gram_of(courses2)
    fades = jnp.dot(fade2, unit - gram1, precision=lax.Precision.HIGHEST)
    base = base_maps(voxel_maps, grad1, fades, scale1 * fade2)
    maps = final_maps(scale2, base, grad2).reshape(size_x, size_y, size_z, chans)
    return (jnp.transpose(maps, (3, 0, 1, 2)), half2)


def solution(mesh):
    return jax.shard_map(
        per_device,
        mesh=mesh,
        in_specs=(P("gx", "gy", "gz", None), P(None, "gx", "gy", "gz"), P("gx", "gy", "gz")),
        out_specs=(P(None, "gx", "gy", "gz"), P()),
        check_vma=False,
    )
```

time: 631 us -> 203 us (0.32); the launches traced: 621 us -> 202 us
  waiting for transfers between devices: 383 us -> 65.3 us
  blocking collectives: 93.6 us -> 0 us
  matrix products: 42.8 us -> 3.18 us
  Pallas kernels: 0 us -> 29.6 us
  starting transfers between devices: 51.6 us -> 77.2 us
  between operations: 18.2 us -> 7.86 us
  other arithmetic: 11.2 us -> 0.99 us
    psum x2 -> x0, waiting for transfers between devices: 257 us -> none  [per_device(): courses = lax.psum(partial_courses, ('gx', 'gy', 'gz'))]
    psum x2 -> x0, blocking collectives: 93.6 us -> none  [per_device(): energy = lax.psum(jnp.sum(grad * grad), ('gx', 'gy', 'gz')) / all_cells]
    ppermute x24 -> x34, waiting for transfers between devices: 125 us -> 65.3 us  [the longest x16 21.9 us: shifted(): return (lax.ppermute(upper, axis, up), lax.ppermute(lower, axis, down))]
    dot_general x20 -> x4, matrix products: 42.8 us -> 3.18 us  [the longest x2 1.82 us: gram_of(): gram = jnp.dot(courses, courses.T, precision=lax.Precision.HIGHEST)]
    pallas_call x0 -> x22, Pallas kernels: none -> 29.6 us  [call(): pl.pallas_call(body, out_shape=shapes, in_specs=[pl.BlockSpec(memory_spac...]
    ppermute x24 -> x34, starting transfers between devices: 51.5 us -> 77.2 us  [the longest x16 32.8 us: shifted(): return (lax.ppermute(upper, axis, up), lax.ppermute(lower, axis, down))]
    unnamed x17 -> x50, local copies, waits for them, and re-layouts: 4.93 us -> 12.9 us
  transfers between devices with their start and end apart: 26 -> 34, of which waited for: 24 -> 24; matrix products, arithmetic and copies ran while one was open for 1% -> 4% of each run, Pallas kernels for 0% -> 7%
where the time goes in v1:
time: 203 us; the launch traced here: 202 us
  starting transfers between devices  77.2 us (38%)
  waiting for transfers between devices  65.3 us (32%)
  Pallas kernels  29.6 us (15%)
  local copies, waits for them, and re-layouts  18.2 us (9%)
  between operations  7.86 us (4%)
  matrix products  3.18 us (2%)
    ppermute x16, starting transfers between devices, shifted(): return (lax.ppermute(upper, axis, up), lax.ppermute(lower, axis, down))  32.8 us
    pallas_call x22, Pallas kernels, call(): pl.pallas_call(body, out_shape=shapes, in_specs=[pl.BlockSpec(memory_spac...  29.6 us
    ppermute x10, starting transfers between devices, hypercube_sum(): value = value + lax.ppermute(value.astype(BF16), axis, pairs).astype(F32)  22.7 us
    ppermute x16, waiting for transfers between devices, shifted(): return (lax.ppermute(upper, axis, up), lax.ppermute(lower, axis, down))  21.9 us
    ppermute x3, waiting for transfers between devices, along_x(): got = lax.ppermute(block, 'gx', [(0, 1), (1, 0)])  20 us
    ppermute x10, waiting for transfers between devices, hypercube_sum(): value = value + lax.ppermute(value.astype(BF16), axis, pairs).astype(F32)  19 us
    ppermute x5, starting transfers between devices, hypercube_sum(): value = value + lax.ppermute(value, axis, pairs)  15.5 us
    unnamed x50, local copies, waits for them, and re-layouts  12.9 us
  transfers between devices with their start and end apart: 34, of which 24 were waited for; matrix products, arithmetic and copies ran while one was open for 4% of the time, Pallas kernels for 7%

profile of v1, /device:TPU:0, one launch (start us, length us, event | category | flops | bytes accessed | tf_op | source)
XLA Modules:
  0.0 202.3 jit_solution(4170417979220655392)
XLA Ops:
  0.6 1.6 copy-done.4
  2.7 3.0 %collective-permute-start = (bf16[512,512]{1,0:T(8,128)(2,1)S(1)}, bf16[512,512]{1,0:T(8,128)(2,1)S(1)}, u32[]{:S(2)}, u32[]{:S(2)}) collective-permute-start(bf16[512,512]{1,0:T(8,128)(2,1)S(1)} %pack_maps.1.refs_0_), channel_id=1, source_target_pairs={{0,16},{16,0},{1,17},{17,1},{2,18},{18,2},{3,19},{19,3},{4,20},{20... | collective-permute-start | bytes 1572872 | tf_op jit(solution)/shard_map/ppermute | solution.py:319
  6.3 11.4 %collective-permute-done.refs_0_ = bf16[512,512]{1,0:T(8,128)(2,1)S(1)} collective-permute-done((bf16[512,512]{1,0:T(8,128)(2,1)S(1)}, bf16[512,512]{1,0:T(8,128)(2,1)S(1)}, u32[]{:S(2)}, u32[]{:S(2)}) %collective-permute-start) | collective-permute-done | bytes 524320 | tf_op jit(solution)/shard_map/ppermute | solution.py:319
  18.1 1.4 collective-permute-start.1
  19.6 1.3 collective-permute-start.2
  20.9 4.1 %collective-permute-done.2.refs_2_ = bf16[512,256]{1,0:T(8,128)(2,1)S(1)} collective-permute-done((bf16[512,256]{1,0:T(8,128)(2,1)S(1)}, bf16[512,256]{1,0:T(8,128)(2,1)S(1)}, u32[]{:S(2)}, u32[]{:S(2)}) %collective-permute-start.2) | collective-permute-done | bytes 262176 | tf_op jit(solution)/shard_map/ppermute | solution.py:263
  25.4 3.8 %collective-permute-start.3 = (bf16[512,128]{1,0:T(8,128)(2,1)S(1)}, bf16[512,128]{1,0:T(8,128)(2,1)S(1)}, u32[]{:S(2)}, u32[]{:S(2)}) collective-permute-start(bf16[512,128]{1,0:T(8,128)(2,1)S(1)} %get-tuple-element.33), channel_id=1, source_target_pairs={{0,1},{1,2},{2,3},{4,5},{5,6},{6,7},{8,9},{9,10},{10,11},{12,13},{... | collective-permute-start | bytes 393224 | tf_op jit(solution)/shard_map/ppermute | solution.py:263
  29.2 1.3 collective-permute-start.4
  31.8 4.2 %collective-permute-done.4.refs_1_ = bf16[512,128]{1,0:T(8,128)(2,1)S(1)} collective-permute-done((bf16[512,128]{1,0:T(8,128)(2,1)S(1)}, bf16[512,128]{1,0:T(8,128)(2,1)S(1)}, u32[]{:S(2)}, u32[]{:S(2)}) %collective-permute-start.4) | collective-permute-done | bytes 131104 | tf_op jit(solution)/shard_map/ppermute | solution.py:263
  36.0 1.7 courses_of.2
  37.8 1.6 collective-permute-start.5
  39.4 2.7 %collective-permute-done.5 = bf16[64,512]{1,0:T(8,128)(2,1)S(1)} collective-permute-done((bf16[64,512]{1,0:T(8,128)(2,1)S(1)}, bf16[64,512]{1,0:T(8,128)(2,1)S(1)}, u32[]{:S(2)}, u32[]{:S(2)}) %collective-permute-start.5) | collective-permute-done | bytes 65568 | tf_op jit(solution)/shard_map/ppermute | solution.py:277
  42.2 2.2 %collective-permute-start.6 = (bf16[64,512]{1,0:T(8,128)(2,1)S(1)}, bf16[64,512]{1,0:T(8,128)(2,1)S(1)}, u32[]{:S(2)}, u32[]{:S(2)}) collective-permute-start(bf16[64,512]{1,0:T(8,128)(2,1)S(1)} %fusion.9), channel_id=1, source_target_pairs={{0,4},{4,0},{8,12},{12,8},{1,5},{5,1},{9,13},{13,9},{2,6},{6,2},{1... | collective-permute-start | bytes 196616 | tf_op jit(solution)/shard_map/ppermute | solution.py:277
  45.4 2.7 %collective-permute-start.7 = (bf16[64,512]{1,0:T(8,128)(2,1)S(1)}, bf16[64,512]{1,0:T(8,128)(2,1)S(1)}, u32[]{:S(2)}, u32[]{:S(2)}) collective-permute-start(bf16[64,512]{1,0:T(8,128)(2,1)S(1)} %fusion.1), channel_id=1, source_target_pairs={{0,8},{4,12},{8,0},{12,4},{1,9},{5,13},{9,1},{13,5},{2,10},{6,14},... | collective-permute-start | bytes 196616 | tf_op jit(solution)/shard_map/ppermute | solution.py:277
  48.1 2.4 %collective-permute-done.7 = bf16[64,512]{1,0:T(8,128)(2,1)S(1)} collective-permute-done((bf16[64,512]{1,0:T(8,128)(2,1)S(1)}, bf16[64,512]{1,0:T(8,128)(2,1)S(1)}, u32[]{:S(2)}, u32[]{:S(2)}) %collective-permute-start.7) | collective-permute-done | bytes 65568 | tf_op jit(solution)/shard_map/ppermute | solution.py:277
  50.6 1.6 collective-permute-start.8
  52.2 2.7 %collective-permute-done.8 = bf16[64,512]{1,0:T(8,128)(2,1)S(1)} collective-permute-done((bf16[64,512]{1,0:T(8,128)(2,1)S(1)}, bf16[64,512]{1,0:T(8,128)(2,1)S(1)}, u32[]{:S(2)}, u32[]{:S(2)}) %collective-permute-start.8) | collective-permute-done | bytes 65568 | tf_op jit(solution)/shard_map/ppermute | solution.py:277
  54.9 2.7 %collective-permute-start.9 = (bf16[64,512]{1,0:T(8,128)(2,1)S(1)}, bf16[64,512]{1,0:T(8,128)(2,1)S(1)}, u32[]{:S(2)}, u32[]{:S(2)}) collective-permute-start(bf16[64,512]{1,0:T(8,128)(2,1)S(1)} %fusion.2), channel_id=1, source_target_pairs={{0,2},{1,3},{2,0},{3,1},{4,6},{5,7},{6,4},{7,5},{8,10},{9,11},{10,... | collective-permute-start | bytes 196616 | tf_op jit(solution)/shard_map/ppermute | solution.py:277
  57.6 2.6 %collective-permute-done.9 = bf16[64,512]{1,0:T(8,128)(2,1)S(1)} collective-permute-done((bf16[64,512]{1,0:T(8,128)(2,1)S(1)}, bf16[64,512]{1,0:T(8,128)(2,1)S(1)}, u32[]{:S(2)}, u32[]{:S(2)}) %collective-permute-start.9) | collective-permute-done | bytes 65568 | tf_op jit(solution)/shard_map/ppermute | solution.py:277
  60.2 1.4 raw_gradient.2.refs_0_
  61.6 1.6 collective-permute-start.10
  64.2 8.6 %collective-permute-done.10.refs_0_ = bf16[512,512]{1,0:T(8,128)(2,1)S(1)} collective-permute-done((bf16[512,512]{1,0:T(8,128)(2,1)S(1)}, bf16[512,512]{1,0:T(8,128)(2,1)S(1)}, u32[]{:S(2)}, u32[]{:S(2)}) %collective-permute-start.10) | collective-permute-done | bytes 524320 | tf_op jit(solution)/shard_map/ppermute | solution.py:319
  73.8 2.1 %collective-permute-start.11 = (bf16[512,512]{1,0:T(8,128)(2,1)S(1)}, bf16[512,512]{1,0:T(8,128)(2,1)}, u32[]{:S(2)}, u32[]{:S(2)}) collective-permute-start(bf16[512,512]{1,0:T(8,128)(2,1)S(1)} %get-tuple-element.11.refs_1_), channel_id=1, source_target_pairs={{0,4},{4,8},{8,12},{1,5},{5,9},{9,13},{2,6},{6,10},{10,14},{3,7},{... | collective-permute-start | bytes 1572872 | tf_op jit(solution)/shard_map/ppermute | solution.py:263
  77.2 1.5 dynamic-slice_bitcast_fusion.refs_3_
  78.7 1.8 collective-permute-done.12.refs_2_
  81.5 2.2 %filter_y2.1 = bf16[512,512]{1,0:T(8,128)(2,1)S(1)} custom-call(bf16[512,512]{1,0:T(8,128)(2,1)} %collective-permute-done.11.refs_0_, bf16[512,512]{1,0:T(8,128)(2,1)S(1)} %copy-done.14, bf16[512,512]{1,0:T(8,128)(2,1)} %collective-permute-done.12.refs_2_, bf16[1536,512]{1,0:T(8,128)(2,1)S(1)} %dynamic-slice_bitcast_fusion.refs_3_), custom_call_target="tpu_custom_call" | custom-call | flops 100000000 | bytes 3145728 | tf_op jit(solution)/shard_map/filter_y2/pallas_call | solution.py:46
  84.4 3.5 %collective-permute-start.13 = (bf16[512,256]{1,0:T(8,128)(2,1)}, bf16[512,256]{1,0:T(8,128)(2,1)S(1)}, u32[]{:S(2)}, u32[]{:S(2)}) collective-permute-start(bf16[512,256]{1,0:T(8,128)(2,1)} %get-tuple-element.25.refs_2_), channel_id=1, source_target_pairs={{0,1},{1,2},{2,3},{4,5},{5,6},{6,7},{8,9},{9,10},{10,11},{12,13},{... | collective-permute-start | bytes 786440 | tf_op jit(solution)/shard_map/ppermute | solution.py:263
  87.9 1.5 collective-permute-start.14
  89.4 1.3 dynamic-slice_bitcast_fusion.1.refs_4_
  90.7 1.4 collective-permute-done.13.refs_0_
  92.1 4.1 %collective-permute-done.14.refs_3_ = bf16[512,256]{1,0:T(8,128)(2,1)S(1)} collective-permute-done((bf16[512,256]{1,0:T(8,128)(2,1)S(1)}, bf16[512,256]{1,0:T(8,128)(2,1)S(1)}, u32[]{:S(2)}, u32[]{:S(2)}) %collective-permute-start.14) | collective-permute-done | bytes 262176 | tf_op jit(solution)/shard_map/ppermute | solution.py:263
  96.2 2.2 %copy-done.1 = bf16[8,16,32,512]{3,2,1,0:T(8,128)(2,1)S(1)} copy-done((bf16[8,16,32,512]{3,2,1,0:T(8,128)(2,1)S(1)}, bf16[8,16,32,512]{3,2,1,0:T(8,128)(2,1)}, u32[]{:S(2)}) %copy-start.1) | copy-done | bytes 4194328
  98.4 3.8 %courses_of.3 = f32[64,512]{1,0:T(8,128)S(1)} custom-call(s32[1]{0:T(128)} %bitcast.18.count_ref, bf16[512,256]{1,0:T(8,128)(2,1)S(1)} %collective-permute-done.13.refs_0_, bf16[512,256]{1,0:T(8,128)(2,1)S(1)} %get-tuple-element.24.refs_1_, bf16[512,256]{1,0:T(8,128)(2,1)} %get-tuple-element.25.refs_2_, ...), custom_call_target="tpu_custom_call" | custom-call | flops 1000000000 | bytes 6291456 | tf_op jit(solution)/shard_map/courses_of/pallas_call | solution.py:46
  102.2 1.6 collective-permute-start.15
  103.8 2.7 %collective-permute-done.15 = bf16[64,512]{1,0:T(8,128)(2,1)S(1)} collective-permute-done((bf16[64,512]{1,0:T(8,128)(2,1)S(1)}, bf16[64,512]{1,0:T(8,128)(2,1)S(1)}, u32[]{:S(2)}, u32[]{:S(2)}) %collective-permute-start.15) | collective-permute-done | bytes 65568 | tf_op jit(solution)/shard_map/ppermute | solution.py:277
  106.5 4.7 %collective-permute-start.16 = (bf16[64,512]{1,0:T(8,128)(2,1)S(1)}, bf16[64,512]{1,0:T(8,128)(2,1)S(1)}, u32[]{:S(2)}, u32[]{:S(2)}) collective-permute-start(bf16[64,512]{1,0:T(8,128)(2,1)S(1)} %fusion.13), channel_id=1, source_target_pairs={{0,4},{4,0},{8,12},{12,8},{1,5},{5,1},{9,13},{13,9},{2,6},{6,2},{1... | collective-permute-start | bytes 196616 | tf_op jit(solution)/shard_map/ppermute | solution.py:277
  112.1 2.6 %collective-permute-start.17 = (bf16[64,512]{1,0:T(8,128)(2,1)S(1)}, bf16[64,512]{1,0:T(8,128)(2,1)S(1)}, u32[]{:S(2)}, u32[]{:S(2)}) collective-permute-start(bf16[64,512]{1,0:T(8,128)(2,1)S(1)} %fusion.3), channel_id=1, source_target_pairs={{0,8},{4,12},{8,0},{12,4},{1,9},{5,13},{9,1},{13,5},{2,10},{6,14},... | collective-permute-start | bytes 196616 | tf_op jit(solution)/shard_map/ppermute | solution.py:277
  114.8 2.4 %collective-permute-done.17 = bf16[64,512]{1,0:T(8,128)(2,1)S(1)} collective-permute-done((bf16[64,512]{1,0:T(8,128)(2,1)S(1)}, bf16[64,512]{1,0:T(8,128)(2,1)S(1)}, u32[]{:S(2)}, u32[]{:S(2)}) %collective-permute-start.17) | collective-permute-done | bytes 65568 | tf_op jit(solution)/shard_map/ppermute | solution.py:277
  117.2 1.6 collective-permute-start.18
  121.6 1.4 collective-permute-start.19
  123.8 1.3 collective-permute-start.30
  125.1 1.3 collective-permute-start.31
  129.4 2.2 %copy-done.2 = bf16[8,16,32,512]{3,2,1,0:T(8,128)(2,1)S(1)} copy-done((bf16[8,16,32,512]{3,2,1,0:T(8,128)(2,1)S(1)}, bf16[8,16,32,512]{3,2,1,0:T(8,128)(2,1)}, u32[]{:S(2)}) %copy-start.2) | copy-done | bytes 4194328
  131.6 1.4 raw_gradient.3.refs_0_
  133.0 1.6 collective-permute-start.20
  134.6 1.4 faces_z.5
  136.0 3.5 %collective-permute-start.32 = (bf16[512,128]{1,0:T(8,128)(2,1)S(1)}, bf16[512,128]{1,0:T(8,128)(2,1)S(1)}, u32[]{:S(2)}, u32[]{:S(2)}) collective-permute-start(bf16[512,128]{1,0:T(8,128)(2,1)S(1)} %get-tuple-element.29), channel_id=1, source_target_pairs={{0,1},{1,2},{2,3},{4,5},{5,6},{6,7},{8,9},{9,10},{10,11},{12,13},{... | collective-permute-start | bytes 393224 | tf_op jit(solution)/shard_map/ppermute | solution.py:263
  139.5 1.3 collective-permute-start.33
  140.8 1.7 filter_own.5.start
  143.1 4.5 %collective-permute-done.33.refs_1_ = bf16[512,128]{1,0:T(8,128)(2,1)S(1)} collective-permute-done((bf16[512,128]{1,0:T(8,128)(2,1)S(1)}, bf16[512,128]{1,0:T(8,128)(2,1)S(1)}, u32[]{:S(2)}, u32[]{:S(2)}) %collective-permute-start.33) | collective-permute-done | bytes 131104 | tf_op jit(solution)/shard_map/ppermute | solution.py:263
  148.9 1.3 copy-done.11
  152.8 2.7 %collective-permute-start.21 = (bf16[512,256]{1,0:T(8,128)(2,1)}, bf16[512,256]{1,0:T(8,128)(2,1)}, u32[]{:S(2)}, u32[]{:S(2)}) collective-permute-start(bf16[512,256]{1,0:T(8,128)(2,1)} %get-tuple-element.23), channel_id=1, source_target_pairs={{0,4},{4,8},{8,12},{1,5},{5,9},{9,13},{2,6},{6,10},{10,14},{3,7},{... | collective-permute-start | bytes 786440 | tf_op jit(solution)/shard_map/ppermute | solution.py:263
  162.0 1.5 faces_z.4
  163.5 3.8 %collective-permute-start.23 = (bf16[512,128]{1,0:T(8,128)(2,1)S(1)}, bf16[512,128]{1,0:T(8,128)(2,1)S(1)}, u32[]{:S(2)}, u32[]{:S(2)}) collective-permute-start(bf16[512,128]{1,0:T(8,128)(2,1)S(1)} %get-tuple-element.31), channel_id=1, source_target_pairs={{0,1},{1,2},{2,3},{4,5},{5,6},{6,7},{8,9},{9,10},{10,11},{12,13},{... | collective-permute-start | bytes 393224 | tf_op jit(solution)/shard_map/ppermute | solution.py:263
  167.3 1.5 collective-permute-start.24
  168.9 1.6 copy-done.12
  170.5 3.5 %base_maps.1.base_ref = f32[8,512,64]{2,1,0:T(8,128)S(1)} custom-call(f32[8,512,64]{2,1,0:T(8,128)S(1)} %bitcast.25, f32[8,512,64]{2,1,0:T(8,128)S(1)} %copy-done.12, f32[64,64]{1,0:T(8,128)S(1)} %fusion.5.first_ref, f32[64,64]{1,0:T(8,128)S(1)} %fusion.8.second_ref), custom_call_target="tpu_custom_call" | custom-call | flops 1000000000 | bytes 2129920 | tf_op jit(solution)/shard_map/base_maps/pallas_call | solution.py:46
  174.0 1.7 filter_own.4.start
  177.4 3.1 %collective-permute-done.25 = f32[1,1]{1,0:T(1,128)} collective-permute-done((f32[1,1]{1,0:T(1,128)}, f32[1,1]{1,0:T(1,128)}, u32[]{:S(2)}, u32[]{:S(2)}) %collective-permute-start.25) | collective-permute-done | bytes 36 | tf_op jit(solution)/shard_map/ppermute | solution.py:279
  181.9 4.3 %collective-permute-start.26 = (f32[1,1]{1,0:T(1,128)}, f32[1,1]{1,0:T(1,128)}, u32[]{:S(2)}, u32[]{:S(2)}) collective-permute-start(f32[1,1]{1,0:T(1,128)} %add.76), channel_id=1, source_target_pairs={{0,4},{4,0},{8,12},{12,8},{1,5},{5,1},{9,13},{13,9},{2,6},{6,2},{1... | collective-permute-start | bytes 20 | tf_op jit(solution)/shard_map/ppermute | solution.py:279
  186.8 2.6 %collective-permute-start.27 = (f32[1,1]{1,0:T(1,128)}, f32[1,1]{1,0:T(1,128)}, u32[]{:S(2)}, u32[]{:S(2)}) collective-permute-start(f32[1,1]{1,0:T(1,128)} %add.77), channel_id=1, source_target_pairs={{0,8},{4,12},{8,0},{12,4},{1,9},{5,13},{9,1},{13,5},{2,10},{6,14},... | collective-permute-start | bytes 20 | tf_op jit(solution)/shard_map/ppermute | solution.py:279
  191.0 3.7 %collective-permute-start.28 = (f32[1,1]{1,0:T(1,128)}, f32[1,1]{1,0:T(1,128)}, u32[]{:S(2)}, u32[]{:S(2)}) collective-permute-start(f32[1,1]{1,0:T(1,128)} %add.78), channel_id=1, source_target_pairs={{0,1},{1,0},{2,3},{3,2},{4,5},{5,4},{6,7},{7,6},{8,9},{9,8},{10,11... | collective-permute-start | bytes 20 | tf_op jit(solution)/shard_map/ppermute | solution.py:279
  195.6 4.4 %collective-permute-start.29 = (f32[1,1]{1,0:T(1,128)}, f32[1,1]{1,0:T(1,128)}, u32[]{:S(2)}, u32[]{:S(2)}) collective-permute-start(f32[1,1]{1,0:T(1,128)} %add.79), channel_id=1, source_target_pairs={{0,2},{1,3},{2,0},{3,1},{4,6},{5,7},{6,4},{7,5},{8,10},{9,11},{10,... | collective-permute-start | bytes 20 | tf_op jit(solution)/shard_map/ppermute | solution.py:279
  200.8 1.5 final_maps.1
  (102 shorter events, 28.2 us)
Async XLA Ops:
  0.6 1.6 copy-start.4
  2.7 15.0 %collective-permute-start = (bf16[512,512]{1,0:T(8,128)(2,1)S(1)}, bf16[512,512]{1,0:T(8,128)(2,1)S(1)}, u32[]{:S(2)}, u32[]{:S(2)}) collective-permute-start(bf16[512,512]{1,0:T(8,128)(2,1)S(1)} %pack_maps.1.refs_0_), channel_id=1, source_target_pairs={{0,16},{16,0},{1,17},{17,1},{2,18},{18,2},{3,19},{19,3},{4,20},{20... | collective-permute-start | bytes 1572872 | tf_op jit(solution)/shard_map/ppermute | solution.py:319
  5.7 19.2 %copy-start.8 = (bf16[1024,256]{1,0:T(8,128)(2,1)S(1)}, bf16[1024,256]{1,0:T(8,128)(2,1)}, u32[]{:S(2)}) copy-start(bf16[1024,256]{1,0:T(8,128)(2,1)} %constant.57.clone.refs_3_) | copy-start | bytes 1572868
  18.1 13.1 %copy-start.3 = (bf16[1024,512]{1,0:T(8,128)(2,1)S(1)}, bf16[1024,512]{1,0:T(8,128)(2,1)}, u32[]{:S(2)}) copy-start(bf16[1024,512]{1,0:T(8,128)(2,1)} %constant.58.clone.refs_3_) | copy-start | bytes 3145732
  18.1 2.7 %collective-permute-start.1 = (bf16[512,256]{1,0:T(8,128)(2,1)S(1)}, bf16[512,256]{1,0:T(8,128)(2,1)S(1)}, u32[]{:S(2)}, u32[]{:S(2)}) collective-permute-start(bf16[512,256]{1,0:T(8,128)(2,1)S(1)} %get-tuple-element.27), channel_id=1, source_target_pairs={{0,4},{4,8},{8,12},{1,5},{5,9},{9,13},{2,6},{6,10},{10,14},{3,7},{... | collective-permute-start | bytes 786440 | tf_op jit(solution)/shard_map/ppermute | solution.py:263
  19.6 5.4 %collective-permute-start.2 = (bf16[512,256]{1,0:T(8,128)(2,1)S(1)}, bf16[512,256]{1,0:T(8,128)(2,1)S(1)}, u32[]{:S(2)}, u32[]{:S(2)}) collective-permute-start(bf16[512,256]{1,0:T(8,128)(2,1)S(1)} %get-tuple-element.26), channel_id=1, source_target_pairs={{4,0},{8,4},{12,8},{5,1},{9,5},{13,9},{6,2},{10,6},{14,10},{7,3},{... | collective-permute-start | bytes 786440 | tf_op jit(solution)/shard_map/ppermute | solution.py:263
  24.9 11.1 %copy-start = (bf16[8,16,32,512]{3,2,1,0:T(8,128)(2,1)S(1)}, bf16[8,16,32,512]{3,2,1,0:T(8,128)(2,1)}, u32[]{:S(2)}) copy-start(bf16[8,16,32,512]{3,2,1,0:T(8,128)(2,1)} %param.8) | copy-start | bytes 12582916
  25.4 10.7 %copy-start.10 = (bf16[256,512]{1,0:T(8,128)(2,1)S(1)}, bf16[256,512]{1,0:T(8,128)(2,1)}, u32[]{:S(2)}) copy-start(bf16[256,512]{1,0:T(8,128)(2,1)} %constant.59.clone.refs_2_) | copy-start | bytes 786436
  25.4 6.4 %collective-permute-start.3 = (bf16[512,128]{1,0:T(8,128)(2,1)S(1)}, bf16[512,128]{1,0:T(8,128)(2,1)S(1)}, u32[]{:S(2)}, u32[]{:S(2)}) collective-permute-start(bf16[512,128]{1,0:T(8,128)(2,1)S(1)} %get-tuple-element.33), channel_id=1, source_target_pairs={{0,1},{1,2},{2,3},{4,5},{5,6},{6,7},{8,9},{9,10},{10,11},{12,13},{... | collective-permute-start | bytes 393224 | tf_op jit(solution)/shard_map/ppermute | solution.py:263
  29.2 6.9 %collective-permute-start.4 = (bf16[512,128]{1,0:T(8,128)(2,1)S(1)}, bf16[512,128]{1,0:T(8,128)(2,1)S(1)}, u32[]{:S(2)}, u32[]{:S(2)}) collective-permute-start(bf16[512,128]{1,0:T(8,128)(2,1)S(1)} %get-tuple-element.32), channel_id=1, source_target_pairs={{1,0},{2,1},{3,2},{5,4},{6,5},{7,6},{9,8},{10,9},{11,10},{13,12},{... | collective-permute-start | bytes 393224 | tf_op jit(solution)/shard_map/ppermute | solution.py:263
  37.8 4.3 %collective-permute-start.5 = (bf16[64,512]{1,0:T(8,128)(2,1)S(1)}, bf16[64,512]{1,0:T(8,128)(2,1)S(1)}, u32[]{:S(2)}, u32[]{:S(2)}) collective-permute-start(bf16[64,512]{1,0:T(8,128)(2,1)S(1)} %reduce-precision_convert_fusion.1), channel_id=1, source_target_pairs={{0,16},{16,0},{1,17},{17,1},{2,18},{18,2},{3,19},{19,3},{4,20},{20... | collective-permute-start | bytes 196616 | tf_op jit(solution)/shard_map/ppermute | solution.py:277
  42.2 3.1 %collective-permute-start.6 = (bf16[64,512]{1,0:T(8,128)(2,1)S(1)}, bf16[64,512]{1,0:T(8,128)(2,1)S(1)}, u32[]{:S(2)}, u32[]{:S(2)}) collective-permute-start(bf16[64,512]{1,0:T(8,128)(2,1)S(1)} %fusion.9), channel_id=1, source_target_pairs={{0,4},{4,0},{8,12},{12,8},{1,5},{5,1},{9,13},{13,9},{2,6},{6,2},{1... | collective-permute-start | bytes 196616 | tf_op jit(solution)/shard_map/ppermute | solution.py:277
  45.4 5.1 %collective-permute-start.7 = (bf16[64,512]{1,0:T(8,128)(2,1)S(1)}, bf16[64,512]{1,0:T(8,128)(2,1)S(1)}, u32[]{:S(2)}, u32[]{:S(2)}) collective-permute-start(bf16[64,512]{1,0:T(8,128)(2,1)S(1)} %fusion.1), channel_id=1, source_target_pairs={{0,8},{4,12},{8,0},{12,4},{1,9},{5,13},{9,1},{13,5},{2,10},{6,14},... | collective-permute-start | bytes 196616 | tf_op jit(solution)/shard_map/ppermute | solution.py:277
  50.5 68.3 %copy-start.16 = (f32[64,512]{1,0:T(8,128)}, f32[64,512]{1,0:T(8,128)S(1)}, u32[]{:S(2)}) copy-start(f32[64,512]{1,0:T(8,128)S(1)} %get-tuple-element.19) | copy-start | bytes 393220
  50.6 4.3 %collective-permute-start.8 = (bf16[64,512]{1,0:T(8,128)(2,1)S(1)}, bf16[64,512]{1,0:T(8,128)(2,1)S(1)}, u32[]{:S(2)}, u32[]{:S(2)}) collective-permute-start(bf16[64,512]{1,0:T(8,128)(2,1)S(1)} %get-tuple-element.18), channel_id=1, source_target_pairs={{0,1},{1,0},{2,3},{3,2},{4,5},{5,4},{6,7},{7,6},{8,9},{9,8},{10,11... | collective-permute-start | bytes 196616 | tf_op jit(solution)/shard_map/ppermute | solution.py:277
  54.9 6.7 %copy-start.17 = (bf16[64,512]{1,0:T(8,128)(2,1)}, bf16[64,512]{1,0:T(8,128)(2,1)S(1)}, u32[]{:S(2)}) copy-start(bf16[64,512]{1,0:T(8,128)(2,1)S(1)} %collective-permute-done.8) | copy-start | bytes 196612
  54.9 5.2 %collective-permute-start.9 = (bf16[64,512]{1,0:T(8,128)(2,1)S(1)}, bf16[64,512]{1,0:T(8,128)(2,1)S(1)}, u32[]{:S(2)}, u32[]{:S(2)}) collective-permute-start(bf16[64,512]{1,0:T(8,128)(2,1)S(1)} %fusion.2), channel_id=1, source_target_pairs={{0,2},{1,3},{2,0},{3,1},{4,6},{5,7},{6,4},{7,5},{8,10},{9,11},{10,... | collective-permute-start | bytes 196616 | tf_op jit(solution)/shard_map/ppermute | solution.py:277
  60.1 1.4 copy-start.20
  61.6 11.2 %collective-permute-start.10 = (bf16[512,512]{1,0:T(8,128)(2,1)S(1)}, bf16[512,512]{1,0:T(8,128)(2,1)S(1)}, u32[]{:S(2)}, u32[]{:S(2)}) collective-permute-start(bf16[512,512]{1,0:T(8,128)(2,1)S(1)} %raw_gradient.2.refs_0_), channel_id=1, source_target_pairs={{0,16},{16,0},{1,17},{17,1},{2,18},{18,2},{3,19},{19,3},{4,20},{20... | collective-permute-start | bytes 1572872 | tf_op jit(solution)/shard_map/ppermute | solution.py:319
  73.8 4.9 %copy-start.13 = (bf16[512,512]{1,0:T(8,128)(2,1)}, bf16[512,512]{1,0:T(8,128)(2,1)S(1)}, u32[]{:S(2)}) copy-start(bf16[512,512]{1,0:T(8,128)(2,1)S(1)} %get-tuple-element.11.refs_1_) | copy-start | bytes 1572868
  73.8 4.9 %collective-permute-start.11 = (bf16[512,512]{1,0:T(8,128)(2,1)S(1)}, bf16[512,512]{1,0:T(8,128)(2,1)}, u32[]{:S(2)}, u32[]{:S(2)}) collective-permute-start(bf16[512,512]{1,0:T(8,128)(2,1)S(1)} %get-tuple-element.11.refs_1_), channel_id=1, source_target_pairs={{0,4},{4,8},{8,12},{1,5},{5,9},{9,13},{2,6},{6,10},{10,14},{3,7},{... | collective-permute-start | bytes 1572872 | tf_op jit(solution)/shard_map/ppermute | solution.py:263
  75.9 4.6 %collective-permute-start.12 = (bf16[512,512]{1,0:T(8,128)(2,1)S(1)}, bf16[512,512]{1,0:T(8,128)(2,1)}, u32[]{:S(2)}, u32[]{:S(2)}) collective-permute-start(bf16[512,512]{1,0:T(8,128)(2,1)S(1)} %get-tuple-element.11.refs_1_), channel_id=1, source_target_pairs={{4,0},{8,4},{12,8},{5,1},{9,5},{13,9},{6,2},{10,6},{14,10},{7,3},{... | collective-permute-start | bytes 1572872 | tf_op jit(solution)/shard_map/ppermute | solution.py:263
  80.5 1.0 copy-start.14
  84.4 7.7 %collective-permute-start.13 = (bf16[512,256]{1,0:T(8,128)(2,1)}, bf16[512,256]{1,0:T(8,128)(2,1)S(1)}, u32[]{:S(2)}, u32[]{:S(2)}) collective-permute-start(bf16[512,256]{1,0:T(8,128)(2,1)} %get-tuple-element.25.refs_2_), channel_id=1, source_target_pairs={{0,1},{1,2},{2,3},{4,5},{5,6},{6,7},{8,9},{9,10},{10,11},{12,13},{... | collective-permute-start | bytes 786440 | tf_op jit(solution)/shard_map/ppermute | solution.py:263
  87.9 8.3 %collective-permute-start.14 = (bf16[512,256]{1,0:T(8,128)(2,1)S(1)}, bf16[512,256]{1,0:T(8,128)(2,1)S(1)}, u32[]{:S(2)}, u32[]{:S(2)}) collective-permute-start(bf16[512,256]{1,0:T(8,128)(2,1)S(1)} %get-tuple-element.24.refs_1_), channel_id=1, source_target_pairs={{1,0},{2,1},{3,2},{5,4},{6,5},{7,6},{9,8},{10,9},{11,10},{13,12},{... | collective-permute-start | bytes 786440 | tf_op jit(solution)/shard_map/ppermute | solution.py:263
  96.2 2.2 %copy-start.1 = (bf16[8,16,32,512]{3,2,1,0:T(8,128)(2,1)S(1)}, bf16[8,16,32,512]{3,2,1,0:T(8,128)(2,1)}, u32[]{:S(2)}) copy-start(bf16[8,16,32,512]{3,2,1,0:T(8,128)(2,1)} %param.8) | copy-start | bytes 12582916
  98.4 20.5 %copy-start.18 = (bf16[64,512]{1,0:T(8,128)(2,1)S(1)}, bf16[64,512]{1,0:T(8,128)(2,1)}, u32[]{:S(2)}) copy-start(bf16[64,512]{1,0:T(8,128)(2,1)} %copy-done.17) | copy-start | bytes 196612
  98.4 20.5 %copy-start.21 = (bf16[64,512]{1,0:T(8,128)(2,1)S(1)}, bf16[64,512]{1,0:T(8,128)(2,1)}, u32[]{:S(2)}) copy-start(bf16[64,512]{1,0:T(8,128)(2,1)} %copy-done.20) | copy-start | bytes 196612
  102.2 26.0 %copy-start.19 = (bf16[64,512]{1,0:T(8,128)(2,1)S(1)}, bf16[64,512]{1,0:T(8,128)(2,1)}, u32[]{:S(2)}) copy-start(bf16[64,512]{1,0:T(8,128)(2,1)} %copy-done.17) | copy-start | bytes 196612
  102.2 26.0 %copy-start.22 = (bf16[64,512]{1,0:T(8,128)(2,1)S(1)}, bf16[64,512]{1,0:T(8,128)(2,1)}, u32[]{:S(2)}) copy-start(bf16[64,512]{1,0:T(8,128)(2,1)} %copy-done.20) | copy-start | bytes 196612
  102.2 4.3 %collective-permute-start.15 = (bf16[64,512]{1,0:T(8,128)(2,1)S(1)}, bf16[64,512]{1,0:T(8,128)(2,1)S(1)}, u32[]{:S(2)}, u32[]{:S(2)}) collective-permute-start(bf16[64,512]{1,0:T(8,128)(2,1)S(1)} %reduce-precision_convert_fusion), channel_id=1, source_target_pairs={{0,16},{16,0},{1,17},{17,1},{2,18},{18,2},{3,19},{19,3},{4,20},{20... | collective-permute-start | bytes 196616 | tf_op jit(solution)/shard_map/ppermute | solution.py:277
  106.5 5.6 %collective-permute-start.16 = (bf16[64,512]{1,0:T(8,128)(2,1)S(1)}, bf16[64,512]{1,0:T(8,128)(2,1)S(1)}, u32[]{:S(2)}, u32[]{:S(2)}) collective-permute-start(bf16[64,512]{1,0:T(8,128)(2,1)S(1)} %fusion.13), channel_id=1, source_target_pairs={{0,4},{4,0},{8,12},{12,8},{1,5},{5,1},{9,13},{13,9},{2,6},{6,2},{1... | collective-permute-start | bytes 196616 | tf_op jit(solution)/shard_map/ppermute | solution.py:277
  112.1 5.0 %collective-permute-start.17 = (bf16[64,512]{1,0:T(8,128)(2,1)S(1)}, bf16[64,512]{1,0:T(8,128)(2,1)S(1)}, u32[]{:S(2)}, u32[]{:S(2)}) collective-permute-start(bf16[64,512]{1,0:T(8,128)(2,1)S(1)} %fusion.3), channel_id=1, source_target_pairs={{0,8},{4,12},{8,0},{12,4},{1,9},{5,13},{9,1},{13,5},{2,10},{6,14},... | collective-permute-start | bytes 196616 | tf_op jit(solution)/shard_map/ppermute | solution.py:277
  117.2 4.3 %collective-permute-start.18 = (bf16[64,512]{1,0:T(8,128)(2,1)S(1)}, bf16[64,512]{1,0:T(8,128)(2,1)S(1)}, u32[]{:S(2)}, u32[]{:S(2)}) collective-permute-start(bf16[64,512]{1,0:T(8,128)(2,1)S(1)} %fusion.4), channel_id=1, source_target_pairs={{0,1},{1,0},{2,3},{3,2},{4,5},{5,4},{6,7},{7,6},{8,9},{9,8},{10,11... | collective-permute-start | bytes 196616 | tf_op jit(solution)/shard_map/ppermute | solution.py:277
  119.7 9.7 %copy-start.23 = (f32[64,64]{1,0:T(8,128)}, f32[64,64]{1,0:T(8,128)S(1)}, u32[]{:S(2)}) copy-start(f32[64,64]{1,0:T(8,128)S(1)} %get-tuple-element.35) | copy-start | bytes 49156
  121.6 5.2 %collective-permute-start.19 = (bf16[64,512]{1,0:T(8,128)(2,1)S(1)}, bf16[64,512]{1,0:T(8,128)(2,1)S(1)}, u32[]{:S(2)}, u32[]{:S(2)}) collective-permute-start(bf16[64,512]{1,0:T(8,128)(2,1)S(1)} %get-tuple-element.16), channel_id=1, source_target_pairs={{0,2},{1,3},{2,0},{3,1},{4,6},{5,7},{6,4},{7,5},{8,10},{9,11},{10,... | collective-permute-start | bytes 196616 | tf_op jit(solution)/shard_map/ppermute | solution.py:277
  123.8 10.8 %collective-permute-start.30 = (bf16[512,256]{1,0:T(8,128)(2,1)}, bf16[512,256]{1,0:T(8,128)(2,1)S(1)}, u32[]{:S(2)}, u32[]{:S(2)}) collective-permute-start(bf16[512,256]{1,0:T(8,128)(2,1)} %get-tuple-element.21), channel_id=1, source_target_pairs={{0,4},{4,8},{8,12},{1,5},{5,9},{9,13},{2,6},{6,10},{10,14},{3,7},{... | collective-permute-start | bytes 786440 | tf_op jit(solution)/shard_map/ppermute | solution.py:263
  125.1 9.5 %collective-permute-start.31 = (bf16[512,256]{1,0:T(8,128)(2,1)}, bf16[512,256]{1,0:T(8,128)(2,1)}, u32[]{:S(2)}, u32[]{:S(2)}) collective-permute-start(bf16[512,256]{1,0:T(8,128)(2,1)} %get-tuple-element.20), channel_id=1, source_target_pairs={{4,0},{8,4},{12,8},{5,1},{9,5},{13,9},{6,2},{10,6},{14,10},{7,3},{... | collective-permute-start | bytes 786440 | tf_op jit(solution)/shard_map/ppermute | solution.py:263
  129.4 3.6 %copy-start.15 = (bf16[64,512]{1,0:T(8,128)(2,1)}, bf16[64,512]{1,0:T(8,128)(2,1)S(1)}, u32[]{:S(2)}) copy-start(bf16[64,512]{1,0:T(8,128)(2,1)S(1)} %get-tuple-element.36.courses_ref) | copy-start | bytes 196612
  129.4 2.2 %copy-start.2 = (bf16[8,16,32,512]{3,2,1,0:T(8,128)(2,1)S(1)}, bf16[8,16,32,512]{3,2,1,0:T(8,128)(2,1)}, u32[]{:S(2)}) copy-start(bf16[8,16,32,512]{3,2,1,0:T(8,128)(2,1)} %param.8) | copy-start | bytes 12582916
  133.0 17.7 %collective-permute-start.20 = (bf16[512,512]{1,0:T(8,128)(2,1)S(1)}, bf16[512,512]{1,0:T(8,128)(2,1)S(1)}, u32[]{:S(2)}, u32[]{:S(2)}) collective-permute-start(bf16[512,512]{1,0:T(8,128)(2,1)S(1)} %raw_gradient.3.refs_0_), channel_id=1, source_target_pairs={{0,16},{16,0},{1,17},{17,1},{2,18},{18,2},{3,19},{19,3},{4,20},{20... | collective-permute-start | bytes 1572872 | tf_op jit(solution)/shard_map/ppermute | solution.py:319
  136.0 7.1 %collective-permute-start.32 = (bf16[512,128]{1,0:T(8,128)(2,1)S(1)}, bf16[512,128]{1,0:T(8,128)(2,1)S(1)}, u32[]{:S(2)}, u32[]{:S(2)}) collective-permute-start(bf16[512,128]{1,0:T(8,128)(2,1)S(1)} %get-tuple-element.29), channel_id=1, source_target_pairs={{0,1},{1,2},{2,3},{4,5},{5,6},{6,7},{8,9},{9,10},{10,11},{12,13},{... | collective-permute-start | bytes 393224 | tf_op jit(solution)/shard_map/ppermute | solution.py:263
  139.5 8.1 %collective-permute-start.33 = (bf16[512,128]{1,0:T(8,128)(2,1)S(1)}, bf16[512,128]{1,0:T(8,128)(2,1)S(1)}, u32[]{:S(2)}, u32[]{:S(2)}) collective-permute-start(bf16[512,128]{1,0:T(8,128)(2,1)S(1)} %get-tuple-element.28), channel_id=1, source_target_pairs={{1,0},{2,1},{3,2},{5,4},{6,5},{7,6},{9,8},{10,9},{11,10},{13,12},{... | collective-permute-start | bytes 393224 | tf_op jit(solution)/shard_map/ppermute | solution.py:263
  148.9 1.3 copy-start.11
  150.7 7.8 %copy-start.24 = (f32[64,64]{1,0:T(8,128)S(1)}, f32[64,64]{1,0:T(8,128)}, u32[]{:S(2)}) copy-start(f32[64,64]{1,0:T(8,128)} %copy-done.23) | copy-start | bytes 49156
  151.1 17.7 %copy-start.5 = (f32[64,8,16,32]{0,3,2,1:T(8,128)S(1)}, f32[64,8,16,32]{0,3,2,1:T(8,128)}, u32[]{:S(2)}) copy-start(f32[64,8,16,32]{0,3,2,1:T(8,128)} %param.9) | copy-start | bytes 3145732
  152.0 0.8 copy-start.6
  152.8 5.9 %collective-permute-start.21 = (bf16[512,256]{1,0:T(8,128)(2,1)}, bf16[512,256]{1,0:T(8,128)(2,1)}, u32[]{:S(2)}, u32[]{:S(2)}) collective-permute-start(bf16[512,256]{1,0:T(8,128)(2,1)} %get-tuple-element.23), channel_id=1, source_target_pairs={{0,4},{4,8},{8,12},{1,5},{5,9},{9,13},{2,6},{6,10},{10,14},{3,7},{... | collective-permute-start | bytes 786440 | tf_op jit(solution)/shard_map/ppermute | solution.py:263
  155.5 4.4 %collective-permute-start.22 = (bf16[512,256]{1,0:T(8,128)(2,1)}, bf16[512,256]{1,0:T(8,128)(2,1)}, u32[]{:S(2)}, u32[]{:S(2)}) collective-permute-start(bf16[512,256]{1,0:T(8,128)(2,1)} %get-tuple-element.22), channel_id=1, source_target_pairs={{4,0},{8,4},{12,8},{5,1},{9,5},{13,9},{6,2},{10,6},{14,10},{7,3},{... | collective-permute-start | bytes 786440 | tf_op jit(solution)/shard_map/ppermute | solution.py:263
  159.9 1.0 copy-start.7
  161.0 1.0 copy-start.9
  163.5 12.2 %collective-permute-start.23 = (bf16[512,128]{1,0:T(8,128)(2,1)S(1)}, bf16[512,128]{1,0:T(8,128)(2,1)S(1)}, u32[]{:S(2)}, u32[]{:S(2)}) collective-permute-start(bf16[512,128]{1,0:T(8,128)(2,1)S(1)} %get-tuple-element.31), channel_id=1, source_target_pairs={{0,1},{1,2},{2,3},{4,5},{5,6},{6,7},{8,9},{9,10},{10,11},{12,13},{... | collective-permute-start | bytes 393224 | tf_op jit(solution)/shard_map/ppermute | solution.py:263
  167.3 8.4 %collective-permute-start.24 = (bf16[512,128]{1,0:T(8,128)(2,1)S(1)}, bf16[512,128]{1,0:T(8,128)(2,1)S(1)}, u32[]{:S(2)}, u32[]{:S(2)}) collective-permute-start(bf16[512,128]{1,0:T(8,128)(2,1)S(1)} %get-tuple-element.30), channel_id=1, source_target_pairs={{1,0},{2,1},{3,2},{5,4},{6,5},{7,6},{9,8},{10,9},{11,10},{13,12},{... | collective-permute-start | bytes 393224 | tf_op jit(solution)/shard_map/ppermute | solution.py:263
  168.9 1.6 copy-start.12
  177.0 3.6 %collective-permute-start.25 = (f32[1,1]{1,0:T(1,128)}, f32[1,1]{1,0:T(1,128)}, u32[]{:S(2)}, u32[]{:S(2)}) collective-permute-start(f32[1,1]{1,0:T(1,128)} %get-tuple-element.12), channel_id=1, source_target_pairs={{0,16},{16,0},{1,17},{17,1},{2,18},{18,2},{3,19},{19,3},{4,20},{20... | collective-permute-start | bytes 20 | tf_op jit(solution)/shard_map/ppermute | solution.py:279
  181.9 4.4 %collective-permute-start.26 = (f32[1,1]{1,0:T(1,128)}, f32[1,1]{1,0:T(1,128)}, u32[]{:S(2)}, u32[]{:S(2)}) collective-permute-start(f32[1,1]{1,0:T(1,128)} %add.76), channel_id=1, source_target_pairs={{0,4},{4,0},{8,12},{12,8},{1,5},{5,1},{9,13},{13,9},{2,6},{6,2},{1... | collective-permute-start | bytes 20 | tf_op jit(solution)/shard_map/ppermute | solution.py:279
  186.8 3.6 %collective-permute-start.27 = (f32[1,1]{1,0:T(1,128)}, f32[1,1]{1,0:T(1,128)}, u32[]{:S(2)}, u32[]{:S(2)}) collective-permute-start(f32[1,1]{1,0:T(1,128)} %add.77), channel_id=1, source_target_pairs={{0,8},{4,12},{8,0},{12,4},{1,9},{5,13},{9,1},{13,5},{2,10},{6,14},... | collective-permute-start | bytes 20 | tf_op jit(solution)/shard_map/ppermute | solution.py:279
  191.0 3.9 %collective-permute-start.28 = (f32[1,1]{1,0:T(1,128)}, f32[1,1]{1,0:T(1,128)}, u32[]{:S(2)}, u32[]{:S(2)}) collective-permute-start(f32[1,1]{1,0:T(1,128)} %add.78), channel_id=1, source_target_pairs={{0,1},{1,0},{2,3},{3,2},{4,5},{5,4},{6,7},{7,6},{8,9},{9,8},{10,11... | collective-permute-start | bytes 20 | tf_op jit(solution)/shard_map/ppermute | solution.py:279
  195.6 4.5 %collective-permute-start.29 = (f32[1,1]{1,0:T(1,128)}, f32[1,1]{1,0:T(1,128)}, u32[]{:S(2)}, u32[]{:S(2)}) collective-permute-start(f32[1,1]{1,0:T(1,128)} %add.79), channel_id=1, source_target_pairs={{0,2},{1,3},{2,0},{3,1},{4,6},{5,7},{6,4},{7,5},{8,10},{9,11},{10,... | collective-permute-start | bytes 20 | tf_op jit(solution)/shard_map/ppermute | solution.py:279

commit v2 on v1

--- a/solution.py
+++ b/solution.py
@@ -48,7 +48,7 @@
         out_shape=shapes,
         in_specs=[pl.BlockSpec(memory_space=pltpu.SMEM)] * len(smem) + vmem(len(arrays)),
         out_specs=jax.tree.map(lambda _: pl.BlockSpec(memory_space=pltpu.VMEM), shapes),
-        compiler_params=pltpu.CompilerParams(vmem_limit_bytes=40 * 1024 * 1024),
+        compiler_params=pltpu.CompilerParams(vmem_limit_bytes=16 * 1024 * 1024),
         cost_estimate=pl.CostEstimate(flops=flops, bytes_accessed=total, transcendentals=0),
         name=name,
     )(*smem, *arrays)
@@ -73,13 +73,13 @@
     return call(body, jax.ShapeDtypeStruct((layers * chans, plane), BF16), [], [voxel_maps], name="pack_maps")
 
 
-def mix_layers(place, coefs, chans, sources, sums, out_types):
+def mix_layers(place, odd, coefs, chans, sources, sums, out_types, face=0):
     rows, plane = sources[0].shape
     outs = len(out_types)
     base = len(sources)
     tall, wide = 16, 128
 
-    def body(place_ref, *refs):
+    def body(place_ref, odd_ref, *refs):
         ins, adds, results = refs[:base], refs[base : base + len(sums)], refs[base + len(sums) :]
 
         def run(tables):
@@ -112,25 +112,61 @@
         else:
             for v in range(len(coefs)):
                 pl.when(place_ref[0] == v)(functools.partial(run, coefs[v]))
+        if face:
+            send_faces(odd_ref, results[0], face, *results[outs:])
 
     shapes = tuple(jax.ShapeDtypeStruct((rows, plane), t) for t in out_types)
-    return call(body, shapes, [place], [*sources, *sums], name="mix_layers")
-
-
-def blocks_dot(pieces, table, out_type, name):
-    rows, plane = (pieces[0].shape[0], table.shape[1])
-
-    def body(*refs):
-        ins, weights, out = refs[:-2], refs[-2], refs[-1]
-        at, total = 0, None
-        for piece in ins:
-            width = piece.shape[1]
-            term = dot(piece[...], weights[at : at + width, :])
-            total = term if total is None else total + term
-            at += width
-        out[...] = total.astype(out.dtype)
-
-    return call(body, jax.ShapeDtypeStruct((rows, plane), out_type), [], [*pieces, table], name=name)
+    if face:
+        shapes += tuple(jax.ShapeDtypeStruct((rows, face), out_types[0]) for _ in range(2))
+    return call(body, shapes, [place, odd], [*sources, *sums], name="mix_layers")
+
+
+def send_faces(odd_ref, field, face, first, second):
+    plane = field.shape[1]
+
+    def write(low, high):
+        low[...] = field[:, :face].astype(low.dtype)
+        high[...] = field[:, plane - face :].astype(high.dtype)
+
+    pl.when(odd_ref[0] == 0)(lambda: write(second, first))
+    pl.when(odd_ref[0] != 0)(lambda: write(first, second))
+
+
+def swapped_dot(odd_ref, first, middle, second, weights, rows=slice(None)):
+    width = first.shape[1]
+    end = weights.shape[0] - width
+    even = odd_ref[0] == 0
+    from_first = pl.multiple_of(jnp.where(even, end, 0), width)
+    from_second = pl.multiple_of(jnp.where(even, 0, end), width)
+    total = dot(first[rows, :], weights[pl.ds(from_first, width), :])
+    total = total + dot(second[rows, :], weights[pl.ds(from_second, width), :])
+    at = width
+    for piece in middle:
+        total = total + dot(piece[rows, :], weights[at : at + piece.shape[1], :])
+        at += piece.shape[1]
+    return total
+
+
+def filter_lanes(odd, first, middle, second, table, name):
+    rows, plane = first.shape[0], table.shape[1]
+
+    def body(odd_ref, first_ref, middle_ref, second_ref, weights, out):
+        out[...] = swapped_dot(odd_ref, first_ref, [middle_ref], second_ref, weights)
+
+    return call(
+        body, jax.ShapeDtypeStruct((rows, plane), F32), [odd], [first, middle, second, table], name=name
+    )
+
+
+def filter_faces(odd_in, odd_out, first, middle, second, table, name):
+    rows, face = first.shape[0], table.shape[1] // 2
+
+    def body(odd_ref, odd_next, first_ref, middle_ref, second_ref, weights, out_first, out_second):
+        total = swapped_dot(odd_ref, first_ref, [middle_ref], second_ref, weights)
+        send_faces(odd_next, total, face, out_first, out_second)
+
+    shapes = tuple(jax.ShapeDtypeStruct((rows, face), BF16) for _ in range(2))
+    return call(body, shapes, [odd_in, odd_out], [first, middle, second, table], name=name)
 
 
 def live_lanes(count, layer, shape, size_y, size_z):
@@ -138,35 +174,29 @@
     return row < count
 
 
-def courses_of(count, acc, pieces, table, bold, chans, size_y, size_z):
+def courses_of(count, odd, acc, first, middle, second, table, bold, chans, size_y, size_z):
     frames = bold.shape[1]
     plane = size_y * size_z
     layers = bold.shape[0] // plane
-
-    def body(count_ref, *refs):
-        ins = refs[: len(pieces)]
-        rest = refs[len(pieces) :]
-        weights, frames_ref, out = rest[0], rest[1], rest[-1]
-        start = rest[2] if acc is not None else None
+    between = len(middle)
+
+    def body(count_ref, odd_ref, first_ref, *refs):
+        ins, second_ref, weights, frames_ref = refs[:between], *refs[between : between + 3]
+        out = refs[-1]
         total = jnp.zeros((chans, frames), F32)
         for x in range(layers):
             rows = slice(x * chans, (x + 1) * chans)
-            value = start[rows, :] if start is not None else None
-            at = 0
-            for piece in ins:
-                width = piece.shape[1]
-                term = dot(piece[rows, :], weights[at : at + width, :])
-                value = term if value is None else value + term
-                at += width
+            value = swapped_dot(odd_ref, first_ref, ins, second_ref, weights, rows)
+            if acc is not None:
+                value = value + refs[between + 3][rows, :]
             keep = live_lanes(count_ref[0], x, value.shape, size_y, size_z)
             value = jnp.where(keep, value, 0.0).astype(BF16)
             total = total + dot(value, frames_ref[x * plane : (x + 1) * plane, :])
         out[...] = total
 
-    arrays = [*pieces, table, bold] + ([acc] if acc is not None else [])
-    return call(
-        body, jax.ShapeDtypeStruct((chans, frames), F32), [count], arrays, flops=10**9, name="courses_of"
-    )
+    arrays = [first, *middle, second, table, bold] + ([acc] if acc is not None else [])
+    shape = jax.ShapeDtypeStruct((chans, frames), F32)
+    return call(body, shape, [count, odd], arrays, flops=10**9, name="courses_of")
 
 
 def raw_gradient(count, courses, bold, size_y, size_z):
@@ -195,25 +225,21 @@
     )
 
 
-def gradient_of(acc, pieces, table, chans):
+def gradient_of(odd, acc, first, second, table, chans):
     rows, plane = acc.shape
     layers = rows // chans
 
-    def body(start, *refs):
-        ins, weights, out, energy = refs[:-3], refs[-3], refs[-2], refs[-1]
+    def body(odd_ref, start, first_ref, second_ref, weights, out, energy):
         total = jnp.zeros((chans, plane), F32)
         for x in range(layers):
-            at, value = 0, start[x * chans : (x + 1) * chans, :]
-            for piece in ins:
-                width = piece.shape[1]
-                value = value + dot(piece[x * chans : (x + 1) * chans, :], weights[at : at + width, :])
-                at += width
+            at = slice(x * chans, (x + 1) * chans)
+            value = start[at, :] + swapped_dot(odd_ref, first_ref, [], second_ref, weights, at)
             total = total + value * value
             out[x] = value.T
         energy[...] = jnp.sum(total).reshape(1, 1)
 
     shapes = (jax.ShapeDtypeStruct((layers, plane, chans), F32), jax.ShapeDtypeStruct((1, 1), F32))
-    return call(body, shapes, [], [acc, *pieces, table], name="gradient_of")
+    return call(body, shapes, [odd], [acc, first, second, table], name="gradient_of")
 
 
 def base_maps(voxel_maps, grad, first, second):
@@ -256,6 +282,15 @@
     )
 
 
+def swapped(first, second, axis):
+    peers = lax.axis_size(axis)
+    got = []
+    for start, face in ((0, first), (1, second)):
+        pairs = [(i, i + 1) for i in range(start, peers - 1, 2)]
+        got.append(lax.ppermute(face, axis, pairs + [(j, i) for i, j in pairs]))
+    return got
+
+
 def shifted(lower, upper, axis):
     peers = lax.axis_size(axis)
     up = [(i, i + 1) for i in range(peers - 1)]
@@ -280,12 +315,19 @@
     return value
 
 
+def scattered_sum(value):
+    peers = lax.axis_size(AXES)
+    spread = jnp.broadcast_to(value.reshape(1, 1), (peers, 128))
+    return jnp.sum(lax.all_to_all(spread, AXES, 0, 0, tiled=True)[:, :1])
+
+
 def per_device(bold_data, spatial_maps, live_blocks):
     chans, size_x, size_y, size_z = spatial_maps.shape
     frames = bold_data.shape[3]
     plane = size_y * size_z
     parts_x, parts_y, parts_z = (lax.axis_size(a) for a in AXES)
     place_x = lax.axis_index("gx").astype(jnp.int32).reshape(1)
+    odd_y, odd_z = ((lax.axis_index(a) % 2).astype(jnp.int32).reshape(1) for a in AXES[1:])
     count = live_blocks.reshape(1)
     bold = bold_data.reshape(size_x * plane, frames)
     voxel_maps = jnp.transpose(spatial_maps, (1, 2, 3, 0)).reshape(size_x, plane, chans)
@@ -317,8 +359,10 @@
         if pair_x:
             mine, other = coefs_x(matrices)
             got = lax.ppermute(block, "gx", [(0, 1), (1, 0)])
-            sums = mix_layers(place_x, mine, chans, [block], [], [F32] * len(matrices))
-            return mix_layers(place_x, other, chans, [got], list(sums), [BF16] * len(matrices))
+            sums = mix_layers(place_x, odd_y, mine, chans, [block], [], [F32] * len(matrices))
+            return mix_layers(
+                place_x, odd_y, other, chans, [got], list(sums), [BF16] * len(matrices), face=face_y
+            )
         depth = RADIUS * chans
         before, after = shifted(block[:depth], block[-depth:], "gx")
         rest = jnp.zeros((block.shape[0] - depth, plane), BF16)
@@ -328,29 +372,29 @@
             columns = np.arange(size_x) + lo + RADIUS
             inside = (columns >= 0) & (columns < win_x.shape[1])
             tables.append(np.where(inside[None], win_x[:, np.clip(columns, 0, win_x.shape[1] - 1)], 0.0))
-        return mix_layers(place_x, [[tables]], chans, [before, block, after], [], [BF16])
-
-    def along_rest(first):
-        before, after = shifted(first[:, :face_y], first[:, -face_y:], "gy")
-        pieces = [before, first, after]
-        faces = blocks_dot(pieces, table_ends, BF16, "faces_z")
-        below, above = shifted(faces[:, :face_z], faces[:, face_z:], "gz")
-        acc = blocks_dot(pieces, table_own, F32, "filter_own")
-        return acc, [below, above]
-
-    def all_courses(acc, pieces, table):
+        return mix_layers(
+            place_x, odd_y, [[tables]], chans, [before, block, after], [], [BF16], face=face_y
+        )
+
+    def along_rest(field, first, second):
+        first, second = swapped(first, second, "gy")
+        ends = filter_faces(odd_y, odd_z, first, field, second, table_ends, "filter_faces")
+        ends = swapped(*ends, "gz")
+        return filter_lanes(odd_y, first, field, second, table_own, "filter_lanes"), *ends
+
+    def all_courses(acc, first, middle, second, table):
         return hypercube_sum(
-            courses_of(count, acc, pieces, table, bold, chans, size_y, size_z), narrow=True
+            courses_of(count, odd_z, acc, first, middle, second, table, bold, chans, size_y, size_z),
+            narrow=True,
         )
 
     plain = pack_maps(voxel_maps, size_x, chans, plane)
-    (first,) = along_x(plain, [full_x])
-    acc, pieces = along_rest(first)
-    courses1 = all_courses(acc, pieces, table_z)
+    acc, first, second = along_rest(*along_x(plain, [full_x]))
+    courses1 = all_courses(acc, first, [], second, table_z)
     half1 = courses1.astype(BF16)
     raw1 = raw_gradient(count, half1, bold, size_y, size_z)
     if twice:
-        first, second = along_x(raw1, [full_x, full_x @ full_x])
+        once_x, twice_x, *faces1 = along_x(raw1, [full_x, full_x @ full_x])
         square_y = windows(np.linalg.matrix_power(band(size_y * parts_y), 2), size_y, parts_y, reach)
         square_z = windows(np.linalg.matrix_power(band(size_z * parts_z), 2), size_z, parts_z, reach)
         ordered = np.concatenate([unit_z[:, :reach], unit_z[:, reach:]], 1).reshape(size_z, 2, reach)
@@ -363,22 +407,18 @@
         ])
         table_y2 = lax.dynamic_index_in_dim(jnp.asarray(half(tables_y)), lax.axis_index("gy"), 0, False)
         table_z2 = lax.dynamic_index_in_dim(jnp.asarray(half(tables_z)), lax.axis_index("gz"), 0, False)
-        before, after = shifted(second, second, "gy")
-        both = blocks_dot([before, second, after], table_y2, BF16, "filter_y2")
-        wide = reach * size_y
-        lower, upper = both[:, :wide], both[:, wide:]
-        below, above = shifted(lower, upper, "gz")
-        change = all_courses(None, [below, lower, upper, above], table_z2)
-        acc1, pieces1 = along_rest(first)
-        grad1, _ = gradient_of(acc1, pieces1, table_z, chans)
+        first, second = swapped(twice_x, twice_x, "gy")
+        to_first, to_second = filter_faces(odd_y, odd_z, first, twice_x, second, table_y2, "filter_y2")
+        first, second = swapped(to_first, to_second, "gz")
+        even = odd_z[0] == 0
+        between = [jnp.where(even, to_second, to_first), jnp.where(even, to_first, to_second)]
+        change = all_courses(None, first, between, second, table_z2)
+        grad1, _ = gradient_of(odd_z, *along_rest(once_x, *faces1), table_z, chans)
     else:
-        (first,) = along_x(raw1, [full_x])
-        acc1, pieces1 = along_rest(first)
-        grad1, _ = gradient_of(acc1, pieces1, table_z, chans)
+        grad1, _ = gradient_of(odd_z, *along_rest(*along_x(raw1, [full_x])), table_z, chans)
         again = pack_maps(grad1, size_x, chans, plane)
-        (second,) = along_x(again, [full_x])
-        acc2, pieces2 = along_rest(second)
-        change = all_courses(acc2, pieces2, table_z)
+        acc2, first, second = along_rest(*along_x(again, [full_x]))
+        change = all_courses(acc2, first, [], second, table_z)
 
     def gram_of(courses):
         gram = jnp.dot(courses, courses.T, precision=lax.Precision.HIGHEST)
@@ -393,10 +433,8 @@
     courses2 = kept + scale1 * change
     half2 = courses2.astype(BF16)
     raw2 = raw_gradient(count, half2, bold, size_y, size_z)
-    (first,) = along_x(raw2, [full_x])
-    acc, pieces = along_rest(first)
-    grad2, squares = gradient_of(acc, pieces, table_z, chans)
-    energy2 = hypercube_sum(squares, narrow=False) / all_cells
+    grad2, squares = gradient_of(odd_z, *along_rest(*along_x(raw2, [full_x])), table_z, chans)
+    energy2 = scattered_sum(squares) / all_cells
     scale2 = (0.5 / jnp.sqrt(energy2 + 1e-06)).reshape(1)
 
     fade2 = unit - gram_of(courses2)

time: 203 us -> 182 us (0.90)
  waiting for transfers between devices: 65.3 us -> 46.3 us
  local copies, waits for them, and re-layouts: 18.2 us -> 23.8 us
  between operations: 7.86 us -> 4.7 us
  Pallas kernels: 29.6 us -> 26.8 us
  starting transfers between devices: 77.2 us -> 75 us
    ppermute x21 -> x16, starting transfers between devices: 48.3 us -> 21.9 us  [swapped(): got.append(lax.ppermute(face, axis, pairs + [(j, i) for i, j in pairs]))]
    ppermute x21 -> x16, waiting for transfers between devices: 26.3 us -> 6.1 us  [swapped(): got.append(lax.ppermute(face, axis, pairs + [(j, i) for i, j in pairs]))]
    ppermute x10, starting transfers between devices: 22.7 us -> 36.1 us  [hypercube_sum(): value = value + lax.ppermute(value.astype(BF16), axis, pairs).astype(F32)]
    all_to_all x0 -> x1, starting transfers between devices: none -> 10.8 us  [scattered_sum(): return jnp.sum(lax.all_to_all(spread, AXES, 0, 0, tiled=True)[:, :1])]
    unnamed x50 -> x66, local copies, waits for them, and re-layouts: 12.9 us -> 19.7 us
    pallas_call x22, Pallas kernels: 29.6 us -> 26.8 us  [call(): pl.pallas_call(body, out_shape=shapes, in_specs=[pl.BlockSpec(memory_spac...]
    slice x7 -> x0, local copies, waits for them, and re-layouts: 2.49 us -> none  [the longest x3 1.7 us: along_rest(): before, after = shifted(first[:, :face_y], first[:, -face_y:], 'gy')]
  transfers between devices with their start and end apart: 34 -> 30, of which waited for: 24 -> 18; matrix products, arithmetic and copies ran while one was open for 4% -> 3% of each run, Pallas kernels for 7% -> 5%
where the time goes in v2:
time: 182 us
  starting transfers between devices  75 us (41%)
  waiting for transfers between devices  46.3 us (25%)
  Pallas kernels  26.8 us (15%)
  local copies, waits for them, and re-layouts  23.8 us (13%)
  between operations  4.7 us (3%)
  other arithmetic  2.74 us (2%)
  matrix products  2.26 us (1%)
    ppermute x10, starting transfers between devices, hypercube_sum(): value = value + lax.ppermute(value.astype(BF16), axis, pairs).astype(F32)  36.1 us
    pallas_call x22, Pallas kernels, call(): pl.pallas_call(body, out_shape=shapes, in_specs=[pl.BlockSpec(memory_spac...  26.8 us
    ppermute x16, starting transfers between devices, swapped(): got.append(lax.ppermute(face, axis, pairs + [(j, i) for i, j in pairs]))  21.9 us
    ppermute x3, waiting for transfers between devices, along_x(): got = lax.ppermute(block, 'gx', [(0, 1), (1, 0)])  20.3 us
    unnamed x66, local copies, waits for them, and re-layouts  19.7 us
    ppermute x10, waiting for transfers between devices, hypercube_sum(): value = value + lax.ppermute(value.astype(BF16), axis, pairs).astype(F32)  19.3 us
    all_to_all x1, starting transfers between devices, scattered_sum(): return jnp.sum(lax.all_to_all(spread, AXES, 0, 0, tiled=True)[:, :1])  10.8 us
    ppermute x3, starting transfers between devices, along_x(): got = lax.ppermute(block, 'gx', [(0, 1), (1, 0)])  6.19 us
  transfers between devices with their start and end apart: 30, of which 18 were waited for; matrix products, arithmetic and copies ran while one was open for 3% of the time, Pallas kernels for 5%

profile of v2, /device:TPU:0, one launch (start us, length us, event | category | flops | bytes accessed | tf_op | source)
XLA Modules:
  0.0 181.6 jit_solution(13055966591488422503)
XLA Ops:
  0.6 1.6 copy-done.4
  2.7 3.0 %collective-permute-start = (bf16[512,512]{1,0:T(8,128)(2,1)S(1)}, bf16[512,512]{1,0:T(8,128)(2,1)S(1)}, u32[]{:S(2)}, u32[]{:S(2)}) collective-permute-start(bf16[512,512]{1,0:T(8,128)(2,1)S(1)} %pack_maps.1.refs_0_), channel_id=1, source_target_pairs={{0,16},{16,0},{1,17},{17,1},{2,18},{18,2},{3,19},{19,3},{4,20},{20... | collective-permute-start | bytes 1572872 | tf_op jit(solution)/shard_map/ppermute | solution.py:361
  6.3 11.4 %collective-permute-done.refs_0_ = bf16[512,512]{1,0:T(8,128)(2,1)S(1)} collective-permute-done((bf16[512,512]{1,0:T(8,128)(2,1)S(1)}, bf16[512,512]{1,0:T(8,128)(2,1)S(1)}, u32[]{:S(2)}, u32[]{:S(2)}) %collective-permute-start) | collective-permute-done | bytes 524320 | tf_op jit(solution)/shard_map/ppermute | solution.py:361
  20.2 1.9 %collective-permute-start.3 = (bf16[512,128]{1,0:T(8,128)(2,1)S(1)}, bf16[512,128]{1,0:T(8,128)(2,1)S(1)}, u32[]{:S(2)}, u32[]{:S(2)}) collective-permute-start(bf16[512,128]{1,0:T(8,128)(2,1)S(1)} %get-tuple-element.28), channel_id=1, source_target_pairs={{0,1},{2,3},{1,0},{3,2},{4,5},{6,7},{5,4},{7,6},{8,9},{10,11},{9,8... | collective-permute-start | bytes 393224 | tf_op jit(solution)/shard_map/ppermute | solution.py:290
  24.1 1.1 collective-permute-done.3.first_ref
  25.3 1.8 courses_of.2
  27.1 1.8 collective-permute-start.5
  28.9 2.5 %collective-permute-done.5 = bf16[64,512]{1,0:T(8,128)(2,1)S(1)} collective-permute-done((bf16[64,512]{1,0:T(8,128)(2,1)S(1)}, bf16[64,512]{1,0:T(8,128)(2,1)S(1)}, u32[]{:S(2)}, u32[]{:S(2)}) %collective-permute-start.5) | collective-permute-done | bytes 65568 | tf_op jit(solution)/shard_map/ppermute | solution.py:312
  31.4 4.7 %collective-permute-start.6 = (bf16[64,512]{1,0:T(8,128)(2,1)S(1)}, bf16[64,512]{1,0:T(8,128)(2,1)S(1)}, u32[]{:S(2)}, u32[]{:S(2)}) collective-permute-start(bf16[64,512]{1,0:T(8,128)(2,1)S(1)} %fusion.9), channel_id=1, source_target_pairs={{0,4},{4,0},{8,12},{12,8},{1,5},{5,1},{9,13},{13,9},{2,6},{6,2},{1... | collective-permute-start | bytes 196616 | tf_op jit(solution)/shard_map/ppermute | solution.py:312
  36.2 0.9 collective-permute-done.6
  37.1 3.6 %collective-permute-start.7 = (bf16[64,512]{1,0:T(8,128)(2,1)S(1)}, bf16[64,512]{1,0:T(8,128)(2,1)S(1)}, u32[]{:S(2)}, u32[]{:S(2)}) collective-permute-start(bf16[64,512]{1,0:T(8,128)(2,1)S(1)} %fusion.1), channel_id=1, source_target_pairs={{0,8},{4,12},{8,0},{12,4},{1,9},{5,13},{9,1},{13,5},{2,10},{6,14},... | collective-permute-start | bytes 196616 | tf_op jit(solution)/shard_map/ppermute | solution.py:312
  40.7 2.4 %collective-permute-done.7 = bf16[64,512]{1,0:T(8,128)(2,1)S(1)} collective-permute-done((bf16[64,512]{1,0:T(8,128)(2,1)S(1)}, bf16[64,512]{1,0:T(8,128)(2,1)S(1)}, u32[]{:S(2)}, u32[]{:S(2)}) %collective-permute-start.7) | collective-permute-done | bytes 65568 | tf_op jit(solution)/shard_map/ppermute | solution.py:312
  43.2 4.6 %collective-permute-start.8 = (bf16[64,512]{1,0:T(8,128)(2,1)S(1)}, bf16[64,512]{1,0:T(8,128)(2,1)S(1)}, u32[]{:S(2)}, u32[]{:S(2)}) collective-permute-start(bf16[64,512]{1,0:T(8,128)(2,1)S(1)} %get-tuple-element.50), channel_id=1, source_target_pairs={{0,1},{1,0},{2,3},{3,2},{4,5},{5,4},{6,7},{7,6},{8,9},{9,8},{10,11... | collective-permute-start | bytes 196616 | tf_op jit(solution)/shard_map/ppermute | solution.py:312
  47.8 2.2 %collective-permute-done.8 = bf16[64,512]{1,0:T(8,128)(2,1)S(1)} collective-permute-done((bf16[64,512]{1,0:T(8,128)(2,1)S(1)}, bf16[64,512]{1,0:T(8,128)(2,1)S(1)}, u32[]{:S(2)}, u32[]{:S(2)}) %collective-permute-start.8) | collective-permute-done | bytes 65568 | tf_op jit(solution)/shard_map/ppermute | solution.py:312
  50.1 3.5 %collective-permute-start.9 = (bf16[64,512]{1,0:T(8,128)(2,1)S(1)}, bf16[64,512]{1,0:T(8,128)(2,1)S(1)}, u32[]{:S(2)}, u32[]{:S(2)}) collective-permute-start(bf16[64,512]{1,0:T(8,128)(2,1)S(1)} %fusion.2), channel_id=1, source_target_pairs={{0,2},{1,3},{2,0},{3,1},{4,6},{5,7},{6,4},{7,5},{8,10},{9,11},{10,... | collective-permute-start | bytes 196616 | tf_op jit(solution)/shard_map/ppermute | solution.py:312
  53.6 2.2 %collective-permute-done.9 = bf16[64,512]{1,0:T(8,128)(2,1)S(1)} collective-permute-done((bf16[64,512]{1,0:T(8,128)(2,1)S(1)}, bf16[64,512]{1,0:T(8,128)(2,1)S(1)}, u32[]{:S(2)}, u32[]{:S(2)}) %collective-permute-start.9) | collective-permute-done | bytes 65568 | tf_op jit(solution)/shard_map/ppermute | solution.py:312
  56.5 1.4 raw_gradient.2.refs_0_
  57.9 1.6 collective-permute-start.10
  59.5 1.0 mix_layers.8
  60.5 8.9 %collective-permute-done.10.refs_0_ = bf16[512,512]{1,0:T(8,128)(2,1)S(1)} collective-permute-done((bf16[512,512]{1,0:T(8,128)(2,1)S(1)}, bf16[512,512]{1,0:T(8,128)(2,1)S(1)}, u32[]{:S(2)}, u32[]{:S(2)}) %collective-permute-start.10) | collective-permute-done | bytes 524320 | tf_op jit(solution)/shard_map/ppermute | solution.py:361
  69.4 1.0 mix_layers.9
  71.8 1.5 collective-permute-start.12
  73.3 1.5 dynamic-slice_bitcast_fusion.weights
  74.8 2.9 %filter_y2.1 = (bf16[512,256]{1,0:T(8,128)(2,1)}, bf16[512,256]{1,0:T(8,128)(2,1)}) custom-call(s32[1]{0:T(128)} %bitcast.1.odd_ref, s32[1]{0:T(128)} %bitcast.odd_next.odd_ref, bf16[512,512]{1,0:T(8,128)(2,1)S(1)} %collective-permute-done.11.first_ref, bf16[512,512]{1,0:T(8,128)(2,1)S(1)} %get-tuple-element.32.middle_ref, ...), custom_call_target="tpu_custom_call" | custom-call | flops 100000000 | bytes 3145728 | tf_op jit(solution)/shard_map/filter_y2/pallas_call | solution.py:46
  77.7 1.3 collective-permute-start.13
  79.0 1.4 collective-permute-start.14
  80.3 1.3 dynamic-slice_bitcast_fusion.1.refs_3_
  81.6 1.1 broadcast_select_fusion
  82.7 1.7 collective-permute-done.13.first_ref
  84.4 2.2 %copy-done.1 = bf16[8,16,32,512]{3,2,1,0:T(8,128)(2,1)S(1)} copy-done((bf16[8,16,32,512]{3,2,1,0:T(8,128)(2,1)S(1)}, bf16[8,16,32,512]{3,2,1,0:T(8,128)(2,1)}, u32[]{:S(2)}) %copy-start.1) | copy-done | bytes 4194328
  86.6 3.8 %courses_of.3 = f32[64,512]{1,0:T(8,128)S(1)} custom-call(s32[1]{0:T(128)} %bitcast.22.count_ref, s32[1]{0:T(128)} %bitcast.odd_next.odd_ref, bf16[512,256]{1,0:T(8,128)(2,1)} %collective-permute-done.13.first_ref, bf16[512,256]{1,0:T(8,128)(2,1)S(1)} %get-tuple-element.53.refs_0_, bf16[512,256]{1,0:T(8,128)(2,1)S(1)} %get-tuple-element.52.refs_1_, ...), custom_call_target="tpu_custom_call" | custom-call | flops 1000000000 | bytes 6291456 | tf_op jit(solution)/shard_map/courses_of/pallas_call | solution.py:46
  90.5 1.6 collective-permute-start.15
  92.1 2.7 %collective-permute-done.15 = bf16[64,512]{1,0:T(8,128)(2,1)S(1)} collective-permute-done((bf16[64,512]{1,0:T(8,128)(2,1)S(1)}, bf16[64,512]{1,0:T(8,128)(2,1)S(1)}, u32[]{:S(2)}, u32[]{:S(2)}) %collective-permute-start.15) | collective-permute-done | bytes 65568 | tf_op jit(solution)/shard_map/ppermute | solution.py:312
  94.8 6.2 %collective-permute-start.16 = (bf16[64,512]{1,0:T(8,128)(2,1)S(1)}, bf16[64,512]{1,0:T(8,128)(2,1)S(1)}, u32[]{:S(2)}, u32[]{:S(2)}) collective-permute-start(bf16[64,512]{1,0:T(8,128)(2,1)S(1)} %fusion.13), channel_id=1, source_target_pairs={{0,4},{4,0},{8,12},{12,8},{1,5},{5,1},{9,13},{13,9},{2,6},{6,2},{1... | collective-permute-start | bytes 196616 | tf_op jit(solution)/shard_map/ppermute | solution.py:312
  101.0 0.9 collective-permute-done.16
  102.0 3.1 %collective-permute-start.17 = (bf16[64,512]{1,0:T(8,128)(2,1)S(1)}, bf16[64,512]{1,0:T(8,128)(2,1)S(1)}, u32[]{:S(2)}, u32[]{:S(2)}) collective-permute-start(bf16[64,512]{1,0:T(8,128)(2,1)S(1)} %fusion.3), channel_id=1, source_target_pairs={{0,8},{4,12},{8,0},{12,4},{1,9},{5,13},{9,1},{13,5},{2,10},{6,14},... | collective-permute-start | bytes 196616 | tf_op jit(solution)/shard_map/ppermute | solution.py:312
  105.1 2.4 %collective-permute-done.17 = bf16[64,512]{1,0:T(8,128)(2,1)S(1)} collective-permute-done((bf16[64,512]{1,0:T(8,128)(2,1)S(1)}, bf16[64,512]{1,0:T(8,128)(2,1)S(1)}, u32[]{:S(2)}, u32[]{:S(2)}) %collective-permute-start.17) | collective-permute-done | bytes 65568 | tf_op jit(solution)/shard_map/ppermute | solution.py:312
  107.5 4.0 %collective-permute-start.18 = (bf16[64,512]{1,0:T(8,128)(2,1)S(1)}, bf16[64,512]{1,0:T(8,128)(2,1)S(1)}, u32[]{:S(2)}, u32[]{:S(2)}) collective-permute-start(bf16[64,512]{1,0:T(8,128)(2,1)S(1)} %fusion.4), channel_id=1, source_target_pairs={{0,1},{1,0},{2,3},{3,2},{4,5},{5,4},{6,7},{7,6},{8,9},{9,8},{10,11... | collective-permute-start | bytes 196616 | tf_op jit(solution)/shard_map/ppermute | solution.py:312
  111.5 2.2 %collective-permute-done.18 = bf16[64,512]{1,0:T(8,128)(2,1)S(1)} collective-permute-done((bf16[64,512]{1,0:T(8,128)(2,1)S(1)}, bf16[64,512]{1,0:T(8,128)(2,1)S(1)}, u32[]{:S(2)}, u32[]{:S(2)}) %collective-permute-start.18) | collective-permute-done | bytes 65568 | tf_op jit(solution)/shard_map/ppermute | solution.py:312
  113.8 3.0 %collective-permute-start.19 = (bf16[64,512]{1,0:T(8,128)(2,1)S(1)}, bf16[64,512]{1,0:T(8,128)(2,1)S(1)}, u32[]{:S(2)}, u32[]{:S(2)}) collective-permute-start(bf16[64,512]{1,0:T(8,128)(2,1)S(1)} %get-tuple-element.48), channel_id=1, source_target_pairs={{0,2},{1,3},{2,0},{3,1},{4,6},{5,7},{6,4},{7,5},{8,10},{9,11},{10,... | collective-permute-start | bytes 196616 | tf_op jit(solution)/shard_map/ppermute | solution.py:312
  116.8 0.9 select_reduce_fusion.1
  120.7 2.2 %copy-done.2 = bf16[8,16,32,512]{3,2,1,0:T(8,128)(2,1)S(1)} copy-done((bf16[8,16,32,512]{3,2,1,0:T(8,128)(2,1)S(1)}, bf16[8,16,32,512]{3,2,1,0:T(8,128)(2,1)}, u32[]{:S(2)}) %copy-start.2) | copy-done | bytes 4194328
  122.9 1.4 raw_gradient.3.refs_0_
  124.3 1.6 collective-permute-start.20
  127.9 2.1 %collective-permute-start.27 = (bf16[512,128]{1,0:T(8,128)(2,1)S(1)}, bf16[512,128]{1,0:T(8,128)(2,1)S(1)}, u32[]{:S(2)}, u32[]{:S(2)}) collective-permute-start(bf16[512,128]{1,0:T(8,128)(2,1)S(1)} %get-tuple-element.44), channel_id=1, source_target_pairs={{0,1},{2,3},{1,0},{3,2},{4,5},{6,7},{5,4},{7,6},{8,9},{10,11},{9,8... | collective-permute-start | bytes 393224 | tf_op jit(solution)/shard_map/ppermute | solution.py:290
  131.4 1.6 collective-permute-done.27.first_ref
  133.0 1.3 gradient_of.3
  134.2 1.3 copy-done.10
  136.5 6.1 %collective-permute-start.21 = (bf16[512,256]{1,0:T(8,128)(2,1)S(1)}, bf16[512,256]{1,0:T(8,128)(2,1)S(1)}, u32[]{:S(2)}, u32[]{:S(2)}) collective-permute-start(bf16[512,256]{1,0:T(8,128)(2,1)S(1)} %get-tuple-element.35), channel_id=1, source_target_pairs={{0,4},{8,12},{4,0},{12,8},{1,5},{9,13},{5,1},{13,9},{2,6},{10,14},... | collective-permute-start | bytes 786440 | tf_op jit(solution)/shard_map/ppermute | solution.py:290
  143.3 0.9 select_reduce_fusion
  145.7 3.7 %collective-permute-start.23 = (bf16[512,128]{1,0:T(8,128)(2,1)S(1)}, bf16[512,128]{1,0:T(8,128)(2,1)S(1)}, u32[]{:S(2)}, u32[]{:S(2)}) collective-permute-start(bf16[512,128]{1,0:T(8,128)(2,1)S(1)} %get-tuple-element.38), channel_id=1, source_target_pairs={{0,1},{2,3},{1,0},{3,2},{4,5},{6,7},{5,4},{7,6},{8,9},{10,11},{9,8... | collective-permute-start | bytes 393224 | tf_op jit(solution)/shard_map/ppermute | solution.py:290
  150.1 1.0 copy-done.15
  151.2 0.9 copy-done.17
  152.1 0.9 copy-done.19
  153.8 1.4 gradient_of.2
  155.2 1.3 copy-done.12
  156.5 1.3 broadcast_in_dim.14
  157.8 10.8 %all-to-all-start = ((f32[32,1,128]{2,1,0:T(1,128)}), f32[32,1,128]{2,1,0:T(1,128)S(1)}, u32[]{:S(2)}, u32[]{:S(2)}) async-start(f32[32,1,128]{2,1,0:T(1,128)} %broadcast_in_dim.14), calls=%async_computation | async-start | bytes 32768 | tf_op jit(solution)/shard_map/all_to_all | solution.py:321
  168.6 1.6 copy-done.11
  170.1 3.5 %base_maps.1.base_ref = f32[8,512,64]{2,1,0:T(8,128)S(1)} custom-call(f32[8,512,64]{2,1,0:T(8,128)S(1)} %bitcast.29, f32[8,512,64]{2,1,0:T(8,128)S(1)} %copy-done.11, f32[64,64]{1,0:T(8,128)S(1)} %fusion.5.first_ref, f32[64,64]{1,0:T(8,128)S(1)} %fusion.8.second_ref), custom_call_target="tpu_custom_call" | custom-call | flops 1000000000 | bytes 2129920 | tf_op jit(solution)/shard_map/base_maps/pallas_call | solution.py:46
  173.6 1.3 copy-done.6
  176.9 1.6 copy-done.7
  178.5 1.6 copy-done.13
  180.0 1.5 final_maps.1
  (106 shorter events, 17.1 us)
Async XLA Ops:
  0.6 1.6 copy-start.4
  2.7 17.0 %copy-start.8 = (bf16[1024,256]{1,0:T(8,128)(2,1)S(1)}, bf16[1024,256]{1,0:T(8,128)(2,1)}, u32[]{:S(2)}) copy-start(bf16[1024,256]{1,0:T(8,128)(2,1)} %constant.68.clone.weights) | copy-start | bytes 1572868
  2.7 15.0 %collective-permute-start = (bf16[512,512]{1,0:T(8,128)(2,1)S(1)}, bf16[512,512]{1,0:T(8,128)(2,1)S(1)}, u32[]{:S(2)}, u32[]{:S(2)}) collective-permute-start(bf16[512,512]{1,0:T(8,128)(2,1)S(1)} %pack_maps.1.refs_0_), channel_id=1, source_target_pairs={{0,16},{16,0},{1,17},{17,1},{2,18},{18,2},{3,19},{19,3},{4,20},{20... | collective-permute-start | bytes 1572872 | tf_op jit(solution)/shard_map/ppermute | solution.py:361
  5.8 17.6 %copy-start.3 = (bf16[1024,512]{1,0:T(8,128)(2,1)S(1)}, bf16[1024,512]{1,0:T(8,128)(2,1)}, u32[]{:S(2)}) copy-start(bf16[1024,512]{1,0:T(8,128)(2,1)} %constant.69.clone.weights) | copy-start | bytes 3145732
  18.1 1.6 collective-permute-start.1
  18.2 1.5 collective-permute-start.2
  19.7 5.5 %copy-start = (bf16[8,16,32,512]{3,2,1,0:T(8,128)(2,1)S(1)}, bf16[8,16,32,512]{3,2,1,0:T(8,128)(2,1)}, u32[]{:S(2)}) copy-start(bf16[8,16,32,512]{3,2,1,0:T(8,128)(2,1)} %param.8) | copy-start | bytes 12582916
  19.7 5.5 %copy-start.9 = (bf16[256,512]{1,0:T(8,128)(2,1)S(1)}, bf16[256,512]{1,0:T(8,128)(2,1)}, u32[]{:S(2)}) copy-start(bf16[256,512]{1,0:T(8,128)(2,1)} %constant.70.clone.refs_1_.weights) | copy-start | bytes 786436
  20.2 5.0 %collective-permute-start.3 = (bf16[512,128]{1,0:T(8,128)(2,1)S(1)}, bf16[512,128]{1,0:T(8,128)(2,1)S(1)}, u32[]{:S(2)}, u32[]{:S(2)}) collective-permute-start(bf16[512,128]{1,0:T(8,128)(2,1)S(1)} %get-tuple-element.28), channel_id=1, source_target_pairs={{0,1},{2,3},{1,0},{3,2},{4,5},{6,7},{5,4},{7,6},{8,9},{10,11},{9,8... | collective-permute-start | bytes 393224 | tf_op jit(solution)/shard_map/ppermute | solution.py:290
  22.1 3.2 %collective-permute-start.4 = (bf16[512,128]{1,0:T(8,128)(2,1)S(1)}, bf16[512,128]{1,0:T(8,128)(2,1)S(1)}, u32[]{:S(2)}, u32[]{:S(2)}) collective-permute-start(bf16[512,128]{1,0:T(8,128)(2,1)S(1)} %get-tuple-element.29), channel_id=1, source_target_pairs={{1,2},{2,1},{5,6},{6,5},{9,10},{10,9},{13,14},{14,13},{17,18},{18,... | collective-permute-start | bytes 393224 | tf_op jit(solution)/shard_map/ppermute | solution.py:290
  27.1 4.3 %collective-permute-start.5 = (bf16[64,512]{1,0:T(8,128)(2,1)S(1)}, bf16[64,512]{1,0:T(8,128)(2,1)S(1)}, u32[]{:S(2)}, u32[]{:S(2)}) collective-permute-start(bf16[64,512]{1,0:T(8,128)(2,1)S(1)} %reduce-precision_convert_fusion.1), channel_id=1, source_target_pairs={{0,16},{16,0},{1,17},{17,1},{2,18},{18,2},{3,19},{19,3},{4,20},{20... | collective-permute-start | bytes 196616 | tf_op jit(solution)/shard_map/ppermute | solution.py:312
  31.4 5.7 %collective-permute-start.6 = (bf16[64,512]{1,0:T(8,128)(2,1)S(1)}, bf16[64,512]{1,0:T(8,128)(2,1)S(1)}, u32[]{:S(2)}, u32[]{:S(2)}) collective-permute-start(bf16[64,512]{1,0:T(8,128)(2,1)S(1)} %fusion.9), channel_id=1, source_target_pairs={{0,4},{4,0},{8,12},{12,8},{1,5},{5,1},{9,13},{13,9},{2,6},{6,2},{1... | collective-permute-start | bytes 196616 | tf_op jit(solution)/shard_map/ppermute | solution.py:312
  37.1 6.0 %collective-permute-start.7 = (bf16[64,512]{1,0:T(8,128)(2,1)S(1)}, bf16[64,512]{1,0:T(8,128)(2,1)S(1)}, u32[]{:S(2)}, u32[]{:S(2)}) collective-permute-start(bf16[64,512]{1,0:T(8,128)(2,1)S(1)} %fusion.1), channel_id=1, source_target_pairs={{0,8},{4,12},{8,0},{12,4},{1,9},{5,13},{9,1},{13,5},{2,10},{6,14},... | collective-permute-start | bytes 196616 | tf_op jit(solution)/shard_map/ppermute | solution.py:312
  43.2 12.7 %copy-start.25 = (f32[64,512]{1,0:T(8,128)}, f32[64,512]{1,0:T(8,128)S(1)}, u32[]{:S(2)}) copy-start(f32[64,512]{1,0:T(8,128)S(1)} %get-tuple-element.51) | copy-start | bytes 393220
  43.2 6.9 %collective-permute-start.8 = (bf16[64,512]{1,0:T(8,128)(2,1)S(1)}, bf16[64,512]{1,0:T(8,128)(2,1)S(1)}, u32[]{:S(2)}, u32[]{:S(2)}) collective-permute-start(bf16[64,512]{1,0:T(8,128)(2,1)S(1)} %get-tuple-element.50), channel_id=1, source_target_pairs={{0,1},{1,0},{2,3},{3,2},{4,5},{5,4},{6,7},{7,6},{8,9},{9,8},{10,11... | collective-permute-start | bytes 196616 | tf_op jit(solution)/shard_map/ppermute | solution.py:312
  50.1 5.8 %collective-permute-start.9 = (bf16[64,512]{1,0:T(8,128)(2,1)S(1)}, bf16[64,512]{1,0:T(8,128)(2,1)S(1)}, u32[]{:S(2)}, u32[]{:S(2)}) collective-permute-start(bf16[64,512]{1,0:T(8,128)(2,1)S(1)} %fusion.2), channel_id=1, source_target_pairs={{0,2},{1,3},{2,0},{3,1},{4,6},{5,7},{6,4},{7,5},{8,10},{9,11},{10,... | collective-permute-start | bytes 196616 | tf_op jit(solution)/shard_map/ppermute | solution.py:312
  55.9 0.6 copy-start.28
  57.9 11.5 %collective-permute-start.10 = (bf16[512,512]{1,0:T(8,128)(2,1)S(1)}, bf16[512,512]{1,0:T(8,128)(2,1)S(1)}, u32[]{:S(2)}, u32[]{:S(2)}) collective-permute-start(bf16[512,512]{1,0:T(8,128)(2,1)S(1)} %raw_gradient.2.refs_0_), channel_id=1, source_target_pairs={{0,16},{16,0},{1,17},{17,1},{2,18},{18,2},{3,19},{19,3},{4,20},{20... | collective-permute-start | bytes 1572872 | tf_op jit(solution)/shard_map/ppermute | solution.py:361
  70.4 0.7 copy-start.21
  71.1 0.7 copy-start.23
  71.8 3.0 %collective-permute-start.11 = (bf16[512,512]{1,0:T(8,128)(2,1)S(1)}, bf16[512,512]{1,0:T(8,128)(2,1)S(1)}, u32[]{:S(2)}, u32[]{:S(2)}) collective-permute-start(bf16[512,512]{1,0:T(8,128)(2,1)S(1)} %get-tuple-element.32.middle_ref), channel_id=1, source_target_pairs={{0,4},{8,12},{4,0},{12,8},{1,5},{9,13},{5,1},{13,9},{2,6},{10,14},... | collective-permute-start | bytes 1572872 | tf_op jit(solution)/shard_map/ppermute | solution.py:290
  71.8 3.0 %collective-permute-start.12 = (bf16[512,512]{1,0:T(8,128)(2,1)S(1)}, bf16[512,512]{1,0:T(8,128)(2,1)}, u32[]{:S(2)}, u32[]{:S(2)}) collective-permute-start(bf16[512,512]{1,0:T(8,128)(2,1)S(1)} %get-tuple-element.32.middle_ref), channel_id=1, source_target_pairs={{4,8},{8,4},{5,9},{9,5},{6,10},{10,6},{7,11},{11,7},{20,24},{24,20... | collective-permute-start | bytes 1572872 | tf_op jit(solution)/shard_map/ppermute | solution.py:290
  77.7 6.7 %collective-permute-start.13 = (bf16[512,256]{1,0:T(8,128)(2,1)}, bf16[512,256]{1,0:T(8,128)(2,1)}, u32[]{:S(2)}, u32[]{:S(2)}) collective-permute-start(bf16[512,256]{1,0:T(8,128)(2,1)} %get-tuple-element.33), channel_id=1, source_target_pairs={{0,1},{2,3},{1,0},{3,2},{4,5},{6,7},{5,4},{7,6},{8,9},{10,11},{9,8... | collective-permute-start | bytes 786440 | tf_op jit(solution)/shard_map/ppermute | solution.py:290
  79.0 5.4 %collective-permute-start.14 = (bf16[512,256]{1,0:T(8,128)(2,1)}, bf16[512,256]{1,0:T(8,128)(2,1)}, u32[]{:S(2)}, u32[]{:S(2)}) collective-permute-start(bf16[512,256]{1,0:T(8,128)(2,1)} %get-tuple-element.34), channel_id=1, source_target_pairs={{1,2},{2,1},{5,6},{6,5},{9,10},{10,9},{13,14},{14,13},{17,18},{18,... | collective-permute-start | bytes 786440 | tf_op jit(solution)/shard_map/ppermute | solution.py:290
  84.4 2.2 %copy-start.1 = (bf16[8,16,32,512]{3,2,1,0:T(8,128)(2,1)S(1)}, bf16[8,16,32,512]{3,2,1,0:T(8,128)(2,1)}, u32[]{:S(2)}) copy-start(bf16[8,16,32,512]{3,2,1,0:T(8,128)(2,1)} %param.8) | copy-start | bytes 12582916
  86.6 30.2 %copy-start.26 = (f32[64,512]{1,0:T(8,128)S(1)}, f32[64,512]{1,0:T(8,128)}, u32[]{:S(2)}) copy-start(f32[64,512]{1,0:T(8,128)} %copy-done.25) | copy-start | bytes 393220
  86.6 30.2 %copy-start.29 = (bf16[64,512]{1,0:T(8,128)(2,1)S(1)}, bf16[64,512]{1,0:T(8,128)(2,1)}, u32[]{:S(2)}) copy-start(bf16[64,512]{1,0:T(8,128)(2,1)} %copy-done.28) | copy-start | bytes 196612
  90.4 29.9 %copy-start.27 = (f32[64,512]{1,0:T(8,128)S(1)}, f32[64,512]{1,0:T(8,128)}, u32[]{:S(2)}) copy-start(f32[64,512]{1,0:T(8,128)} %copy-done.25) | copy-start | bytes 393220
  90.5 29.9 %copy-start.30 = (bf16[64,512]{1,0:T(8,128)(2,1)S(1)}, bf16[64,512]{1,0:T(8,128)(2,1)}, u32[]{:S(2)}) copy-start(bf16[64,512]{1,0:T(8,128)(2,1)} %copy-done.28) | copy-start | bytes 196612
  90.5 4.3 %collective-permute-start.15 = (bf16[64,512]{1,0:T(8,128)(2,1)S(1)}, bf16[64,512]{1,0:T(8,128)(2,1)S(1)}, u32[]{:S(2)}, u32[]{:S(2)}) collective-permute-start(bf16[64,512]{1,0:T(8,128)(2,1)S(1)} %reduce-precision_convert_fusion), channel_id=1, source_target_pairs={{0,16},{16,0},{1,17},{17,1},{2,18},{18,2},{3,19},{19,3},{4,20},{20... | collective-permute-start | bytes 196616 | tf_op jit(solution)/shard_map/ppermute | solution.py:312
  94.8 7.1 %collective-permute-start.16 = (bf16[64,512]{1,0:T(8,128)(2,1)S(1)}, bf16[64,512]{1,0:T(8,128)(2,1)S(1)}, u32[]{:S(2)}, u32[]{:S(2)}) collective-permute-start(bf16[64,512]{1,0:T(8,128)(2,1)S(1)} %fusion.13), channel_id=1, source_target_pairs={{0,4},{4,0},{8,12},{12,8},{1,5},{5,1},{9,13},{13,9},{2,6},{6,2},{1... | collective-permute-start | bytes 196616 | tf_op jit(solution)/shard_map/ppermute | solution.py:312
  102.0 5.5 %collective-permute-start.17 = (bf16[64,512]{1,0:T(8,128)(2,1)S(1)}, bf16[64,512]{1,0:T(8,128)(2,1)S(1)}, u32[]{:S(2)}, u32[]{:S(2)}) collective-permute-start(bf16[64,512]{1,0:T(8,128)(2,1)S(1)} %fusion.3), channel_id=1, source_target_pairs={{0,8},{4,12},{8,0},{12,4},{1,9},{5,13},{9,1},{13,5},{2,10},{6,14},... | collective-permute-start | bytes 196616 | tf_op jit(solution)/shard_map/ppermute | solution.py:312
  107.5 6.2 %collective-permute-start.18 = (bf16[64,512]{1,0:T(8,128)(2,1)S(1)}, bf16[64,512]{1,0:T(8,128)(2,1)S(1)}, u32[]{:S(2)}, u32[]{:S(2)}) collective-permute-start(bf16[64,512]{1,0:T(8,128)(2,1)S(1)} %fusion.4), channel_id=1, source_target_pairs={{0,1},{1,0},{2,3},{3,2},{4,5},{5,4},{6,7},{7,6},{8,9},{9,8},{10,11... | collective-permute-start | bytes 196616 | tf_op jit(solution)/shard_map/ppermute | solution.py:312
  113.8 5.2 %collective-permute-start.19 = (bf16[64,512]{1,0:T(8,128)(2,1)S(1)}, bf16[64,512]{1,0:T(8,128)(2,1)S(1)}, u32[]{:S(2)}, u32[]{:S(2)}) collective-permute-start(bf16[64,512]{1,0:T(8,128)(2,1)S(1)} %get-tuple-element.48), channel_id=1, source_target_pairs={{0,2},{1,3},{2,0},{3,1},{4,6},{5,7},{6,4},{7,5},{8,10},{9,11},{10,... | collective-permute-start | bytes 196616 | tf_op jit(solution)/shard_map/ppermute | solution.py:312
  117.7 3.0 %copy-start.31 = (f32[64,64]{1,0:T(8,128)}, f32[64,64]{1,0:T(8,128)S(1)}, u32[]{:S(2)}) copy-start(f32[64,64]{1,0:T(8,128)S(1)} %get-tuple-element.55) | copy-start | bytes 49156
  120.7 3.6 %copy-start.20 = (bf16[64,512]{1,0:T(8,128)(2,1)}, bf16[64,512]{1,0:T(8,128)(2,1)S(1)}, u32[]{:S(2)}) copy-start(bf16[64,512]{1,0:T(8,128)(2,1)S(1)} %get-tuple-element.56.courses_ref) | copy-start | bytes 196612
  120.7 2.2 %copy-start.2 = (bf16[8,16,32,512]{3,2,1,0:T(8,128)(2,1)S(1)}, bf16[8,16,32,512]{3,2,1,0:T(8,128)(2,1)}, u32[]{:S(2)}) copy-start(bf16[8,16,32,512]{3,2,1,0:T(8,128)(2,1)} %param.8) | copy-start | bytes 12582916
  122.9 3.0 %copy-start.24 = (bf16[512,256]{1,0:T(8,128)(2,1)S(1)}, bf16[512,256]{1,0:T(8,128)(2,1)}, u32[]{:S(2)}) copy-start(bf16[512,256]{1,0:T(8,128)(2,1)} %copy-done.23) | copy-start | bytes 786436
  122.9 3.0 %copy-start.22 = (bf16[512,256]{1,0:T(8,128)(2,1)S(1)}, bf16[512,256]{1,0:T(8,128)(2,1)}, u32[]{:S(2)}) copy-start(bf16[512,256]{1,0:T(8,128)(2,1)} %copy-done.21) | copy-start | bytes 786436
  124.3 11.8 %collective-permute-start.20 = (bf16[512,512]{1,0:T(8,128)(2,1)S(1)}, bf16[512,512]{1,0:T(8,128)(2,1)S(1)}, u32[]{:S(2)}, u32[]{:S(2)}) collective-permute-start(bf16[512,512]{1,0:T(8,128)(2,1)S(1)} %raw_gradient.3.refs_0_), channel_id=1, source_target_pairs={{0,16},{16,0},{1,17},{17,1},{2,18},{18,2},{3,19},{19,3},{4,20},{20... | collective-permute-start | bytes 1572872 | tf_op jit(solution)/shard_map/ppermute | solution.py:361
  125.9 1.5 collective-permute-start.25
  125.9 1.5 collective-permute-start.26
  127.9 5.0 %collective-permute-start.27 = (bf16[512,128]{1,0:T(8,128)(2,1)S(1)}, bf16[512,128]{1,0:T(8,128)(2,1)S(1)}, u32[]{:S(2)}, u32[]{:S(2)}) collective-permute-start(bf16[512,128]{1,0:T(8,128)(2,1)S(1)} %get-tuple-element.44), channel_id=1, source_target_pairs={{0,1},{2,3},{1,0},{3,2},{4,5},{6,7},{5,4},{7,6},{8,9},{10,11},{9,8... | collective-permute-start | bytes 393224 | tf_op jit(solution)/shard_map/ppermute | solution.py:290
  130.0 3.0 %collective-permute-start.28 = (bf16[512,128]{1,0:T(8,128)(2,1)S(1)}, bf16[512,128]{1,0:T(8,128)(2,1)S(1)}, u32[]{:S(2)}, u32[]{:S(2)}) collective-permute-start(bf16[512,128]{1,0:T(8,128)(2,1)S(1)} %get-tuple-element.45), channel_id=1, source_target_pairs={{1,2},{2,1},{5,6},{6,5},{9,10},{10,9},{13,14},{14,13},{17,18},{18,... | collective-permute-start | bytes 393224 | tf_op jit(solution)/shard_map/ppermute | solution.py:290
  134.2 1.3 copy-start.10
  135.6 9.4 %copy-start.32 = (f32[64,64]{1,0:T(8,128)S(1)}, f32[64,64]{1,0:T(8,128)}, u32[]{:S(2)}) copy-start(f32[64,64]{1,0:T(8,128)} %copy-done.31) | copy-start | bytes 49156
  136.5 13.5 %copy-start.14 = (bf16[512,512]{1,0:T(8,128)(2,1)}, bf16[512,512]{1,0:T(8,128)(2,1)S(1)}, u32[]{:S(2)}) copy-start(bf16[512,512]{1,0:T(8,128)(2,1)S(1)} %get-tuple-element.36.middle_ref) | copy-start | bytes 1572868
  136.5 8.6 %collective-permute-start.21 = (bf16[512,256]{1,0:T(8,128)(2,1)S(1)}, bf16[512,256]{1,0:T(8,128)(2,1)S(1)}, u32[]{:S(2)}, u32[]{:S(2)}) collective-permute-start(bf16[512,256]{1,0:T(8,128)(2,1)S(1)} %get-tuple-element.35), channel_id=1, source_target_pairs={{0,4},{8,12},{4,0},{12,8},{1,5},{9,13},{5,1},{13,9},{2,6},{10,14},... | collective-permute-start | bytes 786440 | tf_op jit(solution)/shard_map/ppermute | solution.py:290
  142.7 2.5 %collective-permute-start.22 = (bf16[512,256]{1,0:T(8,128)(2,1)S(1)}, bf16[512,256]{1,0:T(8,128)(2,1)S(1)}, u32[]{:S(2)}, u32[]{:S(2)}) collective-permute-start(bf16[512,256]{1,0:T(8,128)(2,1)S(1)} %get-tuple-element.37), channel_id=1, source_target_pairs={{4,8},{8,4},{5,9},{9,5},{6,10},{10,6},{7,11},{11,7},{20,24},{24,20... | collective-permute-start | bytes 786440 | tf_op jit(solution)/shard_map/ppermute | solution.py:290
  145.2 4.9 %copy-start.16 = (bf16[512,256]{1,0:T(8,128)(2,1)}, bf16[512,256]{1,0:T(8,128)(2,1)S(1)}, u32[]{:S(2)}) copy-start(bf16[512,256]{1,0:T(8,128)(2,1)S(1)} %collective-permute-done.21.first_ref) | copy-start | bytes 786436
  145.2 4.9 %copy-start.18 = (bf16[512,256]{1,0:T(8,128)(2,1)}, bf16[512,256]{1,0:T(8,128)(2,1)S(1)}, u32[]{:S(2)}) copy-start(bf16[512,256]{1,0:T(8,128)(2,1)S(1)} %collective-permute-done.22.second_ref) | copy-start | bytes 786436
  145.7 8.1 %collective-permute-start.23 = (bf16[512,128]{1,0:T(8,128)(2,1)S(1)}, bf16[512,128]{1,0:T(8,128)(2,1)S(1)}, u32[]{:S(2)}, u32[]{:S(2)}) collective-permute-start(bf16[512,128]{1,0:T(8,128)(2,1)S(1)} %get-tuple-element.38), channel_id=1, source_target_pairs={{0,1},{2,3},{1,0},{3,2},{4,5},{6,7},{5,4},{7,6},{8,9},{10,11},{9,8... | collective-permute-start | bytes 393224 | tf_op jit(solution)/shard_map/ppermute | solution.py:290
  149.4 4.4 %collective-permute-start.24 = (bf16[512,128]{1,0:T(8,128)(2,1)S(1)}, bf16[512,128]{1,0:T(8,128)(2,1)S(1)}, u32[]{:S(2)}, u32[]{:S(2)}) collective-permute-start(bf16[512,128]{1,0:T(8,128)(2,1)S(1)} %get-tuple-element.39), channel_id=1, source_target_pairs={{1,2},{2,1},{5,6},{6,5},{9,10},{10,9},{13,14},{14,13},{17,18},{18,... | collective-permute-start | bytes 393224 | tf_op jit(solution)/shard_map/ppermute | solution.py:290
  150.1 1.0 copy-start.15
  151.2 0.9 copy-start.17
  152.1 0.9 copy-start.19
  153.1 15.5 %copy-start.5 = (f32[64,8,16,32]{0,3,2,1:T(8,128)S(1)}, f32[64,8,16,32]{0,3,2,1:T(8,128)}, u32[]{:S(2)}) copy-start(f32[64,8,16,32]{0,3,2,1:T(8,128)} %param.9) | copy-start | bytes 3145732
  155.2 1.3 copy-start.12
  157.8 17.7 %all-to-all-start = ((f32[32,1,128]{2,1,0:T(1,128)}), f32[32,1,128]{2,1,0:T(1,128)S(1)}, u32[]{:S(2)}, u32[]{:S(2)}) async-start(f32[32,1,128]{2,1,0:T(1,128)} %broadcast_in_dim.14), calls=%async_computation | async-start | bytes 32768 | tf_op jit(solution)/shard_map/all_to_all | solution.py:321
  168.5 1.6 copy-start.11
  173.6 1.3 copy-start.6
  176.9 1.6 copy-start.7
  178.5 1.6 copy-start.13

commit v3 on v0

v3 whole, which is shorter than its diff:
```python
import functools
import math

import jax
import jax.numpy as jnp
import ml_dtypes
import numpy as np
from jax import lax
from jax.experimental import pallas as pl
from jax.experimental.pallas import tpu as pltpu
from jax.sharding import PartitionSpec as P

RADIUS = 8
F32 = jnp.float32
BF16 = jnp.bfloat16
AXES = ("gx", "gy", "gz")


def band(length):
    total = sum(math.exp(-float(d * d) / 32.0) for d in range(-RADIUS, RADIUS + 1))
    gap = np.abs(np.arange(length)[:, None] - np.arange(length)[None, :])
    return np.where(gap <= RADIUS, np.exp(-(gap.astype(np.float64) ** 2) / 32.0) / total, 0.0)


def windows(matrix, size, parts, reach):
    padded = np.pad(matrix, ((0, 0), (reach, reach)))
    return np.stack(
        [padded[p * size : (p + 1) * size, p * size : (p + 1) * size + 2 * reach] for p in range(parts)]
    )


def half(array):
    return np.asarray(array, dtype=ml_dtypes.bfloat16)


def inner_window(size):
    return windows(band(3 * size), size, 3, RADIUS)[1]


PLACE_X, PLACE_Y, PLACE_Z, ODD_Y, ODD_Z, COUNT = range(6)
NT = (((1,), (1,)), ((), ()))
FULL = lax.Precision.HIGHEST


def shape(dims, kind):
    return jax.ShapeDtypeStruct(dims, kind)


def call(body, shapes, info, arrays, flops=10**8, name=None, spaces=None, scratch=()):
    total = sum(a.size * a.dtype.itemsize for a in arrays)
    whole = pl.BlockSpec(memory_space=pltpu.VMEM)
    return pl.pallas_call(
        body,
        out_shape=shapes,
        in_specs=[pl.BlockSpec(memory_space=pltpu.SMEM)] + [spaces or whole] * len(arrays),
        out_specs=jax.tree.map(lambda _: whole, shapes),
        scratch_shapes=scratch,
        compiler_params=pltpu.CompilerParams(vmem_limit_bytes=16 * 1024 * 1024),
        cost_estimate=pl.CostEstimate(flops=flops, bytes_accessed=total, transcendentals=0),
        name=name,
    )(info, *arrays)


def dot(a, b):
    return jnp.dot(a, b, preferred_element_type=F32)


def dot_nt(a, b, precision=None):
    return lax.dot_general(a, b, NT, precision=precision, preferred_element_type=F32)


def unit_of(size):
    return (
        lax.broadcasted_iota(jnp.int32, (size, size), 0) == lax.broadcasted_iota(jnp.int32, (size, size), 1)
    ).astype(F32)


def total_of(value):
    return jnp.sum(jnp.sum(value, axis=1, keepdims=True), axis=0, keepdims=True)


def pack_maps(info, voxel_maps):
    layers, plane, chans = voxel_maps.shape

    def body(_, src, out):
        unit = unit_of(chans).astype(BF16)
        for x in range(layers):
            out[x * chans : (x + 1) * chans, :] = dot_nt(unit, src[x].astype(BF16)).astype(BF16)

    return call(body, shape((layers * chans, plane), BF16), info, [voxel_maps], name="pack_maps")


def pick_tables(info, table_y, table_z):
    def body(info_ref, all_y, all_z, out_y, out_z, sem_y, sem_z):
        copies = [
            pltpu.make_async_copy(all_y.at[info_ref[PLACE_Y]], out_y, sem_y),
            pltpu.make_async_copy(all_z.at[info_ref[PLACE_Z]], out_z, sem_z),
        ]
        for copy in copies:
            copy.start()
        for copy in copies:
            copy.wait()

    shapes = (shape(table_y.shape[1:], BF16), shape(table_z.shape[1:], BF16))
    return call(
        body,
        shapes,
        info,
        [table_y, table_z],
        name="pick_tables",
        spaces=pl.BlockSpec(memory_space=pl.ANY),
        scratch=(pltpu.SemaphoreType.DMA, pltpu.SemaphoreType.DMA),
    )


def send_faces(info_ref, odd, field, face, first, second):
    plane = field.shape[1]

    def write(low, high):
        low[...] = field[:, :face].astype(low.dtype)
        high[...] = field[:, plane - face :].astype(high.dtype)

    pl.when(info_ref[odd] == 0)(lambda: write(second, first))
    pl.when(info_ref[odd] != 0)(lambda: write(first, second))


def swapped_dot(info_ref, odd, first, middle, second, weights, rows=slice(None), sent=False):
    width = first.shape[1]
    end = weights.shape[0] - width
    even = info_ref[odd] == 0

    def at(when_even, when_odd):
        return weights[pl.ds(pl.multiple_of(jnp.where(even, when_even, when_odd), width), width), :]

    total = dot(first[rows, :], at(end, 0)) + dot(second[rows, :], at(0, end))
    if sent:
        high = end - width
        return total + dot(middle[0][rows, :], at(high, width)) + dot(middle[1][rows, :], at(width, high))
    for piece in middle:
        total = total + dot(piece[rows, :], weights[width : width + piece.shape[1], :])
    return total


def mix_layers(info, coefs, chans, sources, sums, out_types, face=0):
    rows, plane = sources[0].shape
    outs = len(out_types)
    base = len(sources)
    tall, wide = 16, 128

    def body(info_ref, *refs):
        ins, adds, results = refs[:base], refs[base : base + len(sums)], refs[base + len(sums) :]

        def run(tables):
            layers = tables[0][0].shape[0]
            for r in range(0, chans, tall):
                for c in range(0, plane, wide):
                    tiles = [
                        [
                            src[s * chans + r : s * chans + r + tall, c : c + wide].astype(F32)
                            for s in range(layers)
                        ]
                        for src in ins
                    ]
                    for o in range(outs):
                        for x in range(layers):
                            at = slice(x * chans + r, x * chans + r + tall)
                            total = adds[o][at, c : c + wide] if adds else None
                            for tile, table in zip(tiles, tables[o]):
                                for s in range(layers):
                                    weight = float(table[x, s])
                                    if weight != 0.0:
                                        term = tile[s] * weight
                                        total = term if total is None else total + term
                            if total is None:
                                total = jnp.zeros((tall, wide), F32)
                            results[o][at, c : c + wide] = total.astype(results[o].dtype)

        if len(coefs) == 1:
            run(coefs[0])
        else:
            for v in range(len(coefs)):
                pl.when(info_ref[PLACE_X] == v)(functools.partial(run, coefs[v]))
        if face:
            send_faces(info_ref, ODD_Y, results[0], face, *results[outs:])

    shapes = tuple(shape((rows, plane), t) for t in out_types)
    if face:
        shapes += (shape((rows, face), out_types[0]),) * 2
    return call(body, shapes, info, [*sources, *sums], name="mix_layers")


def filter_lanes(info, first, middle, second, table):
    def body(info_ref, first_ref, middle_ref, second_ref, weights, out):
        out[...] = swapped_dot(info_ref, ODD_Y, first_ref, [middle_ref], second_ref, weights)

    shapes = shape((first.shape[0], table.shape[1]), F32)
    return call(body, shapes, info, [first, middle, second, table], name="filter_lanes")


def filter_faces(info, first, middle, second, table, below=()):
    rows, face = first.shape[0], table.shape[1] // 2
    extra = below[0].shape[0] if below else 0

    def body(info_ref, first_ref, middle_ref, second_ref, weights, *refs):
        outs = refs[-2:]
        total = swapped_dot(info_ref, ODD_Y, first_ref, [middle_ref], second_ref, weights)
        send_faces(info_ref, ODD_Z, total, face, *(out.at[:rows, :] for out in outs))
        for src, out in zip(refs[:-2], outs):
            out[rows:, :] = src[...]

    shapes = (shape((rows + extra, face), BF16),) * 2
    return call(body, shapes, info, [first, middle, second, table, *below], name="filter_faces")


def live_lanes(info_ref, layer, dims, size_y, size_z):
    row = layer * size_y + lax.broadcasted_iota(jnp.int32, dims, 1) // size_z
    return row < info_ref[COUNT]


def spread_rows(chans, frames, peers):
    rows = chans * frames // (peers * 128)
    return rows if rows and rows * peers * 128 == chans * frames and chans % rows == 0 else 0


def courses_of(info, acc, first, middle, second, table, bold, chans, size_y, size_z, peers):
    frames = bold.shape[1]
    plane = size_y * size_z
    layers = bold.shape[0] // plane
    between = len(middle)
    part = spread_rows(chans, frames, peers)

    def body(info_ref, first_ref, *refs):
        ins, second_ref, weights, frames_ref = refs[:between], *refs[between : between + 3]
        out = refs[-1]
        total = jnp.zeros((chans, frames), F32)
        for x in range(layers):
            rows = slice(x * chans, (x + 1) * chans)
            value = swapped_dot(info_ref, ODD_Z, first_ref, ins, second_ref, weights, rows, sent=between == 2)
            if acc is not None:
                value = value + refs[between + 3][rows, :]
            keep = live_lanes(info_ref, x, value.shape, size_y, size_z)
            value = jnp.where(keep, value, 0.0).astype(BF16)
            total = total + dot(value, frames_ref[x * plane : (x + 1) * plane, :])
        if not part:
            out[...] = total
            return
        across = frames // 128
        for d in range(peers):
            r, c = d // across * part, d % across * 128
            out[d] = total[r : r + part, c : c + 128].astype(BF16)

    arrays = [first, *middle, second, table, bold] + ([acc] if acc is not None else [])
    shapes = shape((peers, part, 128), BF16) if part else shape((chans, frames), F32)
    return call(body, shapes, info, arrays, flops=10**9, name="courses_of")


def sum_parts(info, parts):
    peers = parts.shape[0]

    def body(_, src, out):
        total = src[0].astype(F32)
        for d in range(1, peers):
            total = total + src[d].astype(F32)
        total = total.astype(BF16)
        for d in range(peers):
            out[d] = total

    return call(body, shape(parts.shape, BF16), info, [parts], name="sum_parts")


def whole_courses(src, chans, frames):
    if len(src.shape) == 2:
        return src[...].astype(F32)
    across = frames // 128
    down = src.shape[0] // across
    return jnp.concatenate(
        [
            jnp.concatenate([src[r * across + c].astype(F32) for c in range(across)], axis=1)
            for r in range(down)
        ],
        axis=0,
    )


def write_gradient(info_ref, courses, frames_ref, out, chans, size_y, size_z):
    plane = size_y * size_z
    for x in range(frames_ref.shape[0] // plane):
        value = dot_nt(courses, frames_ref[x * plane : (x + 1) * plane, :])
        keep = live_lanes(info_ref, x, value.shape, size_y, size_z)
        out[x * chans : (x + 1) * chans, :] = jnp.where(keep, value, 0.0).astype(BF16)


def first_gradient(info, parts, bold, chans, size_y, size_z):
    cells, frames = bold.shape

    def body(info_ref, parts_ref, frames_ref, out, half_ref):
        courses = whole_courses(parts_ref, chans, frames).astype(BF16)
        half_ref[...] = courses
        write_gradient(info_ref, courses, frames_ref, out, chans, size_y, size_z)

    shapes = (shape((cells * chans // (size_y * size_z), size_y * size_z), BF16), shape((chans, frames), BF16))
    return call(body, shapes, info, [parts, bold], flops=10**9, name="first_gradient")


def fade_of(courses):
    chans = courses.shape[0]
    wide = courses.astype(F32)
    scale = (0.5 * chans) / total_of(wide * wide)
    return unit_of(chans) - dot_nt(courses, courses) * scale


def first_fade(info, half1):
    chans, frames = half1.shape

    def body(_, half_ref, kept_ref, fade_ref):
        fade = fade_of(half_ref[...])
        fade_ref[...] = fade
        kept_ref[...] = jnp.dot(fade, half_ref[...].astype(F32), precision=FULL, preferred_element_type=F32)

    shapes = (shape((chans, frames), F32), shape((chans, chans), F32))
    return call(body, shapes, info, [half1], name="first_fade")


def second_gradient(info, parts, half1, kept, bold, chans, size_y, size_z, all_cells):
    cells, frames = bold.shape

    def body(info_ref, parts_ref, half1_ref, kept_ref, frames_ref, out, half_ref, scale_ref):
        change = whole_courses(parts_ref, chans, frames)
        energy = jnp.maximum(total_of(half1_ref[...].astype(F32) * change), 0.0) * (1.0 / all_cells)
        scale = 0.5 * lax.rsqrt(energy + 1e-06)
        scale_ref[...] = scale
        courses = (kept_ref[...] + scale * change).astype(BF16)
        half_ref[...] = courses
        write_gradient(info_ref, courses, frames_ref, out, chans, size_y, size_z)

    shapes = (
        shape((cells * chans // (size_y * size_z), size_y * size_z), BF16),
        shape((chans, frames), BF16),
        shape((1, 1), F32),
    )
    return call(body, shapes, info, [parts, half1, kept, bold], flops=10**9, name="second_gradient")


def second_fade(info, half2, fade1, scale1, field, face):
    chans = half2.shape[0]
    rows, plane = field.shape

    def body(info_ref, half_ref, fade_ref, scale_ref, field_ref, fades_ref, out, first, second):
        fade = fade_of(half_ref[...])
        fades_ref[...] = jnp.dot(fade, fade_ref[...], precision=FULL, preferred_element_type=F32)
        weights = fade * scale_ref[...]
        high = weights.astype(BF16)
        low = (weights - high.astype(F32)).astype(BF16)
        for x in range(rows // chans):
            at = slice(x * chans, (x + 1) * chans)
            block = field_ref[at, :]
            out[at, :] = (dot(high, block) + dot(low, block)).astype(BF16)
        send_faces(info_ref, ODD_Y, out, face, first, second)

    shapes = (
        shape((chans, chans), F32),
        shape((rows, plane), BF16),
        shape((rows, face), BF16),
        shape((rows, face), BF16),
    )
    return call(body, shapes, info, [half2, fade1, scale1, field], flops=10**9, name="second_fade")


def faded_maps(info, voxel_maps, fades):
    layers, plane, chans = voxel_maps.shape

    def body(_, maps_ref, fades_ref, out):
        for x in range(layers):
            out[x] = dot_nt(maps_ref[x], fades_ref[...], FULL)

    return call(
        body, shape((layers, plane, chans), F32), info, [voxel_maps, fades], flops=10**9, name="faded_maps"
    )


def whole_gradient(info, acc, first, second, table):
    def body(info_ref, start, first_ref, second_ref, weights, out):
        value = start[...] + swapped_dot(info_ref, ODD_Z, first_ref, [], second_ref, weights)
        out[...] = value.astype(BF16)

    return call(body, shape(acc.shape, BF16), info, [acc, first, second, table], name="whole_gradient")


def gradient_energy(info, acc, first, second, table, peers):
    rows, plane = acc.shape
    tall = min(rows, 128)

    def body(info_ref, start, first_ref, second_ref, weights, out, energy):
        total = jnp.zeros((tall, plane), F32)
        for r in range(0, rows, tall):
            at = slice(r, r + tall)
            value = start[at, :] + swapped_dot(info_ref, ODD_Z, first_ref, [], second_ref, weights, at)
            total = total + value * value
            out[at, :] = value
        energy[...] = jnp.broadcast_to(total_of(total).reshape(1, 1, 1), energy.shape)

    shapes = (shape((rows, plane), F32), shape((peers, 1, 128), F32))
    return call(body, shapes, info, [acc, first, second, table], name="gradient_energy")


def turned_gradients(info, acc, first, second, table, base, grad):
    layers, plane, chans = base.shape
    rows = acc.shape[0]

    def body(info_ref, start, first_ref, second_ref, weights, base_ref, grad_ref, out, turned):
        for x in range(layers):
            at = slice(x * chans, (x + 1) * chans)
            below = slice(rows + x * chans, rows + (x + 1) * chans)
            value = start[at, :] + swapped_dot(info_ref, ODD_Z, first_ref, [], second_ref, weights, below)
            out[x] = base_ref[x] + value.T
            turned[x] = grad_ref[at, :].T

    shapes = (shape(base.shape, F32),) * 2
    return call(body, shapes, info, [acc, first, second, table, base, grad], name="turned_gradients")


def final_maps(info, energies, base, grad, all_cells):
    layers, plane, chans = base.shape
    peers = energies.shape[0]

    def body(_, energies_ref, base_ref, grad_ref, out):
        energy = energies_ref[0]
        for d in range(1, peers):
            energy = energy + energies_ref[d]
        scale = 0.5 * lax.rsqrt(energy[:, :1] * (1.0 / all_cells) + 1e-06)
        for x in range(layers):
            out[x] = base_ref[x] + scale * grad_ref[x]

    return call(body, shape(base.shape, F32), info, [energies, base, grad], name="final_maps")


def swapped(first, second, axis, inner_first=False):
    peers = lax.axis_size(axis)
    got = {}
    for start in (1, 0) if inner_first else (0, 1):
        pairs = [(i, i + 1) for i in range(start, peers - 1, 2)]
        pairs += [(j, i) for i, j in pairs]
        got[start] = lax.ppermute((first, second)[start], axis, pairs)
    return got[0], got[1]


def shifted(lower, upper, axis):
    peers = lax.axis_size(axis)
    up = [(i, i + 1) for i in range(peers - 1)]
    down = [(j, i) for i, j in up]
    return lax.ppermute(upper, axis, up), lax.ppermute(lower, axis, down)


def exchanged(parts):
    return lax.all_to_all(parts, AXES, 0, 0, tiled=True)


def per_device(bold_data, spatial_maps, live_blocks):
    chans, size_x, size_y, size_z = spatial_maps.shape
    frames = bold_data.shape[3]
    plane = size_y * size_z
    parts_x, parts_y, parts_z = (lax.axis_size(a) for a in AXES)
    peers = parts_x * parts_y * parts_z
    places = [lax.axis_index(a).astype(jnp.int32) for a in AXES]
    info = jnp.stack([*places, places[1] % 2, places[2] % 2, live_blocks[0, 0, 0]])
    bold = bold_data.reshape(size_x * plane, frames)
    voxel_maps = jnp.transpose(spatial_maps, (1, 2, 3, 0)).reshape(size_x, plane, chans)
    all_cells = float(chans * size_x * plane * peers)

    win_x, win_y, win_z = (inner_window(s) for s in (size_x, size_y, size_z))
    unit_y, unit_z = np.eye(size_y), np.eye(size_z)
    ends = np.concatenate([np.kron(win_y.T, unit_z[:, :RADIUS]), np.kron(win_y.T, unit_z[:, -RADIUS:])], 1)
    table_ends = jnp.asarray(half(ends))
    table_own = jnp.asarray(half(np.kron(win_y.T, win_z[:, RADIUS:-RADIUS].T)))
    table_z = jnp.asarray(
        half(np.concatenate([np.kron(unit_y, win_z[:, :RADIUS].T), np.kron(unit_y, win_z[:, -RADIUS:].T)]))
    )
    face_y = RADIUS * size_z

    reach = 2 * RADIUS
    twice = parts_x == 2 and size_y == reach and size_z == 2 * reach
    full_x = band(size_x * parts_x)
    own_x = [slice(p * size_x, (p + 1) * size_x) for p in range(parts_x)]

    def along_x(block, matrices):
        kinds = [BF16] * len(matrices)
        if parts_x == 2:
            mine = [[[m[own_x[p], own_x[p]]] for m in matrices] for p in range(2)]
            other = [[[m[own_x[p], own_x[1 - p]]] for m in matrices] for p in range(2)]
            got = lax.ppermute(block, "gx", [(0, 1), (1, 0)])
            sums = mix_layers(info, mine, chans, [block], [], [F32] * len(matrices))
            return mix_layers(info, other, chans, [got], list(sums), kinds, face=face_y)
        depth = RADIUS * chans
        before, after = shifted(block[:depth], block[-depth:], "gx")
        rest = jnp.zeros((block.shape[0] - depth, plane), BF16)
        before, after = jnp.concatenate([rest, before]), jnp.concatenate([after, rest])
        tables = []
        for lo in (-size_x, 0, size_x):
            columns = np.arange(size_x) + lo + RADIUS
            inside = (columns >= 0) & (columns < win_x.shape[1])
            tables.append(np.where(inside[None], win_x[:, np.clip(columns, 0, win_x.shape[1] - 1)], 0.0))
        return mix_layers(info, [[tables]], chans, [before, block, after], [], kinds, face=face_y)

    def along_y(first, second):
        return swapped(first, second, "gy", inner_first=True)

    def along_rest(field, first, second):
        first, second = along_y(first, second)
        ends = swapped(*filter_faces(info, first, field, second, table_ends), "gz")
        return filter_lanes(info, first, field, second, table_own), *ends

    def all_courses(acc, first, middle, second, table):
        parts = courses_of(info, acc, first, middle, second, table, bold, chans, size_y, size_z, peers)
        if not spread_rows(chans, frames, peers):
            return lax.psum(parts, AXES)
        return exchanged(sum_parts(info, exchanged(parts)))

    plain = pack_maps(info, voxel_maps)
    acc, first, second = along_rest(*along_x(plain, [full_x]))
    parts1 = all_courses(acc, first, [], second, table_z)
    raw1, half1 = first_gradient(info, parts1, bold, chans, size_y, size_z)
    if twice:
        square_y = windows(np.linalg.matrix_power(band(size_y * parts_y), 2), size_y, parts_y, reach)
        square_z = windows(np.linalg.matrix_power(band(size_z * parts_z), 2), size_z, parts_z, reach)
        ordered = np.concatenate([unit_z[:, :reach], unit_z[:, reach:]], 1).reshape(size_z, 2, reach)
        tables_y = np.stack([
            np.concatenate([np.kron(w.T, ordered[:, h]) for h in range(2)], 1) for w in square_y
        ])
        tables_z = np.stack([
            np.concatenate([np.kron(unit_y, w[:, h * reach : (h + 1) * reach].T) for h in range(4)])
            for w in square_z
        ])
        table_y2, table_z2 = pick_tables(info, jnp.asarray(half(tables_y)), jnp.asarray(half(tables_z)))
        twice_x, once_x, *_ = along_x(raw1, [full_x @ full_x, full_x])
        first, second = along_y(twice_x, twice_x)
        sent = filter_faces(info, first, twice_x, second, table_y2)
        first, second = swapped(*sent, "gz")
        parts2 = all_courses(None, first, list(sent), second, table_z2)
    else:
        once_x, *faces1 = along_x(raw1, [full_x])
        again = whole_gradient(info, *along_rest(once_x, *faces1), table_z)
        acc2, first, second = along_rest(*along_x(again, [full_x]))
        parts2 = all_courses(acc2, first, [], second, table_z)

    kept, fade1 = first_fade(info, half1)
    raw2, half2, scale1 = second_gradient(
        info, parts2, half1, kept, bold, chans, size_y, size_z, all_cells
    )
    fades, field1, *faces1 = second_fade(info, half2, fade1, scale1, once_x, face_y)
    first1, second1 = along_y(*faces1)
    below = filter_faces(info, first1, field1, second1, table_ends)
    acc1 = filter_lanes(info, first1, field1, second1, table_own)
    base = faded_maps(info, voxel_maps, fades)

    field2, *faces2 = along_x(raw2, [full_x])
    first2, second2 = along_y(*faces2)
    ends = swapped(*filter_faces(info, first2, field2, second2, table_ends, below), "gz")
    acc2 = filter_lanes(info, first2, field2, second2, table_own)
    grad2, energies = gradient_energy(info, acc2, *ends, table_z, peers)
    energies = exchanged(energies)
    base, grad2 = turned_gradients(info, acc1, *ends, table_z, base, grad2)
    maps = final_maps(info, energies, base, grad2, all_cells).reshape(size_x, size_y, size_z, chans)
    return (jnp.transpose(maps, (3, 0, 1, 2)), half2)


def solution(mesh):
    return jax.shard_map(
        per_device,
        mesh=mesh,
        in_specs=(P("gx", "gy", "gz", None), P(None, "gx", "gy", "gz"), P("gx", "gy", "gz")),
        out_specs=(P(None, "gx", "gy", "gz"), P()),
        check_vma=False,
    )
```

time: 631 us -> 179 us (0.28); the launches traced: 621 us -> 178 us
  waiting for transfers between devices: 383 us -> 48.5 us
  blocking collectives: 93.6 us -> 49 us
  matrix products: 42.8 us -> 0 us
  Pallas kernels: 0 us -> 40.7 us
  starting transfers between devices: 51.6 us -> 28.4 us
  between operations: 18.2 us -> 1.81 us
  local copies, waits for them, and re-layouts: 20.9 us -> 9.51 us
  other arithmetic: 11.2 us -> 0.01 us
    psum x2 -> x0, waiting for transfers between devices: 257 us -> none  [per_device(): courses = lax.psum(partial_courses, ('gx', 'gy', 'gz'))]
    psum x2 -> x0, blocking collectives: 93.6 us -> none  [per_device(): energy = lax.psum(jnp.sum(grad * grad), ('gx', 'gy', 'gz')) / all_cells]
    ppermute x24 -> x17, waiting for transfers between devices: 125 us -> 41.8 us  [the longest x3 30.3 us: along_x(): got = lax.ppermute(block, 'gx', [(0, 1), (1, 0)])]
    all_to_all x0 -> x3, blocking collectives: none -> 49 us  [exchanged(): return lax.all_to_all(parts, AXES, 0, 0, tiled=True)]
    dot_general x20 -> x0, matrix products: 42.8 us -> none  [the longest x12 24.9 us: filter_along(): jnp.tensordot(field, band, axes=((axis,), (0,)), precision=lax.Precision....]
    pallas_call x0 -> x27, Pallas kernels: none -> 40.7 us  [call(): pl.pallas_call(body, out_shape=shapes, in_specs=[pl.BlockSpec(memory_spac...]
    ppermute x24 -> x17, starting transfers between devices: 51.5 us -> 15.2 us  [the longest x14 10.8 us: swapped(): got[start] = lax.ppermute((first, second)[start], axis, pairs)]
    all_to_all x0 -> x2, starting transfers between devices: none -> 13.2 us  [exchanged(): return lax.all_to_all(parts, AXES, 0, 0, tiled=True)]
  transfers between devices with their start and end apart: 26 -> 19, of which waited for: 24 -> 10; matrix products, arithmetic and copies ran while one was open for 1% -> 0% of each run, Pallas kernels for 0% -> 10%
where the time goes in v3:
time: 179 us; the launch traced here: 178 us
  blocking collectives  49 us (27%)
  waiting for transfers between devices  48.5 us (27%)
  Pallas kernels  40.7 us (23%)
  starting transfers between devices  28.4 us (16%)
  local copies, waits for them, and re-layouts  9.51 us (5%)
  between operations  1.81 us (1%)
    all_to_all x3, blocking collectives, exchanged(): return lax.all_to_all(parts, AXES, 0, 0, tiled=True)  49 us
    pallas_call x27, Pallas kernels, call(): pl.pallas_call(body, out_shape=shapes, in_specs=[pl.BlockSpec(memory_spac...  40.7 us
    ppermute x3, waiting for transfers between devices, along_x(): got = lax.ppermute(block, 'gx', [(0, 1), (1, 0)])  30.3 us
    all_to_all x2, starting transfers between devices, exchanged(): return lax.all_to_all(parts, AXES, 0, 0, tiled=True)  13.2 us
    ppermute x14, waiting for transfers between devices, swapped(): got[start] = lax.ppermute((first, second)[start], axis, pairs)  11.4 us
    ppermute x14, starting transfers between devices, swapped(): got[start] = lax.ppermute((first, second)[start], axis, pairs)  10.8 us
    unnamed x54, local copies, waits for them, and re-layouts  9.42 us
    all_to_all x2, waiting for transfers between devices, exchanged(): return lax.all_to_all(parts, AXES, 0, 0, tiled=True)  6.78 us
  transfers between devices with their start and end apart: 19, of which 10 were waited for; matrix products, arithmetic and copies ran while one was open for 0% of the time, Pallas kernels for 10%

profile of v3, /device:TPU:0, one launch (start us, length us, event | category | flops | bytes accessed | tf_op | source)
XLA Modules:
  0.0 178.1 jit_solution(8575854265854947318)
XLA Ops:
  1.3 0.1 stack.23._.info_ref
  1.4 1.6 copy-done.3
  3.0 1.0 pack_maps.1.refs_0_
  4.0 3.0 %collective-permute-start = (bf16[512,512]{1,0:T(8,128)(2,1)S(1)}, bf16[512,512]{1,0:T(8,128)(2,1)S(1)}, u32[]{:S(2)}, u32[]{:S(2)}) collective-permute-start(bf16[512,512]{1,0:T(8,128)(2,1)S(1)} %pack_maps.1.refs_0_), channel_id=1, source_target_pairs={{0,16},{16,0},{1,17},{17,1},{2,18},{18,2},{3,19},{19,3},{4,20},{20... | collective-permute-start | bytes 1572872 | tf_op jit(solution)/shard_map/ppermute | solution.py:490
  7.1 1.1 mix_layers.6.refs_1_
  8.1 10.9 %collective-permute-done.refs_0_ = bf16[512,512]{1,0:T(8,128)(2,1)S(1)} collective-permute-done((bf16[512,512]{1,0:T(8,128)(2,1)S(1)}, bf16[512,512]{1,0:T(8,128)(2,1)S(1)}, u32[]{:S(2)}, u32[]{:S(2)}) %collective-permute-start) | collective-permute-done | bytes 524320 | tf_op jit(solution)/shard_map/ppermute | solution.py:490
  19.0 1.0 mix_layers.7
  20.0 0.7 collective-permute-start.2
  20.7 0.8 collective-permute-done.1.first_ref
  21.6 1.0 filter_faces.4
  22.6 1.9 %collective-permute-start.3 = (bf16[512,128]{1,0:T(8,128)(2,1)S(1)}, bf16[512,128]{1,0:T(8,128)(2,1)S(1)}, u32[]{:S(2)}, u32[]{:S(2)}) collective-permute-start(bf16[512,128]{1,0:T(8,128)(2,1)S(1)} %get-tuple-element.40), channel_id=1, source_target_pairs={{0,1},{2,3},{1,0},{3,2},{4,5},{6,7},{5,4},{7,6},{8,9},{10,11},{9,8... | collective-permute-start | bytes 393224 | tf_op jit(solution)/shard_map/ppermute | solution.py:443
  24.5 0.7 collective-permute-start.4
  25.2 1.3 filter_lanes.3.refs_3_
  26.4 1.2 collective-permute-done.3.first_ref
  27.7 2.3 %courses_of.2 = bf16[32,8,128]{2,1,0:T(8,128)(2,1)S(1)} custom-call(s32[6]{0:T(128)S(1)} %stack.23._.info_ref, bf16[512,128]{1,0:T(8,128)(2,1)S(1)} %collective-permute-done.3.first_ref, bf16[512,128]{1,0:T(8,128)(2,1)S(1)} %collective-permute-done.4.refs_0_, bf16[256,512]{1,0:T(8,128)(2,1)S(1)} %copy-done.7, bf16[4096,512]{1,0:T(8,128)(2,1)S(1)} %bitcast.14, ...), custom_call_target="tpu_custom_call" | custom-call | flops 1000000000 | bytes 5767168 | tf_op jit(solution)/shard_map/courses_of/pallas_call | solution.py:52
  30.0 22.0 %all_to_all.25.src = bf16[32,8,128]{2,1,0:T(8,128)(2,1)S(1)} all-to-all(bf16[32,8,128]{2,1,0:T(8,128)(2,1)S(1)} %courses_of.2), channel_id=1, replica_groups=mesh['gx'=2,'gy'=4,'gz'=4] {'gx','gy','gz'}, dimensions={0} | all-to-all | bytes 131072 | tf_op jit(solution)/shard_map/all_to_all | solution.py:455
  51.9 0.6 sum_parts.2
  52.5 9.2 %all_to_all.26.parts_ref = bf16[32,8,128]{2,1,0:T(8,128)(2,1)S(1)} all-to-all(bf16[32,8,128]{2,1,0:T(8,128)(2,1)S(1)} %sum_parts.2), channel_id=1, replica_groups=mesh['gx'=2,'gy'=4,'gz'=4] {'gx','gy','gz'}, dimensions={0} | all-to-all | bytes 131072 | tf_op jit(solution)/shard_map/all_to_all | solution.py:455
  61.7 1.9 %first_gradient.1 = (bf16[512,512]{1,0:T(8,128)(2,1)S(1)}, bf16[64,512]{1,0:T(8,128)(2,1)S(1)}) custom-call(s32[6]{0:T(128)S(1)} %stack.23._.info_ref, bf16[32,8,128]{2,1,0:T(8,128)(2,1)S(1)} %all_to_all.26.parts_ref, bf16[4096,512]{1,0:T(8,128)(2,1)S(1)} %bitcast.15), custom_call_target="tpu_custom_call" | custom-call | flops 1000000000 | bytes 4259840 | tf_op jit(solution)/shard_map/first_gradient/pallas_call | solution.py:52
  63.6 0.7 collective-permute-start.5
  64.3 1.6 mix_layers.8
  66.0 11.2 %collective-permute-done.5.refs_0_ = bf16[512,512]{1,0:T(8,128)(2,1)S(1)} collective-permute-done((bf16[512,512]{1,0:T(8,128)(2,1)S(1)}, bf16[512,512]{1,0:T(8,128)(2,1)S(1)}, u32[]{:S(2)}, u32[]{:S(2)}) %collective-permute-start.5) | collective-permute-done | bytes 524320 | tf_op jit(solution)/shard_map/ppermute | solution.py:490
  77.1 2.4 %mix_layers.9 = (bf16[512,512]{1,0:T(8,128)(2,1)S(1)}, bf16[512,512]{1,0:T(8,128)(2,1)S(1)}, bf16[512,256]{1,0:T(8,128)(2,1)}, bf16[512,256]{1,0:T(8,128)(2,1)}) custom-call(s32[6]{0:T(128)S(1)} %stack.23._.info_ref, bf16[512,512]{1,0:T(8,128)(2,1)S(1)} %collective-permute-done.5.refs_0_, f32[512,512]{1,0:T(8,128)S(1)} %get-tuple-element.43.refs_1_, ...), custom_call_target="tpu_custom_call" | custom-call | flops 100000000 | bytes 2621440 | tf_op jit(solution)/shard_map/mix_layers/pallas_call | solution.py:52
  79.5 0.8 copy-done.22
  80.3 0.7 collective-permute-start.7
  81.0 2.3 %collective-permute-start.6 = (bf16[512,512]{1,0:T(8,128)(2,1)S(1)}, bf16[512,512]{1,0:T(8,128)(2,1)S(1)}, u32[]{:S(2)}, u32[]{:S(2)}) collective-permute-start(bf16[512,512]{1,0:T(8,128)(2,1)S(1)} %get-tuple-element.45.middle_ref), channel_id=1, source_target_pairs={{0,4},{8,12},{4,0},{12,8},{1,5},{9,13},{5,1},{13,9},{2,6},{10,14},... | collective-permute-start | bytes 1572872 | tf_op jit(solution)/shard_map/ppermute | solution.py:443
  83.3 0.7 pick_tables.1
  84.0 0.8 collective-permute-done.6.first_ref
  84.8 1.6 filter_faces.5
  86.4 0.6 collective-permute-start.8
  87.0 0.8 collective-permute-start.9
  87.8 5.0 %collective-permute-done.8.first_ref = bf16[512,256]{1,0:T(8,128)(2,1)S(1)} collective-permute-done((bf16[512,256]{1,0:T(8,128)(2,1)S(1)}, bf16[512,256]{1,0:T(8,128)(2,1)S(1)}, u32[]{:S(2)}, u32[]{:S(2)}) %collective-permute-start.8) | collective-permute-done | bytes 262176 | tf_op jit(solution)/shard_map/ppermute | solution.py:443
  92.8 3.3 %courses_of.3 = bf16[32,8,128]{2,1,0:T(8,128)(2,1)S(1)} custom-call(s32[6]{0:T(128)S(1)} %stack.23._.info_ref, bf16[512,256]{1,0:T(8,128)(2,1)S(1)} %collective-permute-done.8.first_ref, bf16[512,256]{1,0:T(8,128)(2,1)S(1)} %get-tuple-element.47.refs_0_, bf16[512,256]{1,0:T(8,128)(2,1)S(1)} %get-tuple-element.48.refs_1_, ...), custom_call_target="tpu_custom_call" | custom-call | flops 1000000000 | bytes 6291456 | tf_op jit(solution)/shard_map/courses_of/pallas_call | solution.py:52
  96.1 17.9 %all_to_all.27.src = bf16[32,8,128]{2,1,0:T(8,128)(2,1)S(1)} all-to-all(bf16[32,8,128]{2,1,0:T(8,128)(2,1)S(1)} %courses_of.3), channel_id=1, replica_groups=mesh['gx'=2,'gy'=4,'gz'=4] {'gx','gy','gz'}, dimensions={0} | all-to-all | bytes 131072 | tf_op jit(solution)/shard_map/all_to_all | solution.py:455
  114.0 1.2 sum_parts.3
  115.2 2.6 %all-to-all-start.3 = ((bf16[32,8,128]{2,1,0:T(8,128)(2,1)}), bf16[32,8,128]{2,1,0:T(8,128)(2,1)S(1)}, u32[]{:S(2)}, u32[]{:S(2)}) async-start(bf16[32,8,128]{2,1,0:T(8,128)(2,1)} %sum_parts.3), calls=%async_computation.3 | async-start | bytes 131072 | tf_op jit(solution)/shard_map/all_to_all | solution.py:455
  117.8 0.9 first_fade.1
  118.7 6.6 %all-to-all-done.3.parts_ref = bf16[32,8,128]{2,1,0:T(8,128)(2,1)S(1)} async-done(((bf16[32,8,128]{2,1,0:T(8,128)(2,1)}), bf16[32,8,128]{2,1,0:T(8,128)(2,1)S(1)}, u32[]{:S(2)}, u32[]{:S(2)}) %all-to-all-start.3) | async-done | bytes 65568 | tf_op jit(solution)/shard_map/all_to_all | solution.py:455
  125.3 2.2 %copy-done.1 = bf16[8,16,32,512]{3,2,1,0:T(8,128)(2,1)S(1)} copy-done((bf16[8,16,32,512]{3,2,1,0:T(8,128)(2,1)S(1)}, bf16[8,16,32,512]{3,2,1,0:T(8,128)(2,1)}, u32[]{:S(2)}) %copy-start.1) | copy-done | bytes 4194328
  127.5 2.5 %second_gradient.1 = (bf16[512,512]{1,0:T(8,128)(2,1)S(1)}, bf16[64,512]{1,0:T(8,128)(2,1)}, f32[1,1]{1,0:T(1,128)}) custom-call(s32[6]{0:T(128)S(1)} %stack.23._.info_ref, bf16[32,8,128]{2,1,0:T(8,128)(2,1)S(1)} %all-to-all-done.3.parts_ref, bf16[64,512]{1,0:T(8,128)(2,1)S(1)} %get-tuple-element.50.half_ref.half1_ref, ...), custom_call_target="tpu_custom_call" | custom-call | flops 1000000000 | bytes 4456448 | tf_op jit(solution)/shard_map/second_gradient/pallas_call | solution.py:52
  130.0 0.7 collective-permute-start.10
  130.6 0.8 copy-done.24
  131.5 1.7 second_fade.1
  133.3 0.7 collective-permute-start.14
  134.0 1.1 mix_layers.10.refs_1_
  135.1 8.3 %collective-permute-done.10.refs_0_ = bf16[512,512]{1,0:T(8,128)(2,1)S(1)} collective-permute-done((bf16[512,512]{1,0:T(8,128)(2,1)S(1)}, bf16[512,512]{1,0:T(8,128)(2,1)S(1)}, u32[]{:S(2)}, u32[]{:S(2)}) %collective-permute-start.10) | collective-permute-done | bytes 524320 | tf_op jit(solution)/shard_map/ppermute | solution.py:490
  143.4 1.0 mix_layers.11
  144.5 0.7 collective-permute-start.12
  145.2 1.0 filter_faces.6
  146.2 1.0 filter_faces.7
  147.3 0.8 collective-permute-start.15
  148.1 0.8 collective-permute-start.16
  148.9 1.3 filter_lanes.4.start
  150.2 3.6 %collective-permute-done.15.first_ref = bf16[1024,128]{1,0:T(8,128)(2,1)S(1)} collective-permute-done((bf16[1024,128]{1,0:T(8,128)(2,1)S(1)}, bf16[1024,128]{1,0:T(8,128)(2,1)S(1)}, u32[]{:S(2)}, u32[]{:S(2)}) %collective-permute-start.15) | collective-permute-done | bytes 262176 | tf_op jit(solution)/shard_map/ppermute | solution.py:443
  153.7 1.7 gradient_energy.1
  155.4 1.0 copy-done.12
  156.4 10.6 %all-to-all-start.4 = ((f32[32,1,128]{2,1,0:T(1,128)}), f32[32,1,128]{2,1,0:T(1,128)S(1)}, u32[]{:S(2)}, u32[]{:S(2)}) async-start(f32[32,1,128]{2,1,0:T(1,128)} %get-tuple-element.67), calls=%async_computation.4 | async-start | bytes 32768 | tf_op jit(solution)/shard_map/all_to_all | solution.py:455
  167.1 2.4 %faded_maps.1.base_ref = f32[8,512,64]{2,1,0:T(8,128)S(1)} custom-call(s32[6]{0:T(128)S(1)} %stack.23._.info_ref, f32[8,512,64]{2,1,0:T(8,128)S(1)} %bitcast.19, f32[64,64]{1,0:T(8,128)S(1)} %get-tuple-element.68.fades_ref), custom_call_target="tpu_custom_call" | custom-call | flops 1000000000 | bytes 1064960 | tf_op jit(solution)/shard_map/faded_maps/pallas_call | solution.py:52
  169.5 1.3 filter_lanes.5.start
  170.8 1.9 %turned_gradients.1 = (f32[8,512,64]{2,1,0:T(8,128)S(1)}, f32[8,512,64]{2,1,0:T(8,128)S(1)}) custom-call(s32[6]{0:T(128)S(1)} %stack.23._.info_ref, f32[512,512]{1,0:T(8,128)S(1)} %filter_lanes.5.start, bf16[1024,128]{1,0:T(8,128)(2,1)S(1)} %copy-done.15, bf16[1024,128]{1,0:T(8,128)(2,1)S(1)} %copy-done.17, bf16[256,512]{1,0:T(8,128)(2,1)S(1)} %copy-done.7, ...), custom_call_target="tpu_custom_call" | custom-call | flops 100000000 | bytes 3932160 | tf_op jit(solution)/shard_map/turned_gradients/pallas_call | solution.py:52
  172.7 1.3 copy-done.8
  174.0 0.2 all-to-all-done.4.energies_ref
  174.2 1.6 copy-done.9
  175.8 2.3 %final_maps.1 = f32[8,512,64]{2,1,0:T(8,128)} custom-call(s32[6]{0:T(128)S(1)} %stack.23._.info_ref, f32[32,1,128]{2,1,0:T(1,128)S(1)} %all-to-all-done.4.energies_ref, f32[8,512,64]{2,1,0:T(8,128)S(1)} %get-tuple-element.70.base_ref, f32[8,512,64]{2,1,0:T(8,128)S(1)} %copy-done.9), custom_call_target="tpu_custom_call" | custom-call | flops 100000000 | bytes 2113536 | tf_op jit(solution)/shard_map/final_maps/pallas_call | solution.py:52
  (60 shorter events, 0.4 us)
Async XLA Ops:
  1.4 1.6 copy-start.3
  4.0 17.6 %copy-start.5 = (bf16[1024,256]{1,0:T(8,128)(2,1)S(1)}, bf16[1024,256]{1,0:T(8,128)(2,1)}, u32[]{:S(2)}) copy-start(bf16[1024,256]{1,0:T(8,128)(2,1)} %constant.40.clone.weights) | copy-start | bytes 1572868
  4.0 21.1 %copy-start.2 = (bf16[1024,512]{1,0:T(8,128)(2,1)S(1)}, bf16[1024,512]{1,0:T(8,128)(2,1)}, u32[]{:S(2)}) copy-start(bf16[1024,512]{1,0:T(8,128)(2,1)} %constant.41.clone.weights) | copy-start | bytes 3145732
  4.0 15.0 %collective-permute-start = (bf16[512,512]{1,0:T(8,128)(2,1)S(1)}, bf16[512,512]{1,0:T(8,128)(2,1)S(1)}, u32[]{:S(2)}, u32[]{:S(2)}) collective-permute-start(bf16[512,512]{1,0:T(8,128)(2,1)S(1)} %pack_maps.1.refs_0_), channel_id=1, source_target_pairs={{0,16},{16,0},{1,17},{17,1},{2,18},{18,2},{3,19},{19,3},{4,20},{20... | collective-permute-start | bytes 1572872 | tf_op jit(solution)/shard_map/ppermute | solution.py:490
  20.0 1.6 collective-permute-start.1
  20.0 1.5 collective-permute-start.2
  21.6 6.1 %copy-start = (bf16[8,16,32,512]{3,2,1,0:T(8,128)(2,1)S(1)}, bf16[8,16,32,512]{3,2,1,0:T(8,128)(2,1)}, u32[]{:S(2)}) copy-start(bf16[8,16,32,512]{3,2,1,0:T(8,128)(2,1)} %param.8) | copy-start | bytes 12582916
  21.6 6.1 %copy-start.7 = (bf16[256,512]{1,0:T(8,128)(2,1)S(1)}, bf16[256,512]{1,0:T(8,128)(2,1)}, u32[]{:S(2)}) copy-start(bf16[256,512]{1,0:T(8,128)(2,1)} %constant.42.clone.refs_1_.weights) | copy-start | bytes 786436
  22.6 5.0 %collective-permute-start.3 = (bf16[512,128]{1,0:T(8,128)(2,1)S(1)}, bf16[512,128]{1,0:T(8,128)(2,1)S(1)}, u32[]{:S(2)}, u32[]{:S(2)}) collective-permute-start(bf16[512,128]{1,0:T(8,128)(2,1)S(1)} %get-tuple-element.40), channel_id=1, source_target_pairs={{0,1},{2,3},{1,0},{3,2},{4,5},{6,7},{5,4},{7,6},{8,9},{10,11},{9,8... | collective-permute-start | bytes 393224 | tf_op jit(solution)/shard_map/ppermute | solution.py:443
  24.5 3.2 %collective-permute-start.4 = (bf16[512,128]{1,0:T(8,128)(2,1)S(1)}, bf16[512,128]{1,0:T(8,128)(2,1)S(1)}, u32[]{:S(2)}, u32[]{:S(2)}) collective-permute-start(bf16[512,128]{1,0:T(8,128)(2,1)S(1)} %get-tuple-element.41), channel_id=1, source_target_pairs={{1,2},{2,1},{5,6},{6,5},{9,10},{10,9},{13,14},{14,13},{17,18},{18,... | collective-permute-start | bytes 393224 | tf_op jit(solution)/shard_map/ppermute | solution.py:443
  25.1 58.1 %slice-start = ((s8[6291456]{0:T(1024)(128)(4,1)}), s8[4194304]{0:T(1024)(128)(4,1)S(1)}, s32[]{:S(2)}) async-start(s8[6291456]{0:T(1024)(128)(4,1)} %bitcast.20), calls=%async_computation.5 | async-start | bytes 8388608
  27.6 55.6 %slice-start.1 = ((s8[6291456]{0:T(1024)(128)(4,1)}), s8[2097152]{0:T(1024)(128)(4,1)S(1)}, s32[]{:S(2)}) async-start(s8[6291456]{0:T(1024)(128)(4,1)} %bitcast.20), calls=%async_computation.6 | async-start | bytes 4194304
  61.7 21.6 %copy-start.6 = (bf16[4,1024,512]{2,1,0:T(8,128)(2,1)S(1)}, bf16[4,1024,512]{2,1,0:T(8,128)(2,1)}, u32[]{:S(2)}) copy-start(bf16[4,1024,512]{2,1,0:T(8,128)(2,1)} %constant.44.clone.all_z) | copy-start | bytes 12582916
  63.6 13.5 %collective-permute-start.5 = (bf16[512,512]{1,0:T(8,128)(2,1)S(1)}, bf16[512,512]{1,0:T(8,128)(2,1)S(1)}, u32[]{:S(2)}, u32[]{:S(2)}) collective-permute-start(bf16[512,512]{1,0:T(8,128)(2,1)S(1)} %get-tuple-element.42.refs_0_), channel_id=1, source_target_pairs={{0,16},{16,0},{1,17},{17,1},{2,18},{18,2},{3,19},{19,3},{4,20},{20... | collective-permute-start | bytes 1572872 | tf_op jit(solution)/shard_map/ppermute | solution.py:490
  79.5 0.8 copy-start.22
  80.3 3.8 %collective-permute-start.7 = (bf16[512,512]{1,0:T(8,128)(2,1)S(1)}, bf16[512,512]{1,0:T(8,128)(2,1)S(1)}, u32[]{:S(2)}, u32[]{:S(2)}) collective-permute-start(bf16[512,512]{1,0:T(8,128)(2,1)S(1)} %get-tuple-element.45.middle_ref), channel_id=1, source_target_pairs={{4,8},{8,4},{5,9},{9,5},{6,10},{10,6},{7,11},{11,7},{20,24},{24,20... | collective-permute-start | bytes 1572872 | tf_op jit(solution)/shard_map/ppermute | solution.py:443
  81.0 3.8 %collective-permute-start.6 = (bf16[512,512]{1,0:T(8,128)(2,1)S(1)}, bf16[512,512]{1,0:T(8,128)(2,1)S(1)}, u32[]{:S(2)}, u32[]{:S(2)}) collective-permute-start(bf16[512,512]{1,0:T(8,128)(2,1)S(1)} %get-tuple-element.45.middle_ref), channel_id=1, source_target_pairs={{0,4},{8,12},{4,0},{12,8},{1,5},{9,13},{5,1},{13,9},{2,6},{10,14},... | collective-permute-start | bytes 1572872 | tf_op jit(solution)/shard_map/ppermute | solution.py:443
  86.4 6.4 %collective-permute-start.8 = (bf16[512,256]{1,0:T(8,128)(2,1)S(1)}, bf16[512,256]{1,0:T(8,128)(2,1)S(1)}, u32[]{:S(2)}, u32[]{:S(2)}) collective-permute-start(bf16[512,256]{1,0:T(8,128)(2,1)S(1)} %get-tuple-element.47.refs_0_), channel_id=1, source_target_pairs={{0,1},{2,3},{1,0},{3,2},{4,5},{6,7},{5,4},{7,6},{8,9},{10,11},{9,8... | collective-permute-start | bytes 786440 | tf_op jit(solution)/shard_map/ppermute | solution.py:443
  87.0 5.9 %collective-permute-start.9 = (bf16[512,256]{1,0:T(8,128)(2,1)S(1)}, bf16[512,256]{1,0:T(8,128)(2,1)S(1)}, u32[]{:S(2)}, u32[]{:S(2)}) collective-permute-start(bf16[512,256]{1,0:T(8,128)(2,1)S(1)} %get-tuple-element.48.refs_1_), channel_id=1, source_target_pairs={{1,2},{2,1},{5,6},{6,5},{9,10},{10,9},{13,14},{14,13},{17,18},{18,... | collective-permute-start | bytes 786440 | tf_op jit(solution)/shard_map/ppermute | solution.py:443
  115.2 10.1 %all-to-all-start.3 = ((bf16[32,8,128]{2,1,0:T(8,128)(2,1)}), bf16[32,8,128]{2,1,0:T(8,128)(2,1)S(1)}, u32[]{:S(2)}, u32[]{:S(2)}) async-start(bf16[32,8,128]{2,1,0:T(8,128)(2,1)} %sum_parts.3), calls=%async_computation.3 | async-start | bytes 131072 | tf_op jit(solution)/shard_map/all_to_all | solution.py:455
  125.3 2.2 %copy-start.1 = (bf16[8,16,32,512]{3,2,1,0:T(8,128)(2,1)S(1)}, bf16[8,16,32,512]{3,2,1,0:T(8,128)(2,1)}, u32[]{:S(2)}) copy-start(bf16[8,16,32,512]{3,2,1,0:T(8,128)(2,1)} %param.8) | copy-start | bytes 12582916
  127.5 3.1 %copy-start.23 = (bf16[512,512]{1,0:T(8,128)(2,1)S(1)}, bf16[512,512]{1,0:T(8,128)(2,1)}, u32[]{:S(2)}) copy-start(bf16[512,512]{1,0:T(8,128)(2,1)} %copy-done.22) | copy-start | bytes 1572868
  130.0 13.4 %collective-permute-start.10 = (bf16[512,512]{1,0:T(8,128)(2,1)S(1)}, bf16[512,512]{1,0:T(8,128)(2,1)S(1)}, u32[]{:S(2)}, u32[]{:S(2)}) collective-permute-start(bf16[512,512]{1,0:T(8,128)(2,1)S(1)} %get-tuple-element.52.refs_0_), channel_id=1, source_target_pairs={{0,16},{16,0},{1,17},{17,1},{2,18},{18,2},{3,19},{19,3},{4,20},{20... | collective-permute-start | bytes 1572872 | tf_op jit(solution)/shard_map/ppermute | solution.py:490
  130.6 0.8 copy-start.24
  133.2 13.0 %copy-start.10 = (bf16[512,512]{1,0:T(8,128)(2,1)}, bf16[512,512]{1,0:T(8,128)(2,1)S(1)}, u32[]{:S(2)}) copy-start(bf16[512,512]{1,0:T(8,128)(2,1)S(1)} %get-tuple-element.61.middle_ref) | copy-start | bytes 1572868
  133.2 11.9 %collective-permute-start.13 = (bf16[512,256]{1,0:T(8,128)(2,1)S(1)}, bf16[512,256]{1,0:T(8,128)(2,1)S(1)}, u32[]{:S(2)}, u32[]{:S(2)}) collective-permute-start(bf16[512,256]{1,0:T(8,128)(2,1)S(1)} %get-tuple-element.60), channel_id=1, source_target_pairs={{0,4},{8,12},{4,0},{12,8},{1,5},{9,13},{5,1},{13,9},{2,6},{10,14},... | collective-permute-start | bytes 786440 | tf_op jit(solution)/shard_map/ppermute | solution.py:443
  133.3 11.9 %collective-permute-start.14 = (bf16[512,256]{1,0:T(8,128)(2,1)S(1)}, bf16[512,256]{1,0:T(8,128)(2,1)S(1)}, u32[]{:S(2)}, u32[]{:S(2)}) collective-permute-start(bf16[512,256]{1,0:T(8,128)(2,1)S(1)} %get-tuple-element.62), channel_id=1, source_target_pairs={{4,8},{8,4},{5,9},{9,5},{6,10},{10,6},{7,11},{11,7},{20,24},{24,20... | collective-permute-start | bytes 786440 | tf_op jit(solution)/shard_map/ppermute | solution.py:443
  144.4 1.8 %collective-permute-start.11 = (bf16[512,256]{1,0:T(8,128)(2,1)S(1)}, bf16[512,256]{1,0:T(8,128)(2,1)S(1)}, u32[]{:S(2)}, u32[]{:S(2)}) collective-permute-start(bf16[512,256]{1,0:T(8,128)(2,1)S(1)} %get-tuple-element.53), channel_id=1, source_target_pairs={{0,4},{8,12},{4,0},{12,8},{1,5},{9,13},{5,1},{13,9},{2,6},{10,14},... | collective-permute-start | bytes 786440 | tf_op jit(solution)/shard_map/ppermute | solution.py:443
  144.5 1.8 collective-permute-start.12
  145.2 1.1 copy-start.18
  145.2 2.1 %copy-start.20 = (bf16[512,256]{1,0:T(8,128)(2,1)}, bf16[512,256]{1,0:T(8,128)(2,1)S(1)}, u32[]{:S(2)}) copy-start(bf16[512,256]{1,0:T(8,128)(2,1)S(1)} %collective-permute-done.14.second_ref) | copy-start | bytes 786436
  147.3 6.4 %collective-permute-start.15 = (bf16[1024,128]{1,0:T(8,128)(2,1)S(1)}, bf16[1024,128]{1,0:T(8,128)(2,1)S(1)}, u32[]{:S(2)}, u32[]{:S(2)}) collective-permute-start(bf16[1024,128]{1,0:T(8,128)(2,1)S(1)} %get-tuple-element.65), channel_id=1, source_target_pairs={{0,1},{2,3},{1,0},{3,2},{4,5},{6,7},{5,4},{7,6},{8,9},{10,11},{9,8... | collective-permute-start | bytes 786440 | tf_op jit(solution)/shard_map/ppermute | solution.py:443
  148.1 18.9 %copy-start.4 = (f32[64,8,16,32]{0,3,2,1:T(8,128)S(1)}, f32[64,8,16,32]{0,3,2,1:T(8,128)}, u32[]{:S(2)}) copy-start(f32[64,8,16,32]{0,3,2,1:T(8,128)} %param.9) | copy-start | bytes 3145732
  148.1 5.6 %collective-permute-start.16 = (bf16[1024,128]{1,0:T(8,128)(2,1)S(1)}, bf16[1024,128]{1,0:T(8,128)(2,1)S(1)}, u32[]{:S(2)}, u32[]{:S(2)}) collective-permute-start(bf16[1024,128]{1,0:T(8,128)(2,1)S(1)} %get-tuple-element.66), channel_id=1, source_target_pairs={{1,2},{2,1},{5,6},{6,5},{9,10},{10,9},{13,14},{14,13},{17,18},{18,... | collective-permute-start | bytes 786440 | tf_op jit(solution)/shard_map/ppermute | solution.py:443
  153.7 1.7 copy-start.14
  153.7 1.7 copy-start.16
  155.4 1.0 copy-start.12
  156.4 17.8 %all-to-all-start.4 = ((f32[32,1,128]{2,1,0:T(1,128)}), f32[32,1,128]{2,1,0:T(1,128)S(1)}, u32[]{:S(2)}, u32[]{:S(2)}) async-start(f32[32,1,128]{2,1,0:T(1,128)} %get-tuple-element.67), calls=%async_computation.4 | async-start | bytes 32768 | tf_op jit(solution)/shard_map/all_to_all | solution.py:455
  167.0 2.4 %copy-start.11 = (bf16[512,512]{1,0:T(8,128)(2,1)S(1)}, bf16[512,512]{1,0:T(8,128)(2,1)}, u32[]{:S(2)}) copy-start(bf16[512,512]{1,0:T(8,128)(2,1)} %copy-done.10) | copy-start | bytes 1572868
  167.1 2.4 %copy-start.19 = (bf16[512,256]{1,0:T(8,128)(2,1)S(1)}, bf16[512,256]{1,0:T(8,128)(2,1)}, u32[]{:S(2)}) copy-start(bf16[512,256]{1,0:T(8,128)(2,1)} %copy-done.18) | copy-start | bytes 786436
  167.1 2.4 %copy-start.21 = (bf16[512,256]{1,0:T(8,128)(2,1)S(1)}, bf16[512,256]{1,0:T(8,128)(2,1)}, u32[]{:S(2)}) copy-start(bf16[512,256]{1,0:T(8,128)(2,1)} %copy-done.20) | copy-start | bytes 786436
  169.5 1.3 copy-start.13
  169.5 1.3 copy-start.15
  169.5 1.3 copy-start.17
  172.7 1.3 copy-start.8
  174.2 1.6 copy-start.9

commit v4 on v3

--- a/solution.py
+++ b/solution.py
@@ -46,19 +46,35 @@
     return jax.ShapeDtypeStruct(dims, kind)
 
 
-def call(body, shapes, info, arrays, flops=10**8, name=None, spaces=None, scratch=()):
+def call(body, shapes, info, needs, arrays, flops=10**8, name=None, spaces=None, outs=None, scratch=(), after=()):
     total = sum(a.size * a.dtype.itemsize for a in arrays)
-    whole = pl.BlockSpec(memory_space=pltpu.VMEM)
+    whole, anywhere = pl.BlockSpec(memory_space=pltpu.VMEM), pl.BlockSpec(memory_space=pl.ANY)
+    count, ends = len(needs), len(needs) + len(arrays)
+
+    def wrapped(*refs):
+        numbers = {need: ref for need, ref in zip(needs, refs)}
+        body(Numbers(numbers), *refs[count:ends], *refs[ends + len(after) :])
+
     return pl.pallas_call(
-        body,
+        wrapped,
         out_shape=shapes,
-        in_specs=[pl.BlockSpec(memory_space=pltpu.SMEM)] + [spaces or whole] * len(arrays),
-        out_specs=jax.tree.map(lambda _: whole, shapes),
+        in_specs=[pl.BlockSpec(memory_space=pltpu.SMEM)] * count
+        + [spaces or whole] * len(arrays)
+        + [anywhere] * len(after),
+        out_specs=jax.tree.map(lambda _: outs or whole, shapes),
         scratch_shapes=scratch,
         compiler_params=pltpu.CompilerParams(vmem_limit_bytes=16 * 1024 * 1024),
         cost_estimate=pl.CostEstimate(flops=flops, bytes_accessed=total, transcendentals=0),
         name=name,
-    )(info, *arrays)
+    )(*(info[need] for need in needs), *arrays, *after)
+
+
+class Numbers:
+    def __init__(self, refs):
+        self.refs = refs
+
+    def __getitem__(self, need):
+        return self.refs[need][0]
 
 
 def dot(a, b):
@@ -87,7 +103,7 @@
         for x in range(layers):
             out[x * chans : (x + 1) * chans, :] = dot_nt(unit, src[x].astype(BF16)).astype(BF16)
 
-    return call(body, shape((layers * chans, plane), BF16), info, [voxel_maps], name="pack_maps")
+    return call(body, shape((layers * chans, plane), BF16), info, [], [voxel_maps], name="pack_maps")
 
 
 def pick_tables(info, table_y, table_z):
@@ -106,6 +122,7 @@
         body,
         shapes,
         info,
+        [PLACE_Y, PLACE_Z],
         [table_y, table_z],
         name="pick_tables",
         spaces=pl.BlockSpec(memory_space=pl.ANY),
@@ -141,7 +158,7 @@
     return total
 
 
-def mix_layers(info, coefs, chans, sources, sums, out_types, face=0):
+def mix_layers(info, coefs, chans, sources, sums, out_types, face=0, after=()):
     rows, plane = sources[0].shape
     outs = len(out_types)
     base = len(sources)
@@ -186,7 +203,8 @@
     shapes = tuple(shape((rows, plane), t) for t in out_types)
     if face:
         shapes += (shape((rows, face), out_types[0]),) * 2
-    return call(body, shapes, info, [*sources, *sums], name="mix_layers")
+    needs = ([PLACE_X] if len(coefs) > 1 else []) + ([ODD_Y] if face else [])
+    return call(body, shapes, info, needs, [*sources, *sums], name="mix_layers", after=after)
 
 
 def filter_lanes(info, first, middle, second, table):
@@ -194,10 +212,10 @@
         out[...] = swapped_dot(info_ref, ODD_Y, first_ref, [middle_ref], second_ref, weights)
 
     shapes = shape((first.shape[0], table.shape[1]), F32)
-    return call(body, shapes, info, [first, middle, second, table], name="filter_lanes")
-
-
-def filter_faces(info, first, middle, second, table, below=()):
+    return call(body, shapes, info, [ODD_Y], [first, middle, second, table], name="filter_lanes")
+
+
+def filter_faces(info, first, middle, second, table, below=(), after=()):
     rows, face = first.shape[0], table.shape[1] // 2
     extra = below[0].shape[0] if below else 0
 
@@ -209,7 +227,8 @@
             out[rows:, :] = src[...]
 
     shapes = (shape((rows + extra, face), BF16),) * 2
-    return call(body, shapes, info, [first, middle, second, table, *below], name="filter_faces")
+    arrays = [first, middle, second, table, *below]
+    return call(body, shapes, info, [ODD_Y, ODD_Z], arrays, name="filter_faces", after=after)
 
 
 def live_lanes(info_ref, layer, dims, size_y, size_z):
@@ -217,21 +236,14 @@
     return row < info_ref[COUNT]
 
 
-def spread_rows(chans, frames, peers):
-    rows = chans * frames // (peers * 128)
-    return rows if rows and rows * peers * 128 == chans * frames and chans % rows == 0 else 0
-
-
-def courses_of(info, acc, first, middle, second, table, bold, chans, size_y, size_z, peers):
+def courses_of(info, acc, first, middle, second, table, bold, chans, size_y, size_z):
     frames = bold.shape[1]
     plane = size_y * size_z
     layers = bold.shape[0] // plane
     between = len(middle)
-    part = spread_rows(chans, frames, peers)
 
     def body(info_ref, first_ref, *refs):
         ins, second_ref, weights, frames_ref = refs[:between], *refs[between : between + 3]
-        out = refs[-1]
         total = jnp.zeros((chans, frames), F32)
         for x in range(layers):
             rows = slice(x * chans, (x + 1) * chans)
@@ -241,45 +253,11 @@
             keep = live_lanes(info_ref, x, value.shape, size_y, size_z)
             value = jnp.where(keep, value, 0.0).astype(BF16)
             total = total + dot(value, frames_ref[x * plane : (x + 1) * plane, :])
-        if not part:
-            out[...] = total
-            return
-        across = frames // 128
-        for d in range(peers):
-            r, c = d // across * part, d % across * 128
-            out[d] = total[r : r + part, c : c + 128].astype(BF16)
+        refs[-1][...] = total
 
     arrays = [first, *middle, second, table, bold] + ([acc] if acc is not None else [])
-    shapes = shape((peers, part, 128), BF16) if part else shape((chans, frames), F32)
-    return call(body, shapes, info, arrays, flops=10**9, name="courses_of")
-
-
-def sum_parts(info, parts):
-    peers = parts.shape[0]
-
-    def body(_, src, out):
-        total = src[0].astype(F32)
-        for d in range(1, peers):
-            total = total + src[d].astype(F32)
-        total = total.astype(BF16)
-        for d in range(peers):
-            out[d] = total
-
-    return call(body, shape(parts.shape, BF16), info, [parts], name="sum_parts")
-
-
-def whole_courses(src, chans, frames):
-    if len(src.shape) == 2:
-        return src[...].astype(F32)
-    across = frames // 128
-    down = src.shape[0] // across
-    return jnp.concatenate(
-        [
-            jnp.concatenate([src[r * across + c].astype(F32) for c in range(across)], axis=1)
-            for r in range(down)
-        ],
-        axis=0,
-    )
+    shapes = shape((chans, frames), F32)
+    return call(body, shapes, info, [COUNT, ODD_Z], arrays, flops=10**9, name="courses_of")
 
 
 def write_gradient(info_ref, courses, frames_ref, out, chans, size_y, size_z):
@@ -290,16 +268,16 @@
         out[x * chans : (x + 1) * chans, :] = jnp.where(keep, value, 0.0).astype(BF16)
 
 
-def first_gradient(info, parts, bold, chans, size_y, size_z):
+def first_gradient(info, sums, bold, chans, size_y, size_z):
     cells, frames = bold.shape
 
-    def body(info_ref, parts_ref, frames_ref, out, half_ref):
-        courses = whole_courses(parts_ref, chans, frames).astype(BF16)
+    def body(info_ref, sums_ref, frames_ref, out, half_ref):
+        courses = sums_ref[...].astype(BF16)
         half_ref[...] = courses
         write_gradient(info_ref, courses, frames_ref, out, chans, size_y, size_z)
 
     shapes = (shape((cells * chans // (size_y * size_z), size_y * size_z), BF16), shape((chans, frames), BF16))
-    return call(body, shapes, info, [parts, bold], flops=10**9, name="first_gradient")
+    return call(body, shapes, info, [COUNT], [sums, bold], flops=10**9, name="first_gradient")
 
 
 def fade_of(courses):
@@ -318,14 +296,14 @@
         kept_ref[...] = jnp.dot(fade, half_ref[...].astype(F32), precision=FULL, preferred_element_type=F32)
 
     shapes = (shape((chans, frames), F32), shape((chans, chans), F32))
-    return call(body, shapes, info, [half1], name="first_fade")
-
-
-def second_gradient(info, parts, half1, kept, bold, chans, size_y, size_z, all_cells):
+    return call(body, shapes, info, [], [half1], name="first_fade")
+
+
+def second_gradient(info, change, half1, kept, bold, chans, size_y, size_z, all_cells):
     cells, frames = bold.shape
 
-    def body(info_ref, parts_ref, half1_ref, kept_ref, frames_ref, out, half_ref, scale_ref):
-        change = whole_courses(parts_ref, chans, frames)
+    def body(info_ref, change_ref, half1_ref, kept_ref, frames_ref, out, half_ref, scale_ref):
+        change = change_ref[...]
         energy = jnp.maximum(total_of(half1_ref[...].astype(F32) * change), 0.0) * (1.0 / all_cells)
         scale = 0.5 * lax.rsqrt(energy + 1e-06)
         scale_ref[...] = scale
@@ -338,7 +316,8 @@
         shape((chans, frames), BF16),
         shape((1, 1), F32),
     )
-    return call(body, shapes, info, [parts, half1, kept, bold], flops=10**9, name="second_gradient")
+    arrays = [change, half1, kept, bold]
+    return call(body, shapes, info, [COUNT], arrays, flops=10**9, name="second_gradient")
 
 
 def second_fade(info, half2, fade1, scale1, field, face):
@@ -363,7 +342,8 @@
         shape((rows, face), BF16),
         shape((rows, face), BF16),
     )
-    return call(body, shapes, info, [half2, fade1, scale1, field], flops=10**9, name="second_fade")
+    arrays = [half2, fade1, scale1, field]
+    return call(body, shapes, info, [ODD_Y], arrays, flops=10**9, name="second_fade")
 
 
 def faded_maps(info, voxel_maps, fades):
@@ -373,9 +353,8 @@
         for x in range(layers):
             out[x] = dot_nt(maps_ref[x], fades_ref[...], FULL)
 
-    return call(
-        body, shape((layers, plane, chans), F32), info, [voxel_maps, fades], flops=10**9, name="faded_maps"
-    )
+    shapes = shape((layers, plane, chans), F32)
+    return call(body, shapes, info, [], [voxel_maps, fades], flops=10**9, name="faded_maps")
 
 
 def whole_gradient(info, acc, first, second, table):
@@ -383,10 +362,11 @@
         value = start[...] + swapped_dot(info_ref, ODD_Z, first_ref, [], second_ref, weights)
         out[...] = value.astype(BF16)
 
-    return call(body, shape(acc.shape, BF16), info, [acc, first, second, table], name="whole_gradient")
-
-
-def gradient_energy(info, acc, first, second, table, peers):
+    arrays = [acc, first, second, table]
+    return call(body, shape(acc.shape, BF16), info, [ODD_Z], arrays, name="whole_gradient")
+
+
+def gradient_energy(info, acc, first, second, table, peers, after=()):
     rows, plane = acc.shape
     tall = min(rows, 128)
 
@@ -400,38 +380,41 @@
         energy[...] = jnp.broadcast_to(total_of(total).reshape(1, 1, 1), energy.shape)
 
     shapes = (shape((rows, plane), F32), shape((peers, 1, 128), F32))
-    return call(body, shapes, info, [acc, first, second, table], name="gradient_energy")
-
-
-def turned_gradients(info, acc, first, second, table, base, grad):
+    arrays = [acc, first, second, table]
+    return call(body, shapes, info, [ODD_Z], arrays, name="gradient_energy", after=after)
+
+
+def final_maps(info, energies, base, acc, first, second, table, grad, all_cells):
     layers, plane, chans = base.shape
     rows = acc.shape[0]
-
-    def body(info_ref, start, first_ref, second_ref, weights, base_ref, grad_ref, out, turned):
+    peers = energies.shape[0]
+
+    def body(info_ref, energies_ref, base_ref, start, first_ref, second_ref, weights, grad_ref, out, held, sems):
+        energy = energies_ref[0]
+        for d in range(1, peers):
+            energy = energy + energies_ref[d]
+        scale = 0.5 * lax.rsqrt(energy[:, :1] * (1.0 / all_cells) + 1e-06)
+        copies = []
         for x in range(layers):
             at = slice(x * chans, (x + 1) * chans)
             below = slice(rows + x * chans, rows + (x + 1) * chans)
             value = start[at, :] + swapped_dot(info_ref, ODD_Z, first_ref, [], second_ref, weights, below)
-            out[x] = base_ref[x] + value.T
-            turned[x] = grad_ref[at, :].T
-
-    shapes = (shape(base.shape, F32),) * 2
-    return call(body, shapes, info, [acc, first, second, table, base, grad], name="turned_gradients")
-
-
-def final_maps(info, energies, base, grad, all_cells):
-    layers, plane, chans = base.shape
-    peers = energies.shape[0]
-
-    def body(_, energies_ref, base_ref, grad_ref, out):
-        energy = energies_ref[0]
-        for d in range(1, peers):
-            energy = energy + energies_ref[d]
-        scale = 0.5 * lax.rsqrt(energy[:, :1] * (1.0 / all_cells) + 1e-06)
-        for x in range(layers):
-            out[x] = base_ref[x] + scale * grad_ref[x]
-
-    return call(body, shape(base.shape, F32), info, [energies, base, grad], name="final_maps")
+            held[x] = base_ref[x] + (value + scale * grad_ref[at, :]).T
+            copies.append(pltpu.make_async_copy(held.at[x], out.at[x], sems.at[x]))
+            copies[-1].start()
+        for copy in copies:
+            copy.wait()
+
+    return call(
+        body,
+        shape(base.shape, F32),
+        info,
+        [ODD_Z],
+        [energies, base, acc, first, second, table, grad],
+        name="final_maps",
+        outs=pl.BlockSpec(memory_space=pl.ANY),
+        scratch=(pltpu.VMEM(base.shape, F32), pltpu.SemaphoreType.DMA((layers,))),
+    )
 
 
 def swapped(first, second, axis, inner_first=False):
@@ -455,6 +438,20 @@
     return lax.all_to_all(parts, AXES, 0, 0, tiled=True)
 
 
+def hypercube_sum(value):
+    steps = []
+    for axis in AXES:
+        peers = lax.axis_size(axis)
+        if peers & (peers - 1):
+            return lax.psum(value, AXES)
+        steps += [(axis, 1 << b) for b in range(peers.bit_length() - 1)]
+    for axis, bit in steps:
+        pairs = [(i, i ^ bit) for i in range(lax.axis_size(axis))]
+        value = lax.reduce_precision(value, 8, 7)
+        value = value + lax.ppermute(value.astype(BF16), axis, pairs).astype(F32)
+    return value
+
+
 def per_device(bold_data, spatial_maps, live_blocks):
     chans, size_x, size_y, size_z = spatial_maps.shape
     frames = bold_data.shape[3]
@@ -462,7 +459,8 @@
     parts_x, parts_y, parts_z = (lax.axis_size(a) for a in AXES)
     peers = parts_x * parts_y * parts_z
     places = [lax.axis_index(a).astype(jnp.int32) for a in AXES]
-    info = jnp.stack([*places, places[1] % 2, places[2] % 2, live_blocks[0, 0, 0]])
+    numbers = [*places, places[1] % 2, places[2] % 2, live_blocks]
+    info = [number.reshape(1) for number in numbers]
     bold = bold_data.reshape(size_x * plane, frames)
     voxel_maps = jnp.transpose(spatial_maps, (1, 2, 3, 0)).reshape(size_x, plane, chans)
     all_cells = float(chans * size_x * plane * peers)
@@ -482,14 +480,14 @@
     full_x = band(size_x * parts_x)
     own_x = [slice(p * size_x, (p + 1) * size_x) for p in range(parts_x)]
 
-    def along_x(block, matrices):
+    def along_x(block, matrices, beside=()):
         kinds = [BF16] * len(matrices)
         if parts_x == 2:
             mine = [[[m[own_x[p], own_x[p]]] for m in matrices] for p in range(2)]
             other = [[[m[own_x[p], own_x[1 - p]]] for m in matrices] for p in range(2)]
             got = lax.ppermute(block, "gx", [(0, 1), (1, 0)])
             sums = mix_layers(info, mine, chans, [block], [], [F32] * len(matrices))
-            return mix_layers(info, other, chans, [got], list(sums), kinds, face=face_y)
+            return mix_layers(info, other, chans, [got], list(sums), kinds, face=face_y, after=beside)
         depth = RADIUS * chans
         before, after = shifted(block[:depth], block[-depth:], "gx")
         rest = jnp.zeros((block.shape[0] - depth, plane), BF16)
@@ -510,15 +508,15 @@
         return filter_lanes(info, first, field, second, table_own), *ends
 
     def all_courses(acc, first, middle, second, table):
-        parts = courses_of(info, acc, first, middle, second, table, bold, chans, size_y, size_z, peers)
-        if not spread_rows(chans, frames, peers):
-            return lax.psum(parts, AXES)
-        return exchanged(sum_parts(info, exchanged(parts)))
+        return hypercube_sum(
+            courses_of(info, acc, first, middle, second, table, bold, chans, size_y, size_z)
+        )
 
     plain = pack_maps(info, voxel_maps)
     acc, first, second = along_rest(*along_x(plain, [full_x]))
-    parts1 = all_courses(acc, first, [], second, table_z)
-    raw1, half1 = first_gradient(info, parts1, bold, chans, size_y, size_z)
+    courses1 = all_courses(acc, first, [], second, table_z)
+    raw1, half1 = first_gradient(info, courses1, bold, chans, size_y, size_z)
+    kept, fade1 = first_fade(info, half1)
     if twice:
         square_y = windows(np.linalg.matrix_power(band(size_y * parts_y), 2), size_y, parts_y, reach)
         square_z = windows(np.linalg.matrix_power(band(size_z * parts_z), 2), size_z, parts_z, reach)
@@ -531,20 +529,19 @@
             for w in square_z
         ])
         table_y2, table_z2 = pick_tables(info, jnp.asarray(half(tables_y)), jnp.asarray(half(tables_z)))
-        twice_x, once_x, *_ = along_x(raw1, [full_x @ full_x, full_x])
+        twice_x, once_x, *_ = along_x(raw1, [full_x @ full_x, full_x], [kept])
         first, second = along_y(twice_x, twice_x)
         sent = filter_faces(info, first, twice_x, second, table_y2)
         first, second = swapped(*sent, "gz")
-        parts2 = all_courses(None, first, list(sent), second, table_z2)
+        change = all_courses(None, first, list(sent), second, table_z2)
     else:
         once_x, *faces1 = along_x(raw1, [full_x])
         again = whole_gradient(info, *along_rest(once_x, *faces1), table_z)
         acc2, first, second = along_rest(*along_x(again, [full_x]))
-        parts2 = all_courses(acc2, first, [], second, table_z)
-
-    kept, fade1 = first_fade(info, half1)
+        change = all_courses(acc2, first, [], second, table_z)
+
     raw2, half2, scale1 = second_gradient(
-        info, parts2, half1, kept, bold, chans, size_y, size_z, all_cells
+        info, change, half1, kept, bold, chans, size_y, size_z, all_cells
     )
     fades, field1, *faces1 = second_fade(info, half2, fade1, scale1, once_x, face_y)
     first1, second1 = along_y(*faces1)
@@ -552,14 +549,13 @@
     acc1 = filter_lanes(info, first1, field1, second1, table_own)
     base = faded_maps(info, voxel_maps, fades)
 
-    field2, *faces2 = along_x(raw2, [full_x])
+    field2, *faces2 = along_x(raw2, [full_x], [base])
     first2, second2 = along_y(*faces2)
-    ends = swapped(*filter_faces(info, first2, field2, second2, table_ends, below), "gz")
+    ends = swapped(*filter_faces(info, first2, field2, second2, table_ends, below, [acc1]), "gz")
     acc2 = filter_lanes(info, first2, field2, second2, table_own)
     grad2, energies = gradient_energy(info, acc2, *ends, table_z, peers)
-    energies = exchanged(energies)
-    base, grad2 = turned_gradients(info, acc1, *ends, table_z, base, grad2)
-    maps = final_maps(info, energies, base, grad2, all_cells).reshape(size_x, size_y, size_z, chans)
+    maps = final_maps(info, exchanged(energies), base, acc1, *ends, table_z, grad2, all_cells)
+    maps = maps.reshape(size_x, size_y, size_z, chans)
     return (jnp.transpose(maps, (3, 0, 1, 2)), half2)
 
 

time: 179 us -> 157 us (0.88)
  blocking collectives: 49 us -> 19.5 us
  starting transfers between devices: 28.4 us -> 53 us
  Pallas kernels: 40.7 us -> 23.6 us
  waiting for transfers between devices: 48.5 us -> 56.4 us
  local copies, waits for them, and re-layouts: 9.51 us -> 2.47 us
    ppermute x0 -> x10, starting transfers between devices: none -> 34.2 us  [hypercube_sum(): value = value + lax.ppermute(value.astype(BF16), axis, pairs).astype(F32)]
    all_to_all x3 -> x1, blocking collectives: 49 us -> 19.5 us  [exchanged(): return lax.all_to_all(parts, AXES, 0, 0, tiled=True)]
    ppermute x0 -> x10, waiting for transfers between devices: none -> 20.9 us  [hypercube_sum(): value = value + lax.ppermute(value.astype(BF16), axis, pairs).astype(F32)]
    pallas_call x27 -> x24, Pallas kernels: 40.7 us -> 23.6 us  [call(): pl.pallas_call(wrapped, out_shape=shapes, in_specs=[pl.BlockSpec(memory_s...]
    all_to_all x2 -> x0, starting transfers between devices: 13.2 us -> none  [exchanged(): return lax.all_to_all(parts, AXES, 0, 0, tiled=True)]
    unnamed x54 -> x20, local copies, waits for them, and re-layouts: 9.42 us -> 2.47 us
    all_to_all x2 -> x0, waiting for transfers between devices: 6.78 us -> none  [exchanged(): return lax.all_to_all(parts, AXES, 0, 0, tiled=True)]
    ppermute x3, waiting for transfers between devices: 30.3 us -> 24.6 us  [along_x(): got = lax.ppermute(block, 'gx', [(0, 1), (1, 0)])]
  transfers between devices with their start and end apart: 19 -> 27, of which waited for: 10 -> 18; matrix products, arithmetic and copies ran while one was open for 0% -> 0% of each run, Pallas kernels for 10% -> 6%
where the time goes in v4:
time: 157 us
  waiting for transfers between devices  56.4 us (36%)
  starting transfers between devices  53 us (34%)
  Pallas kernels  23.6 us (15%)
  blocking collectives  19.5 us (12%)
  local copies, waits for them, and re-layouts  2.47 us (2%)
  between operations  1.86 us (1%)
    ppermute x10, starting transfers between devices, hypercube_sum(): value = value + lax.ppermute(value.astype(BF16), axis, pairs).astype(F32)  34.2 us
    ppermute x3, waiting for transfers between devices, along_x(): got = lax.ppermute(block, 'gx', [(0, 1), (1, 0)])  24.6 us
    pallas_call x24, Pallas kernels, call(): pl.pallas_call(wrapped, out_shape=shapes, in_specs=[pl.BlockSpec(memory_s...  23.6 us
    ppermute x10, waiting for transfers between devices, hypercube_sum(): value = value + lax.ppermute(value.astype(BF16), axis, pairs).astype(F32)  20.9 us
    all_to_all x1, blocking collectives, exchanged(): return lax.all_to_all(parts, AXES, 0, 0, tiled=True)  19.5 us
    ppermute x14, starting transfers between devices, swapped(): got[start] = lax.ppermute((first, second)[start], axis, pairs)  12.7 us
    ppermute x14, waiting for transfers between devices, swapped(): got[start] = lax.ppermute((first, second)[start], axis, pairs)  10.8 us
    ppermute x3, starting transfers between devices, along_x(): got = lax.ppermute(block, 'gx', [(0, 1), (1, 0)])  6.1 us
  transfers between devices with their start and end apart: 27, of which 18 were waited for; matrix products, arithmetic and copies ran while one was open for 0% of the time, Pallas kernels for 6%

profile of v4, /device:TPU:0, one launch (start us, length us, event | category | flops | bytes accessed | tf_op | source)
XLA Modules:
  0.0 157.0 jit_solution(3654336648517531050)
XLA Ops:
  0.6 1.6 %copy-done.2 = f32[64,8,16,32]{0,3,2,1:T(8,128)S(1)} copy-done((f32[64,8,16,32]{0,3,2,1:T(8,128)S(1)}, f32[64,8,16,32]{0,3,2,1:T(8,128)}, u32[]{:S(2)}) %copy-start.2) | copy-done | bytes 1048600
  2.2 0.5 pack_maps.1.refs_1_
  2.7 3.0 %collective-permute-start = (bf16[512,512]{1,0:T(8,128)(2,1)S(1)}, bf16[512,512]{1,0:T(8,128)(2,1)S(1)}, u32[]{:S(2)}, u32[]{:S(2)}) collective-permute-start(bf16[512,512]{1,0:T(8,128)(2,1)S(1)} %pack_maps.1.refs_1_), channel_id=1, source_target_pairs={{0,16},{16,0},{1,17},{17,1},{2,18},{18,2},{3,19},{19,3},{4,20},{20... | collective-permute-start | bytes 1572872 | tf_op jit(solution)/shard_map/ppermute | solution.py:488
  5.8 0.5 mix_layers.6.refs_3_
  6.3 11.4 %collective-permute-done.refs_2_ = bf16[512,512]{1,0:T(8,128)(2,1)S(1)} collective-permute-done((bf16[512,512]{1,0:T(8,128)(2,1)S(1)}, bf16[512,512]{1,0:T(8,128)(2,1)S(1)}, u32[]{:S(2)}, u32[]{:S(2)}) %collective-permute-start) | collective-permute-done | bytes 524320 | tf_op jit(solution)/shard_map/ppermute | solution.py:488
  18.2 0.7 collective-permute-start.2
  18.9 0.8 collective-permute-done.1.refs_2_.refs_1_
  20.2 1.9 %collective-permute-start.3 = (bf16[512,128]{1,0:T(8,128)(2,1)S(1)}, bf16[512,128]{1,0:T(8,128)(2,1)S(1)}, u32[]{:S(2)}, u32[]{:S(2)}) collective-permute-start(bf16[512,128]{1,0:T(8,128)(2,1)S(1)} %get-tuple-element.38), channel_id=1, source_target_pairs={{0,1},{2,3},{1,0},{3,2},{4,5},{6,7},{5,4},{7,6},{8,9},{10,11},{9,8... | collective-permute-start | bytes 393224 | tf_op jit(solution)/shard_map/ppermute | solution.py:426
  22.1 0.7 collective-permute-start.4
  23.4 0.7 filter_lanes.3.refs_6_
  24.1 1.1 collective-permute-done.3.refs_2_
  25.3 1.8 %courses_of.2 = f32[64,512]{1,0:T(8,128)S(1)} custom-call(s32[1]{0:T(128)} %bitcast.13.refs_0_, s32[1]{0:T(128)} %bitcast.refs_1_.refs_0_, bf16[512,128]{1,0:T(8,128)(2,1)S(1)} %collective-permute-done.3.refs_2_, bf16[512,128]{1,0:T(8,128)(2,1)S(1)} %collective-permute-done.4.refs_3_, bf16[256,512]{1,0:T(8,128)(2,1)S(1)} %copy-done.6, ...), custom_call_target="tpu_custom_call" | custom-call | flops 1000000000 | bytes 5767168 | tf_op jit(solution)/shard_map/courses_of/pallas_call | solution.py:58
  27.1 1.8 %collective-permute-start.5 = (bf16[64,512]{1,0:T(8,128)(2,1)S(1)}, bf16[64,512]{1,0:T(8,128)(2,1)S(1)}, u32[]{:S(2)}, u32[]{:S(2)}) collective-permute-start(bf16[64,512]{1,0:T(8,128)(2,1)S(1)} %reduce-precision_convert_fusion.1), channel_id=1, source_target_pairs={{0,16},{16,0},{1,17},{17,1},{2,18},{18,2},{3,19},{19,3},{4,20},{20... | collective-permute-start | bytes 196616 | tf_op jit(solution)/shard_map/ppermute | solution.py:451
  28.9 2.5 %collective-permute-done.5 = bf16[64,512]{1,0:T(8,128)(2,1)S(1)} collective-permute-done((bf16[64,512]{1,0:T(8,128)(2,1)S(1)}, bf16[64,512]{1,0:T(8,128)(2,1)S(1)}, u32[]{:S(2)}, u32[]{:S(2)}) %collective-permute-start.5) | collective-permute-done | bytes 65568 | tf_op jit(solution)/shard_map/ppermute | solution.py:451
  31.4 4.8 %collective-permute-start.6 = (bf16[64,512]{1,0:T(8,128)(2,1)S(1)}, bf16[64,512]{1,0:T(8,128)(2,1)S(1)}, u32[]{:S(2)}, u32[]{:S(2)}) collective-permute-start(bf16[64,512]{1,0:T(8,128)(2,1)S(1)} %fusion.4), channel_id=1, source_target_pairs={{0,4},{4,0},{8,12},{12,8},{1,5},{5,1},{9,13},{13,9},{2,6},{6,2},{1... | collective-permute-start | bytes 196616 | tf_op jit(solution)/shard_map/ppermute | solution.py:451
  36.2 0.9 collective-permute-done.6
  37.1 3.6 %collective-permute-start.7 = (bf16[64,512]{1,0:T(8,128)(2,1)S(1)}, bf16[64,512]{1,0:T(8,128)(2,1)S(1)}, u32[]{:S(2)}, u32[]{:S(2)}) collective-permute-start(bf16[64,512]{1,0:T(8,128)(2,1)S(1)} %fusion), channel_id=1, source_target_pairs={{0,8},{4,12},{8,0},{12,4},{1,9},{5,13},{9,1},{13,5},{2,10},{6,14},... | collective-permute-start | bytes 196616 | tf_op jit(solution)/shard_map/ppermute | solution.py:451
  40.7 2.4 %collective-permute-done.7 = bf16[64,512]{1,0:T(8,128)(2,1)S(1)} collective-permute-done((bf16[64,512]{1,0:T(8,128)(2,1)S(1)}, bf16[64,512]{1,0:T(8,128)(2,1)S(1)}, u32[]{:S(2)}, u32[]{:S(2)}) %collective-permute-start.7) | collective-permute-done | bytes 65568 | tf_op jit(solution)/shard_map/ppermute | solution.py:451
  43.2 4.6 %collective-permute-start.8 = (bf16[64,512]{1,0:T(8,128)(2,1)S(1)}, bf16[64,512]{1,0:T(8,128)(2,1)S(1)}, u32[]{:S(2)}, u32[]{:S(2)}) collective-permute-start(bf16[64,512]{1,0:T(8,128)(2,1)S(1)} %get-tuple-element.70), channel_id=1, source_target_pairs={{0,1},{1,0},{2,3},{3,2},{4,5},{5,4},{6,7},{7,6},{8,9},{9,8},{10,11... | collective-permute-start | bytes 196616 | tf_op jit(solution)/shard_map/ppermute | solution.py:451
  47.8 2.2 %collective-permute-done.8 = bf16[64,512]{1,0:T(8,128)(2,1)S(1)} collective-permute-done((bf16[64,512]{1,0:T(8,128)(2,1)S(1)}, bf16[64,512]{1,0:T(8,128)(2,1)S(1)}, u32[]{:S(2)}, u32[]{:S(2)}) %collective-permute-start.8) | collective-permute-done | bytes 65568 | tf_op jit(solution)/shard_map/ppermute | solution.py:451
  50.1 3.5 %collective-permute-start.9 = (bf16[64,512]{1,0:T(8,128)(2,1)S(1)}, bf16[64,512]{1,0:T(8,128)(2,1)S(1)}, u32[]{:S(2)}, u32[]{:S(2)}) collective-permute-start(bf16[64,512]{1,0:T(8,128)(2,1)S(1)} %fusion.1), channel_id=1, source_target_pairs={{0,2},{1,3},{2,0},{3,1},{4,6},{5,7},{6,4},{7,5},{8,10},{9,11},{10,... | collective-permute-start | bytes 196616 | tf_op jit(solution)/shard_map/ppermute | solution.py:451
  53.6 2.2 %collective-permute-done.9 = bf16[64,512]{1,0:T(8,128)(2,1)S(1)} collective-permute-done((bf16[64,512]{1,0:T(8,128)(2,1)S(1)}, bf16[64,512]{1,0:T(8,128)(2,1)S(1)}, u32[]{:S(2)}, u32[]{:S(2)}) %collective-permute-start.9) | collective-permute-done | bytes 65568 | tf_op jit(solution)/shard_map/ppermute | solution.py:451
  55.9 1.4 first_gradient.1
  57.3 1.6 %collective-permute-start.10 = (bf16[512,512]{1,0:T(8,128)(2,1)S(1)}, bf16[512,512]{1,0:T(8,128)(2,1)S(1)}, u32[]{:S(2)}, u32[]{:S(2)}) collective-permute-start(bf16[512,512]{1,0:T(8,128)(2,1)S(1)} %get-tuple-element.40.refs_1_), channel_id=1, source_target_pairs={{0,16},{16,0},{1,17},{17,1},{2,18},{18,2},{3,19},{19,3},{4,20},{20... | collective-permute-start | bytes 1572872 | tf_op jit(solution)/shard_map/ppermute | solution.py:488
  58.9 1.0 mix_layers.8
  60.3 8.5 %collective-permute-done.10.refs_2_ = bf16[512,512]{1,0:T(8,128)(2,1)S(1)} collective-permute-done((bf16[512,512]{1,0:T(8,128)(2,1)S(1)}, bf16[512,512]{1,0:T(8,128)(2,1)S(1)}, u32[]{:S(2)}, u32[]{:S(2)}) %collective-permute-start.10) | collective-permute-done | bytes 524320 | tf_op jit(solution)/shard_map/ppermute | solution.py:488
  68.8 1.8 %mix_layers.9 = (bf16[512,512]{1,0:T(8,128)(2,1)S(1)}, bf16[512,512]{1,0:T(8,128)(2,1)S(1)}, bf16[512,256]{1,0:T(8,128)(2,1)}, bf16[512,256]{1,0:T(8,128)(2,1)}) custom-call(s32[1]{0:T(128)} %bitcast.2.refs_0_, s32[1]{0:T(128)} %bitcast.1.refs_1_.refs_0_, bf16[512,512]{1,0:T(8,128)(2,1)S(1)} %collective-permute-done.10.refs_2_, ...), custom_call_target="tpu_custom_call" | custom-call | flops 100000000 | bytes 2621440 | tf_op jit(solution)/shard_map/mix_layers/pallas_call | solution.py:58
  70.6 0.7 collective-permute-start.12
  71.3 2.6 %collective-permute-start.11 = (bf16[512,512]{1,0:T(8,128)(2,1)S(1)}, bf16[512,512]{1,0:T(8,128)(2,1)S(1)}, u32[]{:S(2)}, u32[]{:S(2)}) collective-permute-start(bf16[512,512]{1,0:T(8,128)(2,1)S(1)} %get-tuple-element.45.refs_3_), channel_id=1, source_target_pairs={{0,4},{8,12},{4,0},{12,8},{1,5},{9,13},{5,1},{13,9},{2,6},{10,14},... | collective-permute-start | bytes 1572872 | tf_op jit(solution)/shard_map/ppermute | solution.py:426
  74.2 1.3 collective-permute-done.11.refs_2_
  75.5 1.0 filter_faces.5
  76.5 1.3 collective-permute-start.13
  77.8 0.8 collective-permute-start.14
  78.7 4.3 %collective-permute-done.13.refs_2_ = bf16[512,256]{1,0:T(8,128)(2,1)S(1)} collective-permute-done((bf16[512,256]{1,0:T(8,128)(2,1)S(1)}, bf16[512,256]{1,0:T(8,128)(2,1)S(1)}, u32[]{:S(2)}, u32[]{:S(2)}) %collective-permute-start.13) | collective-permute-done | bytes 262176 | tf_op jit(solution)/shard_map/ppermute | solution.py:426
  83.0 2.8 %courses_of.3 = f32[64,512]{1,0:T(8,128)S(1)} custom-call(s32[1]{0:T(128)} %bitcast.15.refs_0_, s32[1]{0:T(128)} %bitcast.refs_1_.refs_0_, bf16[512,256]{1,0:T(8,128)(2,1)S(1)} %collective-permute-done.13.refs_2_, bf16[512,256]{1,0:T(8,128)(2,1)S(1)} %get-tuple-element.47.refs_3_, bf16[512,256]{1,0:T(8,128)(2,1)S(1)} %get-tuple-element.48.refs_4_, ...), custom_call_target="tpu_custom_call" | custom-call | flops 1000000000 | bytes 6291456 | tf_op jit(solution)/shard_map/courses_of/pallas_call | solution.py:58
  85.8 1.6 collective-permute-start.15
  87.3 2.8 %collective-permute-done.15 = bf16[64,512]{1,0:T(8,128)(2,1)S(1)} collective-permute-done((bf16[64,512]{1,0:T(8,128)(2,1)S(1)}, bf16[64,512]{1,0:T(8,128)(2,1)S(1)}, u32[]{:S(2)}, u32[]{:S(2)}) %collective-permute-start.15) | collective-permute-done | bytes 65568 | tf_op jit(solution)/shard_map/ppermute | solution.py:451
  90.1 3.3 %collective-permute-start.16 = (bf16[64,512]{1,0:T(8,128)(2,1)S(1)}, bf16[64,512]{1,0:T(8,128)(2,1)S(1)}, u32[]{:S(2)}, u32[]{:S(2)}) collective-permute-start(bf16[64,512]{1,0:T(8,128)(2,1)S(1)} %fusion.5), channel_id=1, source_target_pairs={{0,4},{4,0},{8,12},{12,8},{1,5},{5,1},{9,13},{13,9},{2,6},{6,2},{1... | collective-permute-start | bytes 196616 | tf_op jit(solution)/shard_map/ppermute | solution.py:451
  93.4 0.9 collective-permute-done.16
  94.4 4.0 %collective-permute-start.17 = (bf16[64,512]{1,0:T(8,128)(2,1)S(1)}, bf16[64,512]{1,0:T(8,128)(2,1)S(1)}, u32[]{:S(2)}, u32[]{:S(2)}) collective-permute-start(bf16[64,512]{1,0:T(8,128)(2,1)S(1)} %fusion.2), channel_id=1, source_target_pairs={{0,8},{4,12},{8,0},{12,4},{1,9},{5,13},{9,1},{13,5},{2,10},{6,14},... | collective-permute-start | bytes 196616 | tf_op jit(solution)/shard_map/ppermute | solution.py:451
  98.4 2.4 %collective-permute-done.17 = bf16[64,512]{1,0:T(8,128)(2,1)S(1)} collective-permute-done((bf16[64,512]{1,0:T(8,128)(2,1)S(1)}, bf16[64,512]{1,0:T(8,128)(2,1)S(1)}, u32[]{:S(2)}, u32[]{:S(2)}) %collective-permute-start.17) | collective-permute-done | bytes 65568 | tf_op jit(solution)/shard_map/ppermute | solution.py:451
  100.9 4.0 %collective-permute-start.18 = (bf16[64,512]{1,0:T(8,128)(2,1)S(1)}, bf16[64,512]{1,0:T(8,128)(2,1)S(1)}, u32[]{:S(2)}, u32[]{:S(2)}) collective-permute-start(bf16[64,512]{1,0:T(8,128)(2,1)S(1)} %get-tuple-element.68), channel_id=1, source_target_pairs={{0,1},{1,0},{2,3},{3,2},{4,5},{5,4},{6,7},{7,6},{8,9},{9,8},{10,11... | collective-permute-start | bytes 196616 | tf_op jit(solution)/shard_map/ppermute | solution.py:451
  104.9 2.2 %collective-permute-done.18 = bf16[64,512]{1,0:T(8,128)(2,1)S(1)} collective-permute-done((bf16[64,512]{1,0:T(8,128)(2,1)S(1)}, bf16[64,512]{1,0:T(8,128)(2,1)S(1)}, u32[]{:S(2)}, u32[]{:S(2)}) %collective-permute-start.18) | collective-permute-done | bytes 65568 | tf_op jit(solution)/shard_map/ppermute | solution.py:451
  107.1 3.0 %collective-permute-start.19 = (bf16[64,512]{1,0:T(8,128)(2,1)S(1)}, bf16[64,512]{1,0:T(8,128)(2,1)S(1)}, u32[]{:S(2)}, u32[]{:S(2)}) collective-permute-start(bf16[64,512]{1,0:T(8,128)(2,1)S(1)} %fusion.3), channel_id=1, source_target_pairs={{0,2},{1,3},{2,0},{3,1},{4,6},{5,7},{6,4},{7,5},{8,10},{9,11},{10,... | collective-permute-start | bytes 196616 | tf_op jit(solution)/shard_map/ppermute | solution.py:451
  110.1 2.3 %collective-permute-done.19 = bf16[64,512]{1,0:T(8,128)(2,1)S(1)} collective-permute-done((bf16[64,512]{1,0:T(8,128)(2,1)S(1)}, bf16[64,512]{1,0:T(8,128)(2,1)S(1)}, u32[]{:S(2)}, u32[]{:S(2)}) %collective-permute-start.19) | collective-permute-done | bytes 65568 | tf_op jit(solution)/shard_map/ppermute | solution.py:451
  112.4 1.9 %second_gradient.1 = (bf16[512,512]{1,0:T(8,128)(2,1)S(1)}, bf16[64,512]{1,0:T(8,128)(2,1)}, f32[1,1]{1,0:T(1,128)}) custom-call(s32[1]{0:T(128)} %bitcast.16.refs_0_, f32[64,512]{1,0:T(8,128)S(1)} %convert_add_fusion.refs_1_, bf16[64,512]{1,0:T(8,128)(2,1)S(1)} %get-tuple-element.43.refs_0_.refs_2_, f32[64,512]{1,0:T(8,128)S(1)} %get-tuple-element.44.refs_5_.refs_3_, ...), custom_call_target="tpu_custom_call" | custom-call | flops 1000000000 | bytes 4521984 | tf_op jit(solution)/shard_map/second_gradient/pallas_call | solution.py:58
  114.3 1.5 collective-permute-start.20
  115.8 0.8 copy-done.7
  116.6 1.3 second_fade.1
  118.0 0.7 collective-permute-start.24
  118.7 1.8 %faded_maps.1.refs_4_.refs_2_ = f32[8,512,64]{2,1,0:T(8,128)S(1)} custom-call(f32[8,512,64]{2,1,0:T(8,128)S(1)} %bitcast.22, f32[64,64]{1,0:T(8,128)S(1)} %get-tuple-element.55.refs_1_), custom_call_target="tpu_custom_call" | custom-call | flops 1000000000 | bytes 1064960 | tf_op jit(solution)/shard_map/faded_maps/pallas_call | solution.py:58
  120.5 0.5 mix_layers.10.refs_3_
  121.1 4.7 %collective-permute-done.20.refs_2_ = bf16[512,512]{1,0:T(8,128)(2,1)S(1)} collective-permute-done((bf16[512,512]{1,0:T(8,128)(2,1)S(1)}, bf16[512,512]{1,0:T(8,128)(2,1)S(1)}, u32[]{:S(2)}, u32[]{:S(2)}) %collective-permute-start.20) | collective-permute-done | bytes 524320 | tf_op jit(solution)/shard_map/ppermute | solution.py:488
  126.3 0.7 collective-permute-start.22
  127.0 0.5 filter_faces.6
  127.5 0.7 filter_lanes.5.refs_8_.refs_3_
  128.2 0.5 filter_faces.7
  128.7 1.8 %collective-permute-start.25 = (bf16[1024,128]{1,0:T(8,128)(2,1)S(1)}, bf16[1024,128]{1,0:T(8,128)(2,1)S(1)}, u32[]{:S(2)}, u32[]{:S(2)}) collective-permute-start(bf16[1024,128]{1,0:T(8,128)(2,1)S(1)} %get-tuple-element.64), channel_id=1, source_target_pairs={{0,1},{2,3},{1,0},{3,2},{4,5},{6,7},{5,4},{7,6},{8,9},{10,11},{9,8... | collective-permute-start | bytes 786440 | tf_op jit(solution)/shard_map/ppermute | solution.py:426
  130.5 0.7 collective-permute-start.26
  131.2 0.7 filter_lanes.4.refs_1_
  131.9 3.2 %collective-permute-done.25.refs_2_.refs_4_ = bf16[1024,128]{1,0:T(8,128)(2,1)S(1)} collective-permute-done((bf16[1024,128]{1,0:T(8,128)(2,1)S(1)}, bf16[1024,128]{1,0:T(8,128)(2,1)S(1)}, u32[]{:S(2)}, u32[]{:S(2)}) %collective-permute-start.25) | collective-permute-done | bytes 262176 | tf_op jit(solution)/shard_map/ppermute | solution.py:426
  135.1 0.5 gradient_energy.1
  135.7 19.5 %all_to_all.5.refs_1_ = f32[32,1,128]{2,1,0:T(1,128)S(1)} all-to-all(f32[32,1,128]{2,1,0:T(1,128)S(1)} %get-tuple-element.66), channel_id=1, replica_groups=mesh['gx'=2,'gy'=4,'gz'=4] {'gx','gy','gz'}, dimensions={0} | all-to-all | bytes 32768 | tf_op jit(solution)/shard_map/all_to_all | solution.py:438
  155.1 1.7 %final_maps.1 = f32[8,512,64]{2,1,0:T(8,128)} custom-call(s32[1]{0:T(128)} %bitcast.refs_1_.refs_0_, f32[32,1,128]{2,1,0:T(1,128)S(1)} %all_to_all.5.refs_1_, f32[8,512,64]{2,1,0:T(8,128)S(1)} %faded_maps.1.refs_4_.refs_2_, f32[512,512]{1,0:T(8,128)S(1)} %filter_lanes.5.refs_8_.refs_3_, bf16[1024,128]{1,0:T(8,128)(2,1)S(1)} %collective-permute-done.25.refs_2_.refs_4_, ...), custom_call_target="tpu_custom_call" | custom-call | flops 100000000 | bytes 3948544 | tf_op jit(solution)/shard_map/final_maps/pallas_call | solution.py:58
  (48 shorter events, 2.5 us)
Async XLA Ops:
  0.6 1.6 %copy-start.2 = (f32[64,8,16,32]{0,3,2,1:T(8,128)S(1)}, f32[64,8,16,32]{0,3,2,1:T(8,128)}, u32[]{:S(2)}) copy-start(f32[64,8,16,32]{0,3,2,1:T(8,128)} %param.9) | copy-start | bytes 3145732
  2.7 17.0 %copy-start.4 = (bf16[1024,256]{1,0:T(8,128)(2,1)S(1)}, bf16[1024,256]{1,0:T(8,128)(2,1)}, u32[]{:S(2)}) copy-start(bf16[1024,256]{1,0:T(8,128)(2,1)} %constant.40.clone.refs_5_) | copy-start | bytes 1572868
  2.7 15.0 %collective-permute-start = (bf16[512,512]{1,0:T(8,128)(2,1)S(1)}, bf16[512,512]{1,0:T(8,128)(2,1)S(1)}, u32[]{:S(2)}, u32[]{:S(2)}) collective-permute-start(bf16[512,512]{1,0:T(8,128)(2,1)S(1)} %pack_maps.1.refs_1_), channel_id=1, source_target_pairs={{0,16},{16,0},{1,17},{17,1},{2,18},{18,2},{3,19},{19,3},{4,20},{20... | collective-permute-start | bytes 1572872 | tf_op jit(solution)/shard_map/ppermute | solution.py:488
  5.8 17.6 %copy-start.1 = (bf16[1024,512]{1,0:T(8,128)(2,1)S(1)}, bf16[1024,512]{1,0:T(8,128)(2,1)}, u32[]{:S(2)}) copy-start(bf16[1024,512]{1,0:T(8,128)(2,1)} %constant.41.clone.refs_4_) | copy-start | bytes 3145732
  18.1 1.6 %collective-permute-start.1 = (bf16[512,256]{1,0:T(8,128)(2,1)S(1)}, bf16[512,256]{1,0:T(8,128)(2,1)S(1)}, u32[]{:S(2)}, u32[]{:S(2)}) collective-permute-start(bf16[512,256]{1,0:T(8,128)(2,1)S(1)} %get-tuple-element.35), channel_id=1, source_target_pairs={{0,4},{8,12},{4,0},{12,8},{1,5},{9,13},{5,1},{13,9},{2,6},{10,14},... | collective-permute-start | bytes 786440 | tf_op jit(solution)/shard_map/ppermute | solution.py:426
  18.2 1.5 collective-permute-start.2
  19.7 5.5 %copy-start = (bf16[8,16,32,512]{3,2,1,0:T(8,128)(2,1)S(1)}, bf16[8,16,32,512]{3,2,1,0:T(8,128)(2,1)}, u32[]{:S(2)}) copy-start(bf16[8,16,32,512]{3,2,1,0:T(8,128)(2,1)} %param.8) | copy-start | bytes 12582916
  19.7 5.5 %copy-start.6 = (bf16[256,512]{1,0:T(8,128)(2,1)S(1)}, bf16[256,512]{1,0:T(8,128)(2,1)}, u32[]{:S(2)}) copy-start(bf16[256,512]{1,0:T(8,128)(2,1)} %constant.42.clone.refs_4_.refs_6_) | copy-start | bytes 786436
  20.2 5.0 %collective-permute-start.3 = (bf16[512,128]{1,0:T(8,128)(2,1)S(1)}, bf16[512,128]{1,0:T(8,128)(2,1)S(1)}, u32[]{:S(2)}, u32[]{:S(2)}) collective-permute-start(bf16[512,128]{1,0:T(8,128)(2,1)S(1)} %get-tuple-element.38), channel_id=1, source_target_pairs={{0,1},{2,3},{1,0},{3,2},{4,5},{6,7},{5,4},{7,6},{8,9},{10,11},{9,8... | collective-permute-start | bytes 393224 | tf_op jit(solution)/shard_map/ppermute | solution.py:426
  22.1 3.2 %collective-permute-start.4 = (bf16[512,128]{1,0:T(8,128)(2,1)S(1)}, bf16[512,128]{1,0:T(8,128)(2,1)S(1)}, u32[]{:S(2)}, u32[]{:S(2)}) collective-permute-start(bf16[512,128]{1,0:T(8,128)(2,1)S(1)} %get-tuple-element.39), channel_id=1, source_target_pairs={{1,2},{2,1},{5,6},{6,5},{9,10},{10,9},{13,14},{14,13},{17,18},{18,... | collective-permute-start | bytes 393224 | tf_op jit(solution)/shard_map/ppermute | solution.py:426
  25.3 48.7 %slice-start = ((s8[6291456]{0:T(1024)(128)(4,1)}), s8[4194304]{0:T(1024)(128)(4,1)S(1)}, s32[]{:S(2)}) async-start(s8[6291456]{0:T(1024)(128)(4,1)} %bitcast.23), calls=%async_computation.1 | async-start | bytes 8388608
  27.1 4.3 %collective-permute-start.5 = (bf16[64,512]{1,0:T(8,128)(2,1)S(1)}, bf16[64,512]{1,0:T(8,128)(2,1)S(1)}, u32[]{:S(2)}, u32[]{:S(2)}) collective-permute-start(bf16[64,512]{1,0:T(8,128)(2,1)S(1)} %reduce-precision_convert_fusion.1), channel_id=1, source_target_pairs={{0,16},{16,0},{1,17},{17,1},{2,18},{18,2},{3,19},{19,3},{4,20},{20... | collective-permute-start | bytes 196616 | tf_op jit(solution)/shard_map/ppermute | solution.py:451
  31.4 5.7 %collective-permute-start.6 = (bf16[64,512]{1,0:T(8,128)(2,1)S(1)}, bf16[64,512]{1,0:T(8,128)(2,1)S(1)}, u32[]{:S(2)}, u32[]{:S(2)}) collective-permute-start(bf16[64,512]{1,0:T(8,128)(2,1)S(1)} %fusion.4), channel_id=1, source_target_pairs={{0,4},{4,0},{8,12},{12,8},{1,5},{5,1},{9,13},{13,9},{2,6},{6,2},{1... | collective-permute-start | bytes 196616 | tf_op jit(solution)/shard_map/ppermute | solution.py:451
  37.1 6.0 %collective-permute-start.7 = (bf16[64,512]{1,0:T(8,128)(2,1)S(1)}, bf16[64,512]{1,0:T(8,128)(2,1)S(1)}, u32[]{:S(2)}, u32[]{:S(2)}) collective-permute-start(bf16[64,512]{1,0:T(8,128)(2,1)S(1)} %fusion), channel_id=1, source_target_pairs={{0,8},{4,12},{8,0},{12,4},{1,9},{5,13},{9,1},{13,5},{2,10},{6,14},... | collective-permute-start | bytes 196616 | tf_op jit(solution)/shard_map/ppermute | solution.py:451
  43.2 6.9 %collective-permute-start.8 = (bf16[64,512]{1,0:T(8,128)(2,1)S(1)}, bf16[64,512]{1,0:T(8,128)(2,1)S(1)}, u32[]{:S(2)}, u32[]{:S(2)}) collective-permute-start(bf16[64,512]{1,0:T(8,128)(2,1)S(1)} %get-tuple-element.70), channel_id=1, source_target_pairs={{0,1},{1,0},{2,3},{3,2},{4,5},{5,4},{6,7},{7,6},{8,9},{9,8},{10,11... | collective-permute-start | bytes 196616 | tf_op jit(solution)/shard_map/ppermute | solution.py:451
  50.1 5.8 %collective-permute-start.9 = (bf16[64,512]{1,0:T(8,128)(2,1)S(1)}, bf16[64,512]{1,0:T(8,128)(2,1)S(1)}, u32[]{:S(2)}, u32[]{:S(2)}) collective-permute-start(bf16[64,512]{1,0:T(8,128)(2,1)S(1)} %fusion.1), channel_id=1, source_target_pairs={{0,2},{1,3},{2,0},{3,1},{4,6},{5,7},{6,4},{7,5},{8,10},{9,11},{10,... | collective-permute-start | bytes 196616 | tf_op jit(solution)/shard_map/ppermute | solution.py:451
  55.9 18.0 %slice-start.1 = ((s8[6291456]{0:T(1024)(128)(4,1)}), s8[2097152]{0:T(1024)(128)(4,1)S(1)}, s32[]{:S(2)}) async-start(s8[6291456]{0:T(1024)(128)(4,1)} %bitcast.23), calls=%async_computation.2 | async-start | bytes 4194304
  55.9 18.0 %copy-start.5 = (bf16[4,1024,512]{2,1,0:T(8,128)(2,1)S(1)}, bf16[4,1024,512]{2,1,0:T(8,128)(2,1)}, u32[]{:S(2)}) copy-start(bf16[4,1024,512]{2,1,0:T(8,128)(2,1)} %constant.44.clone.refs_3_) | copy-start | bytes 12582916
  57.3 11.5 %collective-permute-start.10 = (bf16[512,512]{1,0:T(8,128)(2,1)S(1)}, bf16[512,512]{1,0:T(8,128)(2,1)S(1)}, u32[]{:S(2)}, u32[]{:S(2)}) collective-permute-start(bf16[512,512]{1,0:T(8,128)(2,1)S(1)} %get-tuple-element.40.refs_1_), channel_id=1, source_target_pairs={{0,16},{16,0},{1,17},{17,1},{2,18},{18,2},{3,19},{19,3},{4,20},{20... | collective-permute-start | bytes 1572872 | tf_op jit(solution)/shard_map/ppermute | solution.py:488
  70.6 3.5 %collective-permute-start.12 = (bf16[512,512]{1,0:T(8,128)(2,1)S(1)}, bf16[512,512]{1,0:T(8,128)(2,1)S(1)}, u32[]{:S(2)}, u32[]{:S(2)}) collective-permute-start(bf16[512,512]{1,0:T(8,128)(2,1)S(1)} %get-tuple-element.45.refs_3_), channel_id=1, source_target_pairs={{4,8},{8,4},{5,9},{9,5},{6,10},{10,6},{7,11},{11,7},{20,24},{24,20... | collective-permute-start | bytes 1572872 | tf_op jit(solution)/shard_map/ppermute | solution.py:426
  71.3 4.1 %collective-permute-start.11 = (bf16[512,512]{1,0:T(8,128)(2,1)S(1)}, bf16[512,512]{1,0:T(8,128)(2,1)S(1)}, u32[]{:S(2)}, u32[]{:S(2)}) collective-permute-start(bf16[512,512]{1,0:T(8,128)(2,1)S(1)} %get-tuple-element.45.refs_3_), channel_id=1, source_target_pairs={{0,4},{8,12},{4,0},{12,8},{1,5},{9,13},{5,1},{13,9},{2,6},{10,14},... | collective-permute-start | bytes 1572872 | tf_op jit(solution)/shard_map/ppermute | solution.py:426
  76.5 6.4 %collective-permute-start.13 = (bf16[512,256]{1,0:T(8,128)(2,1)S(1)}, bf16[512,256]{1,0:T(8,128)(2,1)S(1)}, u32[]{:S(2)}, u32[]{:S(2)}) collective-permute-start(bf16[512,256]{1,0:T(8,128)(2,1)S(1)} %get-tuple-element.47.refs_3_), channel_id=1, source_target_pairs={{0,1},{2,3},{1,0},{3,2},{4,5},{6,7},{5,4},{7,6},{8,9},{10,11},{9,8... | collective-permute-start | bytes 786440 | tf_op jit(solution)/shard_map/ppermute | solution.py:426
  77.8 5.1 %collective-permute-start.14 = (bf16[512,256]{1,0:T(8,128)(2,1)S(1)}, bf16[512,256]{1,0:T(8,128)(2,1)S(1)}, u32[]{:S(2)}, u32[]{:S(2)}) collective-permute-start(bf16[512,256]{1,0:T(8,128)(2,1)S(1)} %get-tuple-element.48.refs_4_), channel_id=1, source_target_pairs={{1,2},{2,1},{5,6},{6,5},{9,10},{10,9},{13,14},{14,13},{17,18},{18,... | collective-permute-start | bytes 786440 | tf_op jit(solution)/shard_map/ppermute | solution.py:426
  85.8 4.3 %collective-permute-start.15 = (bf16[64,512]{1,0:T(8,128)(2,1)S(1)}, bf16[64,512]{1,0:T(8,128)(2,1)S(1)}, u32[]{:S(2)}, u32[]{:S(2)}) collective-permute-start(bf16[64,512]{1,0:T(8,128)(2,1)S(1)} %reduce-precision_convert_fusion), channel_id=1, source_target_pairs={{0,16},{16,0},{1,17},{17,1},{2,18},{18,2},{3,19},{19,3},{4,20},{20... | collective-permute-start | bytes 196616 | tf_op jit(solution)/shard_map/ppermute | solution.py:451
  90.1 4.2 %collective-permute-start.16 = (bf16[64,512]{1,0:T(8,128)(2,1)S(1)}, bf16[64,512]{1,0:T(8,128)(2,1)S(1)}, u32[]{:S(2)}, u32[]{:S(2)}) collective-permute-start(bf16[64,512]{1,0:T(8,128)(2,1)S(1)} %fusion.5), channel_id=1, source_target_pairs={{0,4},{4,0},{8,12},{12,8},{1,5},{5,1},{9,13},{13,9},{2,6},{6,2},{1... | collective-permute-start | bytes 196616 | tf_op jit(solution)/shard_map/ppermute | solution.py:451
  94.4 6.5 %collective-permute-start.17 = (bf16[64,512]{1,0:T(8,128)(2,1)S(1)}, bf16[64,512]{1,0:T(8,128)(2,1)S(1)}, u32[]{:S(2)}, u32[]{:S(2)}) collective-permute-start(bf16[64,512]{1,0:T(8,128)(2,1)S(1)} %fusion.2), channel_id=1, source_target_pairs={{0,8},{4,12},{8,0},{12,4},{1,9},{5,13},{9,1},{13,5},{2,10},{6,14},... | collective-permute-start | bytes 196616 | tf_op jit(solution)/shard_map/ppermute | solution.py:451
  100.9 6.2 %collective-permute-start.18 = (bf16[64,512]{1,0:T(8,128)(2,1)S(1)}, bf16[64,512]{1,0:T(8,128)(2,1)S(1)}, u32[]{:S(2)}, u32[]{:S(2)}) collective-permute-start(bf16[64,512]{1,0:T(8,128)(2,1)S(1)} %get-tuple-element.68), channel_id=1, source_target_pairs={{0,1},{1,0},{2,3},{3,2},{4,5},{5,4},{6,7},{7,6},{8,9},{9,8},{10,11... | collective-permute-start | bytes 196616 | tf_op jit(solution)/shard_map/ppermute | solution.py:451
  107.1 5.2 %collective-permute-start.19 = (bf16[64,512]{1,0:T(8,128)(2,1)S(1)}, bf16[64,512]{1,0:T(8,128)(2,1)S(1)}, u32[]{:S(2)}, u32[]{:S(2)}) collective-permute-start(bf16[64,512]{1,0:T(8,128)(2,1)S(1)} %fusion.3), channel_id=1, source_target_pairs={{0,2},{1,3},{2,0},{3,1},{4,6},{5,7},{6,4},{7,5},{8,10},{9,11},{10,... | collective-permute-start | bytes 196616 | tf_op jit(solution)/shard_map/ppermute | solution.py:451
  114.3 4.4 %copy-start.3 = (f32[64,8,16,32]{0,3,2,1:T(8,128)S(1)}, f32[64,8,16,32]{0,3,2,1:T(8,128)}, u32[]{:S(2)}) copy-start(f32[64,8,16,32]{0,3,2,1:T(8,128)} %param.9) | copy-start | bytes 3145732
  114.3 11.5 %collective-permute-start.20 = (bf16[512,512]{1,0:T(8,128)(2,1)S(1)}, bf16[512,512]{1,0:T(8,128)(2,1)S(1)}, u32[]{:S(2)}, u32[]{:S(2)}) collective-permute-start(bf16[512,512]{1,0:T(8,128)(2,1)S(1)} %get-tuple-element.50.refs_1_), channel_id=1, source_target_pairs={{0,16},{16,0},{1,17},{17,1},{2,18},{18,2},{3,19},{19,3},{4,20},{20... | collective-permute-start | bytes 1572872 | tf_op jit(solution)/shard_map/ppermute | solution.py:488
  115.8 0.8 copy-start.7
  117.9 9.0 %collective-permute-start.23 = (bf16[512,256]{1,0:T(8,128)(2,1)S(1)}, bf16[512,256]{1,0:T(8,128)(2,1)S(1)}, u32[]{:S(2)}, u32[]{:S(2)}) collective-permute-start(bf16[512,256]{1,0:T(8,128)(2,1)S(1)} %get-tuple-element.59), channel_id=1, source_target_pairs={{0,4},{8,12},{4,0},{12,8},{1,5},{9,13},{5,1},{13,9},{2,6},{10,14},... | collective-permute-start | bytes 786440 | tf_op jit(solution)/shard_map/ppermute | solution.py:426
  118.0 9.0 %collective-permute-start.24 = (bf16[512,256]{1,0:T(8,128)(2,1)S(1)}, bf16[512,256]{1,0:T(8,128)(2,1)S(1)}, u32[]{:S(2)}, u32[]{:S(2)}) collective-permute-start(bf16[512,256]{1,0:T(8,128)(2,1)S(1)} %get-tuple-element.61), channel_id=1, source_target_pairs={{4,8},{8,4},{5,9},{9,5},{6,10},{10,6},{7,11},{11,7},{20,24},{24,20... | collective-permute-start | bytes 786440 | tf_op jit(solution)/shard_map/ppermute | solution.py:426
  126.2 2.0 %collective-permute-start.21 = (bf16[512,256]{1,0:T(8,128)(2,1)S(1)}, bf16[512,256]{1,0:T(8,128)(2,1)S(1)}, u32[]{:S(2)}, u32[]{:S(2)}) collective-permute-start(bf16[512,256]{1,0:T(8,128)(2,1)S(1)} %get-tuple-element.56), channel_id=1, source_target_pairs={{0,4},{8,12},{4,0},{12,8},{1,5},{9,13},{5,1},{13,9},{2,6},{10,14},... | collective-permute-start | bytes 786440 | tf_op jit(solution)/shard_map/ppermute | solution.py:426
  126.3 1.9 %collective-permute-start.22 = (bf16[512,256]{1,0:T(8,128)(2,1)S(1)}, bf16[512,256]{1,0:T(8,128)(2,1)S(1)}, u32[]{:S(2)}, u32[]{:S(2)}) collective-permute-start(bf16[512,256]{1,0:T(8,128)(2,1)S(1)} %get-tuple-element.58), channel_id=1, source_target_pairs={{4,8},{8,4},{5,9},{9,5},{6,10},{10,6},{7,11},{11,7},{20,24},{24,20... | collective-permute-start | bytes 786440 | tf_op jit(solution)/shard_map/ppermute | solution.py:426
  128.7 6.4 %collective-permute-start.25 = (bf16[1024,128]{1,0:T(8,128)(2,1)S(1)}, bf16[1024,128]{1,0:T(8,128)(2,1)S(1)}, u32[]{:S(2)}, u32[]{:S(2)}) collective-permute-start(bf16[1024,128]{1,0:T(8,128)(2,1)S(1)} %get-tuple-element.64), channel_id=1, source_target_pairs={{0,1},{2,3},{1,0},{3,2},{4,5},{6,7},{5,4},{7,6},{8,9},{10,11},{9,8... | collective-permute-start | bytes 786440 | tf_op jit(solution)/shard_map/ppermute | solution.py:426
  130.5 4.6 %collective-permute-start.26 = (bf16[1024,128]{1,0:T(8,128)(2,1)S(1)}, bf16[1024,128]{1,0:T(8,128)(2,1)S(1)}, u32[]{:S(2)}, u32[]{:S(2)}) collective-permute-start(bf16[1024,128]{1,0:T(8,128)(2,1)S(1)} %get-tuple-element.65), channel_id=1, source_target_pairs={{1,2},{2,1},{5,6},{6,5},{9,10},{10,9},{13,14},{14,13},{17,18},{18,... | collective-permute-start | bytes 786440 | tf_op jit(solution)/shard_map/ppermute | solution.py:426

commit v5 on v4

--- a/solution.py
+++ b/solution.py
@@ -131,14 +131,23 @@
 
 
 def send_faces(info_ref, odd, field, face, first, second):
-    plane = field.shape[1]
-
-    def write(low, high):
-        low[...] = field[:, :face].astype(low.dtype)
-        high[...] = field[:, plane - face :].astype(high.dtype)
-
-    pl.when(info_ref[odd] == 0)(lambda: write(second, first))
-    pl.when(info_ref[odd] != 0)(lambda: write(first, second))
+    rows, plane = field.shape
+
+    def write(target, lanes):
+        for at, ref in zip((0, rows // 2), target) if isinstance(target, tuple) else [(0, target)]:
+            ref[...] = field[at : at + ref.shape[0], lanes].astype(ref.dtype)
+
+    low, high = slice(0, face), slice(plane - face, plane)
+
+    @pl.when(info_ref[odd] == 0)
+    def _():
+        write(first, high)
+        write(second, low)
+
+    @pl.when(info_ref[odd] != 0)
+    def _():
+        write(first, low)
+        write(second, high)
 
 
 def swapped_dot(info_ref, odd, first, middle, second, weights, rows=slice(None), sent=False):
@@ -149,13 +158,21 @@
     def at(when_even, when_odd):
         return weights[pl.ds(pl.multiple_of(jnp.where(even, when_even, when_odd), width), width), :]
 
-    total = dot(first[rows, :], at(end, 0)) + dot(second[rows, :], at(0, end))
+    total = dot(first[rows, :], at(end, 0))
+    if isinstance(second, tuple):
+        total = total + jnp.concatenate([dot(piece[...], at(0, end)) for piece in second], axis=0)
+    else:
+        total = total + dot(second[rows, :], at(0, end))
     if sent:
         high = end - width
         return total + dot(middle[0][rows, :], at(high, width)) + dot(middle[1][rows, :], at(width, high))
     for piece in middle:
         total = total + dot(piece[rows, :], weights[width : width + piece.shape[1], :])
     return total
+
+
+def faces_shape(rows, face):
+    return (shape((rows, face), BF16),) + (shape((rows // 2, face), BF16),) * 2
 
 
 def mix_layers(info, coefs, chans, sources, sums, out_types, face=0, after=()):
@@ -197,37 +214,40 @@
         else:
             for v in range(len(coefs)):
                 pl.when(info_ref[PLACE_X] == v)(functools.partial(run, coefs[v]))
-        if face:
-            send_faces(info_ref, ODD_Y, results[0], face, *results[outs:])
+        if face == plane:
+            for at, ref in zip((0, rows // 2), results[outs:]):
+                ref[...] = results[0][at : at + rows // 2, :]
+        elif face:
+            send_faces(info_ref, ODD_Y, results[0], face, results[outs], results[outs + 1 :])
 
     shapes = tuple(shape((rows, plane), t) for t in out_types)
     if face:
-        shapes += (shape((rows, face), out_types[0]),) * 2
+        shapes += faces_shape(rows, face)[face == plane :]
     needs = ([PLACE_X] if len(coefs) > 1 else []) + ([ODD_Y] if face else [])
     return call(body, shapes, info, needs, [*sources, *sums], name="mix_layers", after=after)
 
 
 def filter_lanes(info, first, middle, second, table):
-    def body(info_ref, first_ref, middle_ref, second_ref, weights, out):
-        out[...] = swapped_dot(info_ref, ODD_Y, first_ref, [middle_ref], second_ref, weights)
+    def body(info_ref, first_ref, middle_ref, upper, lower, weights, out):
+        out[...] = swapped_dot(info_ref, ODD_Y, first_ref, [middle_ref], (upper, lower), weights)
 
     shapes = shape((first.shape[0], table.shape[1]), F32)
-    return call(body, shapes, info, [ODD_Y], [first, middle, second, table], name="filter_lanes")
+    return call(body, shapes, info, [ODD_Y], [first, middle, *second, table], name="filter_lanes")
 
 
 def filter_faces(info, first, middle, second, table, below=(), after=()):
     rows, face = first.shape[0], table.shape[1] // 2
     extra = below[0].shape[0] if below else 0
 
-    def body(info_ref, first_ref, middle_ref, second_ref, weights, *refs):
+    def body(info_ref, first_ref, middle_ref, upper, lower, weights, *refs):
         outs = refs[-2:]
-        total = swapped_dot(info_ref, ODD_Y, first_ref, [middle_ref], second_ref, weights)
+        total = swapped_dot(info_ref, ODD_Y, first_ref, [middle_ref], (upper, lower), weights)
         send_faces(info_ref, ODD_Z, total, face, *(out.at[:rows, :] for out in outs))
         for src, out in zip(refs[:-2], outs):
             out[rows:, :] = src[...]
 
     shapes = (shape((rows + extra, face), BF16),) * 2
-    arrays = [first, middle, second, table, *below]
+    arrays = [first, middle, *second, table, *below]
     return call(body, shapes, info, [ODD_Y, ODD_Z], arrays, name="filter_faces", after=after)
 
 
@@ -324,7 +344,7 @@
     chans = half2.shape[0]
     rows, plane = field.shape
 
-    def body(info_ref, half_ref, fade_ref, scale_ref, field_ref, fades_ref, out, first, second):
+    def body(info_ref, half_ref, fade_ref, scale_ref, field_ref, fades_ref, out, first, *second):
         fade = fade_of(half_ref[...])
         fades_ref[...] = jnp.dot(fade, fade_ref[...], precision=FULL, preferred_element_type=F32)
         weights = fade * scale_ref[...]
@@ -336,12 +356,7 @@
             out[at, :] = (dot(high, block) + dot(low, block)).astype(BF16)
         send_faces(info_ref, ODD_Y, out, face, first, second)
 
-    shapes = (
-        shape((chans, chans), F32),
-        shape((rows, plane), BF16),
-        shape((rows, face), BF16),
-        shape((rows, face), BF16),
-    )
+    shapes = (shape((chans, chans), F32), shape((rows, plane), BF16), *faces_shape(rows, face))
     arrays = [half2, fade1, scale1, field]
     return call(body, shapes, info, [ODD_Y], arrays, flops=10**9, name="second_fade")
 
@@ -417,14 +432,13 @@
     )
 
 
-def swapped(first, second, axis, inner_first=False):
-    peers = lax.axis_size(axis)
-    got = {}
-    for start in (1, 0) if inner_first else (0, 1):
-        pairs = [(i, i + 1) for i in range(start, peers - 1, 2)]
-        pairs += [(j, i) for i, j in pairs]
-        got[start] = lax.ppermute((first, second)[start], axis, pairs)
-    return got[0], got[1]
+def swap(face, axis, start):
+    pairs = [(i, i + 1) for i in range(start, lax.axis_size(axis) - 1, 2)]
+    return lax.ppermute(face, axis, pairs + [(j, i) for i, j in pairs])
+
+
+def swapped(first, second, axis):
+    return swap(first, axis, 0), swap(second, axis, 1)
 
 
 def shifted(lower, upper, axis):
@@ -480,14 +494,14 @@
     full_x = band(size_x * parts_x)
     own_x = [slice(p * size_x, (p + 1) * size_x) for p in range(parts_x)]
 
-    def along_x(block, matrices, beside=()):
+    def along_x(block, matrices, beside=(), face=face_y):
         kinds = [BF16] * len(matrices)
         if parts_x == 2:
             mine = [[[m[own_x[p], own_x[p]]] for m in matrices] for p in range(2)]
             other = [[[m[own_x[p], own_x[1 - p]]] for m in matrices] for p in range(2)]
             got = lax.ppermute(block, "gx", [(0, 1), (1, 0)])
             sums = mix_layers(info, mine, chans, [block], [], [F32] * len(matrices))
-            return mix_layers(info, other, chans, [got], list(sums), kinds, face=face_y, after=beside)
+            return mix_layers(info, other, chans, [got], list(sums), kinds, face=face, after=beside)
         depth = RADIUS * chans
         before, after = shifted(block[:depth], block[-depth:], "gx")
         rest = jnp.zeros((block.shape[0] - depth, plane), BF16)
@@ -499,11 +513,12 @@
             tables.append(np.where(inside[None], win_x[:, np.clip(columns, 0, win_x.shape[1] - 1)], 0.0))
         return mix_layers(info, [[tables]], chans, [before, block, after], [], kinds, face=face_y)
 
-    def along_y(first, second):
-        return swapped(first, second, "gy", inner_first=True)
-
-    def along_rest(field, first, second):
-        first, second = along_y(first, second)
+    def along_y(first, *second):
+        second = tuple(swap(piece, "gy", 1) for piece in second)
+        return swap(first, "gy", 0), second
+
+    def along_rest(field, *faces):
+        first, second = along_y(*faces)
         ends = swapped(*filter_faces(info, first, field, second, table_ends), "gz")
         return filter_lanes(info, first, field, second, table_own), *ends
 
@@ -529,8 +544,8 @@
             for w in square_z
         ])
         table_y2, table_z2 = pick_tables(info, jnp.asarray(half(tables_y)), jnp.asarray(half(tables_z)))
-        twice_x, once_x, *_ = along_x(raw1, [full_x @ full_x, full_x], [kept])
-        first, second = along_y(twice_x, twice_x)
+        twice_x, once_x, *faces = along_x(raw1, [full_x @ full_x, full_x], [kept], plane)
+        first, second = along_y(twice_x, *faces)
         sent = filter_faces(info, first, twice_x, second, table_y2)
         first, second = swapped(*sent, "gz")
         change = all_courses(None, first, list(sent), second, table_z2)

time: 157 us -> 162 us (1.032)
  starting transfers between devices: 53 us -> 60.4 us
  waiting for transfers between devices: 56.4 us -> 51.5 us
  blocking collectives: 19.5 us -> 22.3 us
    ppermute x10, starting transfers between devices: 34.2 us -> 38.3 us  [hypercube_sum(): value = value + lax.ppermute(value.astype(BF16), axis, pairs).astype(F32)]
    ppermute x14 -> x18, starting transfers between devices: 12.7 us -> 16 us  [swap(): return lax.ppermute(face, axis, pairs + [(j, i) for i, j in pairs])]
    ppermute x3, waiting for transfers between devices: 24.6 us -> 21.4 us  [along_x(): got = lax.ppermute(block, 'gx', [(0, 1), (1, 0)])]
    all_to_all x1, blocking collectives: 19.5 us -> 22.3 us  [exchanged(): return lax.all_to_all(parts, AXES, 0, 0, tiled=True)]
    ppermute x14 -> x18, waiting for transfers between devices: 10.8 us -> 9.08 us  [swap(): return lax.ppermute(face, axis, pairs + [(j, i) for i, j in pairs])]
  transfers between devices with their start and end apart: 27 -> 31, of which waited for: 18 -> 18; matrix products, arithmetic and copies ran while one was open for 0% -> 0% of each run, Pallas kernels for 6% -> 5%
where the time goes in v5:
time: 162 us
  starting transfers between devices  60.4 us (37%)
  waiting for transfers between devices  51.5 us (32%)
  Pallas kernels  22.8 us (14%)
  blocking collectives  22.3 us (14%)
  local copies, waits for them, and re-layouts  2.47 us (2%)
  between operations  1.95 us (1%)
    ppermute x10, starting transfers between devices, hypercube_sum(): value = value + lax.ppermute(value.astype(BF16), axis, pairs).astype(F32)  38.3 us
    pallas_call x24, Pallas kernels, call(): pl.pallas_call(wrapped, out_shape=shapes, in_specs=[pl.BlockSpec(memory_s...  22.8 us
    all_to_all x1, blocking collectives, exchanged(): return lax.all_to_all(parts, AXES, 0, 0, tiled=True)  22.3 us
    ppermute x3, waiting for transfers between devices, along_x(): got = lax.ppermute(block, 'gx', [(0, 1), (1, 0)])  21.4 us
    ppermute x10, waiting for transfers between devices, hypercube_sum(): value = value + lax.ppermute(value.astype(BF16), axis, pairs).astype(F32)  20.9 us
    ppermute x18, starting transfers between devices, swap(): return lax.ppermute(face, axis, pairs + [(j, i) for i, j in pairs])  16 us
    ppermute x18, waiting for transfers between devices, swap(): return lax.ppermute(face, axis, pairs + [(j, i) for i, j in pairs])  9.08 us
    ppermute x3, starting transfers between devices, along_x(): got = lax.ppermute(block, 'gx', [(0, 1), (1, 0)])  6.11 us
  transfers between devices with their start and end apart: 31, of which 18 were waited for; matrix products, arithmetic and copies ran while one was open for 0% of the time, Pallas kernels for 5%

profile of v5, /device:TPU:0, one launch (start us, length us, event | category | flops | bytes accessed | tf_op | source)
XLA Modules:
  0.0 161.7 jit_solution(17971764700745287081)
XLA Ops:
  0.6 1.6 copy-done.2
  2.7 3.0 %collective-permute-start = (bf16[512,512]{1,0:T(8,128)(2,1)S(1)}, bf16[512,512]{1,0:T(8,128)(2,1)S(1)}, u32[]{:S(2)}, u32[]{:S(2)}) collective-permute-start(bf16[512,512]{1,0:T(8,128)(2,1)S(1)} %pack_maps.1.refs_1_), channel_id=1, source_target_pairs={{0,16},{16,0},{1,17},{17,1},{2,18},{18,2},{3,19},{19,3},{4,20},{20... | collective-permute-start | bytes 1572872 | tf_op jit(solution)/shard_map/ppermute | solution.py:502
  5.8 0.5 mix_layers.6.refs_3_
  6.3 11.4 %collective-permute-done.refs_2_ = bf16[512,512]{1,0:T(8,128)(2,1)S(1)} collective-permute-done((bf16[512,512]{1,0:T(8,128)(2,1)S(1)}, bf16[512,512]{1,0:T(8,128)(2,1)S(1)}, u32[]{:S(2)}, u32[]{:S(2)}) %collective-permute-start) | collective-permute-done | bytes 524320 | tf_op jit(solution)/shard_map/ppermute | solution.py:502
  18.2 0.7 collective-permute-start.2
  18.9 0.7 collective-permute-start.3
  20.2 1.9 %collective-permute-start.4 = (bf16[512,128]{1,0:T(8,128)(2,1)S(1)}, bf16[512,128]{1,0:T(8,128)(2,1)S(1)}, u32[]{:S(2)}, u32[]{:S(2)}) collective-permute-start(bf16[512,128]{1,0:T(8,128)(2,1)S(1)} %get-tuple-element.44), channel_id=1, source_target_pairs={{0,1},{2,3},{1,0},{3,2},{4,5},{6,7},{5,4},{7,6},{8,9},{10,11},{9,8... | collective-permute-start | bytes 393224 | tf_op jit(solution)/shard_map/ppermute | solution.py:437
  22.1 0.7 collective-permute-start.5
  23.4 0.7 filter_lanes.3.refs_6_
  24.1 1.1 collective-permute-done.4.refs_2_
  25.3 1.8 %courses_of.2 = f32[64,512]{1,0:T(8,128)S(1)} custom-call(s32[1]{0:T(128)} %bitcast.13.refs_0_, s32[1]{0:T(128)} %bitcast.refs_1_.refs_0_, bf16[512,128]{1,0:T(8,128)(2,1)S(1)} %collective-permute-done.4.refs_2_, bf16[512,128]{1,0:T(8,128)(2,1)S(1)} %collective-permute-done.5.refs_3_, bf16[256,512]{1,0:T(8,128)(2,1)S(1)} %copy-done.6, ...), custom_call_target="tpu_custom_call" | custom-call | flops 1000000000 | bytes 5767168 | tf_op jit(solution)/shard_map/courses_of/pallas_call | solution.py:58
  27.0 1.8 %collective-permute-start.6 = (bf16[64,512]{1,0:T(8,128)(2,1)S(1)}, bf16[64,512]{1,0:T(8,128)(2,1)S(1)}, u32[]{:S(2)}, u32[]{:S(2)}) collective-permute-start(bf16[64,512]{1,0:T(8,128)(2,1)S(1)} %reduce-precision_convert_fusion.1), channel_id=1, source_target_pairs={{0,16},{16,0},{1,17},{17,1},{2,18},{18,2},{3,19},{19,3},{4,20},{20... | collective-permute-start | bytes 196616 | tf_op jit(solution)/shard_map/ppermute | solution.py:465
  28.8 2.5 %collective-permute-done.6 = bf16[64,512]{1,0:T(8,128)(2,1)S(1)} collective-permute-done((bf16[64,512]{1,0:T(8,128)(2,1)S(1)}, bf16[64,512]{1,0:T(8,128)(2,1)S(1)}, u32[]{:S(2)}, u32[]{:S(2)}) %collective-permute-start.6) | collective-permute-done | bytes 65568 | tf_op jit(solution)/shard_map/ppermute | solution.py:465
  31.4 6.4 %collective-permute-start.7 = (bf16[64,512]{1,0:T(8,128)(2,1)S(1)}, bf16[64,512]{1,0:T(8,128)(2,1)S(1)}, u32[]{:S(2)}, u32[]{:S(2)}) collective-permute-start(bf16[64,512]{1,0:T(8,128)(2,1)S(1)} %fusion.4), channel_id=1, source_target_pairs={{0,4},{4,0},{8,12},{12,8},{1,5},{5,1},{9,13},{13,9},{2,6},{6,2},{1... | collective-permute-start | bytes 196616 | tf_op jit(solution)/shard_map/ppermute | solution.py:465
  37.8 0.9 collective-permute-done.7
  38.8 2.9 %collective-permute-start.8 = (bf16[64,512]{1,0:T(8,128)(2,1)S(1)}, bf16[64,512]{1,0:T(8,128)(2,1)S(1)}, u32[]{:S(2)}, u32[]{:S(2)}) collective-permute-start(bf16[64,512]{1,0:T(8,128)(2,1)S(1)} %fusion), channel_id=1, source_target_pairs={{0,8},{4,12},{8,0},{12,4},{1,9},{5,13},{9,1},{13,5},{2,10},{6,14},... | collective-permute-start | bytes 196616 | tf_op jit(solution)/shard_map/ppermute | solution.py:465
  41.6 2.4 %collective-permute-done.8 = bf16[64,512]{1,0:T(8,128)(2,1)S(1)} collective-permute-done((bf16[64,512]{1,0:T(8,128)(2,1)S(1)}, bf16[64,512]{1,0:T(8,128)(2,1)S(1)}, u32[]{:S(2)}, u32[]{:S(2)}) %collective-permute-start.8) | collective-permute-done | bytes 65568 | tf_op jit(solution)/shard_map/ppermute | solution.py:465
  44.1 4.9 %collective-permute-start.9 = (bf16[64,512]{1,0:T(8,128)(2,1)S(1)}, bf16[64,512]{1,0:T(8,128)(2,1)S(1)}, u32[]{:S(2)}, u32[]{:S(2)}) collective-permute-start(bf16[64,512]{1,0:T(8,128)(2,1)S(1)} %get-tuple-element.80), channel_id=1, source_target_pairs={{0,1},{1,0},{2,3},{3,2},{4,5},{5,4},{6,7},{7,6},{8,9},{9,8},{10,11... | collective-permute-start | bytes 196616 | tf_op jit(solution)/shard_map/ppermute | solution.py:465
  49.0 2.2 %collective-permute-done.9 = bf16[64,512]{1,0:T(8,128)(2,1)S(1)} collective-permute-done((bf16[64,512]{1,0:T(8,128)(2,1)S(1)}, bf16[64,512]{1,0:T(8,128)(2,1)S(1)}, u32[]{:S(2)}, u32[]{:S(2)}) %collective-permute-start.9) | collective-permute-done | bytes 65568 | tf_op jit(solution)/shard_map/ppermute | solution.py:465
  51.2 3.5 %collective-permute-start.10 = (bf16[64,512]{1,0:T(8,128)(2,1)S(1)}, bf16[64,512]{1,0:T(8,128)(2,1)S(1)}, u32[]{:S(2)}, u32[]{:S(2)}) collective-permute-start(bf16[64,512]{1,0:T(8,128)(2,1)S(1)} %fusion.1), channel_id=1, source_target_pairs={{0,2},{1,3},{2,0},{3,1},{4,6},{5,7},{6,4},{7,5},{8,10},{9,11},{10,... | collective-permute-start | bytes 196616 | tf_op jit(solution)/shard_map/ppermute | solution.py:465
  54.8 2.2 %collective-permute-done.10 = bf16[64,512]{1,0:T(8,128)(2,1)S(1)} collective-permute-done((bf16[64,512]{1,0:T(8,128)(2,1)S(1)}, bf16[64,512]{1,0:T(8,128)(2,1)S(1)}, u32[]{:S(2)}, u32[]{:S(2)}) %collective-permute-start.10) | collective-permute-done | bytes 65568 | tf_op jit(solution)/shard_map/ppermute | solution.py:465
  57.1 1.4 first_gradient.1
  58.5 1.6 collective-permute-start.11
  60.0 1.0 mix_layers.8
  61.5 8.5 %collective-permute-done.11.refs_2_ = bf16[512,512]{1,0:T(8,128)(2,1)S(1)} collective-permute-done((bf16[512,512]{1,0:T(8,128)(2,1)S(1)}, bf16[512,512]{1,0:T(8,128)(2,1)S(1)}, u32[]{:S(2)}, u32[]{:S(2)}) %collective-permute-start.11) | collective-permute-done | bytes 524320 | tf_op jit(solution)/shard_map/ppermute | solution.py:502
  70.0 1.0 mix_layers.9
  71.1 0.7 collective-permute-start.13
  71.8 0.7 collective-permute-start.14
  73.0 1.0 filter_faces.5
  74.0 1.3 collective-permute-start.15
  75.3 0.8 collective-permute-start.16
  76.2 4.3 %collective-permute-done.15.refs_2_ = bf16[512,256]{1,0:T(8,128)(2,1)S(1)} collective-permute-done((bf16[512,256]{1,0:T(8,128)(2,1)S(1)}, bf16[512,256]{1,0:T(8,128)(2,1)S(1)}, u32[]{:S(2)}, u32[]{:S(2)}) %collective-permute-start.15) | collective-permute-done | bytes 262176 | tf_op jit(solution)/shard_map/ppermute | solution.py:437
  80.5 2.8 %courses_of.3 = f32[64,512]{1,0:T(8,128)S(1)} custom-call(s32[1]{0:T(128)} %bitcast.15.refs_0_, s32[1]{0:T(128)} %bitcast.refs_1_.refs_0_, bf16[512,256]{1,0:T(8,128)(2,1)S(1)} %collective-permute-done.15.refs_2_, bf16[512,256]{1,0:T(8,128)(2,1)S(1)} %get-tuple-element.55.refs_3_, bf16[512,256]{1,0:T(8,128)(2,1)S(1)} %get-tuple-element.56.refs_4_, ...), custom_call_target="tpu_custom_call" | custom-call | flops 1000000000 | bytes 6291456 | tf_op jit(solution)/shard_map/courses_of/pallas_call | solution.py:58
  83.3 1.6 collective-permute-start.17
  84.8 2.8 %collective-permute-done.17 = bf16[64,512]{1,0:T(8,128)(2,1)S(1)} collective-permute-done((bf16[64,512]{1,0:T(8,128)(2,1)S(1)}, bf16[64,512]{1,0:T(8,128)(2,1)S(1)}, u32[]{:S(2)}, u32[]{:S(2)}) %collective-permute-start.17) | collective-permute-done | bytes 65568 | tf_op jit(solution)/shard_map/ppermute | solution.py:465
  87.6 6.9 %collective-permute-start.18 = (bf16[64,512]{1,0:T(8,128)(2,1)S(1)}, bf16[64,512]{1,0:T(8,128)(2,1)S(1)}, u32[]{:S(2)}, u32[]{:S(2)}) collective-permute-start(bf16[64,512]{1,0:T(8,128)(2,1)S(1)} %fusion.5), channel_id=1, source_target_pairs={{0,4},{4,0},{8,12},{12,8},{1,5},{5,1},{9,13},{13,9},{2,6},{6,2},{1... | collective-permute-start | bytes 196616 | tf_op jit(solution)/shard_map/ppermute | solution.py:465
  94.5 0.9 collective-permute-done.18
  95.4 3.5 %collective-permute-start.19 = (bf16[64,512]{1,0:T(8,128)(2,1)S(1)}, bf16[64,512]{1,0:T(8,128)(2,1)S(1)}, u32[]{:S(2)}, u32[]{:S(2)}) collective-permute-start(bf16[64,512]{1,0:T(8,128)(2,1)S(1)} %fusion.2), channel_id=1, source_target_pairs={{0,8},{4,12},{8,0},{12,4},{1,9},{5,13},{9,1},{13,5},{2,10},{6,14},... | collective-permute-start | bytes 196616 | tf_op jit(solution)/shard_map/ppermute | solution.py:465
  98.9 2.4 %collective-permute-done.19 = bf16[64,512]{1,0:T(8,128)(2,1)S(1)} collective-permute-done((bf16[64,512]{1,0:T(8,128)(2,1)S(1)}, bf16[64,512]{1,0:T(8,128)(2,1)S(1)}, u32[]{:S(2)}, u32[]{:S(2)}) %collective-permute-start.19) | collective-permute-done | bytes 65568 | tf_op jit(solution)/shard_map/ppermute | solution.py:465
  101.4 4.0 %collective-permute-start.20 = (bf16[64,512]{1,0:T(8,128)(2,1)S(1)}, bf16[64,512]{1,0:T(8,128)(2,1)S(1)}, u32[]{:S(2)}, u32[]{:S(2)}) collective-permute-start(bf16[64,512]{1,0:T(8,128)(2,1)S(1)} %get-tuple-element.78), channel_id=1, source_target_pairs={{0,1},{1,0},{2,3},{3,2},{4,5},{5,4},{6,7},{7,6},{8,9},{9,8},{10,11... | collective-permute-start | bytes 196616 | tf_op jit(solution)/shard_map/ppermute | solution.py:465
  105.3 2.2 %collective-permute-done.20 = bf16[64,512]{1,0:T(8,128)(2,1)S(1)} collective-permute-done((bf16[64,512]{1,0:T(8,128)(2,1)S(1)}, bf16[64,512]{1,0:T(8,128)(2,1)S(1)}, u32[]{:S(2)}, u32[]{:S(2)}) %collective-permute-start.20) | collective-permute-done | bytes 65568 | tf_op jit(solution)/shard_map/ppermute | solution.py:465
  107.6 3.0 %collective-permute-start.21 = (bf16[64,512]{1,0:T(8,128)(2,1)S(1)}, bf16[64,512]{1,0:T(8,128)(2,1)S(1)}, u32[]{:S(2)}, u32[]{:S(2)}) collective-permute-start(bf16[64,512]{1,0:T(8,128)(2,1)S(1)} %fusion.3), channel_id=1, source_target_pairs={{0,2},{1,3},{2,0},{3,1},{4,6},{5,7},{6,4},{7,5},{8,10},{9,11},{10,... | collective-permute-start | bytes 196616 | tf_op jit(solution)/shard_map/ppermute | solution.py:465
  110.6 2.3 %collective-permute-done.21 = bf16[64,512]{1,0:T(8,128)(2,1)S(1)} collective-permute-done((bf16[64,512]{1,0:T(8,128)(2,1)S(1)}, bf16[64,512]{1,0:T(8,128)(2,1)S(1)}, u32[]{:S(2)}, u32[]{:S(2)}) %collective-permute-start.21) | collective-permute-done | bytes 65568 | tf_op jit(solution)/shard_map/ppermute | solution.py:465
  112.8 1.9 %second_gradient.1 = (bf16[512,512]{1,0:T(8,128)(2,1)S(1)}, bf16[64,512]{1,0:T(8,128)(2,1)}, f32[1,1]{1,0:T(1,128)}) custom-call(s32[1]{0:T(128)} %bitcast.16.refs_0_, f32[64,512]{1,0:T(8,128)S(1)} %convert_add_fusion.refs_1_, bf16[64,512]{1,0:T(8,128)(2,1)S(1)} %get-tuple-element.49.refs_0_.refs_2_, f32[64,512]{1,0:T(8,128)S(1)} %get-tuple-element.50.refs_5_.refs_3_, ...), custom_call_target="tpu_custom_call" | custom-call | flops 1000000000 | bytes 4521984 | tf_op jit(solution)/shard_map/second_gradient/pallas_call | solution.py:58
  114.8 1.5 collective-permute-start.22
  116.3 0.8 copy-done.7
  117.1 1.3 second_fade.1
  118.4 0.7 collective-permute-start.27
  119.1 3.3 %collective-permute-start.26 = (bf16[512,256]{1,0:T(8,128)(2,1)S(1)}, bf16[512,256]{1,0:T(8,128)(2,1)S(1)}, u32[]{:S(2)}, u32[]{:S(2)}) collective-permute-start(bf16[512,256]{1,0:T(8,128)(2,1)S(1)} %get-tuple-element.68), channel_id=1, source_target_pairs={{0,4},{8,12},{4,0},{12,8},{1,5},{9,13},{5,1},{13,9},{2,6},{10,14},... | collective-permute-start | bytes 786440 | tf_op jit(solution)/shard_map/ppermute | solution.py:437
  122.4 1.8 %faded_maps.1.refs_4_.refs_2_ = f32[8,512,64]{2,1,0:T(8,128)S(1)} custom-call(f32[8,512,64]{2,1,0:T(8,128)S(1)} %bitcast.22, f32[64,64]{1,0:T(8,128)S(1)} %get-tuple-element.63.refs_1_), custom_call_target="tpu_custom_call" | custom-call | flops 1000000000 | bytes 1064960 | tf_op jit(solution)/shard_map/faded_maps/pallas_call | solution.py:58
  124.2 0.5 mix_layers.10.refs_3_
  124.7 1.5 collective-permute-done.22.refs_2_
  126.7 0.7 collective-permute-start.28
  127.4 0.7 collective-permute-start.24
  128.1 0.7 collective-permute-start.25
  129.3 0.7 filter_lanes.5.refs_9_.refs_3_
  130.0 0.5 filter_faces.7
  130.5 1.8 %collective-permute-start.29 = (bf16[1024,128]{1,0:T(8,128)(2,1)S(1)}, bf16[1024,128]{1,0:T(8,128)(2,1)S(1)}, u32[]{:S(2)}, u32[]{:S(2)}) collective-permute-start(bf16[1024,128]{1,0:T(8,128)(2,1)S(1)} %get-tuple-element.74), channel_id=1, source_target_pairs={{0,1},{2,3},{1,0},{3,2},{4,5},{6,7},{5,4},{7,6},{8,9},{10,11},{9,8... | collective-permute-start | bytes 786440 | tf_op jit(solution)/shard_map/ppermute | solution.py:437
  132.3 0.7 collective-permute-start.30
  133.0 0.7 filter_lanes.4.refs_1_
  133.7 3.2 %collective-permute-done.29.refs_2_.refs_4_ = bf16[1024,128]{1,0:T(8,128)(2,1)S(1)} collective-permute-done((bf16[1024,128]{1,0:T(8,128)(2,1)S(1)}, bf16[1024,128]{1,0:T(8,128)(2,1)S(1)}, u32[]{:S(2)}, u32[]{:S(2)}) %collective-permute-start.29) | collective-permute-done | bytes 262176 | tf_op jit(solution)/shard_map/ppermute | solution.py:437
  137.0 0.5 gradient_energy.1
  137.5 22.3 %all_to_all.5.refs_1_ = f32[32,1,128]{2,1,0:T(1,128)S(1)} all-to-all(f32[32,1,128]{2,1,0:T(1,128)S(1)} %get-tuple-element.76), channel_id=1, replica_groups=mesh['gx'=2,'gy'=4,'gz'=4] {'gx','gy','gz'}, dimensions={0} | all-to-all | bytes 32768 | tf_op jit(solution)/shard_map/all_to_all | solution.py:452
  159.8 1.7 %final_maps.1 = f32[8,512,64]{2,1,0:T(8,128)} custom-call(s32[1]{0:T(128)} %bitcast.refs_1_.refs_0_, f32[32,1,128]{2,1,0:T(1,128)S(1)} %all_to_all.5.refs_1_, f32[8,512,64]{2,1,0:T(8,128)S(1)} %faded_maps.1.refs_4_.refs_2_, f32[512,512]{1,0:T(8,128)S(1)} %filter_lanes.5.refs_9_.refs_3_, bf16[1024,128]{1,0:T(8,128)(2,1)S(1)} %collective-permute-done.29.refs_2_.refs_4_, ...), custom_call_target="tpu_custom_call" | custom-call | flops 100000000 | bytes 3948544 | tf_op jit(solution)/shard_map/final_maps/pallas_call | solution.py:58
  (56 shorter events, 3.9 us)
Async XLA Ops:
  0.6 1.6 copy-start.2
  2.7 17.0 %copy-start.4 = (bf16[1024,256]{1,0:T(8,128)(2,1)S(1)}, bf16[1024,256]{1,0:T(8,128)(2,1)}, u32[]{:S(2)}) copy-start(bf16[1024,256]{1,0:T(8,128)(2,1)} %constant.40.clone.refs_6_) | copy-start | bytes 1572868
  2.7 15.0 %collective-permute-start = (bf16[512,512]{1,0:T(8,128)(2,1)S(1)}, bf16[512,512]{1,0:T(8,128)(2,1)S(1)}, u32[]{:S(2)}, u32[]{:S(2)}) collective-permute-start(bf16[512,512]{1,0:T(8,128)(2,1)S(1)} %pack_maps.1.refs_1_), channel_id=1, source_target_pairs={{0,16},{16,0},{1,17},{17,1},{2,18},{18,2},{3,19},{19,3},{4,20},{20... | collective-permute-start | bytes 1572872 | tf_op jit(solution)/shard_map/ppermute | solution.py:502
  5.8 17.6 %copy-start.1 = (bf16[1024,512]{1,0:T(8,128)(2,1)S(1)}, bf16[1024,512]{1,0:T(8,128)(2,1)}, u32[]{:S(2)}) copy-start(bf16[1024,512]{1,0:T(8,128)(2,1)} %constant.41.clone.refs_5_) | copy-start | bytes 3145732
  18.1 1.6 collective-permute-start.1
  18.2 1.4 collective-permute-start.2
  18.9 0.7 collective-permute-start.3
  19.7 5.5 %copy-start = (bf16[8,16,32,512]{3,2,1,0:T(8,128)(2,1)S(1)}, bf16[8,16,32,512]{3,2,1,0:T(8,128)(2,1)}, u32[]{:S(2)}) copy-start(bf16[8,16,32,512]{3,2,1,0:T(8,128)(2,1)} %param.8) | copy-start | bytes 12582916
  19.7 5.5 %copy-start.6 = (bf16[256,512]{1,0:T(8,128)(2,1)S(1)}, bf16[256,512]{1,0:T(8,128)(2,1)}, u32[]{:S(2)}) copy-start(bf16[256,512]{1,0:T(8,128)(2,1)} %constant.42.clone.refs_4_.refs_6_) | copy-start | bytes 786436
  20.2 5.0 %collective-permute-start.4 = (bf16[512,128]{1,0:T(8,128)(2,1)S(1)}, bf16[512,128]{1,0:T(8,128)(2,1)S(1)}, u32[]{:S(2)}, u32[]{:S(2)}) collective-permute-start(bf16[512,128]{1,0:T(8,128)(2,1)S(1)} %get-tuple-element.44), channel_id=1, source_target_pairs={{0,1},{2,3},{1,0},{3,2},{4,5},{6,7},{5,4},{7,6},{8,9},{10,11},{9,8... | collective-permute-start | bytes 393224 | tf_op jit(solution)/shard_map/ppermute | solution.py:437
  22.1 3.2 %collective-permute-start.5 = (bf16[512,128]{1,0:T(8,128)(2,1)S(1)}, bf16[512,128]{1,0:T(8,128)(2,1)S(1)}, u32[]{:S(2)}, u32[]{:S(2)}) collective-permute-start(bf16[512,128]{1,0:T(8,128)(2,1)S(1)} %get-tuple-element.45), channel_id=1, source_target_pairs={{1,2},{2,1},{5,6},{6,5},{9,10},{10,9},{13,14},{14,13},{17,18},{18,... | collective-permute-start | bytes 393224 | tf_op jit(solution)/shard_map/ppermute | solution.py:437
  25.2 47.2 %slice-start = ((s8[6291456]{0:T(1024)(128)(4,1)}), s8[4194304]{0:T(1024)(128)(4,1)S(1)}, s32[]{:S(2)}) async-start(s8[6291456]{0:T(1024)(128)(4,1)} %bitcast.23), calls=%async_computation.1 | async-start | bytes 8388608
  27.0 4.3 %collective-permute-start.6 = (bf16[64,512]{1,0:T(8,128)(2,1)S(1)}, bf16[64,512]{1,0:T(8,128)(2,1)S(1)}, u32[]{:S(2)}, u32[]{:S(2)}) collective-permute-start(bf16[64,512]{1,0:T(8,128)(2,1)S(1)} %reduce-precision_convert_fusion.1), channel_id=1, source_target_pairs={{0,16},{16,0},{1,17},{17,1},{2,18},{18,2},{3,19},{19,3},{4,20},{20... | collective-permute-start | bytes 196616 | tf_op jit(solution)/shard_map/ppermute | solution.py:465
  31.4 7.3 %collective-permute-start.7 = (bf16[64,512]{1,0:T(8,128)(2,1)S(1)}, bf16[64,512]{1,0:T(8,128)(2,1)S(1)}, u32[]{:S(2)}, u32[]{:S(2)}) collective-permute-start(bf16[64,512]{1,0:T(8,128)(2,1)S(1)} %fusion.4), channel_id=1, source_target_pairs={{0,4},{4,0},{8,12},{12,8},{1,5},{5,1},{9,13},{13,9},{2,6},{6,2},{1... | collective-permute-start | bytes 196616 | tf_op jit(solution)/shard_map/ppermute | solution.py:465
  38.8 5.3 %collective-permute-start.8 = (bf16[64,512]{1,0:T(8,128)(2,1)S(1)}, bf16[64,512]{1,0:T(8,128)(2,1)S(1)}, u32[]{:S(2)}, u32[]{:S(2)}) collective-permute-start(bf16[64,512]{1,0:T(8,128)(2,1)S(1)} %fusion), channel_id=1, source_target_pairs={{0,8},{4,12},{8,0},{12,4},{1,9},{5,13},{9,1},{13,5},{2,10},{6,14},... | collective-permute-start | bytes 196616 | tf_op jit(solution)/shard_map/ppermute | solution.py:465
  44.1 7.1 %collective-permute-start.9 = (bf16[64,512]{1,0:T(8,128)(2,1)S(1)}, bf16[64,512]{1,0:T(8,128)(2,1)S(1)}, u32[]{:S(2)}, u32[]{:S(2)}) collective-permute-start(bf16[64,512]{1,0:T(8,128)(2,1)S(1)} %get-tuple-element.80), channel_id=1, source_target_pairs={{0,1},{1,0},{2,3},{3,2},{4,5},{5,4},{6,7},{7,6},{8,9},{9,8},{10,11... | collective-permute-start | bytes 196616 | tf_op jit(solution)/shard_map/ppermute | solution.py:465
  51.2 5.8 %collective-permute-start.10 = (bf16[64,512]{1,0:T(8,128)(2,1)S(1)}, bf16[64,512]{1,0:T(8,128)(2,1)S(1)}, u32[]{:S(2)}, u32[]{:S(2)}) collective-permute-start(bf16[64,512]{1,0:T(8,128)(2,1)S(1)} %fusion.1), channel_id=1, source_target_pairs={{0,2},{1,3},{2,0},{3,1},{4,6},{5,7},{6,4},{7,5},{8,10},{9,11},{10,... | collective-permute-start | bytes 196616 | tf_op jit(solution)/shard_map/ppermute | solution.py:465
  57.1 15.4 %slice-start.1 = ((s8[6291456]{0:T(1024)(128)(4,1)}), s8[2097152]{0:T(1024)(128)(4,1)S(1)}, s32[]{:S(2)}) async-start(s8[6291456]{0:T(1024)(128)(4,1)} %bitcast.23), calls=%async_computation.2 | async-start | bytes 4194304
  57.1 15.4 %copy-start.5 = (bf16[4,1024,512]{2,1,0:T(8,128)(2,1)S(1)}, bf16[4,1024,512]{2,1,0:T(8,128)(2,1)}, u32[]{:S(2)}) copy-start(bf16[4,1024,512]{2,1,0:T(8,128)(2,1)} %constant.44.clone.refs_3_) | copy-start | bytes 12582916
  58.5 11.5 %collective-permute-start.11 = (bf16[512,512]{1,0:T(8,128)(2,1)S(1)}, bf16[512,512]{1,0:T(8,128)(2,1)S(1)}, u32[]{:S(2)}, u32[]{:S(2)}) collective-permute-start(bf16[512,512]{1,0:T(8,128)(2,1)S(1)} %get-tuple-element.46.refs_1_), channel_id=1, source_target_pairs={{0,16},{16,0},{1,17},{17,1},{2,18},{18,2},{3,19},{19,3},{4,20},{20... | collective-permute-start | bytes 1572872 | tf_op jit(solution)/shard_map/ppermute | solution.py:502
  71.0 2.0 %collective-permute-start.12 = (bf16[512,512]{1,0:T(8,128)(2,1)S(1)}, bf16[512,512]{1,0:T(8,128)(2,1)S(1)}, u32[]{:S(2)}, u32[]{:S(2)}) collective-permute-start(bf16[512,512]{1,0:T(8,128)(2,1)S(1)} %get-tuple-element.51.refs_3_), channel_id=1, source_target_pairs={{0,4},{8,12},{4,0},{12,8},{1,5},{9,13},{5,1},{13,9},{2,6},{10,14},... | collective-permute-start | bytes 1572872 | tf_op jit(solution)/shard_map/ppermute | solution.py:437
  71.1 1.6 %collective-permute-start.13 = (bf16[256,512]{1,0:T(8,128)(2,1)S(1)}, bf16[256,512]{1,0:T(8,128)(2,1)S(1)}, u32[]{:S(2)}, u32[]{:S(2)}) collective-permute-start(bf16[256,512]{1,0:T(8,128)(2,1)S(1)} %get-tuple-element.52), channel_id=1, source_target_pairs={{4,8},{8,4},{5,9},{9,5},{6,10},{10,6},{7,11},{11,7},{20,24},{24,20... | collective-permute-start | bytes 786440 | tf_op jit(solution)/shard_map/ppermute | solution.py:437
  71.8 0.9 collective-permute-start.14
  74.0 6.4 %collective-permute-start.15 = (bf16[512,256]{1,0:T(8,128)(2,1)S(1)}, bf16[512,256]{1,0:T(8,128)(2,1)S(1)}, u32[]{:S(2)}, u32[]{:S(2)}) collective-permute-start(bf16[512,256]{1,0:T(8,128)(2,1)S(1)} %get-tuple-element.55.refs_3_), channel_id=1, source_target_pairs={{0,1},{2,3},{1,0},{3,2},{4,5},{6,7},{5,4},{7,6},{8,9},{10,11},{9,8... | collective-permute-start | bytes 786440 | tf_op jit(solution)/shard_map/ppermute | solution.py:437
  75.3 5.1 %collective-permute-start.16 = (bf16[512,256]{1,0:T(8,128)(2,1)S(1)}, bf16[512,256]{1,0:T(8,128)(2,1)S(1)}, u32[]{:S(2)}, u32[]{:S(2)}) collective-permute-start(bf16[512,256]{1,0:T(8,128)(2,1)S(1)} %get-tuple-element.56.refs_4_), channel_id=1, source_target_pairs={{1,2},{2,1},{5,6},{6,5},{9,10},{10,9},{13,14},{14,13},{17,18},{18,... | collective-permute-start | bytes 786440 | tf_op jit(solution)/shard_map/ppermute | solution.py:437
  83.3 4.3 %collective-permute-start.17 = (bf16[64,512]{1,0:T(8,128)(2,1)S(1)}, bf16[64,512]{1,0:T(8,128)(2,1)S(1)}, u32[]{:S(2)}, u32[]{:S(2)}) collective-permute-start(bf16[64,512]{1,0:T(8,128)(2,1)S(1)} %reduce-precision_convert_fusion), channel_id=1, source_target_pairs={{0,16},{16,0},{1,17},{17,1},{2,18},{18,2},{3,19},{19,3},{4,20},{20... | collective-permute-start | bytes 196616 | tf_op jit(solution)/shard_map/ppermute | solution.py:465
  87.6 7.8 %collective-permute-start.18 = (bf16[64,512]{1,0:T(8,128)(2,1)S(1)}, bf16[64,512]{1,0:T(8,128)(2,1)S(1)}, u32[]{:S(2)}, u32[]{:S(2)}) collective-permute-start(bf16[64,512]{1,0:T(8,128)(2,1)S(1)} %fusion.5), channel_id=1, source_target_pairs={{0,4},{4,0},{8,12},{12,8},{1,5},{5,1},{9,13},{13,9},{2,6},{6,2},{1... | collective-permute-start | bytes 196616 | tf_op jit(solution)/shard_map/ppermute | solution.py:465
  95.4 5.9 %collective-permute-start.19 = (bf16[64,512]{1,0:T(8,128)(2,1)S(1)}, bf16[64,512]{1,0:T(8,128)(2,1)S(1)}, u32[]{:S(2)}, u32[]{:S(2)}) collective-permute-start(bf16[64,512]{1,0:T(8,128)(2,1)S(1)} %fusion.2), channel_id=1, source_target_pairs={{0,8},{4,12},{8,0},{12,4},{1,9},{5,13},{9,1},{13,5},{2,10},{6,14},... | collective-permute-start | bytes 196616 | tf_op jit(solution)/shard_map/ppermute | solution.py:465
  101.4 6.2 %collective-permute-start.20 = (bf16[64,512]{1,0:T(8,128)(2,1)S(1)}, bf16[64,512]{1,0:T(8,128)(2,1)S(1)}, u32[]{:S(2)}, u32[]{:S(2)}) collective-permute-start(bf16[64,512]{1,0:T(8,128)(2,1)S(1)} %get-tuple-element.78), channel_id=1, source_target_pairs={{0,1},{1,0},{2,3},{3,2},{4,5},{5,4},{6,7},{7,6},{8,9},{9,8},{10,11... | collective-permute-start | bytes 196616 | tf_op jit(solution)/shard_map/ppermute | solution.py:465
  107.6 5.2 %collective-permute-start.21 = (bf16[64,512]{1,0:T(8,128)(2,1)S(1)}, bf16[64,512]{1,0:T(8,128)(2,1)S(1)}, u32[]{:S(2)}, u32[]{:S(2)}) collective-permute-start(bf16[64,512]{1,0:T(8,128)(2,1)S(1)} %fusion.3), channel_id=1, source_target_pairs={{0,2},{1,3},{2,0},{3,1},{4,6},{5,7},{6,4},{7,5},{8,10},{9,11},{10,... | collective-permute-start | bytes 196616 | tf_op jit(solution)/shard_map/ppermute | solution.py:465
  114.8 7.6 %copy-start.3 = (f32[64,8,16,32]{0,3,2,1:T(8,128)S(1)}, f32[64,8,16,32]{0,3,2,1:T(8,128)}, u32[]{:S(2)}) copy-start(f32[64,8,16,32]{0,3,2,1:T(8,128)} %param.9) | copy-start | bytes 3145732
  114.8 11.5 %collective-permute-start.22 = (bf16[512,512]{1,0:T(8,128)(2,1)S(1)}, bf16[512,512]{1,0:T(8,128)(2,1)S(1)}, u32[]{:S(2)}, u32[]{:S(2)}) collective-permute-start(bf16[512,512]{1,0:T(8,128)(2,1)S(1)} %get-tuple-element.58.refs_1_), channel_id=1, source_target_pairs={{0,16},{16,0},{1,17},{17,1},{2,18},{18,2},{3,19},{19,3},{4,20},{20... | collective-permute-start | bytes 1572872 | tf_op jit(solution)/shard_map/ppermute | solution.py:502
  116.3 0.8 copy-start.7
  118.4 9.7 %collective-permute-start.27 = (bf16[256,256]{1,0:T(8,128)(2,1)S(1)}, bf16[256,256]{1,0:T(8,128)(2,1)S(1)}, u32[]{:S(2)}, u32[]{:S(2)}) collective-permute-start(bf16[256,256]{1,0:T(8,128)(2,1)S(1)} %get-tuple-element.70), channel_id=1, source_target_pairs={{4,8},{8,4},{5,9},{9,5},{6,10},{10,6},{7,11},{11,7},{20,24},{24,20... | collective-permute-start | bytes 393224 | tf_op jit(solution)/shard_map/ppermute | solution.py:437
  119.1 9.7 %collective-permute-start.26 = (bf16[512,256]{1,0:T(8,128)(2,1)S(1)}, bf16[512,256]{1,0:T(8,128)(2,1)S(1)}, u32[]{:S(2)}, u32[]{:S(2)}) collective-permute-start(bf16[512,256]{1,0:T(8,128)(2,1)S(1)} %get-tuple-element.68), channel_id=1, source_target_pairs={{0,4},{8,12},{4,0},{12,8},{1,5},{9,13},{5,1},{13,9},{2,6},{10,14},... | collective-permute-start | bytes 786440 | tf_op jit(solution)/shard_map/ppermute | solution.py:437
  126.7 3.4 %collective-permute-start.23 = (bf16[512,256]{1,0:T(8,128)(2,1)S(1)}, bf16[512,256]{1,0:T(8,128)(2,1)S(1)}, u32[]{:S(2)}, u32[]{:S(2)}) collective-permute-start(bf16[512,256]{1,0:T(8,128)(2,1)S(1)} %get-tuple-element.64), channel_id=1, source_target_pairs={{0,4},{8,12},{4,0},{12,8},{1,5},{9,13},{5,1},{13,9},{2,6},{10,14},... | collective-permute-start | bytes 786440 | tf_op jit(solution)/shard_map/ppermute | solution.py:437
  126.7 2.0 %collective-permute-start.28 = (bf16[256,256]{1,0:T(8,128)(2,1)S(1)}, bf16[256,256]{1,0:T(8,128)(2,1)S(1)}, u32[]{:S(2)}, u32[]{:S(2)}) collective-permute-start(bf16[256,256]{1,0:T(8,128)(2,1)S(1)} %get-tuple-element.71), channel_id=1, source_target_pairs={{4,8},{8,4},{5,9},{9,5},{6,10},{10,6},{7,11},{11,7},{20,24},{24,20... | collective-permute-start | bytes 393224 | tf_op jit(solution)/shard_map/ppermute | solution.py:437
  127.4 2.6 %collective-permute-start.24 = (bf16[256,256]{1,0:T(8,128)(2,1)S(1)}, bf16[256,256]{1,0:T(8,128)(2,1)S(1)}, u32[]{:S(2)}, u32[]{:S(2)}) collective-permute-start(bf16[256,256]{1,0:T(8,128)(2,1)S(1)} %get-tuple-element.66), channel_id=1, source_target_pairs={{4,8},{8,4},{5,9},{9,5},{6,10},{10,6},{7,11},{11,7},{20,24},{24,20... | collective-permute-start | bytes 393224 | tf_op jit(solution)/shard_map/ppermute | solution.py:437
  128.1 1.9 %collective-permute-start.25 = (bf16[256,256]{1,0:T(8,128)(2,1)S(1)}, bf16[256,256]{1,0:T(8,128)(2,1)S(1)}, u32[]{:S(2)}, u32[]{:S(2)}) collective-permute-start(bf16[256,256]{1,0:T(8,128)(2,1)S(1)} %get-tuple-element.67), channel_id=1, source_target_pairs={{4,8},{8,4},{5,9},{9,5},{6,10},{10,6},{7,11},{11,7},{20,24},{24,20... | collective-permute-start | bytes 393224 | tf_op jit(solution)/shard_map/ppermute | solution.py:437
  130.5 6.4 %collective-permute-start.29 = (bf16[1024,128]{1,0:T(8,128)(2,1)S(1)}, bf16[1024,128]{1,0:T(8,128)(2,1)S(1)}, u32[]{:S(2)}, u32[]{:S(2)}) collective-permute-start(bf16[1024,128]{1,0:T(8,128)(2,1)S(1)} %get-tuple-element.74), channel_id=1, source_target_pairs={{0,1},{2,3},{1,0},{3,2},{4,5},{6,7},{5,4},{7,6},{8,9},{10,11},{9,8... | collective-permute-start | bytes 786440 | tf_op jit(solution)/shard_map/ppermute | solution.py:437
  132.3 4.6 %collective-permute-start.30 = (bf16[1024,128]{1,0:T(8,128)(2,1)S(1)}, bf16[1024,128]{1,0:T(8,128)(2,1)S(1)}, u32[]{:S(2)}, u32[]{:S(2)}) collective-permute-start(bf16[1024,128]{1,0:T(8,128)(2,1)S(1)} %get-tuple-element.75), channel_id=1, source_target_pairs={{1,2},{2,1},{5,6},{6,5},{9,10},{10,9},{13,14},{14,13},{17,18},{18,... | collective-permute-start | bytes 786440 | tf_op jit(solution)/shard_map/ppermute | solution.py:437

commit v6 on v4

--- a/solution.py
+++ b/solution.py
@@ -130,15 +130,25 @@
     )
 
 
-def send_faces(info_ref, odd, field, face, first, second):
+def send_faces(info_ref, odd, field, face, first=None, second=None):
     plane = field.shape[1]
-
-    def write(low, high):
-        low[...] = field[:, :face].astype(low.dtype)
-        high[...] = field[:, plane - face :].astype(high.dtype)
-
-    pl.when(info_ref[odd] == 0)(lambda: write(second, first))
-    pl.when(info_ref[odd] != 0)(lambda: write(first, second))
+    low, high = slice(0, face), slice(plane - face, plane)
+
+    def write(of_first, of_second):
+        for ref, lanes in ((first, of_first), (second, of_second)):
+            if ref is not None:
+                ref[...] = field[:, lanes].astype(ref.dtype)
+
+    pl.when(info_ref[odd] == 0)(lambda: write(high, low))
+    pl.when(info_ref[odd] != 0)(lambda: write(low, high))
+
+
+def cut_face(info, field, face):
+    def body(info_ref, field_ref, out):
+        send_faces(info_ref, ODD_Y, field_ref, face, second=out)
+
+    shapes = shape((field.shape[0], face), field.dtype)
+    return call(body, shapes, info, [ODD_Y], [field], flops=10**9, name="cut_face")
 
 
 def swapped_dot(info_ref, odd, first, middle, second, weights, rows=slice(None), sent=False):
@@ -198,11 +208,11 @@
             for v in range(len(coefs)):
                 pl.when(info_ref[PLACE_X] == v)(functools.partial(run, coefs[v]))
         if face:
-            send_faces(info_ref, ODD_Y, results[0], face, *results[outs:])
+            send_faces(info_ref, ODD_Y, results[0], face, first=results[outs])
 
     shapes = tuple(shape((rows, plane), t) for t in out_types)
     if face:
-        shapes += (shape((rows, face), out_types[0]),) * 2
+        shapes += (shape((rows, face), out_types[0]),)
     needs = ([PLACE_X] if len(coefs) > 1 else []) + ([ODD_Y] if face else [])
     return call(body, shapes, info, needs, [*sources, *sums], name="mix_layers", after=after)
 
@@ -324,7 +334,7 @@
     chans = half2.shape[0]
     rows, plane = field.shape
 
-    def body(info_ref, half_ref, fade_ref, scale_ref, field_ref, fades_ref, out, first, second):
+    def body(info_ref, half_ref, fade_ref, scale_ref, field_ref, fades_ref, out, first):
         fade = fade_of(half_ref[...])
         fades_ref[...] = jnp.dot(fade, fade_ref[...], precision=FULL, preferred_element_type=F32)
         weights = fade * scale_ref[...]
@@ -334,12 +344,11 @@
             at = slice(x * chans, (x + 1) * chans)
             block = field_ref[at, :]
             out[at, :] = (dot(high, block) + dot(low, block)).astype(BF16)
-        send_faces(info_ref, ODD_Y, out, face, first, second)
+        send_faces(info_ref, ODD_Y, out, face, first=first)
 
     shapes = (
         shape((chans, chans), F32),
         shape((rows, plane), BF16),
-        shape((rows, face), BF16),
         shape((rows, face), BF16),
     )
     arrays = [half2, fade1, scale1, field]
@@ -480,14 +489,14 @@
     full_x = band(size_x * parts_x)
     own_x = [slice(p * size_x, (p + 1) * size_x) for p in range(parts_x)]
 
-    def along_x(block, matrices, beside=()):
+    def along_x(block, matrices, beside=(), face=face_y):
         kinds = [BF16] * len(matrices)
         if parts_x == 2:
             mine = [[[m[own_x[p], own_x[p]]] for m in matrices] for p in range(2)]
             other = [[[m[own_x[p], own_x[1 - p]]] for m in matrices] for p in range(2)]
             got = lax.ppermute(block, "gx", [(0, 1), (1, 0)])
             sums = mix_layers(info, mine, chans, [block], [], [F32] * len(matrices))
-            return mix_layers(info, other, chans, [got], list(sums), kinds, face=face_y, after=beside)
+            return mix_layers(info, other, chans, [got], list(sums), kinds, face=face, after=beside)
         depth = RADIUS * chans
         before, after = shifted(block[:depth], block[-depth:], "gx")
         rest = jnp.zeros((block.shape[0] - depth, plane), BF16)
@@ -499,11 +508,11 @@
             tables.append(np.where(inside[None], win_x[:, np.clip(columns, 0, win_x.shape[1] - 1)], 0.0))
         return mix_layers(info, [[tables]], chans, [before, block, after], [], kinds, face=face_y)
 
-    def along_y(first, second):
-        return swapped(first, second, "gy", inner_first=True)
-
-    def along_rest(field, first, second):
-        first, second = along_y(first, second)
+    def along_y(field, first):
+        return swapped(first, cut_face(info, field, face_y), "gy", inner_first=True)
+
+    def along_rest(field, first):
+        first, second = along_y(field, first)
         ends = swapped(*filter_faces(info, first, field, second, table_ends), "gz")
         return filter_lanes(info, first, field, second, table_own), *ends
 
@@ -529,28 +538,28 @@
             for w in square_z
         ])
         table_y2, table_z2 = pick_tables(info, jnp.asarray(half(tables_y)), jnp.asarray(half(tables_z)))
-        twice_x, once_x, *_ = along_x(raw1, [full_x @ full_x, full_x], [kept])
-        first, second = along_y(twice_x, twice_x)
+        twice_x, once_x = along_x(raw1, [full_x @ full_x, full_x], [kept], 0)
+        first, second = swapped(twice_x, twice_x, "gy", inner_first=True)
         sent = filter_faces(info, first, twice_x, second, table_y2)
         first, second = swapped(*sent, "gz")
         change = all_courses(None, first, list(sent), second, table_z2)
     else:
-        once_x, *faces1 = along_x(raw1, [full_x])
-        again = whole_gradient(info, *along_rest(once_x, *faces1), table_z)
+        once_x, face1 = along_x(raw1, [full_x])
+        again = whole_gradient(info, *along_rest(once_x, face1), table_z)
         acc2, first, second = along_rest(*along_x(again, [full_x]))
         change = all_courses(acc2, first, [], second, table_z)
 
     raw2, half2, scale1 = second_gradient(
         info, change, half1, kept, bold, chans, size_y, size_z, all_cells
     )
-    fades, field1, *faces1 = second_fade(info, half2, fade1, scale1, once_x, face_y)
-    first1, second1 = along_y(*faces1)
+    fades, field1, face1 = second_fade(info, half2, fade1, scale1, once_x, face_y)
+    first1, second1 = along_y(field1, face1)
     below = filter_faces(info, first1, field1, second1, table_ends)
     acc1 = filter_lanes(info, first1, field1, second1, table_own)
     base = faded_maps(info, voxel_maps, fades)
 
-    field2, *faces2 = along_x(raw2, [full_x], [base])
-    first2, second2 = along_y(*faces2)
+    field2, face2 = along_x(raw2, [full_x], [base])
+    first2, second2 = along_y(field2, face2)
     ends = swapped(*filter_faces(info, first2, field2, second2, table_ends, below, [acc1]), "gz")
     acc2 = filter_lanes(info, first2, field2, second2, table_own)
     grad2, energies = gradient_energy(info, acc2, *ends, table_z, peers)

time: 157 us -> 157 us (level)
  starting transfers between devices: 53 us -> 58.2 us
  blocking collectives: 19.5 us -> 15.9 us
  waiting for transfers between devices: 56.4 us -> 54.7 us
    ppermute x14, starting transfers between devices: 12.7 us -> 21.5 us  [swapped(): got[start] = lax.ppermute((first, second)[start], axis, pairs)]
    ppermute x10, starting transfers between devices: 34.2 us -> 30.5 us  [hypercube_sum(): value = value + lax.ppermute(value.astype(BF16), axis, pairs).astype(F32)]
    all_to_all x1, blocking collectives: 19.5 us -> 15.9 us  [exchanged(): return lax.all_to_all(parts, AXES, 0, 0, tiled=True)]
    ppermute x3, waiting for transfers between devices: 24.6 us -> 21.3 us  [along_x(): got = lax.ppermute(block, 'gx', [(0, 1), (1, 0)])]
    pallas_call x24 -> x27, Pallas kernels: 23.6 us -> 22.8 us  [call(): pl.pallas_call(wrapped, out_shape=shapes, in_specs=[pl.BlockSpec(memory_s...]
where the time goes in v6:
time: 157 us; the launch traced here: 156 us
  starting transfers between devices  58.2 us (37%)
  waiting for transfers between devices  54.7 us (35%)
  Pallas kernels  22.8 us (15%)
  blocking collectives  15.9 us (10%)
  local copies, waits for them, and re-layouts  2.47 us (2%)
  between operations  1.85 us (1%)
    ppermute x10, starting transfers between devices, hypercube_sum(): value = value + lax.ppermute(value.astype(BF16), axis, pairs).astype(F32)  30.5 us
    pallas_call x27, Pallas kernels, call(): pl.pallas_call(wrapped, out_shape=shapes, in_specs=[pl.BlockSpec(memory_s...  22.8 us
    ppermute x14, starting transfers between devices, swapped(): got[start] = lax.ppermute((first, second)[start], axis, pairs)  21.5 us
    ppermute x3, waiting for transfers between devices, along_x(): got = lax.ppermute(block, 'gx', [(0, 1), (1, 0)])  21.3 us
    ppermute x10, waiting for transfers between devices, hypercube_sum(): value = value + lax.ppermute(value.astype(BF16), axis, pairs).astype(F32)  21.2 us
    all_to_all x1, blocking collectives, exchanged(): return lax.all_to_all(parts, AXES, 0, 0, tiled=True)  15.9 us
    ppermute x14, waiting for transfers between devices, swapped(): got[start] = lax.ppermute((first, second)[start], axis, pairs)  12.3 us
    ppermute x3, starting transfers between devices, along_x(): got = lax.ppermute(block, 'gx', [(0, 1), (1, 0)])  6.1 us
  transfers between devices with their start and end apart: 27, of which 18 were waited for; matrix products, arithmetic and copies ran while one was open for 0% of the time, Pallas kernels for 6%

profile of v6, /device:TPU:0, one launch (start us, length us, event | category | flops | bytes accessed | tf_op | source)
XLA Modules:
  0.0 156.3 jit_solution(10167913555522950836)
XLA Ops:
  0.6 1.6 %copy-done.2 = f32[64,8,16,32]{0,3,2,1:T(8,128)S(1)} copy-done((f32[64,8,16,32]{0,3,2,1:T(8,128)S(1)}, f32[64,8,16,32]{0,3,2,1:T(8,128)}, u32[]{:S(2)}) %copy-start.2) | copy-done | bytes 1048600
  2.7 3.0 %collective-permute-start = (bf16[512,512]{1,0:T(8,128)(2,1)S(1)}, bf16[512,512]{1,0:T(8,128)(2,1)S(1)}, u32[]{:S(2)}, u32[]{:S(2)}) collective-permute-start(bf16[512,512]{1,0:T(8,128)(2,1)S(1)} %pack_maps.1.refs_1_), channel_id=1, source_target_pairs={{0,16},{16,0},{1,17},{17,1},{2,18},{18,2},{3,19},{19,3},{4,20},{20... | collective-permute-start | bytes 1572872 | tf_op jit(solution)/shard_map/ppermute | solution.py:497
  5.7 0.5 mix_layers.6.refs_3_
  6.3 11.4 %collective-permute-done.refs_2_ = bf16[512,512]{1,0:T(8,128)(2,1)S(1)} collective-permute-done((bf16[512,512]{1,0:T(8,128)(2,1)S(1)}, bf16[512,512]{1,0:T(8,128)(2,1)S(1)}, u32[]{:S(2)}, u32[]{:S(2)}) %collective-permute-start) | collective-permute-done | bytes 524320 | tf_op jit(solution)/shard_map/ppermute | solution.py:497
  18.2 0.8 collective-permute-start.2
  19.0 3.1 %collective-permute-start.1 = (bf16[512,256]{1,0:T(8,128)(2,1)S(1)}, bf16[512,256]{1,0:T(8,128)(2,1)S(1)}, u32[]{:S(2)}, u32[]{:S(2)}) collective-permute-start(bf16[512,256]{1,0:T(8,128)(2,1)S(1)} %get-tuple-element.32), channel_id=1, source_target_pairs={{0,4},{8,12},{4,0},{12,8},{1,5},{9,13},{5,1},{13,9},{2,6},{10,14},... | collective-permute-start | bytes 786440 | tf_op jit(solution)/shard_map/ppermute | solution.py:435
  22.1 1.2 collective-permute-done.1.refs_2_.refs_1_
  23.7 1.6 %collective-permute-start.3 = (bf16[512,128]{1,0:T(8,128)(2,1)S(1)}, bf16[512,128]{1,0:T(8,128)(2,1)S(1)}, u32[]{:S(2)}, u32[]{:S(2)}) collective-permute-start(bf16[512,128]{1,0:T(8,128)(2,1)S(1)} %get-tuple-element.34), channel_id=1, source_target_pairs={{0,1},{2,3},{1,0},{3,2},{4,5},{6,7},{5,4},{7,6},{8,9},{10,11},{9,8... | collective-permute-start | bytes 393224 | tf_op jit(solution)/shard_map/ppermute | solution.py:435
  25.4 0.7 collective-permute-start.4
  26.7 0.7 filter_lanes.3.refs_6_
  27.4 1.4 collective-permute-done.3.refs_2_
  28.8 1.8 %courses_of.2 = f32[64,512]{1,0:T(8,128)S(1)} custom-call(s32[1]{0:T(128)} %bitcast.13.refs_0_, s32[1]{0:T(128)} %bitcast.refs_1_.refs_0_, bf16[512,128]{1,0:T(8,128)(2,1)S(1)} %collective-permute-done.3.refs_2_, bf16[512,128]{1,0:T(8,128)(2,1)S(1)} %collective-permute-done.4.refs_3_, bf16[256,512]{1,0:T(8,128)(2,1)S(1)} %copy-done.6, ...), custom_call_target="tpu_custom_call" | custom-call | flops 1000000000 | bytes 5767168 | tf_op jit(solution)/shard_map/courses_of/pallas_call | solution.py:58
  30.6 1.6 %collective-permute-start.5 = (bf16[64,512]{1,0:T(8,128)(2,1)S(1)}, bf16[64,512]{1,0:T(8,128)(2,1)S(1)}, u32[]{:S(2)}, u32[]{:S(2)}) collective-permute-start(bf16[64,512]{1,0:T(8,128)(2,1)S(1)} %reduce-precision_convert_fusion.1), channel_id=1, source_target_pairs={{0,16},{16,0},{1,17},{17,1},{2,18},{18,2},{3,19},{19,3},{4,20},{20... | collective-permute-start | bytes 196616 | tf_op jit(solution)/shard_map/ppermute | solution.py:460
  32.2 2.8 %collective-permute-done.5 = bf16[64,512]{1,0:T(8,128)(2,1)S(1)} collective-permute-done((bf16[64,512]{1,0:T(8,128)(2,1)S(1)}, bf16[64,512]{1,0:T(8,128)(2,1)S(1)}, u32[]{:S(2)}, u32[]{:S(2)}) %collective-permute-start.5) | collective-permute-done | bytes 65568 | tf_op jit(solution)/shard_map/ppermute | solution.py:460
  34.9 0.6 collective-permute-start.6
  35.5 0.9 collective-permute-done.6
  36.5 4.3 %collective-permute-start.7 = (bf16[64,512]{1,0:T(8,128)(2,1)S(1)}, bf16[64,512]{1,0:T(8,128)(2,1)S(1)}, u32[]{:S(2)}, u32[]{:S(2)}) collective-permute-start(bf16[64,512]{1,0:T(8,128)(2,1)S(1)} %fusion), channel_id=1, source_target_pairs={{0,8},{4,12},{8,0},{12,4},{1,9},{5,13},{9,1},{13,5},{2,10},{6,14},... | collective-permute-start | bytes 196616 | tf_op jit(solution)/shard_map/ppermute | solution.py:460
  40.8 2.4 %collective-permute-done.7 = bf16[64,512]{1,0:T(8,128)(2,1)S(1)} collective-permute-done((bf16[64,512]{1,0:T(8,128)(2,1)S(1)}, bf16[64,512]{1,0:T(8,128)(2,1)S(1)}, u32[]{:S(2)}, u32[]{:S(2)}) %collective-permute-start.7) | collective-permute-done | bytes 65568 | tf_op jit(solution)/shard_map/ppermute | solution.py:460
  43.3 4.6 %collective-permute-start.8 = (bf16[64,512]{1,0:T(8,128)(2,1)S(1)}, bf16[64,512]{1,0:T(8,128)(2,1)S(1)}, u32[]{:S(2)}, u32[]{:S(2)}) collective-permute-start(bf16[64,512]{1,0:T(8,128)(2,1)S(1)} %get-tuple-element.64), channel_id=1, source_target_pairs={{0,1},{1,0},{2,3},{3,2},{4,5},{5,4},{6,7},{7,6},{8,9},{9,8},{10,11... | collective-permute-start | bytes 196616 | tf_op jit(solution)/shard_map/ppermute | solution.py:460
  47.9 2.2 %collective-permute-done.8 = bf16[64,512]{1,0:T(8,128)(2,1)S(1)} collective-permute-done((bf16[64,512]{1,0:T(8,128)(2,1)S(1)}, bf16[64,512]{1,0:T(8,128)(2,1)S(1)}, u32[]{:S(2)}, u32[]{:S(2)}) %collective-permute-start.8) | collective-permute-done | bytes 65568 | tf_op jit(solution)/shard_map/ppermute | solution.py:460
  50.2 3.5 %collective-permute-start.9 = (bf16[64,512]{1,0:T(8,128)(2,1)S(1)}, bf16[64,512]{1,0:T(8,128)(2,1)S(1)}, u32[]{:S(2)}, u32[]{:S(2)}) collective-permute-start(bf16[64,512]{1,0:T(8,128)(2,1)S(1)} %fusion.1), channel_id=1, source_target_pairs={{0,2},{1,3},{2,0},{3,1},{4,6},{5,7},{6,4},{7,5},{8,10},{9,11},{10,... | collective-permute-start | bytes 196616 | tf_op jit(solution)/shard_map/ppermute | solution.py:460
  53.7 2.2 %collective-permute-done.9 = bf16[64,512]{1,0:T(8,128)(2,1)S(1)} collective-permute-done((bf16[64,512]{1,0:T(8,128)(2,1)S(1)}, bf16[64,512]{1,0:T(8,128)(2,1)S(1)}, u32[]{:S(2)}, u32[]{:S(2)}) %collective-permute-start.9) | collective-permute-done | bytes 65568 | tf_op jit(solution)/shard_map/ppermute | solution.py:460
  56.0 1.4 first_gradient.1
  57.4 1.6 %collective-permute-start.10 = (bf16[512,512]{1,0:T(8,128)(2,1)S(1)}, bf16[512,512]{1,0:T(8,128)(2,1)S(1)}, u32[]{:S(2)}, u32[]{:S(2)}) collective-permute-start(bf16[512,512]{1,0:T(8,128)(2,1)S(1)} %get-tuple-element.36.refs_1_), channel_id=1, source_target_pairs={{0,16},{16,0},{1,17},{17,1},{2,18},{18,2},{3,19},{19,3},{4,20},{20... | collective-permute-start | bytes 1572872 | tf_op jit(solution)/shard_map/ppermute | solution.py:497
  59.0 1.0 mix_layers.8
  60.4 8.5 %collective-permute-done.10.refs_1_ = bf16[512,512]{1,0:T(8,128)(2,1)S(1)} collective-permute-done((bf16[512,512]{1,0:T(8,128)(2,1)S(1)}, bf16[512,512]{1,0:T(8,128)(2,1)S(1)}, u32[]{:S(2)}, u32[]{:S(2)}) %collective-permute-start.10) | collective-permute-done | bytes 524320 | tf_op jit(solution)/shard_map/ppermute | solution.py:497
  68.9 1.0 mix_layers.9
  69.9 0.7 collective-permute-start.12
  70.6 2.6 %collective-permute-start.11 = (bf16[512,512]{1,0:T(8,128)(2,1)S(1)}, bf16[512,512]{1,0:T(8,128)(2,1)S(1)}, u32[]{:S(2)}, u32[]{:S(2)}) collective-permute-start(bf16[512,512]{1,0:T(8,128)(2,1)S(1)} %get-tuple-element.41.refs_3_), channel_id=1, source_target_pairs={{0,4},{8,12},{4,0},{12,8},{1,5},{9,13},{5,1},{13,9},{2,6},{10,14},... | collective-permute-start | bytes 1572872 | tf_op jit(solution)/shard_map/ppermute | solution.py:435
  73.5 1.3 collective-permute-done.11.refs_2_
  74.8 1.0 filter_faces.5
  75.8 1.3 collective-permute-start.13
  77.1 0.8 collective-permute-start.14
  78.0 4.3 %collective-permute-done.13.refs_2_ = bf16[512,256]{1,0:T(8,128)(2,1)S(1)} collective-permute-done((bf16[512,256]{1,0:T(8,128)(2,1)S(1)}, bf16[512,256]{1,0:T(8,128)(2,1)S(1)}, u32[]{:S(2)}, u32[]{:S(2)}) %collective-permute-start.13) | collective-permute-done | bytes 262176 | tf_op jit(solution)/shard_map/ppermute | solution.py:435
  82.3 2.8 %courses_of.3 = f32[64,512]{1,0:T(8,128)S(1)} custom-call(s32[1]{0:T(128)} %bitcast.15.refs_0_, s32[1]{0:T(128)} %bitcast.refs_1_.refs_0_, bf16[512,256]{1,0:T(8,128)(2,1)S(1)} %collective-permute-done.13.refs_2_, bf16[512,256]{1,0:T(8,128)(2,1)S(1)} %get-tuple-element.43.refs_3_, bf16[512,256]{1,0:T(8,128)(2,1)S(1)} %get-tuple-element.44.refs_4_, ...), custom_call_target="tpu_custom_call" | custom-call | flops 1000000000 | bytes 6291456 | tf_op jit(solution)/shard_map/courses_of/pallas_call | solution.py:58
  85.1 1.6 collective-permute-start.15
  86.6 2.8 %collective-permute-done.15 = bf16[64,512]{1,0:T(8,128)(2,1)S(1)} collective-permute-done((bf16[64,512]{1,0:T(8,128)(2,1)S(1)}, bf16[64,512]{1,0:T(8,128)(2,1)S(1)}, u32[]{:S(2)}, u32[]{:S(2)}) %collective-permute-start.15) | collective-permute-done | bytes 65568 | tf_op jit(solution)/shard_map/ppermute | solution.py:460
  89.4 3.3 %collective-permute-start.16 = (bf16[64,512]{1,0:T(8,128)(2,1)S(1)}, bf16[64,512]{1,0:T(8,128)(2,1)S(1)}, u32[]{:S(2)}, u32[]{:S(2)}) collective-permute-start(bf16[64,512]{1,0:T(8,128)(2,1)S(1)} %fusion.5), channel_id=1, source_target_pairs={{0,4},{4,0},{8,12},{12,8},{1,5},{5,1},{9,13},{13,9},{2,6},{6,2},{1... | collective-permute-start | bytes 196616 | tf_op jit(solution)/shard_map/ppermute | solution.py:460
  92.7 0.9 collective-permute-done.16
  93.7 4.0 %collective-permute-start.17 = (bf16[64,512]{1,0:T(8,128)(2,1)S(1)}, bf16[64,512]{1,0:T(8,128)(2,1)S(1)}, u32[]{:S(2)}, u32[]{:S(2)}) collective-permute-start(bf16[64,512]{1,0:T(8,128)(2,1)S(1)} %fusion.2), channel_id=1, source_target_pairs={{0,8},{4,12},{8,0},{12,4},{1,9},{5,13},{9,1},{13,5},{2,10},{6,14},... | collective-permute-start | bytes 196616 | tf_op jit(solution)/shard_map/ppermute | solution.py:460
  97.7 2.4 %collective-permute-done.17 = bf16[64,512]{1,0:T(8,128)(2,1)S(1)} collective-permute-done((bf16[64,512]{1,0:T(8,128)(2,1)S(1)}, bf16[64,512]{1,0:T(8,128)(2,1)S(1)}, u32[]{:S(2)}, u32[]{:S(2)}) %collective-permute-start.17) | collective-permute-done | bytes 65568 | tf_op jit(solution)/shard_map/ppermute | solution.py:460
  100.2 4.0 %collective-permute-start.18 = (bf16[64,512]{1,0:T(8,128)(2,1)S(1)}, bf16[64,512]{1,0:T(8,128)(2,1)S(1)}, u32[]{:S(2)}, u32[]{:S(2)}) collective-permute-start(bf16[64,512]{1,0:T(8,128)(2,1)S(1)} %get-tuple-element.62), channel_id=1, source_target_pairs={{0,1},{1,0},{2,3},{3,2},{4,5},{5,4},{6,7},{7,6},{8,9},{9,8},{10,11... | collective-permute-start | bytes 196616 | tf_op jit(solution)/shard_map/ppermute | solution.py:460
  104.2 2.2 %collective-permute-done.18 = bf16[64,512]{1,0:T(8,128)(2,1)S(1)} collective-permute-done((bf16[64,512]{1,0:T(8,128)(2,1)S(1)}, bf16[64,512]{1,0:T(8,128)(2,1)S(1)}, u32[]{:S(2)}, u32[]{:S(2)}) %collective-permute-start.18) | collective-permute-done | bytes 65568 | tf_op jit(solution)/shard_map/ppermute | solution.py:460
  106.4 3.0 %collective-permute-start.19 = (bf16[64,512]{1,0:T(8,128)(2,1)S(1)}, bf16[64,512]{1,0:T(8,128)(2,1)S(1)}, u32[]{:S(2)}, u32[]{:S(2)}) collective-permute-start(bf16[64,512]{1,0:T(8,128)(2,1)S(1)} %fusion.3), channel_id=1, source_target_pairs={{0,2},{1,3},{2,0},{3,1},{4,6},{5,7},{6,4},{7,5},{8,10},{9,11},{10,... | collective-permute-start | bytes 196616 | tf_op jit(solution)/shard_map/ppermute | solution.py:460
  109.4 2.3 %collective-permute-done.19 = bf16[64,512]{1,0:T(8,128)(2,1)S(1)} collective-permute-done((bf16[64,512]{1,0:T(8,128)(2,1)S(1)}, bf16[64,512]{1,0:T(8,128)(2,1)S(1)}, u32[]{:S(2)}, u32[]{:S(2)}) %collective-permute-start.19) | collective-permute-done | bytes 65568 | tf_op jit(solution)/shard_map/ppermute | solution.py:460
  111.7 1.9 %second_gradient.1 = (bf16[512,512]{1,0:T(8,128)(2,1)S(1)}, bf16[64,512]{1,0:T(8,128)(2,1)}, f32[1,1]{1,0:T(1,128)}) custom-call(s32[1]{0:T(128)} %bitcast.16.refs_0_, f32[64,512]{1,0:T(8,128)S(1)} %convert_add_fusion.refs_1_, bf16[64,512]{1,0:T(8,128)(2,1)S(1)} %get-tuple-element.39.refs_0_.refs_2_, f32[64,512]{1,0:T(8,128)S(1)} %get-tuple-element.40.refs_4_.refs_3_, ...), custom_call_target="tpu_custom_call" | custom-call | flops 1000000000 | bytes 4521984 | tf_op jit(solution)/shard_map/second_gradient/pallas_call | solution.py:58
  113.6 1.5 collective-permute-start.20
  115.1 0.8 copy-done.7
  115.9 1.3 second_fade.1
  117.3 0.8 collective-permute-start.24
  118.1 3.3 %collective-permute-start.23 = (bf16[512,256]{1,0:T(8,128)(2,1)S(1)}, bf16[512,256]{1,0:T(8,128)(2,1)S(1)}, u32[]{:S(2)}, u32[]{:S(2)}) collective-permute-start(bf16[512,256]{1,0:T(8,128)(2,1)S(1)} %get-tuple-element.54), channel_id=1, source_target_pairs={{0,4},{8,12},{4,0},{12,8},{1,5},{9,13},{5,1},{13,9},{2,6},{10,14},... | collective-permute-start | bytes 786440 | tf_op jit(solution)/shard_map/ppermute | solution.py:435
  121.3 0.5 mix_layers.10.refs_3_
  121.9 1.8 %faded_maps.1.refs_4_.refs_2_ = f32[8,512,64]{2,1,0:T(8,128)S(1)} custom-call(f32[8,512,64]{2,1,0:T(8,128)S(1)} %bitcast.22, f32[64,64]{1,0:T(8,128)S(1)} %get-tuple-element.51.refs_1_), custom_call_target="tpu_custom_call" | custom-call | flops 1000000000 | bytes 1064960 | tf_op jit(solution)/shard_map/faded_maps/pallas_call | solution.py:58
  123.7 1.4 collective-permute-done.20.refs_2_
  125.5 0.7 collective-permute-start.22
  126.2 2.6 %collective-permute-start.21 = (bf16[512,256]{1,0:T(8,128)(2,1)S(1)}, bf16[512,256]{1,0:T(8,128)(2,1)S(1)}, u32[]{:S(2)}, u32[]{:S(2)}) collective-permute-start(bf16[512,256]{1,0:T(8,128)(2,1)S(1)} %get-tuple-element.52), channel_id=1, source_target_pairs={{0,4},{8,12},{4,0},{12,8},{1,5},{9,13},{5,1},{13,9},{2,6},{10,14},... | collective-permute-start | bytes 786440 | tf_op jit(solution)/shard_map/ppermute | solution.py:435
  129.3 0.7 filter_lanes.5.refs_8_.refs_3_
  130.5 1.8 %collective-permute-start.25 = (bf16[1024,128]{1,0:T(8,128)(2,1)S(1)}, bf16[1024,128]{1,0:T(8,128)(2,1)S(1)}, u32[]{:S(2)}, u32[]{:S(2)}) collective-permute-start(bf16[1024,128]{1,0:T(8,128)(2,1)S(1)} %get-tuple-element.58), channel_id=1, source_target_pairs={{0,1},{2,3},{1,0},{3,2},{4,5},{6,7},{5,4},{7,6},{8,9},{10,11},{9,8... | collective-permute-start | bytes 786440 | tf_op jit(solution)/shard_map/ppermute | solution.py:435
  132.3 0.7 collective-permute-start.26
  133.0 0.7 filter_lanes.4.refs_1_
  133.7 4.2 %collective-permute-done.25.refs_2_.refs_4_ = bf16[1024,128]{1,0:T(8,128)(2,1)S(1)} collective-permute-done((bf16[1024,128]{1,0:T(8,128)(2,1)S(1)}, bf16[1024,128]{1,0:T(8,128)(2,1)S(1)}, u32[]{:S(2)}, u32[]{:S(2)}) %collective-permute-start.25) | collective-permute-done | bytes 262176 | tf_op jit(solution)/shard_map/ppermute | solution.py:435
  137.9 0.5 gradient_energy.1
  138.5 15.9 %all_to_all.5.refs_1_ = f32[32,1,128]{2,1,0:T(1,128)S(1)} all-to-all(f32[32,1,128]{2,1,0:T(1,128)S(1)} %get-tuple-element.60), channel_id=1, replica_groups=mesh['gx'=2,'gy'=4,'gz'=4] {'gx','gy','gz'}, dimensions={0} | all-to-all | bytes 32768 | tf_op jit(solution)/shard_map/all_to_all | solution.py:447
  154.4 1.7 %final_maps.1 = f32[8,512,64]{2,1,0:T(8,128)} custom-call(s32[1]{0:T(128)} %bitcast.refs_1_.refs_0_, f32[32,1,128]{2,1,0:T(1,128)S(1)} %all_to_all.5.refs_1_, f32[8,512,64]{2,1,0:T(8,128)S(1)} %faded_maps.1.refs_4_.refs_2_, f32[512,512]{1,0:T(8,128)S(1)} %filter_lanes.5.refs_8_.refs_3_, bf16[1024,128]{1,0:T(8,128)(2,1)S(1)} %collective-permute-done.25.refs_2_.refs_4_, ...), custom_call_target="tpu_custom_call" | custom-call | flops 100000000 | bytes 3948544 | tf_op jit(solution)/shard_map/final_maps/pallas_call | solution.py:58
  (51 shorter events, 3.8 us)
Async XLA Ops:
  0.6 1.6 %copy-start.2 = (f32[64,8,16,32]{0,3,2,1:T(8,128)S(1)}, f32[64,8,16,32]{0,3,2,1:T(8,128)}, u32[]{:S(2)}) copy-start(f32[64,8,16,32]{0,3,2,1:T(8,128)} %param.9) | copy-start | bytes 3145732
  2.7 15.0 %collective-permute-start = (bf16[512,512]{1,0:T(8,128)(2,1)S(1)}, bf16[512,512]{1,0:T(8,128)(2,1)S(1)}, u32[]{:S(2)}, u32[]{:S(2)}) collective-permute-start(bf16[512,512]{1,0:T(8,128)(2,1)S(1)} %pack_maps.1.refs_1_), channel_id=1, source_target_pairs={{0,16},{16,0},{1,17},{17,1},{2,18},{18,2},{3,19},{19,3},{4,20},{20... | collective-permute-start | bytes 1572872 | tf_op jit(solution)/shard_map/ppermute | solution.py:497
  18.1 5.2 %copy-start.4 = (bf16[1024,256]{1,0:T(8,128)(2,1)S(1)}, bf16[1024,256]{1,0:T(8,128)(2,1)}, u32[]{:S(2)}) copy-start(bf16[1024,256]{1,0:T(8,128)(2,1)} %constant.40.clone.refs_5_) | copy-start | bytes 1572868
  18.1 8.6 %copy-start.1 = (bf16[1024,512]{1,0:T(8,128)(2,1)S(1)}, bf16[1024,512]{1,0:T(8,128)(2,1)}, u32[]{:S(2)}) copy-start(bf16[1024,512]{1,0:T(8,128)(2,1)} %constant.41.clone.refs_4_) | copy-start | bytes 3145732
  18.2 3.9 %collective-permute-start.2 = (bf16[512,256]{1,0:T(8,128)(2,1)S(1)}, bf16[512,256]{1,0:T(8,128)(2,1)S(1)}, u32[]{:S(2)}, u32[]{:S(2)}) collective-permute-start(bf16[512,256]{1,0:T(8,128)(2,1)S(1)} %cut_face.3), channel_id=1, source_target_pairs={{4,8},{8,4},{5,9},{9,5},{6,10},{10,6},{7,11},{11,7},{20,24},{24,20... | collective-permute-start | bytes 786440 | tf_op jit(solution)/shard_map/ppermute | solution.py:435
  19.0 4.3 %collective-permute-start.1 = (bf16[512,256]{1,0:T(8,128)(2,1)S(1)}, bf16[512,256]{1,0:T(8,128)(2,1)S(1)}, u32[]{:S(2)}, u32[]{:S(2)}) collective-permute-start(bf16[512,256]{1,0:T(8,128)(2,1)S(1)} %get-tuple-element.32), channel_id=1, source_target_pairs={{0,4},{8,12},{4,0},{12,8},{1,5},{9,13},{5,1},{13,9},{2,6},{10,14},... | collective-permute-start | bytes 786440 | tf_op jit(solution)/shard_map/ppermute | solution.py:435
  23.3 5.5 %copy-start = (bf16[8,16,32,512]{3,2,1,0:T(8,128)(2,1)S(1)}, bf16[8,16,32,512]{3,2,1,0:T(8,128)(2,1)}, u32[]{:S(2)}) copy-start(bf16[8,16,32,512]{3,2,1,0:T(8,128)(2,1)} %param.8) | copy-start | bytes 12582916
  23.3 5.5 %copy-start.6 = (bf16[256,512]{1,0:T(8,128)(2,1)S(1)}, bf16[256,512]{1,0:T(8,128)(2,1)}, u32[]{:S(2)}) copy-start(bf16[256,512]{1,0:T(8,128)(2,1)} %constant.42.clone.refs_4_.refs_6_) | copy-start | bytes 786436
  23.7 5.0 %collective-permute-start.3 = (bf16[512,128]{1,0:T(8,128)(2,1)S(1)}, bf16[512,128]{1,0:T(8,128)(2,1)S(1)}, u32[]{:S(2)}, u32[]{:S(2)}) collective-permute-start(bf16[512,128]{1,0:T(8,128)(2,1)S(1)} %get-tuple-element.34), channel_id=1, source_target_pairs={{0,1},{2,3},{1,0},{3,2},{4,5},{6,7},{5,4},{7,6},{8,9},{10,11},{9,8... | collective-permute-start | bytes 393224 | tf_op jit(solution)/shard_map/ppermute | solution.py:435
  25.4 3.4 %collective-permute-start.4 = (bf16[512,128]{1,0:T(8,128)(2,1)S(1)}, bf16[512,128]{1,0:T(8,128)(2,1)S(1)}, u32[]{:S(2)}, u32[]{:S(2)}) collective-permute-start(bf16[512,128]{1,0:T(8,128)(2,1)S(1)} %get-tuple-element.35), channel_id=1, source_target_pairs={{1,2},{2,1},{5,6},{6,5},{9,10},{10,9},{13,14},{14,13},{17,18},{18,... | collective-permute-start | bytes 393224 | tf_op jit(solution)/shard_map/ppermute | solution.py:435
  28.8 44.5 %slice-start = ((s8[6291456]{0:T(1024)(128)(4,1)}), s8[4194304]{0:T(1024)(128)(4,1)S(1)}, s32[]{:S(2)}) async-start(s8[6291456]{0:T(1024)(128)(4,1)} %bitcast.23), calls=%async_computation.1 | async-start | bytes 8388608
  30.6 4.3 %collective-permute-start.5 = (bf16[64,512]{1,0:T(8,128)(2,1)S(1)}, bf16[64,512]{1,0:T(8,128)(2,1)S(1)}, u32[]{:S(2)}, u32[]{:S(2)}) collective-permute-start(bf16[64,512]{1,0:T(8,128)(2,1)S(1)} %reduce-precision_convert_fusion.1), channel_id=1, source_target_pairs={{0,16},{16,0},{1,17},{17,1},{2,18},{18,2},{3,19},{19,3},{4,20},{20... | collective-permute-start | bytes 196616 | tf_op jit(solution)/shard_map/ppermute | solution.py:460
  34.9 1.5 collective-permute-start.6
  36.5 6.8 %collective-permute-start.7 = (bf16[64,512]{1,0:T(8,128)(2,1)S(1)}, bf16[64,512]{1,0:T(8,128)(2,1)S(1)}, u32[]{:S(2)}, u32[]{:S(2)}) collective-permute-start(bf16[64,512]{1,0:T(8,128)(2,1)S(1)} %fusion), channel_id=1, source_target_pairs={{0,8},{4,12},{8,0},{12,4},{1,9},{5,13},{9,1},{13,5},{2,10},{6,14},... | collective-permute-start | bytes 196616 | tf_op jit(solution)/shard_map/ppermute | solution.py:460
  43.3 6.9 %collective-permute-start.8 = (bf16[64,512]{1,0:T(8,128)(2,1)S(1)}, bf16[64,512]{1,0:T(8,128)(2,1)S(1)}, u32[]{:S(2)}, u32[]{:S(2)}) collective-permute-start(bf16[64,512]{1,0:T(8,128)(2,1)S(1)} %get-tuple-element.64), channel_id=1, source_target_pairs={{0,1},{1,0},{2,3},{3,2},{4,5},{5,4},{6,7},{7,6},{8,9},{9,8},{10,11... | collective-permute-start | bytes 196616 | tf_op jit(solution)/shard_map/ppermute | solution.py:460
  50.2 5.8 %collective-permute-start.9 = (bf16[64,512]{1,0:T(8,128)(2,1)S(1)}, bf16[64,512]{1,0:T(8,128)(2,1)S(1)}, u32[]{:S(2)}, u32[]{:S(2)}) collective-permute-start(bf16[64,512]{1,0:T(8,128)(2,1)S(1)} %fusion.1), channel_id=1, source_target_pairs={{0,2},{1,3},{2,0},{3,1},{4,6},{5,7},{6,4},{7,5},{8,10},{9,11},{10,... | collective-permute-start | bytes 196616 | tf_op jit(solution)/shard_map/ppermute | solution.py:460
  56.0 17.2 %slice-start.1 = ((s8[6291456]{0:T(1024)(128)(4,1)}), s8[2097152]{0:T(1024)(128)(4,1)S(1)}, s32[]{:S(2)}) async-start(s8[6291456]{0:T(1024)(128)(4,1)} %bitcast.23), calls=%async_computation.2 | async-start | bytes 4194304
  56.0 17.2 %copy-start.5 = (bf16[4,1024,512]{2,1,0:T(8,128)(2,1)S(1)}, bf16[4,1024,512]{2,1,0:T(8,128)(2,1)}, u32[]{:S(2)}) copy-start(bf16[4,1024,512]{2,1,0:T(8,128)(2,1)} %constant.44.clone.refs_3_) | copy-start | bytes 12582916
  57.4 11.5 %collective-permute-start.10 = (bf16[512,512]{1,0:T(8,128)(2,1)S(1)}, bf16[512,512]{1,0:T(8,128)(2,1)S(1)}, u32[]{:S(2)}, u32[]{:S(2)}) collective-permute-start(bf16[512,512]{1,0:T(8,128)(2,1)S(1)} %get-tuple-element.36.refs_1_), channel_id=1, source_target_pairs={{0,16},{16,0},{1,17},{17,1},{2,18},{18,2},{3,19},{19,3},{4,20},{20... | collective-permute-start | bytes 1572872 | tf_op jit(solution)/shard_map/ppermute | solution.py:497
  69.9 3.5 %collective-permute-start.12 = (bf16[512,512]{1,0:T(8,128)(2,1)S(1)}, bf16[512,512]{1,0:T(8,128)(2,1)S(1)}, u32[]{:S(2)}, u32[]{:S(2)}) collective-permute-start(bf16[512,512]{1,0:T(8,128)(2,1)S(1)} %get-tuple-element.41.refs_3_), channel_id=1, source_target_pairs={{4,8},{8,4},{5,9},{9,5},{6,10},{10,6},{7,11},{11,7},{20,24},{24,20... | collective-permute-start | bytes 1572872 | tf_op jit(solution)/shard_map/ppermute | solution.py:435
  70.6 4.1 %collective-permute-start.11 = (bf16[512,512]{1,0:T(8,128)(2,1)S(1)}, bf16[512,512]{1,0:T(8,128)(2,1)S(1)}, u32[]{:S(2)}, u32[]{:S(2)}) collective-permute-start(bf16[512,512]{1,0:T(8,128)(2,1)S(1)} %get-tuple-element.41.refs_3_), channel_id=1, source_target_pairs={{0,4},{8,12},{4,0},{12,8},{1,5},{9,13},{5,1},{13,9},{2,6},{10,14},... | collective-permute-start | bytes 1572872 | tf_op jit(solution)/shard_map/ppermute | solution.py:435
  75.8 6.4 %collective-permute-start.13 = (bf16[512,256]{1,0:T(8,128)(2,1)S(1)}, bf16[512,256]{1,0:T(8,128)(2,1)S(1)}, u32[]{:S(2)}, u32[]{:S(2)}) collective-permute-start(bf16[512,256]{1,0:T(8,128)(2,1)S(1)} %get-tuple-element.43.refs_3_), channel_id=1, source_target_pairs={{0,1},{2,3},{1,0},{3,2},{4,5},{6,7},{5,4},{7,6},{8,9},{10,11},{9,8... | collective-permute-start | bytes 786440 | tf_op jit(solution)/shard_map/ppermute | solution.py:435
  77.1 5.1 %collective-permute-start.14 = (bf16[512,256]{1,0:T(8,128)(2,1)S(1)}, bf16[512,256]{1,0:T(8,128)(2,1)S(1)}, u32[]{:S(2)}, u32[]{:S(2)}) collective-permute-start(bf16[512,256]{1,0:T(8,128)(2,1)S(1)} %get-tuple-element.44.refs_4_), channel_id=1, source_target_pairs={{1,2},{2,1},{5,6},{6,5},{9,10},{10,9},{13,14},{14,13},{17,18},{18,... | collective-permute-start | bytes 786440 | tf_op jit(solution)/shard_map/ppermute | solution.py:435
  85.1 4.3 %collective-permute-start.15 = (bf16[64,512]{1,0:T(8,128)(2,1)S(1)}, bf16[64,512]{1,0:T(8,128)(2,1)S(1)}, u32[]{:S(2)}, u32[]{:S(2)}) collective-permute-start(bf16[64,512]{1,0:T(8,128)(2,1)S(1)} %reduce-precision_convert_fusion), channel_id=1, source_target_pairs={{0,16},{16,0},{1,17},{17,1},{2,18},{18,2},{3,19},{19,3},{4,20},{20... | collective-permute-start | bytes 196616 | tf_op jit(solution)/shard_map/ppermute | solution.py:460
  89.4 4.2 %collective-permute-start.16 = (bf16[64,512]{1,0:T(8,128)(2,1)S(1)}, bf16[64,512]{1,0:T(8,128)(2,1)S(1)}, u32[]{:S(2)}, u32[]{:S(2)}) collective-permute-start(bf16[64,512]{1,0:T(8,128)(2,1)S(1)} %fusion.5), channel_id=1, source_target_pairs={{0,4},{4,0},{8,12},{12,8},{1,5},{5,1},{9,13},{13,9},{2,6},{6,2},{1... | collective-permute-start | bytes 196616 | tf_op jit(solution)/shard_map/ppermute | solution.py:460
  93.7 6.5 %collective-permute-start.17 = (bf16[64,512]{1,0:T(8,128)(2,1)S(1)}, bf16[64,512]{1,0:T(8,128)(2,1)S(1)}, u32[]{:S(2)}, u32[]{:S(2)}) collective-permute-start(bf16[64,512]{1,0:T(8,128)(2,1)S(1)} %fusion.2), channel_id=1, source_target_pairs={{0,8},{4,12},{8,0},{12,4},{1,9},{5,13},{9,1},{13,5},{2,10},{6,14},... | collective-permute-start | bytes 196616 | tf_op jit(solution)/shard_map/ppermute | solution.py:460
  100.2 6.2 %collective-permute-start.18 = (bf16[64,512]{1,0:T(8,128)(2,1)S(1)}, bf16[64,512]{1,0:T(8,128)(2,1)S(1)}, u32[]{:S(2)}, u32[]{:S(2)}) collective-permute-start(bf16[64,512]{1,0:T(8,128)(2,1)S(1)} %get-tuple-element.62), channel_id=1, source_target_pairs={{0,1},{1,0},{2,3},{3,2},{4,5},{5,4},{6,7},{7,6},{8,9},{9,8},{10,11... | collective-permute-start | bytes 196616 | tf_op jit(solution)/shard_map/ppermute | solution.py:460
  106.4 5.2 %collective-permute-start.19 = (bf16[64,512]{1,0:T(8,128)(2,1)S(1)}, bf16[64,512]{1,0:T(8,128)(2,1)S(1)}, u32[]{:S(2)}, u32[]{:S(2)}) collective-permute-start(bf16[64,512]{1,0:T(8,128)(2,1)S(1)} %fusion.3), channel_id=1, source_target_pairs={{0,2},{1,3},{2,0},{3,1},{4,6},{5,7},{6,4},{7,5},{8,10},{9,11},{10,... | collective-permute-start | bytes 196616 | tf_op jit(solution)/shard_map/ppermute | solution.py:460
  113.6 11.5 %collective-permute-start.20 = (bf16[512,512]{1,0:T(8,128)(2,1)S(1)}, bf16[512,512]{1,0:T(8,128)(2,1)S(1)}, u32[]{:S(2)}, u32[]{:S(2)}) collective-permute-start(bf16[512,512]{1,0:T(8,128)(2,1)S(1)} %get-tuple-element.46.refs_1_), channel_id=1, source_target_pairs={{0,16},{16,0},{1,17},{17,1},{2,18},{18,2},{3,19},{19,3},{4,20},{20... | collective-permute-start | bytes 1572872 | tf_op jit(solution)/shard_map/ppermute | solution.py:497
  115.1 0.8 copy-start.7
  117.2 4.6 %copy-start.3 = (f32[64,8,16,32]{0,3,2,1:T(8,128)S(1)}, f32[64,8,16,32]{0,3,2,1:T(8,128)}, u32[]{:S(2)}) copy-start(f32[64,8,16,32]{0,3,2,1:T(8,128)} %param.9) | copy-start | bytes 3145732
  117.3 11.6 %collective-permute-start.24 = (bf16[512,256]{1,0:T(8,128)(2,1)S(1)}, bf16[512,256]{1,0:T(8,128)(2,1)S(1)}, u32[]{:S(2)}, u32[]{:S(2)}) collective-permute-start(bf16[512,256]{1,0:T(8,128)(2,1)S(1)} %cut_face.5), channel_id=1, source_target_pairs={{4,8},{8,4},{5,9},{9,5},{6,10},{10,6},{7,11},{11,7},{20,24},{24,20... | collective-permute-start | bytes 786440 | tf_op jit(solution)/shard_map/ppermute | solution.py:435
  118.1 10.7 %collective-permute-start.23 = (bf16[512,256]{1,0:T(8,128)(2,1)S(1)}, bf16[512,256]{1,0:T(8,128)(2,1)S(1)}, u32[]{:S(2)}, u32[]{:S(2)}) collective-permute-start(bf16[512,256]{1,0:T(8,128)(2,1)S(1)} %get-tuple-element.54), channel_id=1, source_target_pairs={{0,4},{8,12},{4,0},{12,8},{1,5},{9,13},{5,1},{13,9},{2,6},{10,14},... | collective-permute-start | bytes 786440 | tf_op jit(solution)/shard_map/ppermute | solution.py:435
  125.5 4.5 %collective-permute-start.22 = (bf16[512,256]{1,0:T(8,128)(2,1)S(1)}, bf16[512,256]{1,0:T(8,128)(2,1)S(1)}, u32[]{:S(2)}, u32[]{:S(2)}) collective-permute-start(bf16[512,256]{1,0:T(8,128)(2,1)S(1)} %cut_face.4), channel_id=1, source_target_pairs={{4,8},{8,4},{5,9},{9,5},{6,10},{10,6},{7,11},{11,7},{20,24},{24,20... | collective-permute-start | bytes 786440 | tf_op jit(solution)/shard_map/ppermute | solution.py:435
  126.2 3.8 %collective-permute-start.21 = (bf16[512,256]{1,0:T(8,128)(2,1)S(1)}, bf16[512,256]{1,0:T(8,128)(2,1)S(1)}, u32[]{:S(2)}, u32[]{:S(2)}) collective-permute-start(bf16[512,256]{1,0:T(8,128)(2,1)S(1)} %get-tuple-element.52), channel_id=1, source_target_pairs={{0,4},{8,12},{4,0},{12,8},{1,5},{9,13},{5,1},{13,9},{2,6},{10,14},... | collective-permute-start | bytes 786440 | tf_op jit(solution)/shard_map/ppermute | solution.py:435
  130.5 7.4 %collective-permute-start.25 = (bf16[1024,128]{1,0:T(8,128)(2,1)S(1)}, bf16[1024,128]{1,0:T(8,128)(2,1)S(1)}, u32[]{:S(2)}, u32[]{:S(2)}) collective-permute-start(bf16[1024,128]{1,0:T(8,128)(2,1)S(1)} %get-tuple-element.58), channel_id=1, source_target_pairs={{0,1},{2,3},{1,0},{3,2},{4,5},{6,7},{5,4},{7,6},{8,9},{10,11},{9,8... | collective-permute-start | bytes 786440 | tf_op jit(solution)/shard_map/ppermute | solution.py:435
  132.3 5.6 %collective-permute-start.26 = (bf16[1024,128]{1,0:T(8,128)(2,1)S(1)}, bf16[1024,128]{1,0:T(8,128)(2,1)S(1)}, u32[]{:S(2)}, u32[]{:S(2)}) collective-permute-start(bf16[1024,128]{1,0:T(8,128)(2,1)S(1)} %get-tuple-element.59), channel_id=1, source_target_pairs={{1,2},{2,1},{5,6},{6,5},{9,10},{10,9},{13,14},{14,13},{17,18},{18,... | collective-permute-start | bytes 786440 | tf_op jit(solution)/shard_map/ppermute | solution.py:435

commit v7 on v6

--- a/solution.py
+++ b/solution.py
@@ -151,7 +151,7 @@
     return call(body, shapes, info, [ODD_Y], [field], flops=10**9, name="cut_face")
 
 
-def swapped_dot(info_ref, odd, first, middle, second, weights, rows=slice(None), sent=False):
+def swapped_dot(info_ref, odd, first, middle, second, weights, rows=slice(None)):
     width = first.shape[1]
     end = weights.shape[0] - width
     even = info_ref[odd] == 0
@@ -160,9 +160,6 @@
         return weights[pl.ds(pl.multiple_of(jnp.where(even, when_even, when_odd), width), width), :]
 
     total = dot(first[rows, :], at(end, 0)) + dot(second[rows, :], at(0, end))
-    if sent:
-        high = end - width
-        return total + dot(middle[0][rows, :], at(high, width)) + dot(middle[1][rows, :], at(width, high))
     for piece in middle:
         total = total + dot(piece[rows, :], weights[width : width + piece.shape[1], :])
     return total
@@ -241,31 +238,40 @@
     return call(body, shapes, info, [ODD_Y, ODD_Z], arrays, name="filter_faces", after=after)
 
 
+def filter_sent(info, sent, table):
+    def body(info_ref, first_ref, second_ref, weights, out):
+        width = first_ref.shape[1]
+        even = info_ref[ODD_Z] == 0
+        of_first = pl.multiple_of(jnp.where(even, 2 * width, width), width)
+        of_second = pl.multiple_of(jnp.where(even, width, 2 * width), width)
+        total = dot(first_ref[...], weights[pl.ds(of_first, width), :])
+        out[...] = total + dot(second_ref[...], weights[pl.ds(of_second, width), :])
+
+    shapes = shape((sent[0].shape[0], table.shape[1]), F32)
+    return call(body, shapes, info, [ODD_Z], [*sent, table], name="filter_sent")
+
+
 def live_lanes(info_ref, layer, dims, size_y, size_z):
     row = layer * size_y + lax.broadcasted_iota(jnp.int32, dims, 1) // size_z
     return row < info_ref[COUNT]
 
 
-def courses_of(info, acc, first, middle, second, table, bold, chans, size_y, size_z):
+def courses_of(info, acc, first, second, table, bold, chans, size_y, size_z):
     frames = bold.shape[1]
     plane = size_y * size_z
     layers = bold.shape[0] // plane
-    between = len(middle)
-
-    def body(info_ref, first_ref, *refs):
-        ins, second_ref, weights, frames_ref = refs[:between], *refs[between : between + 3]
+
+    def body(info_ref, start, first_ref, second_ref, weights, frames_ref, out):
         total = jnp.zeros((chans, frames), F32)
         for x in range(layers):
             rows = slice(x * chans, (x + 1) * chans)
-            value = swapped_dot(info_ref, ODD_Z, first_ref, ins, second_ref, weights, rows, sent=between == 2)
-            if acc is not None:
-                value = value + refs[between + 3][rows, :]
+            value = start[rows, :] + swapped_dot(info_ref, ODD_Z, first_ref, [], second_ref, weights, rows)
             keep = live_lanes(info_ref, x, value.shape, size_y, size_z)
             value = jnp.where(keep, value, 0.0).astype(BF16)
             total = total + dot(value, frames_ref[x * plane : (x + 1) * plane, :])
-        refs[-1][...] = total
-
-    arrays = [first, *middle, second, table, bold] + ([acc] if acc is not None else [])
+        out[...] = total
+
+    arrays = [acc, first, second, table, bold]
     shapes = shape((chans, frames), F32)
     return call(body, shapes, info, [COUNT, ODD_Z], arrays, flops=10**9, name="courses_of")
 
@@ -448,16 +454,25 @@
 
 
 def hypercube_sum(value):
-    steps = []
+    rounds = []
     for axis in AXES:
         peers = lax.axis_size(axis)
         if peers & (peers - 1):
             return lax.psum(value, AXES)
-        steps += [(axis, 1 << b) for b in range(peers.bit_length() - 1)]
-    for axis, bit in steps:
-        pairs = [(i, i ^ bit) for i in range(lax.axis_size(axis))]
+        if axis == "gz" and peers == 4:
+            rounds.append((axis, (1, 2, 3)))
+        else:
+            rounds += [(axis, (1 << b,)) for b in range(peers.bit_length() - 1)]
+    for axis, masks in rounds:
         value = lax.reduce_precision(value, 8, 7)
-        value = value + lax.ppermute(value.astype(BF16), axis, pairs).astype(F32)
+        sent = value.astype(BF16)
+        got = []
+        for mask in masks:
+            pairs = [(i, i ^ mask) for i in range(lax.axis_size(axis))]
+            got.append(lax.ppermute(sent, axis, pairs).astype(F32))
+        value = value + got[0]
+        if len(got) == 3:
+            value = value + (got[1] + got[2])
     return value
 
 
@@ -516,14 +531,12 @@
         ends = swapped(*filter_faces(info, first, field, second, table_ends), "gz")
         return filter_lanes(info, first, field, second, table_own), *ends
 
-    def all_courses(acc, first, middle, second, table):
-        return hypercube_sum(
-            courses_of(info, acc, first, middle, second, table, bold, chans, size_y, size_z)
-        )
+    def all_courses(acc, first, second, table):
+        return hypercube_sum(courses_of(info, acc, first, second, table, bold, chans, size_y, size_z))
 
     plain = pack_maps(info, voxel_maps)
     acc, first, second = along_rest(*along_x(plain, [full_x]))
-    courses1 = all_courses(acc, first, [], second, table_z)
+    courses1 = all_courses(acc, first, second, table_z)
     raw1, half1 = first_gradient(info, courses1, bold, chans, size_y, size_z)
     kept, fade1 = first_fade(info, half1)
     if twice:
@@ -542,12 +555,12 @@
         first, second = swapped(twice_x, twice_x, "gy", inner_first=True)
         sent = filter_faces(info, first, twice_x, second, table_y2)
         first, second = swapped(*sent, "gz")
-        change = all_courses(None, first, list(sent), second, table_z2)
+        change = all_courses(filter_sent(info, sent, table_z2), first, second, table_z2)
     else:
         once_x, face1 = along_x(raw1, [full_x])
         again = whole_gradient(info, *along_rest(once_x, face1), table_z)
         acc2, first, second = along_rest(*along_x(again, [full_x]))
-        change = all_courses(acc2, first, [], second, table_z)
+        change = all_courses(acc2, first, second, table_z)
 
     raw2, half2, scale1 = second_gradient(
         info, change, half1, kept, bold, chans, size_y, size_z, all_cells

time: 157 us -> 158 us (level)
  blocking collectives: 15.9 us -> 18.8 us
    all_to_all x1, blocking collectives: 15.9 us -> 18.8 us  [exchanged(): return lax.all_to_all(parts, AXES, 0, 0, tiled=True)]
    ppermute x3, waiting for transfers between devices: 21.3 us -> 23.6 us  [along_x(): got = lax.ppermute(block, 'gx', [(0, 1), (1, 0)])]
    ppermute x14, waiting for transfers between devices: 12.3 us -> 10.6 us  [swapped(): got[start] = lax.ppermute((first, second)[start], axis, pairs)]
    ppermute x10 -> x12, waiting for transfers between devices: 21.2 us -> 20.4 us  [hypercube_sum(): got.append(lax.ppermute(sent, axis, pairs).astype(F32))]
    ppermute x10 -> x12, starting transfers between devices: 30.5 us -> 30.1 us  [hypercube_sum(): got.append(lax.ppermute(sent, axis, pairs).astype(F32))]
    pallas_call x27 -> x28, Pallas kernels: 22.8 us -> 22.5 us  [call(): pl.pallas_call(wrapped, out_shape=shapes, in_specs=[pl.BlockSpec(memory_s...]
  transfers between devices with their start and end apart: 27 -> 29, of which waited for: 18 -> 18; matrix products, arithmetic and copies ran while one was open for 0% -> 0% of each run, Pallas kernels for 6% -> 6%
where the time goes in v7:
time: 158 us
  starting transfers between devices  56.9 us (36%)
  waiting for transfers between devices  54.6 us (35%)
  Pallas kernels  22.5 us (14%)
  blocking collectives  18.8 us (12%)
  local copies, waits for them, and re-layouts  2.47 us (2%)
  between operations  1.84 us (1%)
    ppermute x12, starting transfers between devices, hypercube_sum(): got.append(lax.ppermute(sent, axis, pairs).astype(F32))  30.1 us
    ppermute x3, waiting for transfers between devices, along_x(): got = lax.ppermute(block, 'gx', [(0, 1), (1, 0)])  23.6 us
    pallas_call x28, Pallas kernels, call(): pl.pallas_call(wrapped, out_shape=shapes, in_specs=[pl.BlockSpec(memory_s...  22.5 us
    ppermute x14, starting transfers between devices, swapped(): got[start] = lax.ppermute((first, second)[start], axis, pairs)  20.7 us
    ppermute x12, waiting for transfers between devices, hypercube_sum(): got.append(lax.ppermute(sent, axis, pairs).astype(F32))  20.4 us
    all_to_all x1, blocking collectives, exchanged(): return lax.all_to_all(parts, AXES, 0, 0, tiled=True)  18.8 us
    ppermute x14, waiting for transfers between devices, swapped(): got[start] = lax.ppermute((first, second)[start], axis, pairs)  10.6 us
    ppermute x3, starting transfers between devices, along_x(): got = lax.ppermute(block, 'gx', [(0, 1), (1, 0)])  6.1 us
  transfers between devices with their start and end apart: 29, of which 18 were waited for; matrix products, arithmetic and copies ran while one was open for 0% of the time, Pallas kernels for 6%

profile of v7, /device:TPU:0, one launch (start us, length us, event | category | flops | bytes accessed | tf_op | source)
XLA Modules:
  0.0 157.6 jit_solution(9218637728113727550)
XLA Ops:
  0.6 1.6 %copy-done.2 = f32[64,8,16,32]{0,3,2,1:T(8,128)S(1)} copy-done((f32[64,8,16,32]{0,3,2,1:T(8,128)S(1)}, f32[64,8,16,32]{0,3,2,1:T(8,128)}, u32[]{:S(2)}) %copy-start.2) | copy-done | bytes 1048600
  2.7 3.0 %collective-permute-start = (bf16[512,512]{1,0:T(8,128)(2,1)S(1)}, bf16[512,512]{1,0:T(8,128)(2,1)S(1)}, u32[]{:S(2)}, u32[]{:S(2)}) collective-permute-start(bf16[512,512]{1,0:T(8,128)(2,1)S(1)} %pack_maps.1.refs_1_), channel_id=1, source_target_pairs={{0,16},{16,0},{1,17},{17,1},{2,18},{18,2},{3,19},{19,3},{4,20},{20... | collective-permute-start | bytes 1572872 | tf_op jit(solution)/shard_map/ppermute | solution.py:512
  5.7 0.5 mix_layers.6.refs_3_
  6.3 11.4 %collective-permute-done.refs_2_ = bf16[512,512]{1,0:T(8,128)(2,1)S(1)} collective-permute-done((bf16[512,512]{1,0:T(8,128)(2,1)S(1)}, bf16[512,512]{1,0:T(8,128)(2,1)S(1)}, u32[]{:S(2)}, u32[]{:S(2)}) %collective-permute-start) | collective-permute-done | bytes 524320 | tf_op jit(solution)/shard_map/ppermute | solution.py:512
  18.2 0.8 collective-permute-start.2
  19.0 3.1 %collective-permute-start.1 = (bf16[512,256]{1,0:T(8,128)(2,1)S(1)}, bf16[512,256]{1,0:T(8,128)(2,1)S(1)}, u32[]{:S(2)}, u32[]{:S(2)}) collective-permute-start(bf16[512,256]{1,0:T(8,128)(2,1)S(1)} %get-tuple-element.32), channel_id=1, source_target_pairs={{0,4},{8,12},{4,0},{12,8},{1,5},{9,13},{5,1},{13,9},{2,6},{10,14},... | collective-permute-start | bytes 786440 | tf_op jit(solution)/shard_map/ppermute | solution.py:441
  22.1 1.2 collective-permute-done.1.refs_1_.refs_2_
  23.7 1.6 %collective-permute-start.3 = (bf16[512,128]{1,0:T(8,128)(2,1)S(1)}, bf16[512,128]{1,0:T(8,128)(2,1)S(1)}, u32[]{:S(2)}, u32[]{:S(2)}) collective-permute-start(bf16[512,128]{1,0:T(8,128)(2,1)S(1)} %get-tuple-element.34), channel_id=1, source_target_pairs={{0,1},{2,3},{1,0},{3,2},{4,5},{6,7},{5,4},{7,6},{8,9},{10,11},{9,8... | collective-permute-start | bytes 393224 | tf_op jit(solution)/shard_map/ppermute | solution.py:441
  25.4 0.7 collective-permute-start.4
  26.7 0.7 filter_lanes.3.refs_2_
  27.4 1.4 collective-permute-done.3.refs_3_
  28.8 1.8 %courses_of.2 = f32[64,512]{1,0:T(8,128)S(1)} custom-call(s32[1]{0:T(128)} %bitcast.13.refs_0_, s32[1]{0:T(128)} %bitcast.refs_1_.refs_0_, f32[512,512]{1,0:T(8,128)S(1)} %filter_lanes.3.refs_2_, bf16[512,128]{1,0:T(8,128)(2,1)S(1)} %collective-permute-done.3.refs_3_, bf16[512,128]{1,0:T(8,128)(2,1)S(1)} %collective-permute-done.4.refs_4_, ...), custom_call_target="tpu_custom_call" | custom-call | flops 1000000000 | bytes 5767168 | tf_op jit(solution)/shard_map/courses_of/pallas_call | solution.py:58
  30.6 1.6 %collective-permute-start.5 = (bf16[64,512]{1,0:T(8,128)(2,1)S(1)}, bf16[64,512]{1,0:T(8,128)(2,1)S(1)}, u32[]{:S(2)}, u32[]{:S(2)}) collective-permute-start(bf16[64,512]{1,0:T(8,128)(2,1)S(1)} %reduce-precision_convert_fusion.1), channel_id=1, source_target_pairs={{0,16},{16,0},{1,17},{17,1},{2,18},{18,2},{3,19},{19,3},{4,20},{20... | collective-permute-start | bytes 196616 | tf_op jit(solution)/shard_map/ppermute | solution.py:472
  32.2 2.8 %collective-permute-done.5 = bf16[64,512]{1,0:T(8,128)(2,1)S(1)} collective-permute-done((bf16[64,512]{1,0:T(8,128)(2,1)S(1)}, bf16[64,512]{1,0:T(8,128)(2,1)S(1)}, u32[]{:S(2)}, u32[]{:S(2)}) %collective-permute-start.5) | collective-permute-done | bytes 65568 | tf_op jit(solution)/shard_map/ppermute | solution.py:472
  34.9 0.6 collective-permute-start.6
  35.5 0.9 collective-permute-done.6
  36.5 4.3 %collective-permute-start.7 = (bf16[64,512]{1,0:T(8,128)(2,1)S(1)}, bf16[64,512]{1,0:T(8,128)(2,1)S(1)}, u32[]{:S(2)}, u32[]{:S(2)}) collective-permute-start(bf16[64,512]{1,0:T(8,128)(2,1)S(1)} %fusion), channel_id=1, source_target_pairs={{0,8},{4,12},{8,0},{12,4},{1,9},{5,13},{9,1},{13,5},{2,10},{6,14},... | collective-permute-start | bytes 196616 | tf_op jit(solution)/shard_map/ppermute | solution.py:472
  40.8 2.4 %collective-permute-done.7 = bf16[64,512]{1,0:T(8,128)(2,1)S(1)} collective-permute-done((bf16[64,512]{1,0:T(8,128)(2,1)S(1)}, bf16[64,512]{1,0:T(8,128)(2,1)S(1)}, u32[]{:S(2)}, u32[]{:S(2)}) %collective-permute-start.7) | collective-permute-done | bytes 65568 | tf_op jit(solution)/shard_map/ppermute | solution.py:472
  43.3 3.7 %collective-permute-start.10 = (bf16[64,512]{1,0:T(8,128)(2,1)S(1)}, bf16[64,512]{1,0:T(8,128)(2,1)S(1)}, u32[]{:S(2)}, u32[]{:S(2)}) collective-permute-start(bf16[64,512]{1,0:T(8,128)(2,1)S(1)} %fusion.2), channel_id=1, source_target_pairs={{0,3},{1,2},{2,1},{3,0},{4,7},{5,6},{6,5},{7,4},{8,11},{9,10},{10,... | collective-permute-start | bytes 196616 | tf_op jit(solution)/shard_map/ppermute | solution.py:472
  47.0 2.5 %collective-permute-start.9 = (bf16[64,512]{1,0:T(8,128)(2,1)S(1)}, bf16[64,512]{1,0:T(8,128)(2,1)S(1)}, u32[]{:S(2)}, u32[]{:S(2)}) collective-permute-start(bf16[64,512]{1,0:T(8,128)(2,1)S(1)} %fusion.2), channel_id=1, source_target_pairs={{0,2},{1,3},{2,0},{3,1},{4,6},{5,7},{6,4},{7,5},{8,10},{9,11},{10,... | collective-permute-start | bytes 196616 | tf_op jit(solution)/shard_map/ppermute | solution.py:472
  50.0 3.5 %collective-permute-done.9 = bf16[64,512]{1,0:T(8,128)(2,1)S(1)} collective-permute-done((bf16[64,512]{1,0:T(8,128)(2,1)S(1)}, bf16[64,512]{1,0:T(8,128)(2,1)S(1)}, u32[]{:S(2)}, u32[]{:S(2)}) %collective-permute-start.9) | collective-permute-done | bytes 65568 | tf_op jit(solution)/shard_map/ppermute | solution.py:472
  53.5 0.6 collective-permute-done.8
  54.2 1.4 first_gradient.1
  55.6 1.6 collective-permute-start.11
  57.1 1.0 mix_layers.8
  58.6 9.5 %collective-permute-done.11.refs_1_ = bf16[512,512]{1,0:T(8,128)(2,1)S(1)} collective-permute-done((bf16[512,512]{1,0:T(8,128)(2,1)S(1)}, bf16[512,512]{1,0:T(8,128)(2,1)S(1)}, u32[]{:S(2)}, u32[]{:S(2)}) %collective-permute-start.11) | collective-permute-done | bytes 524320 | tf_op jit(solution)/shard_map/ppermute | solution.py:512
  68.1 1.0 mix_layers.9
  69.1 0.7 collective-permute-start.13
  69.8 1.9 %collective-permute-start.12 = (bf16[512,512]{1,0:T(8,128)(2,1)S(1)}, bf16[512,512]{1,0:T(8,128)(2,1)S(1)}, u32[]{:S(2)}, u32[]{:S(2)}) collective-permute-start(bf16[512,512]{1,0:T(8,128)(2,1)S(1)} %get-tuple-element.41.refs_3_), channel_id=1, source_target_pairs={{0,4},{8,12},{4,0},{12,8},{1,5},{9,13},{5,1},{13,9},{2,6},{10,14},... | collective-permute-start | bytes 1572872 | tf_op jit(solution)/shard_map/ppermute | solution.py:441
  71.9 1.3 collective-permute-done.12.refs_2_
  73.2 1.0 filter_faces.5
  74.2 2.0 %collective-permute-start.14 = (bf16[512,256]{1,0:T(8,128)(2,1)S(1)}, bf16[512,256]{1,0:T(8,128)(2,1)S(1)}, u32[]{:S(2)}, u32[]{:S(2)}) collective-permute-start(bf16[512,256]{1,0:T(8,128)(2,1)S(1)} %get-tuple-element.43.refs_1_), channel_id=1, source_target_pairs={{0,1},{2,3},{1,0},{3,2},{4,5},{6,7},{5,4},{7,6},{8,9},{10,11},{9,8... | collective-permute-start | bytes 786440 | tf_op jit(solution)/shard_map/ppermute | solution.py:441
  76.3 0.8 collective-permute-start.15
  77.6 3.1 %collective-permute-done.14.refs_3_ = bf16[512,256]{1,0:T(8,128)(2,1)S(1)} collective-permute-done((bf16[512,256]{1,0:T(8,128)(2,1)S(1)}, bf16[512,256]{1,0:T(8,128)(2,1)S(1)}, u32[]{:S(2)}, u32[]{:S(2)}) %collective-permute-start.14) | collective-permute-done | bytes 262176 | tf_op jit(solution)/shard_map/ppermute | solution.py:441
  80.7 2.1 %courses_of.3 = f32[64,512]{1,0:T(8,128)S(1)} custom-call(s32[1]{0:T(128)} %bitcast.15.refs_0_, s32[1]{0:T(128)} %bitcast.refs_1_.refs_0_, f32[512,512]{1,0:T(8,128)S(1)} %filter_sent.1.refs_2_, bf16[512,256]{1,0:T(8,128)(2,1)S(1)} %collective-permute-done.14.refs_3_, bf16[512,256]{1,0:T(8,128)(2,1)S(1)} %collective-permute-done.15.refs_4_, ...), custom_call_target="tpu_custom_call" | custom-call | flops 1000000000 | bytes 6815744 | tf_op jit(solution)/shard_map/courses_of/pallas_call | solution.py:58
  82.8 1.6 collective-permute-start.16
  84.3 2.8 %collective-permute-done.16 = bf16[64,512]{1,0:T(8,128)(2,1)S(1)} collective-permute-done((bf16[64,512]{1,0:T(8,128)(2,1)S(1)}, bf16[64,512]{1,0:T(8,128)(2,1)S(1)}, u32[]{:S(2)}, u32[]{:S(2)}) %collective-permute-start.16) | collective-permute-done | bytes 65568 | tf_op jit(solution)/shard_map/ppermute | solution.py:472
  87.1 3.5 %collective-permute-start.17 = (bf16[64,512]{1,0:T(8,128)(2,1)S(1)}, bf16[64,512]{1,0:T(8,128)(2,1)S(1)}, u32[]{:S(2)}, u32[]{:S(2)}) collective-permute-start(bf16[64,512]{1,0:T(8,128)(2,1)S(1)} %fusion.5), channel_id=1, source_target_pairs={{0,4},{4,0},{8,12},{12,8},{1,5},{5,1},{9,13},{13,9},{2,6},{6,2},{1... | collective-permute-start | bytes 196616 | tf_op jit(solution)/shard_map/ppermute | solution.py:472
  90.7 0.9 collective-permute-done.17
  91.6 3.8 %collective-permute-start.18 = (bf16[64,512]{1,0:T(8,128)(2,1)S(1)}, bf16[64,512]{1,0:T(8,128)(2,1)S(1)}, u32[]{:S(2)}, u32[]{:S(2)}) collective-permute-start(bf16[64,512]{1,0:T(8,128)(2,1)S(1)} %fusion.1), channel_id=1, source_target_pairs={{0,8},{4,12},{8,0},{12,4},{1,9},{5,13},{9,1},{13,5},{2,10},{6,14},... | collective-permute-start | bytes 196616 | tf_op jit(solution)/shard_map/ppermute | solution.py:472
  95.4 2.4 %collective-permute-done.18 = bf16[64,512]{1,0:T(8,128)(2,1)S(1)} collective-permute-done((bf16[64,512]{1,0:T(8,128)(2,1)S(1)}, bf16[64,512]{1,0:T(8,128)(2,1)S(1)}, u32[]{:S(2)}, u32[]{:S(2)}) %collective-permute-start.18) | collective-permute-done | bytes 65568 | tf_op jit(solution)/shard_map/ppermute | solution.py:472
  97.9 5.0 %collective-permute-start.21 = (bf16[64,512]{1,0:T(8,128)(2,1)S(1)}, bf16[64,512]{1,0:T(8,128)(2,1)S(1)}, u32[]{:S(2)}, u32[]{:S(2)}) collective-permute-start(bf16[64,512]{1,0:T(8,128)(2,1)S(1)} %fusion.3), channel_id=1, source_target_pairs={{0,3},{1,2},{2,1},{3,0},{4,7},{5,6},{6,5},{7,4},{8,11},{9,10},{10,... | collective-permute-start | bytes 196616 | tf_op jit(solution)/shard_map/ppermute | solution.py:472
  102.9 2.5 %collective-permute-start.20 = (bf16[64,512]{1,0:T(8,128)(2,1)S(1)}, bf16[64,512]{1,0:T(8,128)(2,1)S(1)}, u32[]{:S(2)}, u32[]{:S(2)}) collective-permute-start(bf16[64,512]{1,0:T(8,128)(2,1)S(1)} %fusion.3), channel_id=1, source_target_pairs={{0,2},{1,3},{2,0},{3,1},{4,6},{5,7},{6,4},{7,5},{8,10},{9,11},{10,... | collective-permute-start | bytes 196616 | tf_op jit(solution)/shard_map/ppermute | solution.py:472
  105.9 3.5 %collective-permute-done.20 = bf16[64,512]{1,0:T(8,128)(2,1)S(1)} collective-permute-done((bf16[64,512]{1,0:T(8,128)(2,1)S(1)}, bf16[64,512]{1,0:T(8,128)(2,1)S(1)}, u32[]{:S(2)}, u32[]{:S(2)}) %collective-permute-start.20) | collective-permute-done | bytes 65568 | tf_op jit(solution)/shard_map/ppermute | solution.py:472
  109.4 0.6 collective-permute-done.19
  110.1 1.9 %second_gradient.1 = (bf16[512,512]{1,0:T(8,128)(2,1)S(1)}, bf16[64,512]{1,0:T(8,128)(2,1)}, f32[1,1]{1,0:T(1,128)}) custom-call(s32[1]{0:T(128)} %bitcast.16.refs_0_, f32[64,512]{1,0:T(8,128)S(1)} %add_add_fusion.refs_1_, bf16[64,512]{1,0:T(8,128)(2,1)S(1)} %get-tuple-element.39.refs_0_.refs_2_, f32[64,512]{1,0:T(8,128)S(1)} %get-tuple-element.40.refs_4_.refs_3_, ...), custom_call_target="tpu_custom_call" | custom-call | flops 1000000000 | bytes 4521984 | tf_op jit(solution)/shard_map/second_gradient/pallas_call | solution.py:58
  112.0 1.5 collective-permute-start.22
  113.5 0.8 copy-done.7
  114.3 1.3 second_fade.1
  115.7 0.8 collective-permute-start.26
  116.5 2.9 %collective-permute-start.25 = (bf16[512,256]{1,0:T(8,128)(2,1)S(1)}, bf16[512,256]{1,0:T(8,128)(2,1)S(1)}, u32[]{:S(2)}, u32[]{:S(2)}) collective-permute-start(bf16[512,256]{1,0:T(8,128)(2,1)S(1)} %get-tuple-element.54), channel_id=1, source_target_pairs={{0,4},{8,12},{4,0},{12,8},{1,5},{9,13},{5,1},{13,9},{2,6},{10,14},... | collective-permute-start | bytes 786440 | tf_op jit(solution)/shard_map/ppermute | solution.py:441
  119.4 0.5 mix_layers.10.refs_3_
  120.0 1.8 %faded_maps.1.refs_4_.refs_2_ = f32[8,512,64]{2,1,0:T(8,128)S(1)} custom-call(f32[8,512,64]{2,1,0:T(8,128)S(1)} %bitcast.22, f32[64,64]{1,0:T(8,128)S(1)} %get-tuple-element.51.refs_1_), custom_call_target="tpu_custom_call" | custom-call | flops 1000000000 | bytes 1064960 | tf_op jit(solution)/shard_map/faded_maps/pallas_call | solution.py:58
  121.8 2.7 %collective-permute-done.22.refs_2_ = bf16[512,512]{1,0:T(8,128)(2,1)S(1)} collective-permute-done((bf16[512,512]{1,0:T(8,128)(2,1)S(1)}, bf16[512,512]{1,0:T(8,128)(2,1)S(1)}, u32[]{:S(2)}, u32[]{:S(2)}) %collective-permute-start.22) | collective-permute-done | bytes 524320 | tf_op jit(solution)/shard_map/ppermute | solution.py:512
  124.9 0.7 collective-permute-start.24
  125.6 1.9 %collective-permute-start.23 = (bf16[512,256]{1,0:T(8,128)(2,1)S(1)}, bf16[512,256]{1,0:T(8,128)(2,1)S(1)}, u32[]{:S(2)}, u32[]{:S(2)}) collective-permute-start(bf16[512,256]{1,0:T(8,128)(2,1)S(1)} %get-tuple-element.52), channel_id=1, source_target_pairs={{0,4},{8,12},{4,0},{12,8},{1,5},{9,13},{5,1},{13,9},{2,6},{10,14},... | collective-permute-start | bytes 786440 | tf_op jit(solution)/shard_map/ppermute | solution.py:441
  128.0 0.7 filter_lanes.5.refs_8_.refs_3_
  129.2 2.1 %collective-permute-start.27 = (bf16[1024,128]{1,0:T(8,128)(2,1)S(1)}, bf16[1024,128]{1,0:T(8,128)(2,1)S(1)}, u32[]{:S(2)}, u32[]{:S(2)}) collective-permute-start(bf16[1024,128]{1,0:T(8,128)(2,1)S(1)} %get-tuple-element.58), channel_id=1, source_target_pairs={{0,1},{2,3},{1,0},{3,2},{4,5},{6,7},{5,4},{7,6},{8,9},{10,11},{9,8... | collective-permute-start | bytes 786440 | tf_op jit(solution)/shard_map/ppermute | solution.py:441
  131.3 0.7 collective-permute-start.28
  132.0 0.7 filter_lanes.4.refs_1_
  132.7 3.6 %collective-permute-done.27.refs_2_.refs_4_ = bf16[1024,128]{1,0:T(8,128)(2,1)S(1)} collective-permute-done((bf16[1024,128]{1,0:T(8,128)(2,1)S(1)}, bf16[1024,128]{1,0:T(8,128)(2,1)S(1)}, u32[]{:S(2)}, u32[]{:S(2)}) %collective-permute-start.27) | collective-permute-done | bytes 262176 | tf_op jit(solution)/shard_map/ppermute | solution.py:441
  136.3 0.5 gradient_energy.1
  136.8 18.8 %all_to_all.5.refs_1_ = f32[32,1,128]{2,1,0:T(1,128)S(1)} all-to-all(f32[32,1,128]{2,1,0:T(1,128)S(1)} %get-tuple-element.60), channel_id=1, replica_groups=mesh['gx'=2,'gy'=4,'gz'=4] {'gx','gy','gz'}, dimensions={0} | all-to-all | bytes 32768 | tf_op jit(solution)/shard_map/all_to_all | solution.py:453
  155.7 1.7 %final_maps.1 = f32[8,512,64]{2,1,0:T(8,128)} custom-call(s32[1]{0:T(128)} %bitcast.refs_1_.refs_0_, f32[32,1,128]{2,1,0:T(1,128)S(1)} %all_to_all.5.refs_1_, f32[8,512,64]{2,1,0:T(8,128)S(1)} %faded_maps.1.refs_4_.refs_2_, f32[512,512]{1,0:T(8,128)S(1)} %filter_lanes.5.refs_8_.refs_3_, bf16[1024,128]{1,0:T(8,128)(2,1)S(1)} %collective-permute-done.27.refs_2_.refs_4_, ...), custom_call_target="tpu_custom_call" | custom-call | flops 100000000 | bytes 3948544 | tf_op jit(solution)/shard_map/final_maps/pallas_call | solution.py:58
  (54 shorter events, 5.3 us)
Async XLA Ops:
  0.6 1.6 %copy-start.2 = (f32[64,8,16,32]{0,3,2,1:T(8,128)S(1)}, f32[64,8,16,32]{0,3,2,1:T(8,128)}, u32[]{:S(2)}) copy-start(f32[64,8,16,32]{0,3,2,1:T(8,128)} %param.9) | copy-start | bytes 3145732
  2.7 15.0 %collective-permute-start = (bf16[512,512]{1,0:T(8,128)(2,1)S(1)}, bf16[512,512]{1,0:T(8,128)(2,1)S(1)}, u32[]{:S(2)}, u32[]{:S(2)}) collective-permute-start(bf16[512,512]{1,0:T(8,128)(2,1)S(1)} %pack_maps.1.refs_1_), channel_id=1, source_target_pairs={{0,16},{16,0},{1,17},{17,1},{2,18},{18,2},{3,19},{19,3},{4,20},{20... | collective-permute-start | bytes 1572872 | tf_op jit(solution)/shard_map/ppermute | solution.py:512
  18.1 5.2 %copy-start.4 = (bf16[1024,256]{1,0:T(8,128)(2,1)S(1)}, bf16[1024,256]{1,0:T(8,128)(2,1)}, u32[]{:S(2)}) copy-start(bf16[1024,256]{1,0:T(8,128)(2,1)} %constant.40.clone.refs_5_) | copy-start | bytes 1572868
  18.1 8.6 %copy-start.1 = (bf16[1024,512]{1,0:T(8,128)(2,1)S(1)}, bf16[1024,512]{1,0:T(8,128)(2,1)}, u32[]{:S(2)}) copy-start(bf16[1024,512]{1,0:T(8,128)(2,1)} %constant.41.clone.refs_4_) | copy-start | bytes 3145732
  18.2 3.9 %collective-permute-start.2 = (bf16[512,256]{1,0:T(8,128)(2,1)S(1)}, bf16[512,256]{1,0:T(8,128)(2,1)S(1)}, u32[]{:S(2)}, u32[]{:S(2)}) collective-permute-start(bf16[512,256]{1,0:T(8,128)(2,1)S(1)} %cut_face.3), channel_id=1, source_target_pairs={{4,8},{8,4},{5,9},{9,5},{6,10},{10,6},{7,11},{11,7},{20,24},{24,20... | collective-permute-start | bytes 786440 | tf_op jit(solution)/shard_map/ppermute | solution.py:441
  19.0 4.3 %collective-permute-start.1 = (bf16[512,256]{1,0:T(8,128)(2,1)S(1)}, bf16[512,256]{1,0:T(8,128)(2,1)S(1)}, u32[]{:S(2)}, u32[]{:S(2)}) collective-permute-start(bf16[512,256]{1,0:T(8,128)(2,1)S(1)} %get-tuple-element.32), channel_id=1, source_target_pairs={{0,4},{8,12},{4,0},{12,8},{1,5},{9,13},{5,1},{13,9},{2,6},{10,14},... | collective-permute-start | bytes 786440 | tf_op jit(solution)/shard_map/ppermute | solution.py:441
  23.3 5.5 %copy-start = (bf16[8,16,32,512]{3,2,1,0:T(8,128)(2,1)S(1)}, bf16[8,16,32,512]{3,2,1,0:T(8,128)(2,1)}, u32[]{:S(2)}) copy-start(bf16[8,16,32,512]{3,2,1,0:T(8,128)(2,1)} %param.8) | copy-start | bytes 12582916
  23.3 5.5 %copy-start.6 = (bf16[256,512]{1,0:T(8,128)(2,1)S(1)}, bf16[256,512]{1,0:T(8,128)(2,1)}, u32[]{:S(2)}) copy-start(bf16[256,512]{1,0:T(8,128)(2,1)} %constant.42.clone.refs_5_.refs_4_.refs_6_) | copy-start | bytes 786436
  23.7 5.0 %collective-permute-start.3 = (bf16[512,128]{1,0:T(8,128)(2,1)S(1)}, bf16[512,128]{1,0:T(8,128)(2,1)S(1)}, u32[]{:S(2)}, u32[]{:S(2)}) collective-permute-start(bf16[512,128]{1,0:T(8,128)(2,1)S(1)} %get-tuple-element.34), channel_id=1, source_target_pairs={{0,1},{2,3},{1,0},{3,2},{4,5},{6,7},{5,4},{7,6},{8,9},{10,11},{9,8... | collective-permute-start | bytes 393224 | tf_op jit(solution)/shard_map/ppermute | solution.py:441
  25.4 3.4 %collective-permute-start.4 = (bf16[512,128]{1,0:T(8,128)(2,1)S(1)}, bf16[512,128]{1,0:T(8,128)(2,1)S(1)}, u32[]{:S(2)}, u32[]{:S(2)}) collective-permute-start(bf16[512,128]{1,0:T(8,128)(2,1)S(1)} %get-tuple-element.35), channel_id=1, source_target_pairs={{1,2},{2,1},{5,6},{6,5},{9,10},{10,9},{13,14},{14,13},{17,18},{18,... | collective-permute-start | bytes 393224 | tf_op jit(solution)/shard_map/ppermute | solution.py:441
  28.8 42.9 %slice-start = ((s8[6291456]{0:T(1024)(128)(4,1)}), s8[4194304]{0:T(1024)(128)(4,1)S(1)}, s32[]{:S(2)}) async-start(s8[6291456]{0:T(1024)(128)(4,1)} %bitcast.23), calls=%async_computation.1 | async-start | bytes 8388608
  30.6 4.3 %collective-permute-start.5 = (bf16[64,512]{1,0:T(8,128)(2,1)S(1)}, bf16[64,512]{1,0:T(8,128)(2,1)S(1)}, u32[]{:S(2)}, u32[]{:S(2)}) collective-permute-start(bf16[64,512]{1,0:T(8,128)(2,1)S(1)} %reduce-precision_convert_fusion.1), channel_id=1, source_target_pairs={{0,16},{16,0},{1,17},{17,1},{2,18},{18,2},{3,19},{19,3},{4,20},{20... | collective-permute-start | bytes 196616 | tf_op jit(solution)/shard_map/ppermute | solution.py:472
  34.9 1.5 collective-permute-start.6
  36.5 6.8 %collective-permute-start.7 = (bf16[64,512]{1,0:T(8,128)(2,1)S(1)}, bf16[64,512]{1,0:T(8,128)(2,1)S(1)}, u32[]{:S(2)}, u32[]{:S(2)}) collective-permute-start(bf16[64,512]{1,0:T(8,128)(2,1)S(1)} %fusion), channel_id=1, source_target_pairs={{0,8},{4,12},{8,0},{12,4},{1,9},{5,13},{9,1},{13,5},{2,10},{6,14},... | collective-permute-start | bytes 196616 | tf_op jit(solution)/shard_map/ppermute | solution.py:472
  43.3 6.7 %collective-permute-start.10 = (bf16[64,512]{1,0:T(8,128)(2,1)S(1)}, bf16[64,512]{1,0:T(8,128)(2,1)S(1)}, u32[]{:S(2)}, u32[]{:S(2)}) collective-permute-start(bf16[64,512]{1,0:T(8,128)(2,1)S(1)} %fusion.2), channel_id=1, source_target_pairs={{0,3},{1,2},{2,1},{3,0},{4,7},{5,6},{6,5},{7,4},{8,11},{9,10},{10,... | collective-permute-start | bytes 196616 | tf_op jit(solution)/shard_map/ppermute | solution.py:472
  47.0 6.5 %collective-permute-start.9 = (bf16[64,512]{1,0:T(8,128)(2,1)S(1)}, bf16[64,512]{1,0:T(8,128)(2,1)S(1)}, u32[]{:S(2)}, u32[]{:S(2)}) collective-permute-start(bf16[64,512]{1,0:T(8,128)(2,1)S(1)} %fusion.2), channel_id=1, source_target_pairs={{0,2},{1,3},{2,0},{3,1},{4,6},{5,7},{6,4},{7,5},{8,10},{9,11},{10,... | collective-permute-start | bytes 196616 | tf_op jit(solution)/shard_map/ppermute | solution.py:472
  49.5 4.6 %collective-permute-start.8 = (bf16[64,512]{1,0:T(8,128)(2,1)S(1)}, bf16[64,512]{1,0:T(8,128)(2,1)S(1)}, u32[]{:S(2)}, u32[]{:S(2)}) collective-permute-start(bf16[64,512]{1,0:T(8,128)(2,1)S(1)} %fusion.2), channel_id=1, source_target_pairs={{0,1},{1,0},{2,3},{3,2},{4,5},{5,4},{6,7},{7,6},{8,9},{9,8},{10,11... | collective-permute-start | bytes 196616 | tf_op jit(solution)/shard_map/ppermute | solution.py:472
  54.1 17.5 %slice-start.1 = ((s8[6291456]{0:T(1024)(128)(4,1)}), s8[2097152]{0:T(1024)(128)(4,1)S(1)}, s32[]{:S(2)}) async-start(s8[6291456]{0:T(1024)(128)(4,1)} %bitcast.23), calls=%async_computation.2 | async-start | bytes 4194304
  54.2 17.5 %copy-start.5 = (bf16[4,1024,512]{2,1,0:T(8,128)(2,1)S(1)}, bf16[4,1024,512]{2,1,0:T(8,128)(2,1)}, u32[]{:S(2)}) copy-start(bf16[4,1024,512]{2,1,0:T(8,128)(2,1)} %constant.44.clone.refs_3_) | copy-start | bytes 12582916
  55.6 12.5 %collective-permute-start.11 = (bf16[512,512]{1,0:T(8,128)(2,1)S(1)}, bf16[512,512]{1,0:T(8,128)(2,1)S(1)}, u32[]{:S(2)}, u32[]{:S(2)}) collective-permute-start(bf16[512,512]{1,0:T(8,128)(2,1)S(1)} %get-tuple-element.36.refs_1_), channel_id=1, source_target_pairs={{0,16},{16,0},{1,17},{17,1},{2,18},{18,2},{3,19},{19,3},{4,20},{20... | collective-permute-start | bytes 1572872 | tf_op jit(solution)/shard_map/ppermute | solution.py:512
  69.1 2.8 %collective-permute-start.13 = (bf16[512,512]{1,0:T(8,128)(2,1)S(1)}, bf16[512,512]{1,0:T(8,128)(2,1)S(1)}, u32[]{:S(2)}, u32[]{:S(2)}) collective-permute-start(bf16[512,512]{1,0:T(8,128)(2,1)S(1)} %get-tuple-element.41.refs_3_), channel_id=1, source_target_pairs={{4,8},{8,4},{5,9},{9,5},{6,10},{10,6},{7,11},{11,7},{20,24},{24,20... | collective-permute-start | bytes 1572872 | tf_op jit(solution)/shard_map/ppermute | solution.py:441
  69.8 3.4 %collective-permute-start.12 = (bf16[512,512]{1,0:T(8,128)(2,1)S(1)}, bf16[512,512]{1,0:T(8,128)(2,1)S(1)}, u32[]{:S(2)}, u32[]{:S(2)}) collective-permute-start(bf16[512,512]{1,0:T(8,128)(2,1)S(1)} %get-tuple-element.41.refs_3_), channel_id=1, source_target_pairs={{0,4},{8,12},{4,0},{12,8},{1,5},{9,13},{5,1},{13,9},{2,6},{10,14},... | collective-permute-start | bytes 1572872 | tf_op jit(solution)/shard_map/ppermute | solution.py:441
  74.2 6.4 %collective-permute-start.14 = (bf16[512,256]{1,0:T(8,128)(2,1)S(1)}, bf16[512,256]{1,0:T(8,128)(2,1)S(1)}, u32[]{:S(2)}, u32[]{:S(2)}) collective-permute-start(bf16[512,256]{1,0:T(8,128)(2,1)S(1)} %get-tuple-element.43.refs_1_), channel_id=1, source_target_pairs={{0,1},{2,3},{1,0},{3,2},{4,5},{6,7},{5,4},{7,6},{8,9},{10,11},{9,8... | collective-permute-start | bytes 786440 | tf_op jit(solution)/shard_map/ppermute | solution.py:441
  76.3 4.4 %collective-permute-start.15 = (bf16[512,256]{1,0:T(8,128)(2,1)S(1)}, bf16[512,256]{1,0:T(8,128)(2,1)S(1)}, u32[]{:S(2)}, u32[]{:S(2)}) collective-permute-start(bf16[512,256]{1,0:T(8,128)(2,1)S(1)} %get-tuple-element.44.refs_2_), channel_id=1, source_target_pairs={{1,2},{2,1},{5,6},{6,5},{9,10},{10,9},{13,14},{14,13},{17,18},{18,... | collective-permute-start | bytes 786440 | tf_op jit(solution)/shard_map/ppermute | solution.py:441
  82.8 4.3 %collective-permute-start.16 = (bf16[64,512]{1,0:T(8,128)(2,1)S(1)}, bf16[64,512]{1,0:T(8,128)(2,1)S(1)}, u32[]{:S(2)}, u32[]{:S(2)}) collective-permute-start(bf16[64,512]{1,0:T(8,128)(2,1)S(1)} %reduce-precision_convert_fusion), channel_id=1, source_target_pairs={{0,16},{16,0},{1,17},{17,1},{2,18},{18,2},{3,19},{19,3},{4,20},{20... | collective-permute-start | bytes 196616 | tf_op jit(solution)/shard_map/ppermute | solution.py:472
  87.1 4.5 %collective-permute-start.17 = (bf16[64,512]{1,0:T(8,128)(2,1)S(1)}, bf16[64,512]{1,0:T(8,128)(2,1)S(1)}, u32[]{:S(2)}, u32[]{:S(2)}) collective-permute-start(bf16[64,512]{1,0:T(8,128)(2,1)S(1)} %fusion.5), channel_id=1, source_target_pairs={{0,4},{4,0},{8,12},{12,8},{1,5},{5,1},{9,13},{13,9},{2,6},{6,2},{1... | collective-permute-start | bytes 196616 | tf_op jit(solution)/shard_map/ppermute | solution.py:472
  91.6 6.2 %collective-permute-start.18 = (bf16[64,512]{1,0:T(8,128)(2,1)S(1)}, bf16[64,512]{1,0:T(8,128)(2,1)S(1)}, u32[]{:S(2)}, u32[]{:S(2)}) collective-permute-start(bf16[64,512]{1,0:T(8,128)(2,1)S(1)} %fusion.1), channel_id=1, source_target_pairs={{0,8},{4,12},{8,0},{12,4},{1,9},{5,13},{9,1},{13,5},{2,10},{6,14},... | collective-permute-start | bytes 196616 | tf_op jit(solution)/shard_map/ppermute | solution.py:472
  97.9 8.0 %collective-permute-start.21 = (bf16[64,512]{1,0:T(8,128)(2,1)S(1)}, bf16[64,512]{1,0:T(8,128)(2,1)S(1)}, u32[]{:S(2)}, u32[]{:S(2)}) collective-permute-start(bf16[64,512]{1,0:T(8,128)(2,1)S(1)} %fusion.3), channel_id=1, source_target_pairs={{0,3},{1,2},{2,1},{3,0},{4,7},{5,6},{6,5},{7,4},{8,11},{9,10},{10,... | collective-permute-start | bytes 196616 | tf_op jit(solution)/shard_map/ppermute | solution.py:472
  102.9 6.6 %collective-permute-start.20 = (bf16[64,512]{1,0:T(8,128)(2,1)S(1)}, bf16[64,512]{1,0:T(8,128)(2,1)S(1)}, u32[]{:S(2)}, u32[]{:S(2)}) collective-permute-start(bf16[64,512]{1,0:T(8,128)(2,1)S(1)} %fusion.3), channel_id=1, source_target_pairs={{0,2},{1,3},{2,0},{3,1},{4,6},{5,7},{6,4},{7,5},{8,10},{9,11},{10,... | collective-permute-start | bytes 196616 | tf_op jit(solution)/shard_map/ppermute | solution.py:472
  105.4 4.6 %collective-permute-start.19 = (bf16[64,512]{1,0:T(8,128)(2,1)S(1)}, bf16[64,512]{1,0:T(8,128)(2,1)S(1)}, u32[]{:S(2)}, u32[]{:S(2)}) collective-permute-start(bf16[64,512]{1,0:T(8,128)(2,1)S(1)} %fusion.3), channel_id=1, source_target_pairs={{0,1},{1,0},{2,3},{3,2},{4,5},{5,4},{6,7},{7,6},{8,9},{9,8},{10,11... | collective-permute-start | bytes 196616 | tf_op jit(solution)/shard_map/ppermute | solution.py:472
  112.0 12.5 %collective-permute-start.22 = (bf16[512,512]{1,0:T(8,128)(2,1)S(1)}, bf16[512,512]{1,0:T(8,128)(2,1)S(1)}, u32[]{:S(2)}, u32[]{:S(2)}) collective-permute-start(bf16[512,512]{1,0:T(8,128)(2,1)S(1)} %get-tuple-element.46.refs_1_), channel_id=1, source_target_pairs={{0,16},{16,0},{1,17},{17,1},{2,18},{18,2},{3,19},{19,3},{4,20},{20... | collective-permute-start | bytes 1572872 | tf_op jit(solution)/shard_map/ppermute | solution.py:512
  113.5 0.8 copy-start.7
  115.6 4.3 %copy-start.3 = (f32[64,8,16,32]{0,3,2,1:T(8,128)S(1)}, f32[64,8,16,32]{0,3,2,1:T(8,128)}, u32[]{:S(2)}) copy-start(f32[64,8,16,32]{0,3,2,1:T(8,128)} %param.9) | copy-start | bytes 3145732
  115.7 11.8 %collective-permute-start.26 = (bf16[512,256]{1,0:T(8,128)(2,1)S(1)}, bf16[512,256]{1,0:T(8,128)(2,1)S(1)}, u32[]{:S(2)}, u32[]{:S(2)}) collective-permute-start(bf16[512,256]{1,0:T(8,128)(2,1)S(1)} %cut_face.5), channel_id=1, source_target_pairs={{4,8},{8,4},{5,9},{9,5},{6,10},{10,6},{7,11},{11,7},{20,24},{24,20... | collective-permute-start | bytes 786440 | tf_op jit(solution)/shard_map/ppermute | solution.py:441
  116.5 11.0 %collective-permute-start.25 = (bf16[512,256]{1,0:T(8,128)(2,1)S(1)}, bf16[512,256]{1,0:T(8,128)(2,1)S(1)}, u32[]{:S(2)}, u32[]{:S(2)}) collective-permute-start(bf16[512,256]{1,0:T(8,128)(2,1)S(1)} %get-tuple-element.54), channel_id=1, source_target_pairs={{0,4},{8,12},{4,0},{12,8},{1,5},{9,13},{5,1},{13,9},{2,6},{10,14},... | collective-permute-start | bytes 786440 | tf_op jit(solution)/shard_map/ppermute | solution.py:441
  124.9 3.8 %collective-permute-start.24 = (bf16[512,256]{1,0:T(8,128)(2,1)S(1)}, bf16[512,256]{1,0:T(8,128)(2,1)S(1)}, u32[]{:S(2)}, u32[]{:S(2)}) collective-permute-start(bf16[512,256]{1,0:T(8,128)(2,1)S(1)} %cut_face.4), channel_id=1, source_target_pairs={{4,8},{8,4},{5,9},{9,5},{6,10},{10,6},{7,11},{11,7},{20,24},{24,20... | collective-permute-start | bytes 786440 | tf_op jit(solution)/shard_map/ppermute | solution.py:441
  125.6 3.1 %collective-permute-start.23 = (bf16[512,256]{1,0:T(8,128)(2,1)S(1)}, bf16[512,256]{1,0:T(8,128)(2,1)S(1)}, u32[]{:S(2)}, u32[]{:S(2)}) collective-permute-start(bf16[512,256]{1,0:T(8,128)(2,1)S(1)} %get-tuple-element.52), channel_id=1, source_target_pairs={{0,4},{8,12},{4,0},{12,8},{1,5},{9,13},{5,1},{13,9},{2,6},{10,14},... | collective-permute-start | bytes 786440 | tf_op jit(solution)/shard_map/ppermute | solution.py:441
  129.2 7.1 %collective-permute-start.27 = (bf16[1024,128]{1,0:T(8,128)(2,1)S(1)}, bf16[1024,128]{1,0:T(8,128)(2,1)S(1)}, u32[]{:S(2)}, u32[]{:S(2)}) collective-permute-start(bf16[1024,128]{1,0:T(8,128)(2,1)S(1)} %get-tuple-element.58), channel_id=1, source_target_pairs={{0,1},{2,3},{1,0},{3,2},{4,5},{6,7},{5,4},{7,6},{8,9},{10,11},{9,8... | collective-permute-start | bytes 786440 | tf_op jit(solution)/shard_map/ppermute | solution.py:441
  131.3 5.0 %collective-permute-start.28 = (bf16[1024,128]{1,0:T(8,128)(2,1)S(1)}, bf16[1024,128]{1,0:T(8,128)(2,1)S(1)}, u32[]{:S(2)}, u32[]{:S(2)}) collective-permute-start(bf16[1024,128]{1,0:T(8,128)(2,1)S(1)} %get-tuple-element.59), channel_id=1, source_target_pairs={{1,2},{2,1},{5,6},{6,5},{9,10},{10,9},{13,14},{14,13},{17,18},{18,... | collective-permute-start | bytes 786440 | tf_op jit(solution)/shard_map/ppermute | solution.py:441

commit v8 on v7

--- a/solution.py
+++ b/solution.py
@@ -261,7 +261,7 @@
     plane = size_y * size_z
     layers = bold.shape[0] // plane
 
-    def body(info_ref, start, first_ref, second_ref, weights, frames_ref, out):
+    def body(info_ref, start, first_ref, second_ref, weights, frames_ref, mine, other):
         total = jnp.zeros((chans, frames), F32)
         for x in range(layers):
             rows = slice(x * chans, (x + 1) * chans)
@@ -269,11 +269,27 @@
             keep = live_lanes(info_ref, x, value.shape, size_y, size_z)
             value = jnp.where(keep, value, 0.0).astype(BF16)
             total = total + dot(value, frames_ref[x * plane : (x + 1) * plane, :])
-        out[...] = total
+        part = chans // 2
+
+        @pl.when(info_ref[ODD_Y] == 0)
+        def _():
+            mine[...] = total[:part]
+            other[...] = total[part:].astype(BF16)
+
+        @pl.when(info_ref[ODD_Y] != 0)
+        def _():
+            mine[...] = total[part:]
+            other[...] = total[:part].astype(BF16)
 
     arrays = [acc, first, second, table, bold]
-    shapes = shape((chans, frames), F32)
-    return call(body, shapes, info, [COUNT, ODD_Z], arrays, flops=10**9, name="courses_of")
+    shapes = (shape((chans // 2, frames), F32), shape((chans // 2, frames), BF16))
+    return call(body, shapes, info, [COUNT, ODD_Y, ODD_Z], arrays, flops=10**9, name="courses_of")
+
+
+def whole_courses(info_ref, mine, other):
+    even = info_ref[ODD_Y] == 0
+    mine, other = mine[...].astype(F32), other[...].astype(F32)
+    return jnp.concatenate([jnp.where(even, mine, other), jnp.where(even, other, mine)], axis=0)
 
 
 def write_gradient(info_ref, courses, frames_ref, out, chans, size_y, size_z):
@@ -284,16 +300,16 @@
         out[x * chans : (x + 1) * chans, :] = jnp.where(keep, value, 0.0).astype(BF16)
 
 
-def first_gradient(info, sums, bold, chans, size_y, size_z):
+def first_gradient(info, halves, bold, chans, size_y, size_z):
     cells, frames = bold.shape
 
-    def body(info_ref, sums_ref, frames_ref, out, half_ref):
-        courses = sums_ref[...].astype(BF16)
+    def body(info_ref, mine, other, frames_ref, out, half_ref):
+        courses = whole_courses(info_ref, mine, other).astype(BF16)
         half_ref[...] = courses
         write_gradient(info_ref, courses, frames_ref, out, chans, size_y, size_z)
 
     shapes = (shape((cells * chans // (size_y * size_z), size_y * size_z), BF16), shape((chans, frames), BF16))
-    return call(body, shapes, info, [COUNT], [sums, bold], flops=10**9, name="first_gradient")
+    return call(body, shapes, info, [COUNT, ODD_Y], [*halves, bold], flops=10**9, name="first_gradient")
 
 
 def fade_of(courses):
@@ -315,11 +331,11 @@
     return call(body, shapes, info, [], [half1], name="first_fade")
 
 
-def second_gradient(info, change, half1, kept, bold, chans, size_y, size_z, all_cells):
+def second_gradient(info, halves, half1, kept, bold, chans, size_y, size_z, all_cells):
     cells, frames = bold.shape
 
-    def body(info_ref, change_ref, half1_ref, kept_ref, frames_ref, out, half_ref, scale_ref):
-        change = change_ref[...]
+    def body(info_ref, mine, other, half1_ref, kept_ref, frames_ref, out, half_ref, scale_ref):
+        change = whole_courses(info_ref, mine, other)
         energy = jnp.maximum(total_of(half1_ref[...].astype(F32) * change), 0.0) * (1.0 / all_cells)
         scale = 0.5 * lax.rsqrt(energy + 1e-06)
         scale_ref[...] = scale
@@ -332,8 +348,8 @@
         shape((chans, frames), BF16),
         shape((1, 1), F32),
     )
-    arrays = [change, half1, kept, bold]
-    return call(body, shapes, info, [COUNT], arrays, flops=10**9, name="second_gradient")
+    arrays = [*halves, half1, kept, bold]
+    return call(body, shapes, info, [COUNT, ODD_Y], arrays, flops=10**9, name="second_gradient")
 
 
 def second_fade(info, half2, fade1, scale1, field, face):
@@ -453,27 +469,24 @@
     return lax.all_to_all(parts, AXES, 0, 0, tiled=True)
 
 
-def hypercube_sum(value):
-    rounds = []
-    for axis in AXES:
-        peers = lax.axis_size(axis)
-        if peers & (peers - 1):
-            return lax.psum(value, AXES)
-        if axis == "gz" and peers == 4:
-            rounds.append((axis, (1, 2, 3)))
-        else:
-            rounds += [(axis, (1 << b,)) for b in range(peers.bit_length() - 1)]
-    for axis, masks in rounds:
-        value = lax.reduce_precision(value, 8, 7)
-        sent = value.astype(BF16)
-        got = []
-        for mask in masks:
-            pairs = [(i, i ^ mask) for i in range(lax.axis_size(axis))]
-            got.append(lax.ppermute(sent, axis, pairs).astype(F32))
-        value = value + got[0]
-        if len(got) == 3:
-            value = value + (got[1] + got[2])
-    return value
+def hypercube_sum(mine, other):
+    sizes = [lax.axis_size(axis) for axis in AXES]
+    if any(size & (size - 1) for size in sizes) or sizes[1] < 2:
+        odd = lax.axis_index("gy") % 2
+        place = jnp.arange(2)[:, None, None] == odd
+        sums = lax.psum(jnp.where(place, mine[None], other[None].astype(F32)), AXES).astype(BF16)
+        return sums[odd], sums[1 - odd]
+
+    def across(value, axis, bit):
+        return lax.ppermute(value, axis, [(i, i ^ bit) for i in range(lax.axis_size(axis))])
+
+    value = lax.reduce_precision(mine, 8, 7) + across(other, "gy", 1).astype(F32)
+    for axis, size in zip(AXES, sizes):
+        for step in range(axis == "gy", size.bit_length() - 1):
+            value = lax.reduce_precision(value, 8, 7)
+            value = value + across(value.astype(BF16), axis, 1 << step).astype(F32)
+    mine = value.astype(BF16)
+    return mine, across(mine, "gy", 1)
 
 
 def per_device(bold_data, spatial_maps, live_blocks):
@@ -532,7 +545,7 @@
         return filter_lanes(info, first, field, second, table_own), *ends
 
     def all_courses(acc, first, second, table):
-        return hypercube_sum(courses_of(info, acc, first, second, table, bold, chans, size_y, size_z))
+        return hypercube_sum(*courses_of(info, acc, first, second, table, bold, chans, size_y, size_z))
 
     plain = pack_maps(info, voxel_maps)
     acc, first, second = along_rest(*along_x(plain, [full_x]))

time: 158 us -> 162 us (1.025)
  starting transfers between devices: 56.9 us -> 60.3 us
  waiting for transfers between devices: 54.6 us -> 58 us
  blocking collectives: 18.8 us -> 16.1 us
    ppermute x3, waiting for transfers between devices: 23.6 us -> 26.5 us  [along_x(): got = lax.ppermute(block, 'gx', [(0, 1), (1, 0)])]
    all_to_all x1, blocking collectives: 18.8 us -> 16.1 us  [exchanged(): return lax.all_to_all(parts, AXES, 0, 0, tiled=True)]
    ppermute x14, starting transfers between devices: 20.7 us -> 23.2 us  [swapped(): got[start] = lax.ppermute((first, second)[start], axis, pairs)]
  transfers between devices with their start and end apart: 29 -> 29, of which waited for: 18 -> 20; matrix products, arithmetic and copies ran while one was open for 0% -> 0% of each run, Pallas kernels for 6% -> 6%
where the time goes in v8:
time: 162 us; the launch traced here: 161 us
  starting transfers between devices  60.3 us (37%)
  waiting for transfers between devices  58 us (36%)
  Pallas kernels  22.5 us (14%)
  blocking collectives  16.1 us (10%)
  local copies, waits for them, and re-layouts  2.47 us (2%)
  between operations  1.83 us (1%)
    ppermute x12, starting transfers between devices, across(): lax.ppermute(value, axis, [(i, i ^ bit) for i in range(lax.axis_size(axis...  31 us
    ppermute x3, waiting for transfers between devices, along_x(): got = lax.ppermute(block, 'gx', [(0, 1), (1, 0)])  26.5 us
    ppermute x14, starting transfers between devices, swapped(): got[start] = lax.ppermute((first, second)[start], axis, pairs)  23.2 us
    pallas_call x28, Pallas kernels, call(): pl.pallas_call(wrapped, out_shape=shapes, in_specs=[pl.BlockSpec(memory_s...  22.5 us
    ppermute x12, waiting for transfers between devices, across(): lax.ppermute(value, axis, [(i, i ^ bit) for i in range(lax.axis_size(axis...  20.3 us
    all_to_all x1, blocking collectives, exchanged(): return lax.all_to_all(parts, AXES, 0, 0, tiled=True)  16.1 us
    ppermute x14, waiting for transfers between devices, swapped(): got[start] = lax.ppermute((first, second)[start], axis, pairs)  11.3 us
    ppermute x3, starting transfers between devices, along_x(): got = lax.ppermute(block, 'gx', [(0, 1), (1, 0)])  6.1 us
  transfers between devices with their start and end apart: 29, of which 20 were waited for; matrix products, arithmetic and copies ran while one was open for 0% of the time, Pallas kernels for 6%

profile of v8, /device:TPU:0, one launch (start us, length us, event | category | flops | bytes accessed | tf_op | source)
XLA Modules:
  0.0 161.5 jit_solution(5459794769486373182)
XLA Ops:
  0.6 1.6 copy-done.2
  2.7 3.0 %collective-permute-start = (bf16[512,512]{1,0:T(8,128)(2,1)S(1)}, bf16[512,512]{1,0:T(8,128)(2,1)S(1)}, u32[]{:S(2)}, u32[]{:S(2)}) collective-permute-start(bf16[512,512]{1,0:T(8,128)(2,1)S(1)} %pack_maps.1.refs_1_), channel_id=1, source_target_pairs={{0,16},{16,0},{1,17},{17,1},{2,18},{18,2},{3,19},{19,3},{4,20},{20... | collective-permute-start | bytes 1572872 | tf_op jit(solution)/shard_map/ppermute | solution.py:525
  6.3 11.4 %collective-permute-done.refs_2_ = bf16[512,512]{1,0:T(8,128)(2,1)S(1)} collective-permute-done((bf16[512,512]{1,0:T(8,128)(2,1)S(1)}, bf16[512,512]{1,0:T(8,128)(2,1)S(1)}, u32[]{:S(2)}, u32[]{:S(2)}) %collective-permute-start) | collective-permute-done | bytes 524320 | tf_op jit(solution)/shard_map/ppermute | solution.py:525
  18.2 0.8 collective-permute-start.2
  19.0 3.1 %collective-permute-start.1 = (bf16[512,256]{1,0:T(8,128)(2,1)S(1)}, bf16[512,256]{1,0:T(8,128)(2,1)S(1)}, u32[]{:S(2)}, u32[]{:S(2)}) collective-permute-start(bf16[512,256]{1,0:T(8,128)(2,1)S(1)} %get-tuple-element.36), channel_id=1, source_target_pairs={{0,4},{8,12},{4,0},{12,8},{1,5},{9,13},{5,1},{13,9},{2,6},{10,14},... | collective-permute-start | bytes 786440 | tf_op jit(solution)/shard_map/ppermute | solution.py:457
  22.1 1.2 collective-permute-done.1.refs_1_.refs_2_
  23.7 1.6 %collective-permute-start.3 = (bf16[512,128]{1,0:T(8,128)(2,1)S(1)}, bf16[512,128]{1,0:T(8,128)(2,1)S(1)}, u32[]{:S(2)}, u32[]{:S(2)}) collective-permute-start(bf16[512,128]{1,0:T(8,128)(2,1)S(1)} %get-tuple-element.38), channel_id=1, source_target_pairs={{0,1},{2,3},{1,0},{3,2},{4,5},{6,7},{5,4},{7,6},{8,9},{10,11},{9,8... | collective-permute-start | bytes 393224 | tf_op jit(solution)/shard_map/ppermute | solution.py:457
  25.4 0.7 collective-permute-start.4
  26.7 0.7 filter_lanes.3.refs_3_
  27.4 1.4 collective-permute-done.3.refs_4_
  28.8 1.8 %courses_of.2 = (f32[32,512]{1,0:T(8,128)S(1)}, bf16[32,512]{1,0:T(8,128)(2,1)S(1)}) custom-call(s32[1]{0:T(128)} %bitcast.13.refs_0_, s32[1]{0:T(128)} %bitcast.1.refs_1_.refs_0_, s32[1]{0:T(128)} %bitcast.refs_1_.refs_2_.refs_0_, f32[512,512]{1,0:T(8,128)S(1)} %filter_lanes.3.refs_3_, bf16[512,128]{1,0:T(8,128)(2,1)S(1)} %collective-permute-done.3.refs_4_, ...), custom_call_target="tpu_custom_call" | custom-call | flops 1000000000 | bytes 5767168 | tf_op jit(solution)/shard_map/courses_of/pallas_call | solution.py:58
  30.6 1.7 %collective-permute-start.5 = (bf16[32,512]{1,0:T(8,128)(2,1)S(1)}, bf16[32,512]{1,0:T(8,128)(2,1)S(1)}, u32[]{:S(2)}, u32[]{:S(2)}) collective-permute-start(bf16[32,512]{1,0:T(8,128)(2,1)S(1)} %get-tuple-element.41), channel_id=1, source_target_pairs={{0,4},{4,0},{8,12},{12,8},{1,5},{5,1},{9,13},{13,9},{2,6},{6,2},{1... | collective-permute-start | bytes 98312 | tf_op jit(solution)/shard_map/ppermute | solution.py:481
  32.3 0.9 collective-permute-done.5
  33.2 1.6 collective-permute-start.6
  34.8 2.4 %collective-permute-done.6 = bf16[32,512]{1,0:T(8,128)(2,1)S(1)} collective-permute-done((bf16[32,512]{1,0:T(8,128)(2,1)S(1)}, bf16[32,512]{1,0:T(8,128)(2,1)S(1)}, u32[]{:S(2)}, u32[]{:S(2)}) %collective-permute-start.6) | collective-permute-done | bytes 32800 | tf_op jit(solution)/shard_map/ppermute | solution.py:481
  37.2 3.2 %collective-permute-start.7 = (bf16[32,512]{1,0:T(8,128)(2,1)S(1)}, bf16[32,512]{1,0:T(8,128)(2,1)S(1)}, u32[]{:S(2)}, u32[]{:S(2)}) collective-permute-start(bf16[32,512]{1,0:T(8,128)(2,1)S(1)} %fusion), channel_id=1, source_target_pairs={{0,8},{4,12},{8,0},{12,4},{1,9},{5,13},{9,1},{13,5},{2,10},{6,14},... | collective-permute-start | bytes 98312 | tf_op jit(solution)/shard_map/ppermute | solution.py:481
  40.4 1.9 %collective-permute-done.7 = bf16[32,512]{1,0:T(8,128)(2,1)S(1)} collective-permute-done((bf16[32,512]{1,0:T(8,128)(2,1)S(1)}, bf16[32,512]{1,0:T(8,128)(2,1)S(1)}, u32[]{:S(2)}, u32[]{:S(2)}) %collective-permute-start.7) | collective-permute-done | bytes 32800 | tf_op jit(solution)/shard_map/ppermute | solution.py:481
  42.3 4.6 %collective-permute-start.8 = (bf16[32,512]{1,0:T(8,128)(2,1)S(1)}, bf16[32,512]{1,0:T(8,128)(2,1)S(1)}, u32[]{:S(2)}, u32[]{:S(2)}) collective-permute-start(bf16[32,512]{1,0:T(8,128)(2,1)S(1)} %get-tuple-element.72), channel_id=1, source_target_pairs={{0,1},{1,0},{2,3},{3,2},{4,5},{5,4},{6,7},{7,6},{8,9},{9,8},{10,11... | collective-permute-start | bytes 98312 | tf_op jit(solution)/shard_map/ppermute | solution.py:481
  47.0 1.9 %collective-permute-done.8 = bf16[32,512]{1,0:T(8,128)(2,1)S(1)} collective-permute-done((bf16[32,512]{1,0:T(8,128)(2,1)S(1)}, bf16[32,512]{1,0:T(8,128)(2,1)S(1)}, u32[]{:S(2)}, u32[]{:S(2)}) %collective-permute-start.8) | collective-permute-done | bytes 32800 | tf_op jit(solution)/shard_map/ppermute | solution.py:481
  48.9 3.5 %collective-permute-start.9 = (bf16[32,512]{1,0:T(8,128)(2,1)S(1)}, bf16[32,512]{1,0:T(8,128)(2,1)S(1)}, u32[]{:S(2)}, u32[]{:S(2)}) collective-permute-start(bf16[32,512]{1,0:T(8,128)(2,1)S(1)} %fusion.1), channel_id=1, source_target_pairs={{0,2},{1,3},{2,0},{3,1},{4,6},{5,7},{6,4},{7,5},{8,10},{9,11},{10,... | collective-permute-start | bytes 98312 | tf_op jit(solution)/shard_map/ppermute | solution.py:481
  52.4 1.9 %collective-permute-done.9 = bf16[32,512]{1,0:T(8,128)(2,1)S(1)} collective-permute-done((bf16[32,512]{1,0:T(8,128)(2,1)S(1)}, bf16[32,512]{1,0:T(8,128)(2,1)S(1)}, u32[]{:S(2)}, u32[]{:S(2)}) %collective-permute-start.9) | collective-permute-done | bytes 32800 | tf_op jit(solution)/shard_map/ppermute | solution.py:481
  54.4 1.2 collective-permute-done.10.refs_3_
  55.6 1.4 first_gradient.1
  57.0 1.6 collective-permute-start.11
  58.5 1.0 mix_layers.8
  60.0 11.1 %collective-permute-done.11.refs_1_ = bf16[512,512]{1,0:T(8,128)(2,1)S(1)} collective-permute-done((bf16[512,512]{1,0:T(8,128)(2,1)S(1)}, bf16[512,512]{1,0:T(8,128)(2,1)S(1)}, u32[]{:S(2)}, u32[]{:S(2)}) %collective-permute-start.11) | collective-permute-done | bytes 524320 | tf_op jit(solution)/shard_map/ppermute | solution.py:525
  71.0 1.0 mix_layers.9
  72.0 0.7 collective-permute-start.13
  72.7 3.4 %collective-permute-start.12 = (bf16[512,512]{1,0:T(8,128)(2,1)S(1)}, bf16[512,512]{1,0:T(8,128)(2,1)S(1)}, u32[]{:S(2)}, u32[]{:S(2)}) collective-permute-start(bf16[512,512]{1,0:T(8,128)(2,1)S(1)} %get-tuple-element.47.refs_3_), channel_id=1, source_target_pairs={{0,4},{8,12},{4,0},{12,8},{1,5},{9,13},{5,1},{13,9},{2,6},{10,14},... | collective-permute-start | bytes 1572872 | tf_op jit(solution)/shard_map/ppermute | solution.py:457
  76.4 1.3 collective-permute-done.12.refs_2_
  77.7 1.0 filter_faces.5
  78.7 1.5 collective-permute-start.14
  80.2 0.8 collective-permute-start.15
  81.5 3.6 %collective-permute-done.14.refs_4_ = bf16[512,256]{1,0:T(8,128)(2,1)S(1)} collective-permute-done((bf16[512,256]{1,0:T(8,128)(2,1)S(1)}, bf16[512,256]{1,0:T(8,128)(2,1)S(1)}, u32[]{:S(2)}, u32[]{:S(2)}) %collective-permute-start.14) | collective-permute-done | bytes 262176 | tf_op jit(solution)/shard_map/ppermute | solution.py:457
  85.1 2.1 %courses_of.3 = (f32[32,512]{1,0:T(8,128)S(1)}, bf16[32,512]{1,0:T(8,128)(2,1)S(1)}) custom-call(s32[1]{0:T(128)} %bitcast.15.refs_0_, s32[1]{0:T(128)} %bitcast.1.refs_1_.refs_0_, s32[1]{0:T(128)} %bitcast.refs_1_.refs_2_.refs_0_, f32[512,512]{1,0:T(8,128)S(1)} %filter_sent.1.refs_3_, bf16[512,256]{1,0:T(8,128)(2,1)S(1)} %collective-permute-done.14.refs_4_, ...), custom_call_target="tpu_custom_call" | custom-call | flops 1000000000 | bytes 6815744 | tf_op jit(solution)/shard_map/courses_of/pallas_call | solution.py:58
  87.2 4.5 %collective-permute-start.16 = (bf16[32,512]{1,0:T(8,128)(2,1)S(1)}, bf16[32,512]{1,0:T(8,128)(2,1)S(1)}, u32[]{:S(2)}, u32[]{:S(2)}) collective-permute-start(bf16[32,512]{1,0:T(8,128)(2,1)S(1)} %get-tuple-element.53), channel_id=1, source_target_pairs={{0,4},{4,0},{8,12},{12,8},{1,5},{5,1},{9,13},{13,9},{2,6},{6,2},{1... | collective-permute-start | bytes 98312 | tf_op jit(solution)/shard_map/ppermute | solution.py:481
  91.7 0.9 collective-permute-done.16
  92.6 1.6 collective-permute-start.17
  94.1 2.4 %collective-permute-done.17 = bf16[32,512]{1,0:T(8,128)(2,1)S(1)} collective-permute-done((bf16[32,512]{1,0:T(8,128)(2,1)S(1)}, bf16[32,512]{1,0:T(8,128)(2,1)S(1)}, u32[]{:S(2)}, u32[]{:S(2)}) %collective-permute-start.17) | collective-permute-done | bytes 32800 | tf_op jit(solution)/shard_map/ppermute | solution.py:481
  96.6 2.9 %collective-permute-start.18 = (bf16[32,512]{1,0:T(8,128)(2,1)S(1)}, bf16[32,512]{1,0:T(8,128)(2,1)S(1)}, u32[]{:S(2)}, u32[]{:S(2)}) collective-permute-start(bf16[32,512]{1,0:T(8,128)(2,1)S(1)} %fusion.2), channel_id=1, source_target_pairs={{0,8},{4,12},{8,0},{12,4},{1,9},{5,13},{9,1},{13,5},{2,10},{6,14},... | collective-permute-start | bytes 98312 | tf_op jit(solution)/shard_map/ppermute | solution.py:481
  99.5 1.9 %collective-permute-done.18 = bf16[32,512]{1,0:T(8,128)(2,1)S(1)} collective-permute-done((bf16[32,512]{1,0:T(8,128)(2,1)S(1)}, bf16[32,512]{1,0:T(8,128)(2,1)S(1)}, u32[]{:S(2)}, u32[]{:S(2)}) %collective-permute-start.18) | collective-permute-done | bytes 32800 | tf_op jit(solution)/shard_map/ppermute | solution.py:481
  101.4 4.0 %collective-permute-start.19 = (bf16[32,512]{1,0:T(8,128)(2,1)S(1)}, bf16[32,512]{1,0:T(8,128)(2,1)S(1)}, u32[]{:S(2)}, u32[]{:S(2)}) collective-permute-start(bf16[32,512]{1,0:T(8,128)(2,1)S(1)} %get-tuple-element.70), channel_id=1, source_target_pairs={{0,1},{1,0},{2,3},{3,2},{4,5},{5,4},{6,7},{7,6},{8,9},{9,8},{10,11... | collective-permute-start | bytes 98312 | tf_op jit(solution)/shard_map/ppermute | solution.py:481
  105.4 1.9 %collective-permute-done.19 = bf16[32,512]{1,0:T(8,128)(2,1)S(1)} collective-permute-done((bf16[32,512]{1,0:T(8,128)(2,1)S(1)}, bf16[32,512]{1,0:T(8,128)(2,1)S(1)}, u32[]{:S(2)}, u32[]{:S(2)}) %collective-permute-start.19) | collective-permute-done | bytes 32800 | tf_op jit(solution)/shard_map/ppermute | solution.py:481
  107.3 3.4 %collective-permute-start.20 = (bf16[32,512]{1,0:T(8,128)(2,1)S(1)}, bf16[32,512]{1,0:T(8,128)(2,1)S(1)}, u32[]{:S(2)}, u32[]{:S(2)}) collective-permute-start(bf16[32,512]{1,0:T(8,128)(2,1)S(1)} %fusion.3), channel_id=1, source_target_pairs={{0,2},{1,3},{2,0},{3,1},{4,6},{5,7},{6,4},{7,5},{8,10},{9,11},{10,... | collective-permute-start | bytes 98312 | tf_op jit(solution)/shard_map/ppermute | solution.py:481
  110.6 1.9 %collective-permute-done.20 = bf16[32,512]{1,0:T(8,128)(2,1)S(1)} collective-permute-done((bf16[32,512]{1,0:T(8,128)(2,1)S(1)}, bf16[32,512]{1,0:T(8,128)(2,1)S(1)}, u32[]{:S(2)}, u32[]{:S(2)}) %collective-permute-start.20) | collective-permute-done | bytes 32800 | tf_op jit(solution)/shard_map/ppermute | solution.py:481
  112.6 1.2 collective-permute-done.21.refs_3_
  113.8 1.9 %second_gradient.1 = (bf16[512,512]{1,0:T(8,128)(2,1)S(1)}, bf16[64,512]{1,0:T(8,128)(2,1)}, f32[1,1]{1,0:T(1,128)}) custom-call(s32[1]{0:T(128)} %bitcast.16.refs_0_, s32[1]{0:T(128)} %bitcast.1.refs_1_.refs_0_, bf16[32,512]{1,0:T(8,128)(2,1)S(1)} %add_convert_fusion.refs_2_, bf16[32,512]{1,0:T(8,128)(2,1)S(1)} %collective-permute-done.21.refs_3_, ...), custom_call_target="tpu_custom_call" | custom-call | flops 1000000000 | bytes 4456448 | tf_op jit(solution)/shard_map/second_gradient/pallas_call | solution.py:58
  115.7 1.5 collective-permute-start.22
  117.2 0.8 copy-done.7
  118.1 1.3 second_fade.1
  119.4 0.8 collective-permute-start.26
  120.2 3.2 %collective-permute-start.25 = (bf16[512,256]{1,0:T(8,128)(2,1)S(1)}, bf16[512,256]{1,0:T(8,128)(2,1)S(1)}, u32[]{:S(2)}, u32[]{:S(2)}) collective-permute-start(bf16[512,256]{1,0:T(8,128)(2,1)S(1)} %get-tuple-element.62), channel_id=1, source_target_pairs={{0,4},{8,12},{4,0},{12,8},{1,5},{9,13},{5,1},{13,9},{2,6},{10,14},... | collective-permute-start | bytes 786440 | tf_op jit(solution)/shard_map/ppermute | solution.py:457
  123.9 1.8 %faded_maps.1.refs_4_.refs_2_ = f32[8,512,64]{2,1,0:T(8,128)S(1)} custom-call(f32[8,512,64]{2,1,0:T(8,128)S(1)} %bitcast.22, f32[64,64]{1,0:T(8,128)S(1)} %get-tuple-element.59.refs_1_), custom_call_target="tpu_custom_call" | custom-call | flops 1000000000 | bytes 1064960 | tf_op jit(solution)/shard_map/faded_maps/pallas_call | solution.py:58
  125.7 4.0 %collective-permute-done.22.refs_2_ = bf16[512,512]{1,0:T(8,128)(2,1)S(1)} collective-permute-done((bf16[512,512]{1,0:T(8,128)(2,1)S(1)}, bf16[512,512]{1,0:T(8,128)(2,1)S(1)}, u32[]{:S(2)}, u32[]{:S(2)}) %collective-permute-start.22) | collective-permute-done | bytes 524320 | tf_op jit(solution)/shard_map/ppermute | solution.py:525
  130.2 0.7 collective-permute-start.24
  130.9 3.2 %collective-permute-start.23 = (bf16[512,256]{1,0:T(8,128)(2,1)S(1)}, bf16[512,256]{1,0:T(8,128)(2,1)S(1)}, u32[]{:S(2)}, u32[]{:S(2)}) collective-permute-start(bf16[512,256]{1,0:T(8,128)(2,1)S(1)} %get-tuple-element.60), channel_id=1, source_target_pairs={{0,4},{8,12},{4,0},{12,8},{1,5},{9,13},{5,1},{13,9},{2,6},{10,14},... | collective-permute-start | bytes 786440 | tf_op jit(solution)/shard_map/ppermute | solution.py:457
  134.5 0.7 filter_lanes.5.refs_8_.refs_3_
  135.7 2.0 %collective-permute-start.27 = (bf16[1024,128]{1,0:T(8,128)(2,1)S(1)}, bf16[1024,128]{1,0:T(8,128)(2,1)S(1)}, u32[]{:S(2)}, u32[]{:S(2)}) collective-permute-start(bf16[1024,128]{1,0:T(8,128)(2,1)S(1)} %get-tuple-element.66), channel_id=1, source_target_pairs={{0,1},{2,3},{1,0},{3,2},{4,5},{6,7},{5,4},{7,6},{8,9},{10,11},{9,8... | collective-permute-start | bytes 786440 | tf_op jit(solution)/shard_map/ppermute | solution.py:457
  137.7 0.7 collective-permute-start.28
  138.4 0.7 filter_lanes.4.refs_1_
  139.1 3.8 %collective-permute-done.27.refs_2_.refs_4_ = bf16[1024,128]{1,0:T(8,128)(2,1)S(1)} collective-permute-done((bf16[1024,128]{1,0:T(8,128)(2,1)S(1)}, bf16[1024,128]{1,0:T(8,128)(2,1)S(1)}, u32[]{:S(2)}, u32[]{:S(2)}) %collective-permute-start.27) | collective-permute-done | bytes 262176 | tf_op jit(solution)/shard_map/ppermute | solution.py:457
  142.9 0.5 gradient_energy.1
  143.5 16.1 %all_to_all.5.refs_1_ = f32[32,1,128]{2,1,0:T(1,128)S(1)} all-to-all(f32[32,1,128]{2,1,0:T(1,128)S(1)} %get-tuple-element.68), channel_id=1, replica_groups=mesh['gx'=2,'gy'=4,'gz'=4] {'gx','gy','gz'}, dimensions={0} | all-to-all | bytes 32768 | tf_op jit(solution)/shard_map/all_to_all | solution.py:469
  159.6 1.7 %final_maps.1 = f32[8,512,64]{2,1,0:T(8,128)} custom-call(s32[1]{0:T(128)} %bitcast.refs_1_.refs_2_.refs_0_, f32[32,1,128]{2,1,0:T(1,128)S(1)} %all_to_all.5.refs_1_, f32[8,512,64]{2,1,0:T(8,128)S(1)} %faded_maps.1.refs_4_.refs_2_, f32[512,512]{1,0:T(8,128)S(1)} %filter_lanes.5.refs_8_.refs_3_, ...), custom_call_target="tpu_custom_call" | custom-call | flops 100000000 | bytes 3948544 | tf_op jit(solution)/shard_map/final_maps/pallas_call | solution.py:58
  (54 shorter events, 5.2 us)
Async XLA Ops:
  0.6 1.6 copy-start.2
  2.7 15.0 %collective-permute-start = (bf16[512,512]{1,0:T(8,128)(2,1)S(1)}, bf16[512,512]{1,0:T(8,128)(2,1)S(1)}, u32[]{:S(2)}, u32[]{:S(2)}) collective-permute-start(bf16[512,512]{1,0:T(8,128)(2,1)S(1)} %pack_maps.1.refs_1_), channel_id=1, source_target_pairs={{0,16},{16,0},{1,17},{17,1},{2,18},{18,2},{3,19},{19,3},{4,20},{20... | collective-permute-start | bytes 1572872 | tf_op jit(solution)/shard_map/ppermute | solution.py:525
  18.1 5.2 %copy-start.4 = (bf16[1024,256]{1,0:T(8,128)(2,1)S(1)}, bf16[1024,256]{1,0:T(8,128)(2,1)}, u32[]{:S(2)}) copy-start(bf16[1024,256]{1,0:T(8,128)(2,1)} %constant.40.clone.refs_5_) | copy-start | bytes 1572868
  18.1 8.6 %copy-start.1 = (bf16[1024,512]{1,0:T(8,128)(2,1)S(1)}, bf16[1024,512]{1,0:T(8,128)(2,1)}, u32[]{:S(2)}) copy-start(bf16[1024,512]{1,0:T(8,128)(2,1)} %constant.41.clone.refs_4_) | copy-start | bytes 3145732
  18.2 3.9 %collective-permute-start.2 = (bf16[512,256]{1,0:T(8,128)(2,1)S(1)}, bf16[512,256]{1,0:T(8,128)(2,1)S(1)}, u32[]{:S(2)}, u32[]{:S(2)}) collective-permute-start(bf16[512,256]{1,0:T(8,128)(2,1)S(1)} %cut_face.3), channel_id=1, source_target_pairs={{4,8},{8,4},{5,9},{9,5},{6,10},{10,6},{7,11},{11,7},{20,24},{24,20... | collective-permute-start | bytes 786440 | tf_op jit(solution)/shard_map/ppermute | solution.py:457
  19.0 4.3 %collective-permute-start.1 = (bf16[512,256]{1,0:T(8,128)(2,1)S(1)}, bf16[512,256]{1,0:T(8,128)(2,1)S(1)}, u32[]{:S(2)}, u32[]{:S(2)}) collective-permute-start(bf16[512,256]{1,0:T(8,128)(2,1)S(1)} %get-tuple-element.36), channel_id=1, source_target_pairs={{0,4},{8,12},{4,0},{12,8},{1,5},{9,13},{5,1},{13,9},{2,6},{10,14},... | collective-permute-start | bytes 786440 | tf_op jit(solution)/shard_map/ppermute | solution.py:457
  23.3 5.5 %copy-start = (bf16[8,16,32,512]{3,2,1,0:T(8,128)(2,1)S(1)}, bf16[8,16,32,512]{3,2,1,0:T(8,128)(2,1)}, u32[]{:S(2)}) copy-start(bf16[8,16,32,512]{3,2,1,0:T(8,128)(2,1)} %param.8) | copy-start | bytes 12582916
  23.3 5.5 %copy-start.6 = (bf16[256,512]{1,0:T(8,128)(2,1)S(1)}, bf16[256,512]{1,0:T(8,128)(2,1)}, u32[]{:S(2)}) copy-start(bf16[256,512]{1,0:T(8,128)(2,1)} %constant.42.clone.refs_6_.refs_4_) | copy-start | bytes 786436
  23.7 5.0 %collective-permute-start.3 = (bf16[512,128]{1,0:T(8,128)(2,1)S(1)}, bf16[512,128]{1,0:T(8,128)(2,1)S(1)}, u32[]{:S(2)}, u32[]{:S(2)}) collective-permute-start(bf16[512,128]{1,0:T(8,128)(2,1)S(1)} %get-tuple-element.38), channel_id=1, source_target_pairs={{0,1},{2,3},{1,0},{3,2},{4,5},{6,7},{5,4},{7,6},{8,9},{10,11},{9,8... | collective-permute-start | bytes 393224 | tf_op jit(solution)/shard_map/ppermute | solution.py:457
  25.4 3.4 %collective-permute-start.4 = (bf16[512,128]{1,0:T(8,128)(2,1)S(1)}, bf16[512,128]{1,0:T(8,128)(2,1)S(1)}, u32[]{:S(2)}, u32[]{:S(2)}) collective-permute-start(bf16[512,128]{1,0:T(8,128)(2,1)S(1)} %get-tuple-element.39), channel_id=1, source_target_pairs={{1,2},{2,1},{5,6},{6,5},{9,10},{10,9},{13,14},{14,13},{17,18},{18,... | collective-permute-start | bytes 393224 | tf_op jit(solution)/shard_map/ppermute | solution.py:457
  28.8 47.3 %slice-start = ((s8[6291456]{0:T(1024)(128)(4,1)}), s8[4194304]{0:T(1024)(128)(4,1)S(1)}, s32[]{:S(2)}) async-start(s8[6291456]{0:T(1024)(128)(4,1)} %bitcast.23), calls=%async_computation.1 | async-start | bytes 8388608
  30.6 2.6 %collective-permute-start.5 = (bf16[32,512]{1,0:T(8,128)(2,1)S(1)}, bf16[32,512]{1,0:T(8,128)(2,1)S(1)}, u32[]{:S(2)}, u32[]{:S(2)}) collective-permute-start(bf16[32,512]{1,0:T(8,128)(2,1)S(1)} %get-tuple-element.41), channel_id=1, source_target_pairs={{0,4},{4,0},{8,12},{12,8},{1,5},{5,1},{9,13},{13,9},{2,6},{6,2},{1... | collective-permute-start | bytes 98312 | tf_op jit(solution)/shard_map/ppermute | solution.py:481
  33.2 4.0 %collective-permute-start.6 = (bf16[32,512]{1,0:T(8,128)(2,1)S(1)}, bf16[32,512]{1,0:T(8,128)(2,1)S(1)}, u32[]{:S(2)}, u32[]{:S(2)}) collective-permute-start(bf16[32,512]{1,0:T(8,128)(2,1)S(1)} %fusion.4), channel_id=1, source_target_pairs={{0,16},{16,0},{1,17},{17,1},{2,18},{18,2},{3,19},{19,3},{4,20},{20... | collective-permute-start | bytes 98312 | tf_op jit(solution)/shard_map/ppermute | solution.py:481
  37.2 5.1 %collective-permute-start.7 = (bf16[32,512]{1,0:T(8,128)(2,1)S(1)}, bf16[32,512]{1,0:T(8,128)(2,1)S(1)}, u32[]{:S(2)}, u32[]{:S(2)}) collective-permute-start(bf16[32,512]{1,0:T(8,128)(2,1)S(1)} %fusion), channel_id=1, source_target_pairs={{0,8},{4,12},{8,0},{12,4},{1,9},{5,13},{9,1},{13,5},{2,10},{6,14},... | collective-permute-start | bytes 98312 | tf_op jit(solution)/shard_map/ppermute | solution.py:481
  42.3 6.5 %collective-permute-start.8 = (bf16[32,512]{1,0:T(8,128)(2,1)S(1)}, bf16[32,512]{1,0:T(8,128)(2,1)S(1)}, u32[]{:S(2)}, u32[]{:S(2)}) collective-permute-start(bf16[32,512]{1,0:T(8,128)(2,1)S(1)} %get-tuple-element.72), channel_id=1, source_target_pairs={{0,1},{1,0},{2,3},{3,2},{4,5},{5,4},{6,7},{7,6},{8,9},{9,8},{10,11... | collective-permute-start | bytes 98312 | tf_op jit(solution)/shard_map/ppermute | solution.py:481
  48.9 5.4 %collective-permute-start.9 = (bf16[32,512]{1,0:T(8,128)(2,1)S(1)}, bf16[32,512]{1,0:T(8,128)(2,1)S(1)}, u32[]{:S(2)}, u32[]{:S(2)}) collective-permute-start(bf16[32,512]{1,0:T(8,128)(2,1)S(1)} %fusion.1), channel_id=1, source_target_pairs={{0,2},{1,3},{2,0},{3,1},{4,6},{5,7},{6,4},{7,5},{8,10},{9,11},{10,... | collective-permute-start | bytes 98312 | tf_op jit(solution)/shard_map/ppermute | solution.py:481
  54.3 1.3 collective-permute-start.10
  55.6 20.5 %slice-start.1 = ((s8[6291456]{0:T(1024)(128)(4,1)}), s8[2097152]{0:T(1024)(128)(4,1)S(1)}, s32[]{:S(2)}) async-start(s8[6291456]{0:T(1024)(128)(4,1)} %bitcast.23), calls=%async_computation.2 | async-start | bytes 4194304
  55.6 20.5 %copy-start.5 = (bf16[4,1024,512]{2,1,0:T(8,128)(2,1)S(1)}, bf16[4,1024,512]{2,1,0:T(8,128)(2,1)}, u32[]{:S(2)}) copy-start(bf16[4,1024,512]{2,1,0:T(8,128)(2,1)} %constant.44.clone.refs_3_) | copy-start | bytes 12582916
  57.0 14.1 %collective-permute-start.11 = (bf16[512,512]{1,0:T(8,128)(2,1)S(1)}, bf16[512,512]{1,0:T(8,128)(2,1)S(1)}, u32[]{:S(2)}, u32[]{:S(2)}) collective-permute-start(bf16[512,512]{1,0:T(8,128)(2,1)S(1)} %get-tuple-element.42.refs_1_), channel_id=1, source_target_pairs={{0,16},{16,0},{1,17},{17,1},{2,18},{18,2},{3,19},{19,3},{4,20},{20... | collective-permute-start | bytes 1572872 | tf_op jit(solution)/shard_map/ppermute | solution.py:525
  72.0 4.3 %collective-permute-start.13 = (bf16[512,512]{1,0:T(8,128)(2,1)S(1)}, bf16[512,512]{1,0:T(8,128)(2,1)S(1)}, u32[]{:S(2)}, u32[]{:S(2)}) collective-permute-start(bf16[512,512]{1,0:T(8,128)(2,1)S(1)} %get-tuple-element.47.refs_3_), channel_id=1, source_target_pairs={{4,8},{8,4},{5,9},{9,5},{6,10},{10,6},{7,11},{11,7},{20,24},{24,20... | collective-permute-start | bytes 1572872 | tf_op jit(solution)/shard_map/ppermute | solution.py:457
  72.7 5.0 %collective-permute-start.12 = (bf16[512,512]{1,0:T(8,128)(2,1)S(1)}, bf16[512,512]{1,0:T(8,128)(2,1)S(1)}, u32[]{:S(2)}, u32[]{:S(2)}) collective-permute-start(bf16[512,512]{1,0:T(8,128)(2,1)S(1)} %get-tuple-element.47.refs_3_), channel_id=1, source_target_pairs={{0,4},{8,12},{4,0},{12,8},{1,5},{9,13},{5,1},{13,9},{2,6},{10,14},... | collective-permute-start | bytes 1572872 | tf_op jit(solution)/shard_map/ppermute | solution.py:457
  78.7 6.4 %collective-permute-start.14 = (bf16[512,256]{1,0:T(8,128)(2,1)S(1)}, bf16[512,256]{1,0:T(8,128)(2,1)S(1)}, u32[]{:S(2)}, u32[]{:S(2)}) collective-permute-start(bf16[512,256]{1,0:T(8,128)(2,1)S(1)} %get-tuple-element.49.refs_1_), channel_id=1, source_target_pairs={{0,1},{2,3},{1,0},{3,2},{4,5},{6,7},{5,4},{7,6},{8,9},{10,11},{9,8... | collective-permute-start | bytes 786440 | tf_op jit(solution)/shard_map/ppermute | solution.py:457
  80.2 4.9 %collective-permute-start.15 = (bf16[512,256]{1,0:T(8,128)(2,1)S(1)}, bf16[512,256]{1,0:T(8,128)(2,1)S(1)}, u32[]{:S(2)}, u32[]{:S(2)}) collective-permute-start(bf16[512,256]{1,0:T(8,128)(2,1)S(1)} %get-tuple-element.50.refs_2_), channel_id=1, source_target_pairs={{1,2},{2,1},{5,6},{6,5},{9,10},{10,9},{13,14},{14,13},{17,18},{18,... | collective-permute-start | bytes 786440 | tf_op jit(solution)/shard_map/ppermute | solution.py:457
  87.2 5.3 %collective-permute-start.16 = (bf16[32,512]{1,0:T(8,128)(2,1)S(1)}, bf16[32,512]{1,0:T(8,128)(2,1)S(1)}, u32[]{:S(2)}, u32[]{:S(2)}) collective-permute-start(bf16[32,512]{1,0:T(8,128)(2,1)S(1)} %get-tuple-element.53), channel_id=1, source_target_pairs={{0,4},{4,0},{8,12},{12,8},{1,5},{5,1},{9,13},{13,9},{2,6},{6,2},{1... | collective-permute-start | bytes 98312 | tf_op jit(solution)/shard_map/ppermute | solution.py:481
  92.6 4.0 %collective-permute-start.17 = (bf16[32,512]{1,0:T(8,128)(2,1)S(1)}, bf16[32,512]{1,0:T(8,128)(2,1)S(1)}, u32[]{:S(2)}, u32[]{:S(2)}) collective-permute-start(bf16[32,512]{1,0:T(8,128)(2,1)S(1)} %fusion.5), channel_id=1, source_target_pairs={{0,16},{16,0},{1,17},{17,1},{2,18},{18,2},{3,19},{19,3},{4,20},{20... | collective-permute-start | bytes 98312 | tf_op jit(solution)/shard_map/ppermute | solution.py:481
  96.6 4.8 %collective-permute-start.18 = (bf16[32,512]{1,0:T(8,128)(2,1)S(1)}, bf16[32,512]{1,0:T(8,128)(2,1)S(1)}, u32[]{:S(2)}, u32[]{:S(2)}) collective-permute-start(bf16[32,512]{1,0:T(8,128)(2,1)S(1)} %fusion.2), channel_id=1, source_target_pairs={{0,8},{4,12},{8,0},{12,4},{1,9},{5,13},{9,1},{13,5},{2,10},{6,14},... | collective-permute-start | bytes 98312 | tf_op jit(solution)/shard_map/ppermute | solution.py:481
  101.4 5.9 %collective-permute-start.19 = (bf16[32,512]{1,0:T(8,128)(2,1)S(1)}, bf16[32,512]{1,0:T(8,128)(2,1)S(1)}, u32[]{:S(2)}, u32[]{:S(2)}) collective-permute-start(bf16[32,512]{1,0:T(8,128)(2,1)S(1)} %get-tuple-element.70), channel_id=1, source_target_pairs={{0,1},{1,0},{2,3},{3,2},{4,5},{5,4},{6,7},{7,6},{8,9},{9,8},{10,11... | collective-permute-start | bytes 98312 | tf_op jit(solution)/shard_map/ppermute | solution.py:481
  107.3 5.2 %collective-permute-start.20 = (bf16[32,512]{1,0:T(8,128)(2,1)S(1)}, bf16[32,512]{1,0:T(8,128)(2,1)S(1)}, u32[]{:S(2)}, u32[]{:S(2)}) collective-permute-start(bf16[32,512]{1,0:T(8,128)(2,1)S(1)} %fusion.3), channel_id=1, source_target_pairs={{0,2},{1,3},{2,0},{3,1},{4,6},{5,7},{6,4},{7,5},{8,10},{9,11},{10,... | collective-permute-start | bytes 98312 | tf_op jit(solution)/shard_map/ppermute | solution.py:481
  112.5 1.3 collective-permute-start.21
  115.7 14.0 %collective-permute-start.22 = (bf16[512,512]{1,0:T(8,128)(2,1)S(1)}, bf16[512,512]{1,0:T(8,128)(2,1)S(1)}, u32[]{:S(2)}, u32[]{:S(2)}) collective-permute-start(bf16[512,512]{1,0:T(8,128)(2,1)S(1)} %get-tuple-element.54.refs_1_), channel_id=1, source_target_pairs={{0,16},{16,0},{1,17},{17,1},{2,18},{18,2},{3,19},{19,3},{4,20},{20... | collective-permute-start | bytes 1572872 | tf_op jit(solution)/shard_map/ppermute | solution.py:525
  117.2 0.8 copy-start.7
  119.3 4.5 %copy-start.3 = (f32[64,8,16,32]{0,3,2,1:T(8,128)S(1)}, f32[64,8,16,32]{0,3,2,1:T(8,128)}, u32[]{:S(2)}) copy-start(f32[64,8,16,32]{0,3,2,1:T(8,128)} %param.9) | copy-start | bytes 3145732
  119.4 14.6 %collective-permute-start.26 = (bf16[512,256]{1,0:T(8,128)(2,1)S(1)}, bf16[512,256]{1,0:T(8,128)(2,1)S(1)}, u32[]{:S(2)}, u32[]{:S(2)}) collective-permute-start(bf16[512,256]{1,0:T(8,128)(2,1)S(1)} %cut_face.5), channel_id=1, source_target_pairs={{4,8},{8,4},{5,9},{9,5},{6,10},{10,6},{7,11},{11,7},{20,24},{24,20... | collective-permute-start | bytes 786440 | tf_op jit(solution)/shard_map/ppermute | solution.py:457
  120.2 13.8 %collective-permute-start.25 = (bf16[512,256]{1,0:T(8,128)(2,1)S(1)}, bf16[512,256]{1,0:T(8,128)(2,1)S(1)}, u32[]{:S(2)}, u32[]{:S(2)}) collective-permute-start(bf16[512,256]{1,0:T(8,128)(2,1)S(1)} %get-tuple-element.62), channel_id=1, source_target_pairs={{0,4},{8,12},{4,0},{12,8},{1,5},{9,13},{5,1},{13,9},{2,6},{10,14},... | collective-permute-start | bytes 786440 | tf_op jit(solution)/shard_map/ppermute | solution.py:457
  130.2 5.0 %collective-permute-start.24 = (bf16[512,256]{1,0:T(8,128)(2,1)S(1)}, bf16[512,256]{1,0:T(8,128)(2,1)S(1)}, u32[]{:S(2)}, u32[]{:S(2)}) collective-permute-start(bf16[512,256]{1,0:T(8,128)(2,1)S(1)} %cut_face.4), channel_id=1, source_target_pairs={{4,8},{8,4},{5,9},{9,5},{6,10},{10,6},{7,11},{11,7},{20,24},{24,20... | collective-permute-start | bytes 786440 | tf_op jit(solution)/shard_map/ppermute | solution.py:457
  130.9 4.4 %collective-permute-start.23 = (bf16[512,256]{1,0:T(8,128)(2,1)S(1)}, bf16[512,256]{1,0:T(8,128)(2,1)S(1)}, u32[]{:S(2)}, u32[]{:S(2)}) collective-permute-start(bf16[512,256]{1,0:T(8,128)(2,1)S(1)} %get-tuple-element.60), channel_id=1, source_target_pairs={{0,4},{8,12},{4,0},{12,8},{1,5},{9,13},{5,1},{13,9},{2,6},{10,14},... | collective-permute-start | bytes 786440 | tf_op jit(solution)/shard_map/ppermute | solution.py:457
  135.7 7.2 %collective-permute-start.27 = (bf16[1024,128]{1,0:T(8,128)(2,1)S(1)}, bf16[1024,128]{1,0:T(8,128)(2,1)S(1)}, u32[]{:S(2)}, u32[]{:S(2)}) collective-permute-start(bf16[1024,128]{1,0:T(8,128)(2,1)S(1)} %get-tuple-element.66), channel_id=1, source_target_pairs={{0,1},{2,3},{1,0},{3,2},{4,5},{6,7},{5,4},{7,6},{8,9},{10,11},{9,8... | collective-permute-start | bytes 786440 | tf_op jit(solution)/shard_map/ppermute | solution.py:457
  137.7 5.2 %collective-permute-start.28 = (bf16[1024,128]{1,0:T(8,128)(2,1)S(1)}, bf16[1024,128]{1,0:T(8,128)(2,1)S(1)}, u32[]{:S(2)}, u32[]{:S(2)}) collective-permute-start(bf16[1024,128]{1,0:T(8,128)(2,1)S(1)} %get-tuple-element.67), channel_id=1, source_target_pairs={{1,2},{2,1},{5,6},{6,5},{9,10},{10,9},{13,14},{14,13},{17,18},{18,... | collective-permute-start | bytes 786440 | tf_op jit(solution)/shard_map/ppermute | solution.py:457

commit v9 on v7

--- a/solution.py
+++ b/solution.py
@@ -95,15 +95,21 @@
     return jnp.sum(jnp.sum(value, axis=1, keepdims=True), axis=0, keepdims=True)
 
 
-def pack_maps(info, voxel_maps):
+def pack_maps(info, voxel_maps, face):
     layers, plane, chans = voxel_maps.shape
-
-    def body(_, src, out):
+    part = chans // 2
+
+    def body(info_ref, src, one, two, first):
         unit = unit_of(chans).astype(BF16)
         for x in range(layers):
-            out[x * chans : (x + 1) * chans, :] = dot_nt(unit, src[x].astype(BF16)).astype(BF16)
-
-    return call(body, shape((layers * chans, plane), BF16), info, [], [voxel_maps], name="pack_maps")
+            turned = dot_nt(unit, src[x].astype(BF16)).astype(BF16)
+            one[x * part : (x + 1) * part, :] = turned[:part]
+            two[x * part : (x + 1) * part, :] = turned[part:]
+        send_faces(info_ref, ODD_Y, two, face, first=first)
+
+    rows = layers * part
+    shapes = (shape((rows, plane), BF16), shape((rows, plane), BF16), shape((rows, face), BF16))
+    return call(body, shapes, info, [ODD_Y], [voxel_maps], name="pack_maps")
 
 
 def pick_tables(info, table_y, table_z):
@@ -256,22 +262,26 @@
     return row < info_ref[COUNT]
 
 
-def courses_of(info, acc, first, second, table, bold, chans, size_y, size_z):
+def courses_of(info, acc, first, second, table, bold, chans, size_y, size_z, ready=()):
     frames = bold.shape[1]
     plane = size_y * size_z
     layers = bold.shape[0] // plane
-
-    def body(info_ref, start, first_ref, second_ref, weights, frames_ref, out):
+    part = acc.shape[0] // layers
+
+    def body(info_ref, start, first_ref, second_ref, weights, frames_ref, *refs):
         total = jnp.zeros((chans, frames), F32)
         for x in range(layers):
-            rows = slice(x * chans, (x + 1) * chans)
+            rows = slice(x * part, (x + 1) * part)
             value = start[rows, :] + swapped_dot(info_ref, ODD_Z, first_ref, [], second_ref, weights, rows)
+            if ready:
+                rows = slice(x * (chans - part), (x + 1) * (chans - part))
+                value = jnp.concatenate([value, refs[0][rows, :].astype(F32)], axis=0)
             keep = live_lanes(info_ref, x, value.shape, size_y, size_z)
             value = jnp.where(keep, value, 0.0).astype(BF16)
             total = total + dot(value, frames_ref[x * plane : (x + 1) * plane, :])
-        out[...] = total
-
-    arrays = [acc, first, second, table, bold]
+        refs[-1][...] = total
+
+    arrays = [acc, first, second, table, bold, *ready]
     shapes = shape((chans, frames), F32)
     return call(body, shapes, info, [COUNT, ODD_Z], arrays, flops=10**9, name="courses_of")
 
@@ -454,25 +464,16 @@
 
 
 def hypercube_sum(value):
-    rounds = []
+    steps = []
     for axis in AXES:
         peers = lax.axis_size(axis)
         if peers & (peers - 1):
             return lax.psum(value, AXES)
-        if axis == "gz" and peers == 4:
-            rounds.append((axis, (1, 2, 3)))
-        else:
-            rounds += [(axis, (1 << b,)) for b in range(peers.bit_length() - 1)]
-    for axis, masks in rounds:
+        steps += [(axis, 1 << b) for b in range(peers.bit_length() - 1)]
+    for axis, bit in steps:
+        pairs = [(i, i ^ bit) for i in range(lax.axis_size(axis))]
         value = lax.reduce_precision(value, 8, 7)
-        sent = value.astype(BF16)
-        got = []
-        for mask in masks:
-            pairs = [(i, i ^ mask) for i in range(lax.axis_size(axis))]
-            got.append(lax.ppermute(sent, axis, pairs).astype(F32))
-        value = value + got[0]
-        if len(got) == 3:
-            value = value + (got[1] + got[2])
+        value = value + lax.ppermute(value.astype(BF16), axis, pairs).astype(F32)
     return value
 
 
@@ -505,6 +506,7 @@
     own_x = [slice(p * size_x, (p + 1) * size_x) for p in range(parts_x)]
 
     def along_x(block, matrices, beside=(), face=face_y):
+        chans = block.shape[0] // size_x
         kinds = [BF16] * len(matrices)
         if parts_x == 2:
             mine = [[[m[own_x[p], own_x[p]]] for m in matrices] for p in range(2)]
@@ -521,7 +523,7 @@
             columns = np.arange(size_x) + lo + RADIUS
             inside = (columns >= 0) & (columns < win_x.shape[1])
             tables.append(np.where(inside[None], win_x[:, np.clip(columns, 0, win_x.shape[1] - 1)], 0.0))
-        return mix_layers(info, [[tables]], chans, [before, block, after], [], kinds, face=face_y)
+        return mix_layers(info, [[tables]], chans, [before, block, after], [], kinds, face=face)
 
     def along_y(field, first):
         return swapped(first, cut_face(info, field, face_y), "gy", inner_first=True)
@@ -531,12 +533,16 @@
         ends = swapped(*filter_faces(info, first, field, second, table_ends), "gz")
         return filter_lanes(info, first, field, second, table_own), *ends
 
-    def all_courses(acc, first, second, table):
-        return hypercube_sum(courses_of(info, acc, first, second, table, bold, chans, size_y, size_z))
-
-    plain = pack_maps(info, voxel_maps)
-    acc, first, second = along_rest(*along_x(plain, [full_x]))
-    courses1 = all_courses(acc, first, second, table_z)
+    def all_courses(acc, first, second, table, ready=()):
+        return hypercube_sum(
+            courses_of(info, acc, first, second, table, bold, chans, size_y, size_z, ready)
+        )
+
+    one, two, face2 = pack_maps(info, voxel_maps, face_y)
+    acc, first, second = along_rest(*along_x(one, [full_x]))
+    two = whole_gradient(info, *along_rest(two, face2), table_z)
+    two = along_x(two, [full_x], face=0)
+    courses1 = all_courses(acc, first, second, table_z, two)
     raw1, half1 = first_gradient(info, courses1, bold, chans, size_y, size_z)
     kept, fade1 = first_fade(info, half1)
     if twice:

time: 158 us -> 155 us (0.981)
  waiting for transfers between devices: 54.6 us -> 43.8 us
  starting transfers between devices: 56.9 us -> 67.3 us
  blocking collectives: 18.8 us -> 15.9 us
    ppermute x3 -> x4, waiting for transfers between devices: 23.6 us -> 9.85 us  [along_x(): got = lax.ppermute(block, 'gx', [(0, 1), (1, 0)])]
    ppermute x14 -> x18, starting transfers between devices: 20.7 us -> 31.9 us  [swapped(): got[start] = lax.ppermute((first, second)[start], axis, pairs)]
    all_to_all x1, blocking collectives: 18.8 us -> 15.9 us  [exchanged(): return lax.all_to_all(parts, AXES, 0, 0, tiled=True)]
    ppermute x14 -> x18, waiting for transfers between devices: 10.6 us -> 12.6 us  [swapped(): got[start] = lax.ppermute((first, second)[start], axis, pairs)]
    ppermute x12 -> x10, starting transfers between devices: 30.1 us -> 28.7 us  [hypercube_sum(): value = value + lax.ppermute(value.astype(BF16), axis, pairs).astype(F32)]
    ppermute x12 -> x10, waiting for transfers between devices: 20.4 us -> 21.3 us  [hypercube_sum(): value = value + lax.ppermute(value.astype(BF16), axis, pairs).astype(F32)]
    pallas_call x28 -> x34, Pallas kernels: 22.5 us -> 23.1 us  [call(): pl.pallas_call(wrapped, out_shape=shapes, in_specs=[pl.BlockSpec(memory_s...]
    ppermute x3 -> x4, starting transfers between devices: 6.1 us -> 6.69 us  [along_x(): got = lax.ppermute(block, 'gx', [(0, 1), (1, 0)])]
  transfers between devices with their start and end apart: 29 -> 32, of which waited for: 18 -> 18; matrix products, arithmetic and copies ran while one was open for 0% -> 0% of each run, Pallas kernels for 6% -> 7%
where the time goes in v9:
time: 155 us
  starting transfers between devices  67.3 us (43%)
  waiting for transfers between devices  43.8 us (28%)
  Pallas kernels  23.1 us (15%)
  blocking collectives  15.9 us (10%)
  local copies, waits for them, and re-layouts  2.47 us (2%)
  between operations  1.97 us (1%)
    ppermute x18, starting transfers between devices, swapped(): got[start] = lax.ppermute((first, second)[start], axis, pairs)  31.9 us
    ppermute x10, starting transfers between devices, hypercube_sum(): value = value + lax.ppermute(value.astype(BF16), axis, pairs).astype(F32)  28.7 us
    pallas_call x34, Pallas kernels, call(): pl.pallas_call(wrapped, out_shape=shapes, in_specs=[pl.BlockSpec(memory_s...  23.1 us
    ppermute x10, waiting for transfers between devices, hypercube_sum(): value = value + lax.ppermute(value.astype(BF16), axis, pairs).astype(F32)  21.3 us
    all_to_all x1, blocking collectives, exchanged(): return lax.all_to_all(parts, AXES, 0, 0, tiled=True)  15.9 us
    ppermute x18, waiting for transfers between devices, swapped(): got[start] = lax.ppermute((first, second)[start], axis, pairs)  12.6 us
    ppermute x4, waiting for transfers between devices, along_x(): got = lax.ppermute(block, 'gx', [(0, 1), (1, 0)])  9.85 us
    ppermute x4, starting transfers between devices, along_x(): got = lax.ppermute(block, 'gx', [(0, 1), (1, 0)])  6.69 us
  transfers between devices with their start and end apart: 32, of which 18 were waited for; matrix products, arithmetic and copies ran while one was open for 0% of the time, Pallas kernels for 7%

profile of v9, /device:TPU:0, one launch (start us, length us, event | category | flops | bytes accessed | tf_op | source)
XLA Modules:
  0.0 154.9 jit_solution(7013999649210602814)
XLA Ops:
  0.7 1.6 %copy-done.2 = f32[64,8,16,32]{0,3,2,1:T(8,128)S(1)} copy-done((f32[64,8,16,32]{0,3,2,1:T(8,128)S(1)}, f32[64,8,16,32]{0,3,2,1:T(8,128)}, u32[]{:S(2)}) %copy-start.2) | copy-done | bytes 1048600
  2.7 3.0 %collective-permute-start = (bf16[256,512]{1,0:T(8,128)(2,1)S(1)}, bf16[256,512]{1,0:T(8,128)(2,1)S(1)}, u32[]{:S(2)}, u32[]{:S(2)}) collective-permute-start(bf16[256,512]{1,0:T(8,128)(2,1)S(1)} %get-tuple-element.37.refs_1_), channel_id=1, source_target_pairs={{0,16},{16,0},{1,17},{17,1},{2,18},{18,2},{3,19},{19,3},{4,20},{20... | collective-permute-start | bytes 786440 | tf_op jit(solution)/shard_map/ppermute | solution.py:514
  5.8 0.8 collective-permute-start.6
  6.6 2.9 %collective-permute-start.5 = (bf16[256,256]{1,0:T(8,128)(2,1)S(1)}, bf16[256,256]{1,0:T(8,128)(2,1)S(1)}, u32[]{:S(2)}, u32[]{:S(2)}) collective-permute-start(bf16[256,256]{1,0:T(8,128)(2,1)S(1)} %get-tuple-element.42), channel_id=1, source_target_pairs={{0,4},{8,12},{4,0},{12,8},{1,5},{9,13},{5,1},{13,9},{2,6},{10,14},... | collective-permute-start | bytes 393224 | tf_op jit(solution)/shard_map/ppermute | solution.py:451
  9.5 1.0 collective-permute-done.5.refs_1_.refs_2_
  10.8 1.6 %collective-permute-start.7 = (bf16[256,128]{1,0:T(8,128)(2,1)S(1)}, bf16[256,128]{1,0:T(8,128)(2,1)S(1)}, u32[]{:S(2)}, u32[]{:S(2)}) collective-permute-start(bf16[256,128]{1,0:T(8,128)(2,1)S(1)} %get-tuple-element.44), channel_id=1, source_target_pairs={{0,1},{2,3},{1,0},{3,2},{4,5},{6,7},{5,4},{7,6},{8,9},{10,11},{9,8... | collective-permute-start | bytes 196616 | tf_op jit(solution)/shard_map/ppermute | solution.py:451
  12.5 0.7 collective-permute-start.8
  13.9 1.3 collective-permute-done.7.refs_2_
  15.5 0.6 collective-permute-start.9
  16.3 0.7 collective-permute-start.2
  17.0 4.6 %collective-permute-start.1 = (bf16[256,256]{1,0:T(8,128)(2,1)S(1)}, bf16[256,256]{1,0:T(8,128)(2,1)S(1)}, u32[]{:S(2)}, u32[]{:S(2)}) collective-permute-start(bf16[256,256]{1,0:T(8,128)(2,1)S(1)} %get-tuple-element.38), channel_id=1, source_target_pairs={{0,4},{8,12},{4,0},{12,8},{1,5},{9,13},{5,1},{13,9},{2,6},{10,14},... | collective-permute-start | bytes 393224 | tf_op jit(solution)/shard_map/ppermute | solution.py:451
  21.6 1.0 collective-permute-done.1.refs_1_.refs_2_
  22.9 4.7 %collective-permute-start.3 = (bf16[256,128]{1,0:T(8,128)(2,1)S(1)}, bf16[256,128]{1,0:T(8,128)(2,1)S(1)}, u32[]{:S(2)}, u32[]{:S(2)}) collective-permute-start(bf16[256,128]{1,0:T(8,128)(2,1)S(1)} %get-tuple-element.40), channel_id=1, source_target_pairs={{0,1},{2,3},{1,0},{3,2},{4,5},{6,7},{5,4},{7,6},{8,9},{10,11},{9,8... | collective-permute-start | bytes 196616 | tf_op jit(solution)/shard_map/ppermute | solution.py:451
  27.6 0.7 collective-permute-start.4
  29.9 1.7 %courses_of.2 = f32[64,512]{1,0:T(8,128)S(1)} custom-call(s32[1]{0:T(128)} %bitcast.13.refs_0_, s32[1]{0:T(128)} %bitcast.refs_1_.refs_0_, f32[256,512]{1,0:T(8,128)S(1)} %filter_lanes.4.refs_2_, bf16[256,128]{1,0:T(8,128)(2,1)S(1)} %collective-permute-done.3.refs_3_, bf16[256,128]{1,0:T(8,128)(2,1)S(1)} %collective-permute-done.4.refs_4_, ...), custom_call_target="tpu_custom_call" | custom-call | flops 1000000000 | bytes 5373952 | tf_op jit(solution)/shard_map/courses_of/pallas_call | solution.py:58
  31.6 1.6 %collective-permute-start.10 = (bf16[64,512]{1,0:T(8,128)(2,1)S(1)}, bf16[64,512]{1,0:T(8,128)(2,1)S(1)}, u32[]{:S(2)}, u32[]{:S(2)}) collective-permute-start(bf16[64,512]{1,0:T(8,128)(2,1)S(1)} %reduce-precision_convert_fusion.1), channel_id=1, source_target_pairs={{0,16},{16,0},{1,17},{17,1},{2,18},{18,2},{3,19},{19,3},{4,20},{20... | collective-permute-start | bytes 196616 | tf_op jit(solution)/shard_map/ppermute | solution.py:476
  33.2 2.9 %collective-permute-done.10 = bf16[64,512]{1,0:T(8,128)(2,1)S(1)} collective-permute-done((bf16[64,512]{1,0:T(8,128)(2,1)S(1)}, bf16[64,512]{1,0:T(8,128)(2,1)S(1)}, u32[]{:S(2)}, u32[]{:S(2)}) %collective-permute-start.10) | collective-permute-done | bytes 65568 | tf_op jit(solution)/shard_map/ppermute | solution.py:476
  36.6 0.9 collective-permute-done.11
  37.5 3.1 %collective-permute-start.12 = (bf16[64,512]{1,0:T(8,128)(2,1)S(1)}, bf16[64,512]{1,0:T(8,128)(2,1)S(1)}, u32[]{:S(2)}, u32[]{:S(2)}) collective-permute-start(bf16[64,512]{1,0:T(8,128)(2,1)S(1)} %fusion), channel_id=1, source_target_pairs={{0,8},{4,12},{8,0},{12,4},{1,9},{5,13},{9,1},{13,5},{2,10},{6,14},... | collective-permute-start | bytes 196616 | tf_op jit(solution)/shard_map/ppermute | solution.py:476
  40.6 2.4 %collective-permute-done.12 = bf16[64,512]{1,0:T(8,128)(2,1)S(1)} collective-permute-done((bf16[64,512]{1,0:T(8,128)(2,1)S(1)}, bf16[64,512]{1,0:T(8,128)(2,1)S(1)}, u32[]{:S(2)}, u32[]{:S(2)}) %collective-permute-start.12) | collective-permute-done | bytes 65568 | tf_op jit(solution)/shard_map/ppermute | solution.py:476
  43.1 4.2 %collective-permute-start.13 = (bf16[64,512]{1,0:T(8,128)(2,1)S(1)}, bf16[64,512]{1,0:T(8,128)(2,1)S(1)}, u32[]{:S(2)}, u32[]{:S(2)}) collective-permute-start(bf16[64,512]{1,0:T(8,128)(2,1)S(1)} %get-tuple-element.74), channel_id=1, source_target_pairs={{0,1},{1,0},{2,3},{3,2},{4,5},{5,4},{6,7},{7,6},{8,9},{9,8},{10,11... | collective-permute-start | bytes 196616 | tf_op jit(solution)/shard_map/ppermute | solution.py:476
  47.3 2.2 %collective-permute-done.13 = bf16[64,512]{1,0:T(8,128)(2,1)S(1)} collective-permute-done((bf16[64,512]{1,0:T(8,128)(2,1)S(1)}, bf16[64,512]{1,0:T(8,128)(2,1)S(1)}, u32[]{:S(2)}, u32[]{:S(2)}) %collective-permute-start.13) | collective-permute-done | bytes 65568 | tf_op jit(solution)/shard_map/ppermute | solution.py:476
  49.6 3.5 %collective-permute-start.14 = (bf16[64,512]{1,0:T(8,128)(2,1)S(1)}, bf16[64,512]{1,0:T(8,128)(2,1)S(1)}, u32[]{:S(2)}, u32[]{:S(2)}) collective-permute-start(bf16[64,512]{1,0:T(8,128)(2,1)S(1)} %fusion.1), channel_id=1, source_target_pairs={{0,2},{1,3},{2,0},{3,1},{4,6},{5,7},{6,4},{7,5},{8,10},{9,11},{10,... | collective-permute-start | bytes 196616 | tf_op jit(solution)/shard_map/ppermute | solution.py:476
  53.1 2.2 %collective-permute-done.14 = bf16[64,512]{1,0:T(8,128)(2,1)S(1)} collective-permute-done((bf16[64,512]{1,0:T(8,128)(2,1)S(1)}, bf16[64,512]{1,0:T(8,128)(2,1)S(1)}, u32[]{:S(2)}, u32[]{:S(2)}) %collective-permute-start.14) | collective-permute-done | bytes 65568 | tf_op jit(solution)/shard_map/ppermute | solution.py:476
  55.4 1.4 first_gradient.1
  56.8 1.6 %collective-permute-start.15 = (bf16[512,512]{1,0:T(8,128)(2,1)S(1)}, bf16[512,512]{1,0:T(8,128)(2,1)S(1)}, u32[]{:S(2)}, u32[]{:S(2)}) collective-permute-start(bf16[512,512]{1,0:T(8,128)(2,1)S(1)} %get-tuple-element.46.refs_1_), channel_id=1, source_target_pairs={{0,16},{16,0},{1,17},{17,1},{2,18},{18,2},{3,19},{19,3},{4,20},{20... | collective-permute-start | bytes 1572872 | tf_op jit(solution)/shard_map/ppermute | solution.py:514
  58.3 1.0 mix_layers.12
  59.8 8.5 %collective-permute-done.15.refs_1_ = bf16[512,512]{1,0:T(8,128)(2,1)S(1)} collective-permute-done((bf16[512,512]{1,0:T(8,128)(2,1)S(1)}, bf16[512,512]{1,0:T(8,128)(2,1)S(1)}, u32[]{:S(2)}, u32[]{:S(2)}) %collective-permute-start.15) | collective-permute-done | bytes 524320 | tf_op jit(solution)/shard_map/ppermute | solution.py:514
  68.3 1.0 mix_layers.13
  69.3 0.7 collective-permute-start.17
  70.0 2.6 %collective-permute-start.16 = (bf16[512,512]{1,0:T(8,128)(2,1)S(1)}, bf16[512,512]{1,0:T(8,128)(2,1)S(1)}, u32[]{:S(2)}, u32[]{:S(2)}) collective-permute-start(bf16[512,512]{1,0:T(8,128)(2,1)S(1)} %get-tuple-element.51.refs_3_), channel_id=1, source_target_pairs={{0,4},{8,12},{4,0},{12,8},{1,5},{9,13},{5,1},{13,9},{2,6},{10,14},... | collective-permute-start | bytes 1572872 | tf_op jit(solution)/shard_map/ppermute | solution.py:451
  72.8 1.3 collective-permute-done.16.refs_2_
  74.1 1.0 filter_faces.7
  75.2 1.3 collective-permute-start.18
  76.5 0.8 collective-permute-start.19
  77.8 3.8 %collective-permute-done.18.refs_3_ = bf16[512,256]{1,0:T(8,128)(2,1)S(1)} collective-permute-done((bf16[512,256]{1,0:T(8,128)(2,1)S(1)}, bf16[512,256]{1,0:T(8,128)(2,1)S(1)}, u32[]{:S(2)}, u32[]{:S(2)}) %collective-permute-start.18) | collective-permute-done | bytes 262176 | tf_op jit(solution)/shard_map/ppermute | solution.py:451
  81.6 2.1 %courses_of.3 = f32[64,512]{1,0:T(8,128)S(1)} custom-call(s32[1]{0:T(128)} %bitcast.15.refs_0_, s32[1]{0:T(128)} %bitcast.refs_1_.refs_0_, f32[512,512]{1,0:T(8,128)S(1)} %filter_sent.1.refs_2_, bf16[512,256]{1,0:T(8,128)(2,1)S(1)} %collective-permute-done.18.refs_3_, bf16[512,256]{1,0:T(8,128)(2,1)S(1)} %collective-permute-done.19.refs_4_, ...), custom_call_target="tpu_custom_call" | custom-call | flops 1000000000 | bytes 6815744 | tf_op jit(solution)/shard_map/courses_of/pallas_call | solution.py:58
  83.7 1.6 %collective-permute-start.20 = (bf16[64,512]{1,0:T(8,128)(2,1)S(1)}, bf16[64,512]{1,0:T(8,128)(2,1)S(1)}, u32[]{:S(2)}, u32[]{:S(2)}) collective-permute-start(bf16[64,512]{1,0:T(8,128)(2,1)S(1)} %reduce-precision_convert_fusion), channel_id=1, source_target_pairs={{0,16},{16,0},{1,17},{17,1},{2,18},{18,2},{3,19},{19,3},{4,20},{20... | collective-permute-start | bytes 196616 | tf_op jit(solution)/shard_map/ppermute | solution.py:476
  85.3 2.8 %collective-permute-done.20 = bf16[64,512]{1,0:T(8,128)(2,1)S(1)} collective-permute-done((bf16[64,512]{1,0:T(8,128)(2,1)S(1)}, bf16[64,512]{1,0:T(8,128)(2,1)S(1)}, u32[]{:S(2)}, u32[]{:S(2)}) %collective-permute-start.20) | collective-permute-done | bytes 65568 | tf_op jit(solution)/shard_map/ppermute | solution.py:476
  88.1 3.3 %collective-permute-start.21 = (bf16[64,512]{1,0:T(8,128)(2,1)S(1)}, bf16[64,512]{1,0:T(8,128)(2,1)S(1)}, u32[]{:S(2)}, u32[]{:S(2)}) collective-permute-start(bf16[64,512]{1,0:T(8,128)(2,1)S(1)} %fusion.5), channel_id=1, source_target_pairs={{0,4},{4,0},{8,12},{12,8},{1,5},{5,1},{9,13},{13,9},{2,6},{6,2},{1... | collective-permute-start | bytes 196616 | tf_op jit(solution)/shard_map/ppermute | solution.py:476
  91.4 0.9 collective-permute-done.21
  92.3 4.0 %collective-permute-start.22 = (bf16[64,512]{1,0:T(8,128)(2,1)S(1)}, bf16[64,512]{1,0:T(8,128)(2,1)S(1)}, u32[]{:S(2)}, u32[]{:S(2)}) collective-permute-start(bf16[64,512]{1,0:T(8,128)(2,1)S(1)} %fusion.2), channel_id=1, source_target_pairs={{0,8},{4,12},{8,0},{12,4},{1,9},{5,13},{9,1},{13,5},{2,10},{6,14},... | collective-permute-start | bytes 196616 | tf_op jit(solution)/shard_map/ppermute | solution.py:476
  96.4 2.4 %collective-permute-done.22 = bf16[64,512]{1,0:T(8,128)(2,1)S(1)} collective-permute-done((bf16[64,512]{1,0:T(8,128)(2,1)S(1)}, bf16[64,512]{1,0:T(8,128)(2,1)S(1)}, u32[]{:S(2)}, u32[]{:S(2)}) %collective-permute-start.22) | collective-permute-done | bytes 65568 | tf_op jit(solution)/shard_map/ppermute | solution.py:476
  98.8 4.0 %collective-permute-start.23 = (bf16[64,512]{1,0:T(8,128)(2,1)S(1)}, bf16[64,512]{1,0:T(8,128)(2,1)S(1)}, u32[]{:S(2)}, u32[]{:S(2)}) collective-permute-start(bf16[64,512]{1,0:T(8,128)(2,1)S(1)} %get-tuple-element.72), channel_id=1, source_target_pairs={{0,1},{1,0},{2,3},{3,2},{4,5},{5,4},{6,7},{7,6},{8,9},{9,8},{10,11... | collective-permute-start | bytes 196616 | tf_op jit(solution)/shard_map/ppermute | solution.py:476
  102.8 2.2 %collective-permute-done.23 = bf16[64,512]{1,0:T(8,128)(2,1)S(1)} collective-permute-done((bf16[64,512]{1,0:T(8,128)(2,1)S(1)}, bf16[64,512]{1,0:T(8,128)(2,1)S(1)}, u32[]{:S(2)}, u32[]{:S(2)}) %collective-permute-start.23) | collective-permute-done | bytes 65568 | tf_op jit(solution)/shard_map/ppermute | solution.py:476
  105.1 3.0 %collective-permute-start.24 = (bf16[64,512]{1,0:T(8,128)(2,1)S(1)}, bf16[64,512]{1,0:T(8,128)(2,1)S(1)}, u32[]{:S(2)}, u32[]{:S(2)}) collective-permute-start(bf16[64,512]{1,0:T(8,128)(2,1)S(1)} %fusion.3), channel_id=1, source_target_pairs={{0,2},{1,3},{2,0},{3,1},{4,6},{5,7},{6,4},{7,5},{8,10},{9,11},{10,... | collective-permute-start | bytes 196616 | tf_op jit(solution)/shard_map/ppermute | solution.py:476
  108.0 2.3 %collective-permute-done.24 = bf16[64,512]{1,0:T(8,128)(2,1)S(1)} collective-permute-done((bf16[64,512]{1,0:T(8,128)(2,1)S(1)}, bf16[64,512]{1,0:T(8,128)(2,1)S(1)}, u32[]{:S(2)}, u32[]{:S(2)}) %collective-permute-start.24) | collective-permute-done | bytes 65568 | tf_op jit(solution)/shard_map/ppermute | solution.py:476
  110.3 1.9 %second_gradient.1 = (bf16[512,512]{1,0:T(8,128)(2,1)S(1)}, bf16[64,512]{1,0:T(8,128)(2,1)}, f32[1,1]{1,0:T(1,128)}) custom-call(s32[1]{0:T(128)} %bitcast.16.refs_0_, f32[64,512]{1,0:T(8,128)S(1)} %convert_add_fusion.refs_1_, bf16[64,512]{1,0:T(8,128)(2,1)S(1)} %get-tuple-element.49.refs_0_.refs_2_, f32[64,512]{1,0:T(8,128)S(1)} %get-tuple-element.50.refs_4_.refs_3_, ...), custom_call_target="tpu_custom_call" | custom-call | flops 1000000000 | bytes 4521984 | tf_op jit(solution)/shard_map/second_gradient/pallas_call | solution.py:58
  112.2 1.5 collective-permute-start.25
  113.7 0.8 copy-done.7
  114.6 1.3 second_fade.1
  115.9 0.8 collective-permute-start.29
  116.7 3.3 %collective-permute-start.28 = (bf16[512,256]{1,0:T(8,128)(2,1)S(1)}, bf16[512,256]{1,0:T(8,128)(2,1)S(1)}, u32[]{:S(2)}, u32[]{:S(2)}) collective-permute-start(bf16[512,256]{1,0:T(8,128)(2,1)S(1)} %get-tuple-element.64), channel_id=1, source_target_pairs={{0,4},{8,12},{4,0},{12,8},{1,5},{9,13},{5,1},{13,9},{2,6},{10,14},... | collective-permute-start | bytes 786440 | tf_op jit(solution)/shard_map/ppermute | solution.py:451
  120.5 1.8 %faded_maps.1.refs_4_.refs_2_ = f32[8,512,64]{2,1,0:T(8,128)S(1)} custom-call(f32[8,512,64]{2,1,0:T(8,128)S(1)} %bitcast.22, f32[64,64]{1,0:T(8,128)S(1)} %get-tuple-element.61.refs_1_), custom_call_target="tpu_custom_call" | custom-call | flops 1000000000 | bytes 1064960 | tf_op jit(solution)/shard_map/faded_maps/pallas_call | solution.py:58
  122.4 1.3 collective-permute-done.25.refs_2_
  124.1 0.7 collective-permute-start.27
  124.8 2.6 %collective-permute-start.26 = (bf16[512,256]{1,0:T(8,128)(2,1)S(1)}, bf16[512,256]{1,0:T(8,128)(2,1)S(1)}, u32[]{:S(2)}, u32[]{:S(2)}) collective-permute-start(bf16[512,256]{1,0:T(8,128)(2,1)S(1)} %get-tuple-element.62), channel_id=1, source_target_pairs={{0,4},{8,12},{4,0},{12,8},{1,5},{9,13},{5,1},{13,9},{2,6},{10,14},... | collective-permute-start | bytes 786440 | tf_op jit(solution)/shard_map/ppermute | solution.py:451
  127.9 0.7 filter_lanes.7.refs_8_.refs_3_
  129.2 1.8 %collective-permute-start.30 = (bf16[1024,128]{1,0:T(8,128)(2,1)S(1)}, bf16[1024,128]{1,0:T(8,128)(2,1)S(1)}, u32[]{:S(2)}, u32[]{:S(2)}) collective-permute-start(bf16[1024,128]{1,0:T(8,128)(2,1)S(1)} %get-tuple-element.68), channel_id=1, source_target_pairs={{0,1},{2,3},{1,0},{3,2},{4,5},{6,7},{5,4},{7,6},{8,9},{10,11},{9,8... | collective-permute-start | bytes 786440 | tf_op jit(solution)/shard_map/ppermute | solution.py:451
  131.0 0.7 collective-permute-start.31
  131.7 0.7 filter_lanes.6.refs_1_
  132.4 4.2 %collective-permute-done.30.refs_2_.refs_4_ = bf16[1024,128]{1,0:T(8,128)(2,1)S(1)} collective-permute-done((bf16[1024,128]{1,0:T(8,128)(2,1)S(1)}, bf16[1024,128]{1,0:T(8,128)(2,1)S(1)}, u32[]{:S(2)}, u32[]{:S(2)}) %collective-permute-start.30) | collective-permute-done | bytes 262176 | tf_op jit(solution)/shard_map/ppermute | solution.py:451
  137.1 15.9 %all_to_all.5.refs_1_ = f32[32,1,128]{2,1,0:T(1,128)S(1)} all-to-all(f32[32,1,128]{2,1,0:T(1,128)S(1)} %get-tuple-element.70), channel_id=1, replica_groups=mesh['gx'=2,'gy'=4,'gz'=4] {'gx','gy','gz'}, dimensions={0} | all-to-all | bytes 32768 | tf_op jit(solution)/shard_map/all_to_all | solution.py:463
  153.0 1.7 %final_maps.1 = f32[8,512,64]{2,1,0:T(8,128)} custom-call(s32[1]{0:T(128)} %bitcast.refs_1_.refs_0_, f32[32,1,128]{2,1,0:T(1,128)S(1)} %all_to_all.5.refs_1_, f32[8,512,64]{2,1,0:T(8,128)S(1)} %faded_maps.1.refs_4_.refs_2_, f32[512,512]{1,0:T(8,128)S(1)} %filter_lanes.7.refs_8_.refs_3_, bf16[1024,128]{1,0:T(8,128)(2,1)S(1)} %collective-permute-done.30.refs_2_.refs_4_, ...), custom_call_target="tpu_custom_call" | custom-call | flops 100000000 | bytes 3948544 | tf_op jit(solution)/shard_map/final_maps/pallas_call | solution.py:58
  (68 shorter events, 7.6 us)
Async XLA Ops:
  0.6 1.6 %copy-start.2 = (f32[64,8,16,32]{0,3,2,1:T(8,128)S(1)}, f32[64,8,16,32]{0,3,2,1:T(8,128)}, u32[]{:S(2)}) copy-start(f32[64,8,16,32]{0,3,2,1:T(8,128)} %param.9) | copy-start | bytes 3145732
  2.7 7.8 %copy-start.4 = (bf16[1024,256]{1,0:T(8,128)(2,1)S(1)}, bf16[1024,256]{1,0:T(8,128)(2,1)}, u32[]{:S(2)}) copy-start(bf16[1024,256]{1,0:T(8,128)(2,1)} %constant.40.clone.refs_5_) | copy-start | bytes 1572868
  2.7 13.3 %collective-permute-start = (bf16[256,512]{1,0:T(8,128)(2,1)S(1)}, bf16[256,512]{1,0:T(8,128)(2,1)S(1)}, u32[]{:S(2)}, u32[]{:S(2)}) collective-permute-start(bf16[256,512]{1,0:T(8,128)(2,1)S(1)} %get-tuple-element.37.refs_1_), channel_id=1, source_target_pairs={{0,16},{16,0},{1,17},{17,1},{2,18},{18,2},{3,19},{19,3},{4,20},{20... | collective-permute-start | bytes 786440 | tf_op jit(solution)/shard_map/ppermute | solution.py:514
  5.8 7.6 %copy-start.1 = (bf16[1024,512]{1,0:T(8,128)(2,1)S(1)}, bf16[1024,512]{1,0:T(8,128)(2,1)}, u32[]{:S(2)}) copy-start(bf16[1024,512]{1,0:T(8,128)(2,1)} %constant.41.clone.refs_4_) | copy-start | bytes 3145732
  5.8 9.4 %copy-start.5 = (bf16[256,512]{1,0:T(8,128)(2,1)S(1)}, bf16[256,512]{1,0:T(8,128)(2,1)}, u32[]{:S(2)}) copy-start(bf16[256,512]{1,0:T(8,128)(2,1)} %constant.42.clone.refs_4_.refs_5_.refs_6_) | copy-start | bytes 786436
  5.8 3.7 %collective-permute-start.6 = (bf16[256,256]{1,0:T(8,128)(2,1)S(1)}, bf16[256,256]{1,0:T(8,128)(2,1)S(1)}, u32[]{:S(2)}, u32[]{:S(2)}) collective-permute-start(bf16[256,256]{1,0:T(8,128)(2,1)S(1)} %cut_face.5), channel_id=1, source_target_pairs={{4,8},{8,4},{5,9},{9,5},{6,10},{10,6},{7,11},{11,7},{20,24},{24,20... | collective-permute-start | bytes 393224 | tf_op jit(solution)/shard_map/ppermute | solution.py:451
  6.6 3.9 %collective-permute-start.5 = (bf16[256,256]{1,0:T(8,128)(2,1)S(1)}, bf16[256,256]{1,0:T(8,128)(2,1)S(1)}, u32[]{:S(2)}, u32[]{:S(2)}) collective-permute-start(bf16[256,256]{1,0:T(8,128)(2,1)S(1)} %get-tuple-element.42), channel_id=1, source_target_pairs={{0,4},{8,12},{4,0},{12,8},{1,5},{9,13},{5,1},{13,9},{2,6},{10,14},... | collective-permute-start | bytes 393224 | tf_op jit(solution)/shard_map/ppermute | solution.py:451
  10.8 4.3 %collective-permute-start.7 = (bf16[256,128]{1,0:T(8,128)(2,1)S(1)}, bf16[256,128]{1,0:T(8,128)(2,1)S(1)}, u32[]{:S(2)}, u32[]{:S(2)}) collective-permute-start(bf16[256,128]{1,0:T(8,128)(2,1)S(1)} %get-tuple-element.44), channel_id=1, source_target_pairs={{0,1},{2,3},{1,0},{3,2},{4,5},{6,7},{5,4},{7,6},{8,9},{10,11},{9,8... | collective-permute-start | bytes 196616 | tf_op jit(solution)/shard_map/ppermute | solution.py:451
  12.5 2.7 %collective-permute-start.8 = (bf16[256,128]{1,0:T(8,128)(2,1)S(1)}, bf16[256,128]{1,0:T(8,128)(2,1)S(1)}, u32[]{:S(2)}, u32[]{:S(2)}) collective-permute-start(bf16[256,128]{1,0:T(8,128)(2,1)S(1)} %get-tuple-element.45), channel_id=1, source_target_pairs={{1,2},{2,1},{5,6},{6,5},{9,10},{10,9},{13,14},{14,13},{17,18},{18,... | collective-permute-start | bytes 196616 | tf_op jit(solution)/shard_map/ppermute | solution.py:451
  15.5 14.1 %collective-permute-start.9 = (bf16[256,512]{1,0:T(8,128)(2,1)S(1)}, bf16[256,512]{1,0:T(8,128)(2,1)S(1)}, u32[]{:S(2)}, u32[]{:S(2)}) collective-permute-start(bf16[256,512]{1,0:T(8,128)(2,1)S(1)} %whole_gradient.1.refs_1_), channel_id=1, source_target_pairs={{0,16},{16,0},{1,17},{17,1},{2,18},{18,2},{3,19},{19,3},{4,20},{20... | collective-permute-start | bytes 786440 | tf_op jit(solution)/shard_map/ppermute | solution.py:514
  16.3 5.3 %collective-permute-start.2 = (bf16[256,256]{1,0:T(8,128)(2,1)S(1)}, bf16[256,256]{1,0:T(8,128)(2,1)S(1)}, u32[]{:S(2)}, u32[]{:S(2)}) collective-permute-start(bf16[256,256]{1,0:T(8,128)(2,1)S(1)} %cut_face.4), channel_id=1, source_target_pairs={{4,8},{8,4},{5,9},{9,5},{6,10},{10,6},{7,11},{11,7},{20,24},{24,20... | collective-permute-start | bytes 393224 | tf_op jit(solution)/shard_map/ppermute | solution.py:451
  17.0 5.6 %collective-permute-start.1 = (bf16[256,256]{1,0:T(8,128)(2,1)S(1)}, bf16[256,256]{1,0:T(8,128)(2,1)S(1)}, u32[]{:S(2)}, u32[]{:S(2)}) collective-permute-start(bf16[256,256]{1,0:T(8,128)(2,1)S(1)} %get-tuple-element.38), channel_id=1, source_target_pairs={{0,4},{8,12},{4,0},{12,8},{1,5},{9,13},{5,1},{13,9},{2,6},{10,14},... | collective-permute-start | bytes 393224 | tf_op jit(solution)/shard_map/ppermute | solution.py:451
  22.6 7.3 %copy-start = (bf16[8,16,32,512]{3,2,1,0:T(8,128)(2,1)S(1)}, bf16[8,16,32,512]{3,2,1,0:T(8,128)(2,1)}, u32[]{:S(2)}) copy-start(bf16[8,16,32,512]{3,2,1,0:T(8,128)(2,1)} %param.8) | copy-start | bytes 12582916
  22.9 6.9 %collective-permute-start.3 = (bf16[256,128]{1,0:T(8,128)(2,1)S(1)}, bf16[256,128]{1,0:T(8,128)(2,1)S(1)}, u32[]{:S(2)}, u32[]{:S(2)}) collective-permute-start(bf16[256,128]{1,0:T(8,128)(2,1)S(1)} %get-tuple-element.40), channel_id=1, source_target_pairs={{0,1},{2,3},{1,0},{3,2},{4,5},{6,7},{5,4},{7,6},{8,9},{10,11},{9,8... | collective-permute-start | bytes 196616 | tf_op jit(solution)/shard_map/ppermute | solution.py:451
  27.6 2.3 %collective-permute-start.4 = (bf16[256,128]{1,0:T(8,128)(2,1)S(1)}, bf16[256,128]{1,0:T(8,128)(2,1)S(1)}, u32[]{:S(2)}, u32[]{:S(2)}) collective-permute-start(bf16[256,128]{1,0:T(8,128)(2,1)S(1)} %get-tuple-element.41), channel_id=1, source_target_pairs={{1,2},{2,1},{5,6},{6,5},{9,10},{10,9},{13,14},{14,13},{17,18},{18,... | collective-permute-start | bytes 196616 | tf_op jit(solution)/shard_map/ppermute | solution.py:451
  29.9 42.7 %slice-start = ((s8[6291456]{0:T(1024)(128)(4,1)}), s8[4194304]{0:T(1024)(128)(4,1)S(1)}, s32[]{:S(2)}) async-start(s8[6291456]{0:T(1024)(128)(4,1)} %bitcast.23), calls=%async_computation.1 | async-start | bytes 8388608
  31.6 4.5 %collective-permute-start.10 = (bf16[64,512]{1,0:T(8,128)(2,1)S(1)}, bf16[64,512]{1,0:T(8,128)(2,1)S(1)}, u32[]{:S(2)}, u32[]{:S(2)}) collective-permute-start(bf16[64,512]{1,0:T(8,128)(2,1)S(1)} %reduce-precision_convert_fusion.1), channel_id=1, source_target_pairs={{0,16},{16,0},{1,17},{17,1},{2,18},{18,2},{3,19},{19,3},{4,20},{20... | collective-permute-start | bytes 196616 | tf_op jit(solution)/shard_map/ppermute | solution.py:476
  36.1 1.4 collective-permute-start.11
  37.5 5.5 %collective-permute-start.12 = (bf16[64,512]{1,0:T(8,128)(2,1)S(1)}, bf16[64,512]{1,0:T(8,128)(2,1)S(1)}, u32[]{:S(2)}, u32[]{:S(2)}) collective-permute-start(bf16[64,512]{1,0:T(8,128)(2,1)S(1)} %fusion), channel_id=1, source_target_pairs={{0,8},{4,12},{8,0},{12,4},{1,9},{5,13},{9,1},{13,5},{2,10},{6,14},... | collective-permute-start | bytes 196616 | tf_op jit(solution)/shard_map/ppermute | solution.py:476
  43.1 6.5 %collective-permute-start.13 = (bf16[64,512]{1,0:T(8,128)(2,1)S(1)}, bf16[64,512]{1,0:T(8,128)(2,1)S(1)}, u32[]{:S(2)}, u32[]{:S(2)}) collective-permute-start(bf16[64,512]{1,0:T(8,128)(2,1)S(1)} %get-tuple-element.74), channel_id=1, source_target_pairs={{0,1},{1,0},{2,3},{3,2},{4,5},{5,4},{6,7},{7,6},{8,9},{9,8},{10,11... | collective-permute-start | bytes 196616 | tf_op jit(solution)/shard_map/ppermute | solution.py:476
  49.6 5.8 %collective-permute-start.14 = (bf16[64,512]{1,0:T(8,128)(2,1)S(1)}, bf16[64,512]{1,0:T(8,128)(2,1)S(1)}, u32[]{:S(2)}, u32[]{:S(2)}) collective-permute-start(bf16[64,512]{1,0:T(8,128)(2,1)S(1)} %fusion.1), channel_id=1, source_target_pairs={{0,2},{1,3},{2,0},{3,1},{4,6},{5,7},{6,4},{7,5},{8,10},{9,11},{10,... | collective-permute-start | bytes 196616 | tf_op jit(solution)/shard_map/ppermute | solution.py:476
  55.4 17.2 %slice-start.1 = ((s8[6291456]{0:T(1024)(128)(4,1)}), s8[2097152]{0:T(1024)(128)(4,1)S(1)}, s32[]{:S(2)}) async-start(s8[6291456]{0:T(1024)(128)(4,1)} %bitcast.23), calls=%async_computation.2 | async-start | bytes 4194304
  55.4 17.2 %copy-start.6 = (bf16[4,1024,512]{2,1,0:T(8,128)(2,1)S(1)}, bf16[4,1024,512]{2,1,0:T(8,128)(2,1)}, u32[]{:S(2)}) copy-start(bf16[4,1024,512]{2,1,0:T(8,128)(2,1)} %constant.44.clone.refs_3_) | copy-start | bytes 12582916
  56.8 11.5 %collective-permute-start.15 = (bf16[512,512]{1,0:T(8,128)(2,1)S(1)}, bf16[512,512]{1,0:T(8,128)(2,1)S(1)}, u32[]{:S(2)}, u32[]{:S(2)}) collective-permute-start(bf16[512,512]{1,0:T(8,128)(2,1)S(1)} %get-tuple-element.46.refs_1_), channel_id=1, source_target_pairs={{0,16},{16,0},{1,17},{17,1},{2,18},{18,2},{3,19},{19,3},{4,20},{20... | collective-permute-start | bytes 1572872 | tf_op jit(solution)/shard_map/ppermute | solution.py:514
  69.3 3.5 %collective-permute-start.17 = (bf16[512,512]{1,0:T(8,128)(2,1)S(1)}, bf16[512,512]{1,0:T(8,128)(2,1)S(1)}, u32[]{:S(2)}, u32[]{:S(2)}) collective-permute-start(bf16[512,512]{1,0:T(8,128)(2,1)S(1)} %get-tuple-element.51.refs_3_), channel_id=1, source_target_pairs={{4,8},{8,4},{5,9},{9,5},{6,10},{10,6},{7,11},{11,7},{20,24},{24,20... | collective-permute-start | bytes 1572872 | tf_op jit(solution)/shard_map/ppermute | solution.py:451
  70.0 4.1 %collective-permute-start.16 = (bf16[512,512]{1,0:T(8,128)(2,1)S(1)}, bf16[512,512]{1,0:T(8,128)(2,1)S(1)}, u32[]{:S(2)}, u32[]{:S(2)}) collective-permute-start(bf16[512,512]{1,0:T(8,128)(2,1)S(1)} %get-tuple-element.51.refs_3_), channel_id=1, source_target_pairs={{0,4},{8,12},{4,0},{12,8},{1,5},{9,13},{5,1},{13,9},{2,6},{10,14},... | collective-permute-start | bytes 1572872 | tf_op jit(solution)/shard_map/ppermute | solution.py:451
  75.2 6.4 %collective-permute-start.18 = (bf16[512,256]{1,0:T(8,128)(2,1)S(1)}, bf16[512,256]{1,0:T(8,128)(2,1)S(1)}, u32[]{:S(2)}, u32[]{:S(2)}) collective-permute-start(bf16[512,256]{1,0:T(8,128)(2,1)S(1)} %get-tuple-element.53.refs_1_), channel_id=1, source_target_pairs={{0,1},{2,3},{1,0},{3,2},{4,5},{6,7},{5,4},{7,6},{8,9},{10,11},{9,8... | collective-permute-start | bytes 786440 | tf_op jit(solution)/shard_map/ppermute | solution.py:451
  76.5 5.1 %collective-permute-start.19 = (bf16[512,256]{1,0:T(8,128)(2,1)S(1)}, bf16[512,256]{1,0:T(8,128)(2,1)S(1)}, u32[]{:S(2)}, u32[]{:S(2)}) collective-permute-start(bf16[512,256]{1,0:T(8,128)(2,1)S(1)} %get-tuple-element.54.refs_2_), channel_id=1, source_target_pairs={{1,2},{2,1},{5,6},{6,5},{9,10},{10,9},{13,14},{14,13},{17,18},{18,... | collective-permute-start | bytes 786440 | tf_op jit(solution)/shard_map/ppermute | solution.py:451
  83.7 4.3 %collective-permute-start.20 = (bf16[64,512]{1,0:T(8,128)(2,1)S(1)}, bf16[64,512]{1,0:T(8,128)(2,1)S(1)}, u32[]{:S(2)}, u32[]{:S(2)}) collective-permute-start(bf16[64,512]{1,0:T(8,128)(2,1)S(1)} %reduce-precision_convert_fusion), channel_id=1, source_target_pairs={{0,16},{16,0},{1,17},{17,1},{2,18},{18,2},{3,19},{19,3},{4,20},{20... | collective-permute-start | bytes 196616 | tf_op jit(solution)/shard_map/ppermute | solution.py:476
  88.1 4.2 %collective-permute-start.21 = (bf16[64,512]{1,0:T(8,128)(2,1)S(1)}, bf16[64,512]{1,0:T(8,128)(2,1)S(1)}, u32[]{:S(2)}, u32[]{:S(2)}) collective-permute-start(bf16[64,512]{1,0:T(8,128)(2,1)S(1)} %fusion.5), channel_id=1, source_target_pairs={{0,4},{4,0},{8,12},{12,8},{1,5},{5,1},{9,13},{13,9},{2,6},{6,2},{1... | collective-permute-start | bytes 196616 | tf_op jit(solution)/shard_map/ppermute | solution.py:476
  92.3 6.5 %collective-permute-start.22 = (bf16[64,512]{1,0:T(8,128)(2,1)S(1)}, bf16[64,512]{1,0:T(8,128)(2,1)S(1)}, u32[]{:S(2)}, u32[]{:S(2)}) collective-permute-start(bf16[64,512]{1,0:T(8,128)(2,1)S(1)} %fusion.2), channel_id=1, source_target_pairs={{0,8},{4,12},{8,0},{12,4},{1,9},{5,13},{9,1},{13,5},{2,10},{6,14},... | collective-permute-start | bytes 196616 | tf_op jit(solution)/shard_map/ppermute | solution.py:476
  98.8 6.2 %collective-permute-start.23 = (bf16[64,512]{1,0:T(8,128)(2,1)S(1)}, bf16[64,512]{1,0:T(8,128)(2,1)S(1)}, u32[]{:S(2)}, u32[]{:S(2)}) collective-permute-start(bf16[64,512]{1,0:T(8,128)(2,1)S(1)} %get-tuple-element.72), channel_id=1, source_target_pairs={{0,1},{1,0},{2,3},{3,2},{4,5},{5,4},{6,7},{7,6},{8,9},{9,8},{10,11... | collective-permute-start | bytes 196616 | tf_op jit(solution)/shard_map/ppermute | solution.py:476
  105.1 5.2 %collective-permute-start.24 = (bf16[64,512]{1,0:T(8,128)(2,1)S(1)}, bf16[64,512]{1,0:T(8,128)(2,1)S(1)}, u32[]{:S(2)}, u32[]{:S(2)}) collective-permute-start(bf16[64,512]{1,0:T(8,128)(2,1)S(1)} %fusion.3), channel_id=1, source_target_pairs={{0,2},{1,3},{2,0},{3,1},{4,6},{5,7},{6,4},{7,5},{8,10},{9,11},{10,... | collective-permute-start | bytes 196616 | tf_op jit(solution)/shard_map/ppermute | solution.py:476
  112.2 11.5 %collective-permute-start.25 = (bf16[512,512]{1,0:T(8,128)(2,1)S(1)}, bf16[512,512]{1,0:T(8,128)(2,1)S(1)}, u32[]{:S(2)}, u32[]{:S(2)}) collective-permute-start(bf16[512,512]{1,0:T(8,128)(2,1)S(1)} %get-tuple-element.56.refs_1_), channel_id=1, source_target_pairs={{0,16},{16,0},{1,17},{17,1},{2,18},{18,2},{3,19},{19,3},{4,20},{20... | collective-permute-start | bytes 1572872 | tf_op jit(solution)/shard_map/ppermute | solution.py:514
  113.7 0.8 copy-start.7
  115.9 4.6 %copy-start.3 = (f32[64,8,16,32]{0,3,2,1:T(8,128)S(1)}, f32[64,8,16,32]{0,3,2,1:T(8,128)}, u32[]{:S(2)}) copy-start(f32[64,8,16,32]{0,3,2,1:T(8,128)} %param.9) | copy-start | bytes 3145732
  115.9 11.6 %collective-permute-start.29 = (bf16[512,256]{1,0:T(8,128)(2,1)S(1)}, bf16[512,256]{1,0:T(8,128)(2,1)S(1)}, u32[]{:S(2)}, u32[]{:S(2)}) collective-permute-start(bf16[512,256]{1,0:T(8,128)(2,1)S(1)} %cut_face.7), channel_id=1, source_target_pairs={{4,8},{8,4},{5,9},{9,5},{6,10},{10,6},{7,11},{11,7},{20,24},{24,20... | collective-permute-start | bytes 786440 | tf_op jit(solution)/shard_map/ppermute | solution.py:451
  116.7 10.7 %collective-permute-start.28 = (bf16[512,256]{1,0:T(8,128)(2,1)S(1)}, bf16[512,256]{1,0:T(8,128)(2,1)S(1)}, u32[]{:S(2)}, u32[]{:S(2)}) collective-permute-start(bf16[512,256]{1,0:T(8,128)(2,1)S(1)} %get-tuple-element.64), channel_id=1, source_target_pairs={{0,4},{8,12},{4,0},{12,8},{1,5},{9,13},{5,1},{13,9},{2,6},{10,14},... | collective-permute-start | bytes 786440 | tf_op jit(solution)/shard_map/ppermute | solution.py:451
  124.1 4.5 %collective-permute-start.27 = (bf16[512,256]{1,0:T(8,128)(2,1)S(1)}, bf16[512,256]{1,0:T(8,128)(2,1)S(1)}, u32[]{:S(2)}, u32[]{:S(2)}) collective-permute-start(bf16[512,256]{1,0:T(8,128)(2,1)S(1)} %cut_face.6), channel_id=1, source_target_pairs={{4,8},{8,4},{5,9},{9,5},{6,10},{10,6},{7,11},{11,7},{20,24},{24,20... | collective-permute-start | bytes 786440 | tf_op jit(solution)/shard_map/ppermute | solution.py:451
  124.8 3.8 %collective-permute-start.26 = (bf16[512,256]{1,0:T(8,128)(2,1)S(1)}, bf16[512,256]{1,0:T(8,128)(2,1)S(1)}, u32[]{:S(2)}, u32[]{:S(2)}) collective-permute-start(bf16[512,256]{1,0:T(8,128)(2,1)S(1)} %get-tuple-element.62), channel_id=1, source_target_pairs={{0,4},{8,12},{4,0},{12,8},{1,5},{9,13},{5,1},{13,9},{2,6},{10,14},... | collective-permute-start | bytes 786440 | tf_op jit(solution)/shard_map/ppermute | solution.py:451
  129.2 7.4 %collective-permute-start.30 = (bf16[1024,128]{1,0:T(8,128)(2,1)S(1)}, bf16[1024,128]{1,0:T(8,128)(2,1)S(1)}, u32[]{:S(2)}, u32[]{:S(2)}) collective-permute-start(bf16[1024,128]{1,0:T(8,128)(2,1)S(1)} %get-tuple-element.68), channel_id=1, source_target_pairs={{0,1},{2,3},{1,0},{3,2},{4,5},{6,7},{5,4},{7,6},{8,9},{10,11},{9,8... | collective-permute-start | bytes 786440 | tf_op jit(solution)/shard_map/ppermute | solution.py:451
  131.0 5.6 %collective-permute-start.31 = (bf16[1024,128]{1,0:T(8,128)(2,1)S(1)}, bf16[1024,128]{1,0:T(8,128)(2,1)S(1)}, u32[]{:S(2)}, u32[]{:S(2)}) collective-permute-start(bf16[1024,128]{1,0:T(8,128)(2,1)S(1)} %get-tuple-element.69), channel_id=1, source_target_pairs={{1,2},{2,1},{5,6},{6,5},{9,10},{10,9},{13,14},{14,13},{17,18},{18,... | collective-permute-start | bytes 786440 | tf_op jit(solution)/shard_map/ppermute | solution.py:451

commit v10 on v9

--- a/solution.py
+++ b/solution.py
@@ -382,13 +382,13 @@
     return call(body, shapes, info, [], [voxel_maps, fades], flops=10**9, name="faded_maps")
 
 
-def whole_gradient(info, acc, first, second, table):
+def whole_gradient(info, acc, first, second, table, after=()):
     def body(info_ref, start, first_ref, second_ref, weights, out):
         value = start[...] + swapped_dot(info_ref, ODD_Z, first_ref, [], second_ref, weights)
         out[...] = value.astype(BF16)
 
     arrays = [acc, first, second, table]
-    return call(body, shape(acc.shape, BF16), info, [ODD_Z], arrays, name="whole_gradient")
+    return call(body, shape(acc.shape, BF16), info, [ODD_Z], arrays, name="whole_gradient", after=after)
 
 
 def gradient_energy(info, acc, first, second, table, peers, after=()):
@@ -529,7 +529,9 @@
         return swapped(first, cut_face(info, field, face_y), "gy", inner_first=True)
 
     def along_rest(field, first):
-        first, second = along_y(field, first)
+        return along_z(field, *along_y(field, first))
+
+    def along_z(field, first, second):
         ends = swapped(*filter_faces(info, first, field, second, table_ends), "gz")
         return filter_lanes(info, first, field, second, table_own), *ends
 
@@ -539,8 +541,10 @@
         )
 
     one, two, face2 = pack_maps(info, voxel_maps, face_y)
-    acc, first, second = along_rest(*along_x(one, [full_x]))
-    two = whole_gradient(info, *along_rest(two, face2), table_z)
+    one, face1 = along_x(one, [full_x])
+    first, second = along_y(one, face1)
+    two = whole_gradient(info, *along_rest(two, face2), table_z, [first, second])
+    acc, first, second = along_z(one, first, second)
     two = along_x(two, [full_x], face=0)
     courses1 = all_courses(acc, first, second, table_z, two)
     raw1, half1 = first_gradient(info, courses1, bold, chans, size_y, size_z)

time: 155 us -> 152 us (0.981)
  starting transfers between devices: 67.3 us -> 57.9 us
  waiting for transfers between devices: 43.8 us -> 51.7 us
  blocking collectives: 15.9 us -> 14.3 us
    ppermute x10, starting transfers between devices: 28.7 us -> 22.6 us  [hypercube_sum(): value = value + lax.ppermute(value.astype(BF16), axis, pairs).astype(F32)]
    ppermute x10, waiting for transfers between devices: 21.3 us -> 26.1 us  [hypercube_sum(): value = value + lax.ppermute(value.astype(BF16), axis, pairs).astype(F32)]
    ppermute x4, waiting for transfers between devices: 9.85 us -> 13.8 us  [along_x(): got = lax.ppermute(block, 'gx', [(0, 1), (1, 0)])]
    ppermute x18, starting transfers between devices: 31.9 us -> 29.9 us  [swapped(): got[start] = lax.ppermute((first, second)[start], axis, pairs)]
    all_to_all x1, blocking collectives: 15.9 us -> 14.3 us  [exchanged(): return lax.all_to_all(parts, AXES, 0, 0, tiled=True)]
  transfers between devices with their start and end apart: 32 -> 32, of which waited for: 18 -> 17; matrix products, arithmetic and copies ran while one was open for 0% -> 0% of each run, Pallas kernels for 7% -> 7%
where the time goes in v10:
time: 152 us
  starting transfers between devices  57.9 us (38%)
  waiting for transfers between devices  51.7 us (34%)
  Pallas kernels  23.1 us (15%)
  blocking collectives  14.3 us (9%)
  local copies, waits for them, and re-layouts  2.48 us (2%)
  between operations  1.99 us (1%)
    ppermute x18, starting transfers between devices, swapped(): got[start] = lax.ppermute((first, second)[start], axis, pairs)  29.9 us
    ppermute x10, waiting for transfers between devices, hypercube_sum(): value = value + lax.ppermute(value.astype(BF16), axis, pairs).astype(F32)  26.1 us
    pallas_call x34, Pallas kernels, call(): pl.pallas_call(wrapped, out_shape=shapes, in_specs=[pl.BlockSpec(memory_s...  23.1 us
    ppermute x10, starting transfers between devices, hypercube_sum(): value = value + lax.ppermute(value.astype(BF16), axis, pairs).astype(F32)  22.6 us
    all_to_all x1, blocking collectives, exchanged(): return lax.all_to_all(parts, AXES, 0, 0, tiled=True)  14.3 us
    ppermute x4, waiting for transfers between devices, along_x(): got = lax.ppermute(block, 'gx', [(0, 1), (1, 0)])  13.8 us
    ppermute x18, waiting for transfers between devices, swapped(): got[start] = lax.ppermute((first, second)[start], axis, pairs)  11.8 us
    ppermute x4, starting transfers between devices, along_x(): got = lax.ppermute(block, 'gx', [(0, 1), (1, 0)])  5.45 us
  transfers between devices with their start and end apart: 32, of which 17 were waited for; matrix products, arithmetic and copies ran while one was open for 0% of the time, Pallas kernels for 7%

profile of v10, /device:TPU:0, one launch (start us, length us, event | category | flops | bytes accessed | tf_op | source)
XLA Modules:
  0.0 151.8 jit_solution(17301390337267202333)
XLA Ops:
  0.7 1.6 %copy-done.2 = f32[64,8,16,32]{0,3,2,1:T(8,128)S(1)} copy-done((f32[64,8,16,32]{0,3,2,1:T(8,128)S(1)}, f32[64,8,16,32]{0,3,2,1:T(8,128)}, u32[]{:S(2)}) %copy-start.2) | copy-done | bytes 1048600
  2.2 0.5 pack_maps.1
  2.7 3.0 %collective-permute-start = (bf16[256,512]{1,0:T(8,128)(2,1)S(1)}, bf16[256,512]{1,0:T(8,128)(2,1)S(1)}, u32[]{:S(2)}, u32[]{:S(2)}) collective-permute-start(bf16[256,512]{1,0:T(8,128)(2,1)S(1)} %get-tuple-element.37.refs_1_), channel_id=1, source_target_pairs={{0,16},{16,0},{1,17},{17,1},{2,18},{18,2},{3,19},{19,3},{4,20},{20... | collective-permute-start | bytes 786440 | tf_op jit(solution)/shard_map/ppermute | solution.py:514
  5.8 0.7 collective-permute-start.6
  6.5 2.9 %collective-permute-start.5 = (bf16[256,256]{1,0:T(8,128)(2,1)S(1)}, bf16[256,256]{1,0:T(8,128)(2,1)S(1)}, u32[]{:S(2)}, u32[]{:S(2)}) collective-permute-start(bf16[256,256]{1,0:T(8,128)(2,1)S(1)} %get-tuple-element.42), channel_id=1, source_target_pairs={{0,4},{8,12},{4,0},{12,8},{1,5},{9,13},{5,1},{13,9},{2,6},{10,14},... | collective-permute-start | bytes 393224 | tf_op jit(solution)/shard_map/ppermute | solution.py:451
  9.7 2.4 %collective-permute-done.refs_2_ = bf16[256,512]{1,0:T(8,128)(2,1)S(1)} collective-permute-done((bf16[256,512]{1,0:T(8,128)(2,1)S(1)}, bf16[256,512]{1,0:T(8,128)(2,1)S(1)}, u32[]{:S(2)}, u32[]{:S(2)}) %collective-permute-start) | collective-permute-done | bytes 262176 | tf_op jit(solution)/shard_map/ppermute | solution.py:514
  12.4 0.8 collective-permute-start.2
  13.2 3.1 %collective-permute-start.1 = (bf16[256,256]{1,0:T(8,128)(2,1)S(1)}, bf16[256,256]{1,0:T(8,128)(2,1)S(1)}, u32[]{:S(2)}, u32[]{:S(2)}) collective-permute-start(bf16[256,256]{1,0:T(8,128)(2,1)S(1)} %get-tuple-element.38), channel_id=1, source_target_pairs={{0,4},{8,12},{4,0},{12,8},{1,5},{9,13},{5,1},{13,9},{2,6},{10,14},... | collective-permute-start | bytes 393224 | tf_op jit(solution)/shard_map/ppermute | solution.py:451
  16.6 1.6 %collective-permute-start.7 = (bf16[256,128]{1,0:T(8,128)(2,1)S(1)}, bf16[256,128]{1,0:T(8,128)(2,1)S(1)}, u32[]{:S(2)}, u32[]{:S(2)}) collective-permute-start(bf16[256,128]{1,0:T(8,128)(2,1)S(1)} %get-tuple-element.44), channel_id=1, source_target_pairs={{0,1},{2,3},{1,0},{3,2},{4,5},{6,7},{5,4},{7,6},{8,9},{10,11},{9,8... | collective-permute-start | bytes 196616 | tf_op jit(solution)/shard_map/ppermute | solution.py:451
  18.3 0.7 collective-permute-start.8
  19.4 1.6 %collective-permute-done.7.refs_2_ = bf16[256,128]{1,0:T(8,128)(2,1)S(1)} collective-permute-done((bf16[256,128]{1,0:T(8,128)(2,1)S(1)}, bf16[256,128]{1,0:T(8,128)(2,1)S(1)}, u32[]{:S(2)}, u32[]{:S(2)}) %collective-permute-start.7) | collective-permute-done | bytes 65568 | tf_op jit(solution)/shard_map/ppermute | solution.py:451
  21.3 1.6 %collective-permute-start.9 = (bf16[256,512]{1,0:T(8,128)(2,1)S(1)}, bf16[256,512]{1,0:T(8,128)(2,1)S(1)}, u32[]{:S(2)}, u32[]{:S(2)}) collective-permute-start(bf16[256,512]{1,0:T(8,128)(2,1)S(1)} %whole_gradient.1.refs_1_), channel_id=1, source_target_pairs={{0,16},{16,0},{1,17},{17,1},{2,18},{18,2},{3,19},{19,3},{4,20},{20... | collective-permute-start | bytes 786440 | tf_op jit(solution)/shard_map/ppermute | solution.py:514
  23.2 4.6 %collective-permute-start.3 = (bf16[256,128]{1,0:T(8,128)(2,1)S(1)}, bf16[256,128]{1,0:T(8,128)(2,1)S(1)}, u32[]{:S(2)}, u32[]{:S(2)}) collective-permute-start(bf16[256,128]{1,0:T(8,128)(2,1)S(1)} %get-tuple-element.40), channel_id=1, source_target_pairs={{0,1},{2,3},{1,0},{3,2},{4,5},{6,7},{5,4},{7,6},{8,9},{10,11},{9,8... | collective-permute-start | bytes 196616 | tf_op jit(solution)/shard_map/ppermute | solution.py:451
  27.8 0.7 collective-permute-start.4
  30.1 1.7 %courses_of.2 = f32[64,512]{1,0:T(8,128)S(1)} custom-call(s32[1]{0:T(128)} %bitcast.13.refs_0_, s32[1]{0:T(128)} %bitcast.refs_1_.refs_0_, f32[256,512]{1,0:T(8,128)S(1)} %filter_lanes.4.refs_2_, bf16[256,128]{1,0:T(8,128)(2,1)S(1)} %collective-permute-done.3.refs_3_, bf16[256,128]{1,0:T(8,128)(2,1)S(1)} %collective-permute-done.4.refs_4_, ...), custom_call_target="tpu_custom_call" | custom-call | flops 1000000000 | bytes 5373952 | tf_op jit(solution)/shard_map/courses_of/pallas_call | solution.py:58
  31.9 0.6 collective-permute-start.10
  32.4 3.7 %collective-permute-done.10 = bf16[64,512]{1,0:T(8,128)(2,1)S(1)} collective-permute-done((bf16[64,512]{1,0:T(8,128)(2,1)S(1)}, bf16[64,512]{1,0:T(8,128)(2,1)S(1)}, u32[]{:S(2)}, u32[]{:S(2)}) %collective-permute-start.10) | collective-permute-done | bytes 65568 | tf_op jit(solution)/shard_map/ppermute | solution.py:476
  36.3 1.2 collective-permute-done.11
  37.8 4.1 %collective-permute-done.12 = bf16[64,512]{1,0:T(8,128)(2,1)S(1)} collective-permute-done((bf16[64,512]{1,0:T(8,128)(2,1)S(1)}, bf16[64,512]{1,0:T(8,128)(2,1)S(1)}, u32[]{:S(2)}, u32[]{:S(2)}) %collective-permute-start.12) | collective-permute-done | bytes 65568 | tf_op jit(solution)/shard_map/ppermute | solution.py:476
  42.0 4.2 %collective-permute-start.13 = (bf16[64,512]{1,0:T(8,128)(2,1)S(1)}, bf16[64,512]{1,0:T(8,128)(2,1)S(1)}, u32[]{:S(2)}, u32[]{:S(2)}) collective-permute-start(bf16[64,512]{1,0:T(8,128)(2,1)S(1)} %get-tuple-element.74), channel_id=1, source_target_pairs={{0,1},{1,0},{2,3},{3,2},{4,5},{5,4},{6,7},{7,6},{8,9},{9,8},{10,11... | collective-permute-start | bytes 196616 | tf_op jit(solution)/shard_map/ppermute | solution.py:476
  46.2 2.2 %collective-permute-done.13 = bf16[64,512]{1,0:T(8,128)(2,1)S(1)} collective-permute-done((bf16[64,512]{1,0:T(8,128)(2,1)S(1)}, bf16[64,512]{1,0:T(8,128)(2,1)S(1)}, u32[]{:S(2)}, u32[]{:S(2)}) %collective-permute-start.13) | collective-permute-done | bytes 65568 | tf_op jit(solution)/shard_map/ppermute | solution.py:476
  48.4 3.6 %collective-permute-start.14 = (bf16[64,512]{1,0:T(8,128)(2,1)S(1)}, bf16[64,512]{1,0:T(8,128)(2,1)S(1)}, u32[]{:S(2)}, u32[]{:S(2)}) collective-permute-start(bf16[64,512]{1,0:T(8,128)(2,1)S(1)} %fusion.1), channel_id=1, source_target_pairs={{0,2},{1,3},{2,0},{3,1},{4,6},{5,7},{6,4},{7,5},{8,10},{9,11},{10,... | collective-permute-start | bytes 196616 | tf_op jit(solution)/shard_map/ppermute | solution.py:476
  52.0 2.2 %collective-permute-done.14 = bf16[64,512]{1,0:T(8,128)(2,1)S(1)} collective-permute-done((bf16[64,512]{1,0:T(8,128)(2,1)S(1)}, bf16[64,512]{1,0:T(8,128)(2,1)S(1)}, u32[]{:S(2)}, u32[]{:S(2)}) %collective-permute-start.14) | collective-permute-done | bytes 65568 | tf_op jit(solution)/shard_map/ppermute | solution.py:476
  54.3 1.4 first_gradient.1
  55.7 0.6 collective-permute-start.15
  56.3 1.0 mix_layers.12
  57.7 8.8 %collective-permute-done.15.refs_1_ = bf16[512,512]{1,0:T(8,128)(2,1)S(1)} collective-permute-done((bf16[512,512]{1,0:T(8,128)(2,1)S(1)}, bf16[512,512]{1,0:T(8,128)(2,1)S(1)}, u32[]{:S(2)}, u32[]{:S(2)}) %collective-permute-start.15) | collective-permute-done | bytes 524320 | tf_op jit(solution)/shard_map/ppermute | solution.py:514
  66.6 1.0 mix_layers.13
  67.5 0.7 collective-permute-start.17
  68.2 2.9 %collective-permute-start.16 = (bf16[512,512]{1,0:T(8,128)(2,1)S(1)}, bf16[512,512]{1,0:T(8,128)(2,1)S(1)}, u32[]{:S(2)}, u32[]{:S(2)}) collective-permute-start(bf16[512,512]{1,0:T(8,128)(2,1)S(1)} %get-tuple-element.51.refs_3_), channel_id=1, source_target_pairs={{0,4},{8,12},{4,0},{12,8},{1,5},{9,13},{5,1},{13,9},{2,6},{10,14},... | collective-permute-start | bytes 1572872 | tf_op jit(solution)/shard_map/ppermute | solution.py:451
  71.4 1.3 collective-permute-done.16.refs_2_
  72.7 1.0 filter_faces.7
  73.7 0.5 collective-permute-start.18
  74.2 0.8 collective-permute-start.19
  75.5 4.6 %collective-permute-done.18.refs_3_ = bf16[512,256]{1,0:T(8,128)(2,1)S(1)} collective-permute-done((bf16[512,256]{1,0:T(8,128)(2,1)S(1)}, bf16[512,256]{1,0:T(8,128)(2,1)S(1)}, u32[]{:S(2)}, u32[]{:S(2)}) %collective-permute-start.18) | collective-permute-done | bytes 262176 | tf_op jit(solution)/shard_map/ppermute | solution.py:451
  80.2 2.1 %courses_of.3 = f32[64,512]{1,0:T(8,128)S(1)} custom-call(s32[1]{0:T(128)} %bitcast.15.refs_0_, s32[1]{0:T(128)} %bitcast.refs_1_.refs_0_, f32[512,512]{1,0:T(8,128)S(1)} %filter_sent.1.refs_2_, bf16[512,256]{1,0:T(8,128)(2,1)S(1)} %collective-permute-done.18.refs_3_, bf16[512,256]{1,0:T(8,128)(2,1)S(1)} %collective-permute-done.19.refs_4_, ...), custom_call_target="tpu_custom_call" | custom-call | flops 1000000000 | bytes 6815744 | tf_op jit(solution)/shard_map/courses_of/pallas_call | solution.py:58
  82.6 4.0 %collective-permute-done.20 = bf16[64,512]{1,0:T(8,128)(2,1)S(1)} collective-permute-done((bf16[64,512]{1,0:T(8,128)(2,1)S(1)}, bf16[64,512]{1,0:T(8,128)(2,1)S(1)}, u32[]{:S(2)}, u32[]{:S(2)}) %collective-permute-start.20) | collective-permute-done | bytes 65568 | tf_op jit(solution)/shard_map/ppermute | solution.py:476
  86.6 3.3 %collective-permute-start.21 = (bf16[64,512]{1,0:T(8,128)(2,1)S(1)}, bf16[64,512]{1,0:T(8,128)(2,1)S(1)}, u32[]{:S(2)}, u32[]{:S(2)}) collective-permute-start(bf16[64,512]{1,0:T(8,128)(2,1)S(1)} %fusion.5), channel_id=1, source_target_pairs={{0,4},{4,0},{8,12},{12,8},{1,5},{5,1},{9,13},{13,9},{2,6},{6,2},{1... | collective-permute-start | bytes 196616 | tf_op jit(solution)/shard_map/ppermute | solution.py:476
  89.9 0.9 collective-permute-done.21
  90.9 4.0 %collective-permute-start.22 = (bf16[64,512]{1,0:T(8,128)(2,1)S(1)}, bf16[64,512]{1,0:T(8,128)(2,1)S(1)}, u32[]{:S(2)}, u32[]{:S(2)}) collective-permute-start(bf16[64,512]{1,0:T(8,128)(2,1)S(1)} %fusion.2), channel_id=1, source_target_pairs={{0,8},{4,12},{8,0},{12,4},{1,9},{5,13},{9,1},{13,5},{2,10},{6,14},... | collective-permute-start | bytes 196616 | tf_op jit(solution)/shard_map/ppermute | solution.py:476
  94.9 2.4 %collective-permute-done.22 = bf16[64,512]{1,0:T(8,128)(2,1)S(1)} collective-permute-done((bf16[64,512]{1,0:T(8,128)(2,1)S(1)}, bf16[64,512]{1,0:T(8,128)(2,1)S(1)}, u32[]{:S(2)}, u32[]{:S(2)}) %collective-permute-start.22) | collective-permute-done | bytes 65568 | tf_op jit(solution)/shard_map/ppermute | solution.py:476
  97.4 4.0 %collective-permute-start.23 = (bf16[64,512]{1,0:T(8,128)(2,1)S(1)}, bf16[64,512]{1,0:T(8,128)(2,1)S(1)}, u32[]{:S(2)}, u32[]{:S(2)}) collective-permute-start(bf16[64,512]{1,0:T(8,128)(2,1)S(1)} %get-tuple-element.72), channel_id=1, source_target_pairs={{0,1},{1,0},{2,3},{3,2},{4,5},{5,4},{6,7},{7,6},{8,9},{9,8},{10,11... | collective-permute-start | bytes 196616 | tf_op jit(solution)/shard_map/ppermute | solution.py:476
  101.3 2.2 %collective-permute-done.23 = bf16[64,512]{1,0:T(8,128)(2,1)S(1)} collective-permute-done((bf16[64,512]{1,0:T(8,128)(2,1)S(1)}, bf16[64,512]{1,0:T(8,128)(2,1)S(1)}, u32[]{:S(2)}, u32[]{:S(2)}) %collective-permute-start.23) | collective-permute-done | bytes 65568 | tf_op jit(solution)/shard_map/ppermute | solution.py:476
  103.6 2.3 %collective-permute-start.24 = (bf16[64,512]{1,0:T(8,128)(2,1)S(1)}, bf16[64,512]{1,0:T(8,128)(2,1)S(1)}, u32[]{:S(2)}, u32[]{:S(2)}) collective-permute-start(bf16[64,512]{1,0:T(8,128)(2,1)S(1)} %fusion.3), channel_id=1, source_target_pairs={{0,2},{1,3},{2,0},{3,1},{4,6},{5,7},{6,4},{7,5},{8,10},{9,11},{10,... | collective-permute-start | bytes 196616 | tf_op jit(solution)/shard_map/ppermute | solution.py:476
  105.9 3.0 %collective-permute-done.24 = bf16[64,512]{1,0:T(8,128)(2,1)S(1)} collective-permute-done((bf16[64,512]{1,0:T(8,128)(2,1)S(1)}, bf16[64,512]{1,0:T(8,128)(2,1)S(1)}, u32[]{:S(2)}, u32[]{:S(2)}) %collective-permute-start.24) | collective-permute-done | bytes 65568 | tf_op jit(solution)/shard_map/ppermute | solution.py:476
  108.9 1.9 %second_gradient.1 = (bf16[512,512]{1,0:T(8,128)(2,1)S(1)}, bf16[64,512]{1,0:T(8,128)(2,1)}, f32[1,1]{1,0:T(1,128)}) custom-call(s32[1]{0:T(128)} %bitcast.16.refs_0_, f32[64,512]{1,0:T(8,128)S(1)} %convert_add_fusion.refs_1_, bf16[64,512]{1,0:T(8,128)(2,1)S(1)} %get-tuple-element.49.refs_0_.refs_2_, f32[64,512]{1,0:T(8,128)S(1)} %get-tuple-element.50.refs_4_.refs_3_, ...), custom_call_target="tpu_custom_call" | custom-call | flops 1000000000 | bytes 4521984 | tf_op jit(solution)/shard_map/second_gradient/pallas_call | solution.py:58
  111.1 0.8 copy-done.7
  111.9 1.3 second_fade.1
  113.2 0.8 collective-permute-start.29
  114.0 3.3 %collective-permute-start.28 = (bf16[512,256]{1,0:T(8,128)(2,1)S(1)}, bf16[512,256]{1,0:T(8,128)(2,1)S(1)}, u32[]{:S(2)}, u32[]{:S(2)}) collective-permute-start(bf16[512,256]{1,0:T(8,128)(2,1)S(1)} %get-tuple-element.64), channel_id=1, source_target_pairs={{0,4},{8,12},{4,0},{12,8},{1,5},{9,13},{5,1},{13,9},{2,6},{10,14},... | collective-permute-start | bytes 786440 | tf_op jit(solution)/shard_map/ppermute | solution.py:451
  117.3 0.5 mix_layers.14.refs_3_
  117.8 1.8 %faded_maps.1.refs_4_.refs_2_ = f32[8,512,64]{2,1,0:T(8,128)S(1)} custom-call(f32[8,512,64]{2,1,0:T(8,128)S(1)} %bitcast.22, f32[64,64]{1,0:T(8,128)S(1)} %get-tuple-element.61.refs_1_), custom_call_target="tpu_custom_call" | custom-call | flops 1000000000 | bytes 1064960 | tf_op jit(solution)/shard_map/faded_maps/pallas_call | solution.py:58
  119.7 2.6 %collective-permute-done.25.refs_2_ = bf16[512,512]{1,0:T(8,128)(2,1)S(1)} collective-permute-done((bf16[512,512]{1,0:T(8,128)(2,1)S(1)}, bf16[512,512]{1,0:T(8,128)(2,1)S(1)}, u32[]{:S(2)}, u32[]{:S(2)}) %collective-permute-start.25) | collective-permute-done | bytes 524320 | tf_op jit(solution)/shard_map/ppermute | solution.py:514
  122.7 0.7 collective-permute-start.27
  123.4 2.6 %collective-permute-start.26 = (bf16[512,256]{1,0:T(8,128)(2,1)S(1)}, bf16[512,256]{1,0:T(8,128)(2,1)S(1)}, u32[]{:S(2)}, u32[]{:S(2)}) collective-permute-start(bf16[512,256]{1,0:T(8,128)(2,1)S(1)} %get-tuple-element.62), channel_id=1, source_target_pairs={{0,4},{8,12},{4,0},{12,8},{1,5},{9,13},{5,1},{13,9},{2,6},{10,14},... | collective-permute-start | bytes 786440 | tf_op jit(solution)/shard_map/ppermute | solution.py:451
  126.5 0.7 filter_lanes.7.refs_8_.refs_3_
  127.2 0.5 filter_faces.9
  127.7 1.8 %collective-permute-start.30 = (bf16[1024,128]{1,0:T(8,128)(2,1)S(1)}, bf16[1024,128]{1,0:T(8,128)(2,1)S(1)}, u32[]{:S(2)}, u32[]{:S(2)}) collective-permute-start(bf16[1024,128]{1,0:T(8,128)(2,1)S(1)} %get-tuple-element.68), channel_id=1, source_target_pairs={{0,1},{2,3},{1,0},{3,2},{4,5},{6,7},{5,4},{7,6},{8,9},{10,11},{9,8... | collective-permute-start | bytes 786440 | tf_op jit(solution)/shard_map/ppermute | solution.py:451
  129.5 0.7 collective-permute-start.31
  130.2 0.7 filter_lanes.6.refs_1_
  130.9 4.2 %collective-permute-done.30.refs_2_.refs_4_ = bf16[1024,128]{1,0:T(8,128)(2,1)S(1)} collective-permute-done((bf16[1024,128]{1,0:T(8,128)(2,1)S(1)}, bf16[1024,128]{1,0:T(8,128)(2,1)S(1)}, u32[]{:S(2)}, u32[]{:S(2)}) %collective-permute-start.30) | collective-permute-done | bytes 262176 | tf_op jit(solution)/shard_map/ppermute | solution.py:451
  135.1 0.5 gradient_energy.1
  135.7 14.3 %all_to_all.5.refs_1_ = f32[32,1,128]{2,1,0:T(1,128)S(1)} all-to-all(f32[32,1,128]{2,1,0:T(1,128)S(1)} %get-tuple-element.70), channel_id=1, replica_groups=mesh['gx'=2,'gy'=4,'gz'=4] {'gx','gy','gz'}, dimensions={0} | all-to-all | bytes 32768 | tf_op jit(solution)/shard_map/all_to_all | solution.py:463
  150.0 1.7 %final_maps.1 = f32[8,512,64]{2,1,0:T(8,128)} custom-call(s32[1]{0:T(128)} %bitcast.refs_1_.refs_0_, f32[32,1,128]{2,1,0:T(1,128)S(1)} %all_to_all.5.refs_1_, f32[8,512,64]{2,1,0:T(8,128)S(1)} %faded_maps.1.refs_4_.refs_2_, f32[512,512]{1,0:T(8,128)S(1)} %filter_lanes.7.refs_8_.refs_3_, bf16[1024,128]{1,0:T(8,128)(2,1)S(1)} %collective-permute-done.30.refs_2_.refs_4_, ...), custom_call_target="tpu_custom_call" | custom-call | flops 100000000 | bytes 3948544 | tf_op jit(solution)/shard_map/final_maps/pallas_call | solution.py:58
  (68 shorter events, 6.0 us)
Async XLA Ops:
  0.6 1.6 %copy-start.2 = (f32[64,8,16,32]{0,3,2,1:T(8,128)S(1)}, f32[64,8,16,32]{0,3,2,1:T(8,128)}, u32[]{:S(2)}) copy-start(f32[64,8,16,32]{0,3,2,1:T(8,128)} %param.9) | copy-start | bytes 3145732
  2.7 9.3 %collective-permute-start = (bf16[256,512]{1,0:T(8,128)(2,1)S(1)}, bf16[256,512]{1,0:T(8,128)(2,1)S(1)}, u32[]{:S(2)}, u32[]{:S(2)}) collective-permute-start(bf16[256,512]{1,0:T(8,128)(2,1)S(1)} %get-tuple-element.37.refs_1_), channel_id=1, source_target_pairs={{0,16},{16,0},{1,17},{17,1},{2,18},{18,2},{3,19},{19,3},{4,20},{20... | collective-permute-start | bytes 786440 | tf_op jit(solution)/shard_map/ppermute | solution.py:514
  5.8 10.5 %collective-permute-start.6 = (bf16[256,256]{1,0:T(8,128)(2,1)S(1)}, bf16[256,256]{1,0:T(8,128)(2,1)S(1)}, u32[]{:S(2)}, u32[]{:S(2)}) collective-permute-start(bf16[256,256]{1,0:T(8,128)(2,1)S(1)} %cut_face.5), channel_id=1, source_target_pairs={{4,8},{8,4},{5,9},{9,5},{6,10},{10,6},{7,11},{11,7},{20,24},{24,20... | collective-permute-start | bytes 393224 | tf_op jit(solution)/shard_map/ppermute | solution.py:451
  6.5 9.8 %collective-permute-start.5 = (bf16[256,256]{1,0:T(8,128)(2,1)S(1)}, bf16[256,256]{1,0:T(8,128)(2,1)S(1)}, u32[]{:S(2)}, u32[]{:S(2)}) collective-permute-start(bf16[256,256]{1,0:T(8,128)(2,1)S(1)} %get-tuple-element.42), channel_id=1, source_target_pairs={{0,4},{8,12},{4,0},{12,8},{1,5},{9,13},{5,1},{13,9},{2,6},{10,14},... | collective-permute-start | bytes 393224 | tf_op jit(solution)/shard_map/ppermute | solution.py:451
  9.6 6.7 %copy-start.4 = (bf16[1024,256]{1,0:T(8,128)(2,1)S(1)}, bf16[1024,256]{1,0:T(8,128)(2,1)}, u32[]{:S(2)}) copy-start(bf16[1024,256]{1,0:T(8,128)(2,1)} %constant.40.clone.refs_5_) | copy-start | bytes 1572868
  12.3 6.6 %copy-start.1 = (bf16[1024,512]{1,0:T(8,128)(2,1)S(1)}, bf16[1024,512]{1,0:T(8,128)(2,1)}, u32[]{:S(2)}) copy-start(bf16[1024,512]{1,0:T(8,128)(2,1)} %constant.41.clone.refs_4_) | copy-start | bytes 3145732
  12.3 8.6 %copy-start.5 = (bf16[256,512]{1,0:T(8,128)(2,1)S(1)}, bf16[256,512]{1,0:T(8,128)(2,1)}, u32[]{:S(2)}) copy-start(bf16[256,512]{1,0:T(8,128)(2,1)} %constant.42.clone.refs_4_.refs_5_.refs_6_) | copy-start | bytes 786436
  12.4 8.6 %collective-permute-start.2 = (bf16[256,256]{1,0:T(8,128)(2,1)S(1)}, bf16[256,256]{1,0:T(8,128)(2,1)S(1)}, u32[]{:S(2)}, u32[]{:S(2)}) collective-permute-start(bf16[256,256]{1,0:T(8,128)(2,1)S(1)} %cut_face.4), channel_id=1, source_target_pairs={{4,8},{8,4},{5,9},{9,5},{6,10},{10,6},{7,11},{11,7},{20,24},{24,20... | collective-permute-start | bytes 393224 | tf_op jit(solution)/shard_map/ppermute | solution.py:451
  13.2 7.8 %collective-permute-start.1 = (bf16[256,256]{1,0:T(8,128)(2,1)S(1)}, bf16[256,256]{1,0:T(8,128)(2,1)S(1)}, u32[]{:S(2)}, u32[]{:S(2)}) collective-permute-start(bf16[256,256]{1,0:T(8,128)(2,1)S(1)} %get-tuple-element.38), channel_id=1, source_target_pairs={{0,4},{8,12},{4,0},{12,8},{1,5},{9,13},{5,1},{13,9},{2,6},{10,14},... | collective-permute-start | bytes 393224 | tf_op jit(solution)/shard_map/ppermute | solution.py:451
  16.6 4.3 %collective-permute-start.7 = (bf16[256,128]{1,0:T(8,128)(2,1)S(1)}, bf16[256,128]{1,0:T(8,128)(2,1)S(1)}, u32[]{:S(2)}, u32[]{:S(2)}) collective-permute-start(bf16[256,128]{1,0:T(8,128)(2,1)S(1)} %get-tuple-element.44), channel_id=1, source_target_pairs={{0,1},{2,3},{1,0},{3,2},{4,5},{6,7},{5,4},{7,6},{8,9},{10,11},{9,8... | collective-permute-start | bytes 196616 | tf_op jit(solution)/shard_map/ppermute | solution.py:451
  18.3 2.7 %collective-permute-start.8 = (bf16[256,128]{1,0:T(8,128)(2,1)S(1)}, bf16[256,128]{1,0:T(8,128)(2,1)S(1)}, u32[]{:S(2)}, u32[]{:S(2)}) collective-permute-start(bf16[256,128]{1,0:T(8,128)(2,1)S(1)} %get-tuple-element.45), channel_id=1, source_target_pairs={{1,2},{2,1},{5,6},{6,5},{9,10},{10,9},{13,14},{14,13},{17,18},{18,... | collective-permute-start | bytes 196616 | tf_op jit(solution)/shard_map/ppermute | solution.py:451
  21.3 8.6 %collective-permute-start.9 = (bf16[256,512]{1,0:T(8,128)(2,1)S(1)}, bf16[256,512]{1,0:T(8,128)(2,1)S(1)}, u32[]{:S(2)}, u32[]{:S(2)}) collective-permute-start(bf16[256,512]{1,0:T(8,128)(2,1)S(1)} %whole_gradient.1.refs_1_), channel_id=1, source_target_pairs={{0,16},{16,0},{1,17},{17,1},{2,18},{18,2},{3,19},{19,3},{4,20},{20... | collective-permute-start | bytes 786440 | tf_op jit(solution)/shard_map/ppermute | solution.py:514
  22.9 7.2 %copy-start = (bf16[8,16,32,512]{3,2,1,0:T(8,128)(2,1)S(1)}, bf16[8,16,32,512]{3,2,1,0:T(8,128)(2,1)}, u32[]{:S(2)}) copy-start(bf16[8,16,32,512]{3,2,1,0:T(8,128)(2,1)} %param.8) | copy-start | bytes 12582916
  23.2 6.9 %collective-permute-start.3 = (bf16[256,128]{1,0:T(8,128)(2,1)S(1)}, bf16[256,128]{1,0:T(8,128)(2,1)S(1)}, u32[]{:S(2)}, u32[]{:S(2)}) collective-permute-start(bf16[256,128]{1,0:T(8,128)(2,1)S(1)} %get-tuple-element.40), channel_id=1, source_target_pairs={{0,1},{2,3},{1,0},{3,2},{4,5},{6,7},{5,4},{7,6},{8,9},{10,11},{9,8... | collective-permute-start | bytes 196616 | tf_op jit(solution)/shard_map/ppermute | solution.py:451
  27.8 2.3 %collective-permute-start.4 = (bf16[256,128]{1,0:T(8,128)(2,1)S(1)}, bf16[256,128]{1,0:T(8,128)(2,1)S(1)}, u32[]{:S(2)}, u32[]{:S(2)}) collective-permute-start(bf16[256,128]{1,0:T(8,128)(2,1)S(1)} %get-tuple-element.41), channel_id=1, source_target_pairs={{1,2},{2,1},{5,6},{6,5},{9,10},{10,9},{13,14},{14,13},{17,18},{18,... | collective-permute-start | bytes 196616 | tf_op jit(solution)/shard_map/ppermute | solution.py:451
  30.1 41.0 %slice-start = ((s8[6291456]{0:T(1024)(128)(4,1)}), s8[4194304]{0:T(1024)(128)(4,1)S(1)}, s32[]{:S(2)}) async-start(s8[6291456]{0:T(1024)(128)(4,1)} %bitcast.23), calls=%async_computation.1 | async-start | bytes 8388608
  31.9 4.3 %collective-permute-start.10 = (bf16[64,512]{1,0:T(8,128)(2,1)S(1)}, bf16[64,512]{1,0:T(8,128)(2,1)S(1)}, u32[]{:S(2)}, u32[]{:S(2)}) collective-permute-start(bf16[64,512]{1,0:T(8,128)(2,1)S(1)} %reduce-precision_convert_fusion.1), channel_id=1, source_target_pairs={{0,16},{16,0},{1,17},{17,1},{2,18},{18,2},{3,19},{19,3},{4,20},{20... | collective-permute-start | bytes 196616 | tf_op jit(solution)/shard_map/ppermute | solution.py:476
  36.2 1.3 collective-permute-start.11
  37.6 4.3 %collective-permute-start.12 = (bf16[64,512]{1,0:T(8,128)(2,1)S(1)}, bf16[64,512]{1,0:T(8,128)(2,1)S(1)}, u32[]{:S(2)}, u32[]{:S(2)}) collective-permute-start(bf16[64,512]{1,0:T(8,128)(2,1)S(1)} %fusion), channel_id=1, source_target_pairs={{0,8},{4,12},{8,0},{12,4},{1,9},{5,13},{9,1},{13,5},{2,10},{6,14},... | collective-permute-start | bytes 196616 | tf_op jit(solution)/shard_map/ppermute | solution.py:476
  42.0 6.5 %collective-permute-start.13 = (bf16[64,512]{1,0:T(8,128)(2,1)S(1)}, bf16[64,512]{1,0:T(8,128)(2,1)S(1)}, u32[]{:S(2)}, u32[]{:S(2)}) collective-permute-start(bf16[64,512]{1,0:T(8,128)(2,1)S(1)} %get-tuple-element.74), channel_id=1, source_target_pairs={{0,1},{1,0},{2,3},{3,2},{4,5},{5,4},{6,7},{7,6},{8,9},{9,8},{10,11... | collective-permute-start | bytes 196616 | tf_op jit(solution)/shard_map/ppermute | solution.py:476
  48.4 5.8 %collective-permute-start.14 = (bf16[64,512]{1,0:T(8,128)(2,1)S(1)}, bf16[64,512]{1,0:T(8,128)(2,1)S(1)}, u32[]{:S(2)}, u32[]{:S(2)}) collective-permute-start(bf16[64,512]{1,0:T(8,128)(2,1)S(1)} %fusion.1), channel_id=1, source_target_pairs={{0,2},{1,3},{2,0},{3,1},{4,6},{5,7},{6,4},{7,5},{8,10},{9,11},{10,... | collective-permute-start | bytes 196616 | tf_op jit(solution)/shard_map/ppermute | solution.py:476
  54.3 16.8 %slice-start.1 = ((s8[6291456]{0:T(1024)(128)(4,1)}), s8[2097152]{0:T(1024)(128)(4,1)S(1)}, s32[]{:S(2)}) async-start(s8[6291456]{0:T(1024)(128)(4,1)} %bitcast.23), calls=%async_computation.2 | async-start | bytes 4194304
  54.3 16.8 %copy-start.6 = (bf16[4,1024,512]{2,1,0:T(8,128)(2,1)S(1)}, bf16[4,1024,512]{2,1,0:T(8,128)(2,1)}, u32[]{:S(2)}) copy-start(bf16[4,1024,512]{2,1,0:T(8,128)(2,1)} %constant.44.clone.refs_3_) | copy-start | bytes 12582916
  55.7 10.8 %collective-permute-start.15 = (bf16[512,512]{1,0:T(8,128)(2,1)S(1)}, bf16[512,512]{1,0:T(8,128)(2,1)S(1)}, u32[]{:S(2)}, u32[]{:S(2)}) collective-permute-start(bf16[512,512]{1,0:T(8,128)(2,1)S(1)} %get-tuple-element.46.refs_1_), channel_id=1, source_target_pairs={{0,16},{16,0},{1,17},{17,1},{2,18},{18,2},{3,19},{19,3},{4,20},{20... | collective-permute-start | bytes 1572872 | tf_op jit(solution)/shard_map/ppermute | solution.py:514
  67.5 3.8 %collective-permute-start.17 = (bf16[512,512]{1,0:T(8,128)(2,1)S(1)}, bf16[512,512]{1,0:T(8,128)(2,1)S(1)}, u32[]{:S(2)}, u32[]{:S(2)}) collective-permute-start(bf16[512,512]{1,0:T(8,128)(2,1)S(1)} %get-tuple-element.51.refs_3_), channel_id=1, source_target_pairs={{4,8},{8,4},{5,9},{9,5},{6,10},{10,6},{7,11},{11,7},{20,24},{24,20... | collective-permute-start | bytes 1572872 | tf_op jit(solution)/shard_map/ppermute | solution.py:451
  68.2 4.4 %collective-permute-start.16 = (bf16[512,512]{1,0:T(8,128)(2,1)S(1)}, bf16[512,512]{1,0:T(8,128)(2,1)S(1)}, u32[]{:S(2)}, u32[]{:S(2)}) collective-permute-start(bf16[512,512]{1,0:T(8,128)(2,1)S(1)} %get-tuple-element.51.refs_3_), channel_id=1, source_target_pairs={{0,4},{8,12},{4,0},{12,8},{1,5},{9,13},{5,1},{13,9},{2,6},{10,14},... | collective-permute-start | bytes 1572872 | tf_op jit(solution)/shard_map/ppermute | solution.py:451
  73.7 6.4 %collective-permute-start.18 = (bf16[512,256]{1,0:T(8,128)(2,1)S(1)}, bf16[512,256]{1,0:T(8,128)(2,1)S(1)}, u32[]{:S(2)}, u32[]{:S(2)}) collective-permute-start(bf16[512,256]{1,0:T(8,128)(2,1)S(1)} %get-tuple-element.53.refs_1_), channel_id=1, source_target_pairs={{0,1},{2,3},{1,0},{3,2},{4,5},{6,7},{5,4},{7,6},{8,9},{10,11},{9,8... | collective-permute-start | bytes 786440 | tf_op jit(solution)/shard_map/ppermute | solution.py:451
  74.2 5.9 %collective-permute-start.19 = (bf16[512,256]{1,0:T(8,128)(2,1)S(1)}, bf16[512,256]{1,0:T(8,128)(2,1)S(1)}, u32[]{:S(2)}, u32[]{:S(2)}) collective-permute-start(bf16[512,256]{1,0:T(8,128)(2,1)S(1)} %get-tuple-element.54.refs_2_), channel_id=1, source_target_pairs={{1,2},{2,1},{5,6},{6,5},{9,10},{10,9},{13,14},{14,13},{17,18},{18,... | collective-permute-start | bytes 786440 | tf_op jit(solution)/shard_map/ppermute | solution.py:451
  82.3 4.3 %collective-permute-start.20 = (bf16[64,512]{1,0:T(8,128)(2,1)S(1)}, bf16[64,512]{1,0:T(8,128)(2,1)S(1)}, u32[]{:S(2)}, u32[]{:S(2)}) collective-permute-start(bf16[64,512]{1,0:T(8,128)(2,1)S(1)} %reduce-precision_convert_fusion), channel_id=1, source_target_pairs={{0,16},{16,0},{1,17},{17,1},{2,18},{18,2},{3,19},{19,3},{4,20},{20... | collective-permute-start | bytes 196616 | tf_op jit(solution)/shard_map/ppermute | solution.py:476
  86.6 4.2 %collective-permute-start.21 = (bf16[64,512]{1,0:T(8,128)(2,1)S(1)}, bf16[64,512]{1,0:T(8,128)(2,1)S(1)}, u32[]{:S(2)}, u32[]{:S(2)}) collective-permute-start(bf16[64,512]{1,0:T(8,128)(2,1)S(1)} %fusion.5), channel_id=1, source_target_pairs={{0,4},{4,0},{8,12},{12,8},{1,5},{5,1},{9,13},{13,9},{2,6},{6,2},{1... | collective-permute-start | bytes 196616 | tf_op jit(solution)/shard_map/ppermute | solution.py:476
  90.9 6.5 %collective-permute-start.22 = (bf16[64,512]{1,0:T(8,128)(2,1)S(1)}, bf16[64,512]{1,0:T(8,128)(2,1)S(1)}, u32[]{:S(2)}, u32[]{:S(2)}) collective-permute-start(bf16[64,512]{1,0:T(8,128)(2,1)S(1)} %fusion.2), channel_id=1, source_target_pairs={{0,8},{4,12},{8,0},{12,4},{1,9},{5,13},{9,1},{13,5},{2,10},{6,14},... | collective-permute-start | bytes 196616 | tf_op jit(solution)/shard_map/ppermute | solution.py:476
  97.4 6.2 %collective-permute-start.23 = (bf16[64,512]{1,0:T(8,128)(2,1)S(1)}, bf16[64,512]{1,0:T(8,128)(2,1)S(1)}, u32[]{:S(2)}, u32[]{:S(2)}) collective-permute-start(bf16[64,512]{1,0:T(8,128)(2,1)S(1)} %get-tuple-element.72), channel_id=1, source_target_pairs={{0,1},{1,0},{2,3},{3,2},{4,5},{5,4},{6,7},{7,6},{8,9},{9,8},{10,11... | collective-permute-start | bytes 196616 | tf_op jit(solution)/shard_map/ppermute | solution.py:476
  103.6 5.2 %collective-permute-start.24 = (bf16[64,512]{1,0:T(8,128)(2,1)S(1)}, bf16[64,512]{1,0:T(8,128)(2,1)S(1)}, u32[]{:S(2)}, u32[]{:S(2)}) collective-permute-start(bf16[64,512]{1,0:T(8,128)(2,1)S(1)} %fusion.3), channel_id=1, source_target_pairs={{0,2},{1,3},{2,0},{3,1},{4,6},{5,7},{6,4},{7,5},{8,10},{9,11},{10,... | collective-permute-start | bytes 196616 | tf_op jit(solution)/shard_map/ppermute | solution.py:476
  110.8 11.5 %collective-permute-start.25 = (bf16[512,512]{1,0:T(8,128)(2,1)S(1)}, bf16[512,512]{1,0:T(8,128)(2,1)S(1)}, u32[]{:S(2)}, u32[]{:S(2)}) collective-permute-start(bf16[512,512]{1,0:T(8,128)(2,1)S(1)} %get-tuple-element.56.refs_1_), channel_id=1, source_target_pairs={{0,16},{16,0},{1,17},{17,1},{2,18},{18,2},{3,19},{19,3},{4,20},{20... | collective-permute-start | bytes 1572872 | tf_op jit(solution)/shard_map/ppermute | solution.py:514
  111.1 0.8 copy-start.7
  113.2 4.6 %copy-start.3 = (f32[64,8,16,32]{0,3,2,1:T(8,128)S(1)}, f32[64,8,16,32]{0,3,2,1:T(8,128)}, u32[]{:S(2)}) copy-start(f32[64,8,16,32]{0,3,2,1:T(8,128)} %param.9) | copy-start | bytes 3145732
  113.2 12.8 %collective-permute-start.29 = (bf16[512,256]{1,0:T(8,128)(2,1)S(1)}, bf16[512,256]{1,0:T(8,128)(2,1)S(1)}, u32[]{:S(2)}, u32[]{:S(2)}) collective-permute-start(bf16[512,256]{1,0:T(8,128)(2,1)S(1)} %cut_face.7), channel_id=1, source_target_pairs={{4,8},{8,4},{5,9},{9,5},{6,10},{10,6},{7,11},{11,7},{20,24},{24,20... | collective-permute-start | bytes 786440 | tf_op jit(solution)/shard_map/ppermute | solution.py:451
  114.0 12.0 %collective-permute-start.28 = (bf16[512,256]{1,0:T(8,128)(2,1)S(1)}, bf16[512,256]{1,0:T(8,128)(2,1)S(1)}, u32[]{:S(2)}, u32[]{:S(2)}) collective-permute-start(bf16[512,256]{1,0:T(8,128)(2,1)S(1)} %get-tuple-element.64), channel_id=1, source_target_pairs={{0,4},{8,12},{4,0},{12,8},{1,5},{9,13},{5,1},{13,9},{2,6},{10,14},... | collective-permute-start | bytes 786440 | tf_op jit(solution)/shard_map/ppermute | solution.py:451
  122.7 4.5 %collective-permute-start.27 = (bf16[512,256]{1,0:T(8,128)(2,1)S(1)}, bf16[512,256]{1,0:T(8,128)(2,1)S(1)}, u32[]{:S(2)}, u32[]{:S(2)}) collective-permute-start(bf16[512,256]{1,0:T(8,128)(2,1)S(1)} %cut_face.6), channel_id=1, source_target_pairs={{4,8},{8,4},{5,9},{9,5},{6,10},{10,6},{7,11},{11,7},{20,24},{24,20... | collective-permute-start | bytes 786440 | tf_op jit(solution)/shard_map/ppermute | solution.py:451
  123.4 3.8 %collective-permute-start.26 = (bf16[512,256]{1,0:T(8,128)(2,1)S(1)}, bf16[512,256]{1,0:T(8,128)(2,1)S(1)}, u32[]{:S(2)}, u32[]{:S(2)}) collective-permute-start(bf16[512,256]{1,0:T(8,128)(2,1)S(1)} %get-tuple-element.62), channel_id=1, source_target_pairs={{0,4},{8,12},{4,0},{12,8},{1,5},{9,13},{5,1},{13,9},{2,6},{10,14},... | collective-permute-start | bytes 786440 | tf_op jit(solution)/shard_map/ppermute | solution.py:451
  127.7 7.4 %collective-permute-start.30 = (bf16[1024,128]{1,0:T(8,128)(2,1)S(1)}, bf16[1024,128]{1,0:T(8,128)(2,1)S(1)}, u32[]{:S(2)}, u32[]{:S(2)}) collective-permute-start(bf16[1024,128]{1,0:T(8,128)(2,1)S(1)} %get-tuple-element.68), channel_id=1, source_target_pairs={{0,1},{2,3},{1,0},{3,2},{4,5},{6,7},{5,4},{7,6},{8,9},{10,11},{9,8... | collective-permute-start | bytes 786440 | tf_op jit(solution)/shard_map/ppermute | solution.py:451
  129.5 5.6 %collective-permute-start.31 = (bf16[1024,128]{1,0:T(8,128)(2,1)S(1)}, bf16[1024,128]{1,0:T(8,128)(2,1)S(1)}, u32[]{:S(2)}, u32[]{:S(2)}) collective-permute-start(bf16[1024,128]{1,0:T(8,128)(2,1)S(1)} %get-tuple-element.69), channel_id=1, source_target_pairs={{1,2},{2,1},{5,6},{6,5},{9,10},{10,9},{13,14},{14,13},{17,18},{18,... | collective-permute-start | bytes 786440 | tf_op jit(solution)/shard_map/ppermute | solution.py:451

commit v11 on v10

--- a/solution.py
+++ b/solution.py
@@ -286,12 +286,15 @@
     return call(body, shapes, info, [COUNT, ODD_Z], arrays, flops=10**9, name="courses_of")
 
 
-def write_gradient(info_ref, courses, frames_ref, out, chans, size_y, size_z):
+def write_gradient(info_ref, courses, frames_ref, outs, chans, size_y, size_z):
     plane = size_y * size_z
     for x in range(frames_ref.shape[0] // plane):
         value = dot_nt(courses, frames_ref[x * plane : (x + 1) * plane, :])
         keep = live_lanes(info_ref, x, value.shape, size_y, size_z)
-        out[x * chans : (x + 1) * chans, :] = jnp.where(keep, value, 0.0).astype(BF16)
+        value = jnp.where(keep, value, 0.0).astype(BF16)
+        part = chans // len(outs)
+        for p, out in enumerate(outs):
+            out[x * part : (x + 1) * part, :] = value[p * part : (p + 1) * part]
 
 
 def first_gradient(info, sums, bold, chans, size_y, size_z):
@@ -300,7 +303,7 @@
     def body(info_ref, sums_ref, frames_ref, out, half_ref):
         courses = sums_ref[...].astype(BF16)
         half_ref[...] = courses
-        write_gradient(info_ref, courses, frames_ref, out, chans, size_y, size_z)
+        write_gradient(info_ref, courses, frames_ref, [out], chans, size_y, size_z)
 
     shapes = (shape((cells * chans // (size_y * size_z), size_y * size_z), BF16), shape((chans, frames), BF16))
     return call(body, shapes, info, [COUNT], [sums, bold], flops=10**9, name="first_gradient")
@@ -328,17 +331,18 @@
 def second_gradient(info, change, half1, kept, bold, chans, size_y, size_z, all_cells):
     cells, frames = bold.shape
 
-    def body(info_ref, change_ref, half1_ref, kept_ref, frames_ref, out, half_ref, scale_ref):
+    def body(info_ref, change_ref, half1_ref, kept_ref, frames_ref, one, two, half_ref, scale_ref):
         change = change_ref[...]
         energy = jnp.maximum(total_of(half1_ref[...].astype(F32) * change), 0.0) * (1.0 / all_cells)
         scale = 0.5 * lax.rsqrt(energy + 1e-06)
         scale_ref[...] = scale
         courses = (kept_ref[...] + scale * change).astype(BF16)
         half_ref[...] = courses
-        write_gradient(info_ref, courses, frames_ref, out, chans, size_y, size_z)
+        write_gradient(info_ref, courses, frames_ref, [one, two], chans, size_y, size_z)
 
     shapes = (
-        shape((cells * chans // (size_y * size_z), size_y * size_z), BF16),
+        shape((cells * chans // (2 * size_y * size_z), size_y * size_z), BF16),
+        shape((cells * chans // (2 * size_y * size_z), size_y * size_z), BF16),
         shape((chans, frames), BF16),
         shape((1, 1), F32),
     )
@@ -391,30 +395,34 @@
     return call(body, shape(acc.shape, BF16), info, [ODD_Z], arrays, name="whole_gradient", after=after)
 
 
-def gradient_energy(info, acc, first, second, table, peers, after=()):
+def gradient_energy(info, acc, first, second, table, peers, before=()):
     rows, plane = acc.shape
     tall = min(rows, 128)
 
-    def body(info_ref, start, first_ref, second_ref, weights, out, energy):
+    def body(info_ref, start, first_ref, second_ref, weights, *refs):
+        out, energy = refs[-2:]
         total = jnp.zeros((tall, plane), F32)
         for r in range(0, rows, tall):
             at = slice(r, r + tall)
             value = start[at, :] + swapped_dot(info_ref, ODD_Z, first_ref, [], second_ref, weights, at)
             total = total + value * value
             out[at, :] = value
-        energy[...] = jnp.broadcast_to(total_of(total).reshape(1, 1, 1), energy.shape)
+        value = jnp.broadcast_to(total_of(total).reshape(1, 1, 1), energy.shape)
+        energy[...] = value + refs[0][...] if before else value
 
     shapes = (shape((rows, plane), F32), shape((peers, 1, 128), F32))
-    arrays = [acc, first, second, table]
-    return call(body, shapes, info, [ODD_Z], arrays, name="gradient_energy", after=after)
-
-
-def final_maps(info, energies, base, acc, first, second, table, grad, all_cells):
+    arrays = [acc, first, second, table, *before]
+    return call(body, shapes, info, [ODD_Z], arrays, name="gradient_energy")
+
+
+def final_maps(info, energies, base, acc, first, second, table, grads, all_cells):
     layers, plane, chans = base.shape
-    rows = acc.shape[0]
+    rows = first.shape[0] - acc.shape[0]
     peers = energies.shape[0]
-
-    def body(info_ref, energies_ref, base_ref, start, first_ref, second_ref, weights, grad_ref, out, held, sems):
+    part = chans // len(grads)
+
+    def body(info_ref, energies_ref, base_ref, start, first_ref, second_ref, weights, *refs):
+        *grad_refs, out, held, sems = refs
         energy = energies_ref[0]
         for d in range(1, peers):
             energy = energy + energies_ref[d]
@@ -424,7 +432,8 @@
             at = slice(x * chans, (x + 1) * chans)
             below = slice(rows + x * chans, rows + (x + 1) * chans)
             value = start[at, :] + swapped_dot(info_ref, ODD_Z, first_ref, [], second_ref, weights, below)
-            held[x] = base_ref[x] + (value + scale * grad_ref[at, :]).T
+            grad = jnp.concatenate([ref[x * part : (x + 1) * part, :] for ref in grad_refs], axis=0)
+            held[x] = base_ref[x] + (value + scale * grad).T
             copies.append(pltpu.make_async_copy(held.at[x], out.at[x], sems.at[x]))
             copies[-1].start()
         for copy in copies:
@@ -435,7 +444,7 @@
         shape(base.shape, F32),
         info,
         [ODD_Z],
-        [energies, base, acc, first, second, table, grad],
+        [energies, base, acc, first, second, table, *grads],
         name="final_maps",
         outs=pl.BlockSpec(memory_space=pl.ANY),
         scratch=(pltpu.VMEM(base.shape, F32), pltpu.SemaphoreType.DMA((layers,))),
@@ -572,7 +581,7 @@
         acc2, first, second = along_rest(*along_x(again, [full_x]))
         change = all_courses(acc2, first, second, table_z)
 
-    raw2, half2, scale1 = second_gradient(
+    *raws2, half2, scale1 = second_gradient(
         info, change, half1, kept, bold, chans, size_y, size_z, all_cells
     )
     fades, field1, face1 = second_fade(info, half2, fade1, scale1, once_x, face_y)
@@ -581,12 +590,18 @@
     acc1 = filter_lanes(info, first1, field1, second1, table_own)
     base = faded_maps(info, voxel_maps, fades)
 
-    field2, face2 = along_x(raw2, [full_x], [base])
-    first2, second2 = along_y(field2, face2)
-    ends = swapped(*filter_faces(info, first2, field2, second2, table_ends, below, [acc1]), "gz")
-    acc2 = filter_lanes(info, first2, field2, second2, table_own)
-    grad2, energies = gradient_energy(info, acc2, *ends, table_z, peers)
-    maps = final_maps(info, exchanged(energies), base, acc1, *ends, table_z, grad2, all_cells)
+    fields = [along_x(raws2[0], [full_x]), along_x(raws2[1], [full_x], [base])]
+    faces = [along_y(*field) for field in fields]
+    ends, accs = [], []
+    for p in range(2):
+        (first, second), field = faces[p], fields[p][0]
+        sent = filter_faces(info, first, field, second, table_ends, ((), below)[p == 0], ((), [acc1])[p == 0])
+        ends.append(swapped(*sent, "gz"))
+        accs.append(filter_lanes(info, first, field, second, table_own))
+    grad_one, energies = gradient_energy(info, accs[0], *ends[0], table_z, peers)
+    grad_two, energies = gradient_energy(info, accs[1], *ends[1], table_z, peers, [energies])
+    grads = [grad_one, grad_two]
+    maps = final_maps(info, exchanged(energies), base, acc1, *ends[0], table_z, grads, all_cells)
     maps = maps.reshape(size_x, size_y, size_z, chans)
     return (jnp.transpose(maps, (3, 0, 1, 2)), half2)
 

time: 152 us -> 154 us (1.013)
  starting transfers between devices: 57.9 us -> 64.7 us
  waiting for transfers between devices: 51.7 us -> 47.2 us
  blocking collectives: 14.3 us -> 12.7 us
    ppermute x18 -> x22, starting transfers between devices: 29.9 us -> 34.9 us  [swapped(): got[start] = lax.ppermute((first, second)[start], axis, pairs)]
    ppermute x18 -> x22, waiting for transfers between devices: 11.8 us -> 8.76 us  [swapped(): got[start] = lax.ppermute((first, second)[start], axis, pairs)]
    ppermute x4 -> x5, starting transfers between devices: 5.45 us -> 7.21 us  [along_x(): got = lax.ppermute(block, 'gx', [(0, 1), (1, 0)])]
    all_to_all x1, blocking collectives: 14.3 us -> 12.7 us  [exchanged(): return lax.all_to_all(parts, AXES, 0, 0, tiled=True)]
    ppermute x4 -> x5, waiting for transfers between devices: 13.8 us -> 12.3 us  [along_x(): got = lax.ppermute(block, 'gx', [(0, 1), (1, 0)])]
    pallas_call x34 -> x40, Pallas kernels: 23.1 us -> 23.8 us  [call(): pl.pallas_call(wrapped, out_shape=shapes, in_specs=[pl.BlockSpec(memory_s...]
  transfers between devices with their start and end apart: 32 -> 37, of which waited for: 17 -> 18; matrix products, arithmetic and copies ran while one was open for 0% -> 0% of each run, Pallas kernels for 7% -> 8%
where the time goes in v11:
time: 154 us; the launch traced here: 153 us
  starting transfers between devices  64.7 us (42%)
  waiting for transfers between devices  47.2 us (31%)
  Pallas kernels  23.8 us (15%)
  blocking collectives  12.7 us (8%)
  local copies, waits for them, and re-layouts  2.48 us (2%)
  between operations  2.08 us (1%)
    ppermute x22, starting transfers between devices, swapped(): got[start] = lax.ppermute((first, second)[start], axis, pairs)  34.9 us
    ppermute x10, waiting for transfers between devices, hypercube_sum(): value = value + lax.ppermute(value.astype(BF16), axis, pairs).astype(F32)  26.1 us
    pallas_call x40, Pallas kernels, call(): pl.pallas_call(wrapped, out_shape=shapes, in_specs=[pl.BlockSpec(memory_s...  23.8 us
    ppermute x10, starting transfers between devices, hypercube_sum(): value = value + lax.ppermute(value.astype(BF16), axis, pairs).astype(F32)  22.6 us
    all_to_all x1, blocking collectives, exchanged(): return lax.all_to_all(parts, AXES, 0, 0, tiled=True)  12.7 us
    ppermute x5, waiting for transfers between devices, along_x(): got = lax.ppermute(block, 'gx', [(0, 1), (1, 0)])  12.3 us
    ppermute x22, waiting for transfers between devices, swapped(): got[start] = lax.ppermute((first, second)[start], axis, pairs)  8.76 us
    ppermute x5, starting transfers between devices, along_x(): got = lax.ppermute(block, 'gx', [(0, 1), (1, 0)])  7.21 us
  transfers between devices with their start and end apart: 37, of which 18 were waited for; matrix products, arithmetic and copies ran while one was open for 0% of the time, Pallas kernels for 8%

profile of v11, /device:TPU:0, one launch (start us, length us, event | category | flops | bytes accessed | tf_op | source)
XLA Modules:
  0.0 153.2 jit_solution(7938509372629488404)
XLA Ops:
  0.7 1.6 %copy-done.3 = f32[64,8,16,32]{0,3,2,1:T(8,128)S(1)} copy-done((f32[64,8,16,32]{0,3,2,1:T(8,128)S(1)}, f32[64,8,16,32]{0,3,2,1:T(8,128)}, u32[]{:S(2)}) %copy-start.3) | copy-done | bytes 1048600
  2.7 3.0 %collective-permute-start = (bf16[256,512]{1,0:T(8,128)(2,1)S(1)}, bf16[256,512]{1,0:T(8,128)(2,1)S(1)}, u32[]{:S(2)}, u32[]{:S(2)}) collective-permute-start(bf16[256,512]{1,0:T(8,128)(2,1)S(1)} %get-tuple-element.44.refs_1_), channel_id=1, source_target_pairs={{0,16},{16,0},{1,17},{17,1},{2,18},{18,2},{3,19},{19,3},{4,20},{20... | collective-permute-start | bytes 786440 | tf_op jit(solution)/shard_map/ppermute | solution.py:523
  5.8 0.7 collective-permute-start.6
  6.5 2.9 %collective-permute-start.5 = (bf16[256,256]{1,0:T(8,128)(2,1)S(1)}, bf16[256,256]{1,0:T(8,128)(2,1)S(1)}, u32[]{:S(2)}, u32[]{:S(2)}) collective-permute-start(bf16[256,256]{1,0:T(8,128)(2,1)S(1)} %get-tuple-element.49), channel_id=1, source_target_pairs={{0,4},{8,12},{4,0},{12,8},{1,5},{9,13},{5,1},{13,9},{2,6},{10,14},... | collective-permute-start | bytes 393224 | tf_op jit(solution)/shard_map/ppermute | solution.py:460
  9.7 2.4 %collective-permute-done.refs_2_ = bf16[256,512]{1,0:T(8,128)(2,1)S(1)} collective-permute-done((bf16[256,512]{1,0:T(8,128)(2,1)S(1)}, bf16[256,512]{1,0:T(8,128)(2,1)S(1)}, u32[]{:S(2)}, u32[]{:S(2)}) %collective-permute-start) | collective-permute-done | bytes 262176 | tf_op jit(solution)/shard_map/ppermute | solution.py:523
  12.4 0.8 collective-permute-start.2
  13.2 3.1 %collective-permute-start.1 = (bf16[256,256]{1,0:T(8,128)(2,1)S(1)}, bf16[256,256]{1,0:T(8,128)(2,1)S(1)}, u32[]{:S(2)}, u32[]{:S(2)}) collective-permute-start(bf16[256,256]{1,0:T(8,128)(2,1)S(1)} %get-tuple-element.45), channel_id=1, source_target_pairs={{0,4},{8,12},{4,0},{12,8},{1,5},{9,13},{5,1},{13,9},{2,6},{10,14},... | collective-permute-start | bytes 393224 | tf_op jit(solution)/shard_map/ppermute | solution.py:460
  16.6 1.6 %collective-permute-start.7 = (bf16[256,128]{1,0:T(8,128)(2,1)S(1)}, bf16[256,128]{1,0:T(8,128)(2,1)S(1)}, u32[]{:S(2)}, u32[]{:S(2)}) collective-permute-start(bf16[256,128]{1,0:T(8,128)(2,1)S(1)} %get-tuple-element.51), channel_id=1, source_target_pairs={{0,1},{2,3},{1,0},{3,2},{4,5},{6,7},{5,4},{7,6},{8,9},{10,11},{9,8... | collective-permute-start | bytes 196616 | tf_op jit(solution)/shard_map/ppermute | solution.py:460
  18.3 0.7 collective-permute-start.8
  19.4 1.6 %collective-permute-done.7.refs_2_ = bf16[256,128]{1,0:T(8,128)(2,1)S(1)} collective-permute-done((bf16[256,128]{1,0:T(8,128)(2,1)S(1)}, bf16[256,128]{1,0:T(8,128)(2,1)S(1)}, u32[]{:S(2)}, u32[]{:S(2)}) %collective-permute-start.7) | collective-permute-done | bytes 65568 | tf_op jit(solution)/shard_map/ppermute | solution.py:460
  21.3 1.6 %collective-permute-start.9 = (bf16[256,512]{1,0:T(8,128)(2,1)S(1)}, bf16[256,512]{1,0:T(8,128)(2,1)S(1)}, u32[]{:S(2)}, u32[]{:S(2)}) collective-permute-start(bf16[256,512]{1,0:T(8,128)(2,1)S(1)} %whole_gradient.1.refs_1_), channel_id=1, source_target_pairs={{0,16},{16,0},{1,17},{17,1},{2,18},{18,2},{3,19},{19,3},{4,20},{20... | collective-permute-start | bytes 786440 | tf_op jit(solution)/shard_map/ppermute | solution.py:523
  23.2 4.6 %collective-permute-start.3 = (bf16[256,128]{1,0:T(8,128)(2,1)S(1)}, bf16[256,128]{1,0:T(8,128)(2,1)S(1)}, u32[]{:S(2)}, u32[]{:S(2)}) collective-permute-start(bf16[256,128]{1,0:T(8,128)(2,1)S(1)} %get-tuple-element.47), channel_id=1, source_target_pairs={{0,1},{2,3},{1,0},{3,2},{4,5},{6,7},{5,4},{7,6},{8,9},{10,11},{9,8... | collective-permute-start | bytes 196616 | tf_op jit(solution)/shard_map/ppermute | solution.py:460
  27.8 0.7 collective-permute-start.4
  30.1 1.7 %courses_of.2 = f32[64,512]{1,0:T(8,128)S(1)} custom-call(s32[1]{0:T(128)} %bitcast.13.refs_0_, s32[1]{0:T(128)} %bitcast.refs_1_.refs_0_, f32[256,512]{1,0:T(8,128)S(1)} %filter_lanes.5.refs_2_, bf16[256,128]{1,0:T(8,128)(2,1)S(1)} %collective-permute-done.3.refs_3_, bf16[256,128]{1,0:T(8,128)(2,1)S(1)} %collective-permute-done.4.refs_4_, ...), custom_call_target="tpu_custom_call" | custom-call | flops 1000000000 | bytes 5373952 | tf_op jit(solution)/shard_map/courses_of/pallas_call | solution.py:58
  31.9 0.6 collective-permute-start.10
  32.4 3.7 %collective-permute-done.10 = bf16[64,512]{1,0:T(8,128)(2,1)S(1)} collective-permute-done((bf16[64,512]{1,0:T(8,128)(2,1)S(1)}, bf16[64,512]{1,0:T(8,128)(2,1)S(1)}, u32[]{:S(2)}, u32[]{:S(2)}) %collective-permute-start.10) | collective-permute-done | bytes 65568 | tf_op jit(solution)/shard_map/ppermute | solution.py:485
  36.3 1.2 collective-permute-done.11
  37.8 4.1 %collective-permute-done.12 = bf16[64,512]{1,0:T(8,128)(2,1)S(1)} collective-permute-done((bf16[64,512]{1,0:T(8,128)(2,1)S(1)}, bf16[64,512]{1,0:T(8,128)(2,1)S(1)}, u32[]{:S(2)}, u32[]{:S(2)}) %collective-permute-start.12) | collective-permute-done | bytes 65568 | tf_op jit(solution)/shard_map/ppermute | solution.py:485
  42.0 4.2 %collective-permute-start.13 = (bf16[64,512]{1,0:T(8,128)(2,1)S(1)}, bf16[64,512]{1,0:T(8,128)(2,1)S(1)}, u32[]{:S(2)}, u32[]{:S(2)}) collective-permute-start(bf16[64,512]{1,0:T(8,128)(2,1)S(1)} %get-tuple-element.88), channel_id=1, source_target_pairs={{0,1},{1,0},{2,3},{3,2},{4,5},{5,4},{6,7},{7,6},{8,9},{9,8},{10,11... | collective-permute-start | bytes 196616 | tf_op jit(solution)/shard_map/ppermute | solution.py:485
  46.2 2.2 %collective-permute-done.13 = bf16[64,512]{1,0:T(8,128)(2,1)S(1)} collective-permute-done((bf16[64,512]{1,0:T(8,128)(2,1)S(1)}, bf16[64,512]{1,0:T(8,128)(2,1)S(1)}, u32[]{:S(2)}, u32[]{:S(2)}) %collective-permute-start.13) | collective-permute-done | bytes 65568 | tf_op jit(solution)/shard_map/ppermute | solution.py:485
  48.4 3.6 %collective-permute-start.14 = (bf16[64,512]{1,0:T(8,128)(2,1)S(1)}, bf16[64,512]{1,0:T(8,128)(2,1)S(1)}, u32[]{:S(2)}, u32[]{:S(2)}) collective-permute-start(bf16[64,512]{1,0:T(8,128)(2,1)S(1)} %fusion.1), channel_id=1, source_target_pairs={{0,2},{1,3},{2,0},{3,1},{4,6},{5,7},{6,4},{7,5},{8,10},{9,11},{10,... | collective-permute-start | bytes 196616 | tf_op jit(solution)/shard_map/ppermute | solution.py:485
  52.0 2.2 %collective-permute-done.14 = bf16[64,512]{1,0:T(8,128)(2,1)S(1)} collective-permute-done((bf16[64,512]{1,0:T(8,128)(2,1)S(1)}, bf16[64,512]{1,0:T(8,128)(2,1)S(1)}, u32[]{:S(2)}, u32[]{:S(2)}) %collective-permute-start.14) | collective-permute-done | bytes 65568 | tf_op jit(solution)/shard_map/ppermute | solution.py:485
  54.3 1.4 first_gradient.1
  55.7 0.6 collective-permute-start.15
  56.3 1.0 mix_layers.14
  57.7 8.8 %collective-permute-done.15.refs_1_ = bf16[512,512]{1,0:T(8,128)(2,1)S(1)} collective-permute-done((bf16[512,512]{1,0:T(8,128)(2,1)S(1)}, bf16[512,512]{1,0:T(8,128)(2,1)S(1)}, u32[]{:S(2)}, u32[]{:S(2)}) %collective-permute-start.15) | collective-permute-done | bytes 524320 | tf_op jit(solution)/shard_map/ppermute | solution.py:523
  66.6 1.0 mix_layers.15
  67.5 0.7 collective-permute-start.17
  68.2 2.9 %collective-permute-start.16 = (bf16[512,512]{1,0:T(8,128)(2,1)S(1)}, bf16[512,512]{1,0:T(8,128)(2,1)S(1)}, u32[]{:S(2)}, u32[]{:S(2)}) collective-permute-start(bf16[512,512]{1,0:T(8,128)(2,1)S(1)} %get-tuple-element.58.refs_3_), channel_id=1, source_target_pairs={{0,4},{8,12},{4,0},{12,8},{1,5},{9,13},{5,1},{13,9},{2,6},{10,14},... | collective-permute-start | bytes 1572872 | tf_op jit(solution)/shard_map/ppermute | solution.py:460
  71.4 1.3 collective-permute-done.16.refs_2_
  72.7 1.0 filter_faces.8
  73.7 0.5 collective-permute-start.18
  74.2 0.8 collective-permute-start.19
  75.5 4.6 %collective-permute-done.18.refs_3_ = bf16[512,256]{1,0:T(8,128)(2,1)S(1)} collective-permute-done((bf16[512,256]{1,0:T(8,128)(2,1)S(1)}, bf16[512,256]{1,0:T(8,128)(2,1)S(1)}, u32[]{:S(2)}, u32[]{:S(2)}) %collective-permute-start.18) | collective-permute-done | bytes 262176 | tf_op jit(solution)/shard_map/ppermute | solution.py:460
  80.2 2.1 %courses_of.3 = f32[64,512]{1,0:T(8,128)S(1)} custom-call(s32[1]{0:T(128)} %bitcast.15.refs_0_, s32[1]{0:T(128)} %bitcast.refs_1_.refs_0_, f32[512,512]{1,0:T(8,128)S(1)} %filter_sent.1.refs_2_, bf16[512,256]{1,0:T(8,128)(2,1)S(1)} %collective-permute-done.18.refs_3_, bf16[512,256]{1,0:T(8,128)(2,1)S(1)} %collective-permute-done.19.refs_4_, ...), custom_call_target="tpu_custom_call" | custom-call | flops 1000000000 | bytes 6815744 | tf_op jit(solution)/shard_map/courses_of/pallas_call | solution.py:58
  82.6 4.0 %collective-permute-done.20 = bf16[64,512]{1,0:T(8,128)(2,1)S(1)} collective-permute-done((bf16[64,512]{1,0:T(8,128)(2,1)S(1)}, bf16[64,512]{1,0:T(8,128)(2,1)S(1)}, u32[]{:S(2)}, u32[]{:S(2)}) %collective-permute-start.20) | collective-permute-done | bytes 65568 | tf_op jit(solution)/shard_map/ppermute | solution.py:485
  86.6 3.3 %collective-permute-start.21 = (bf16[64,512]{1,0:T(8,128)(2,1)S(1)}, bf16[64,512]{1,0:T(8,128)(2,1)S(1)}, u32[]{:S(2)}, u32[]{:S(2)}) collective-permute-start(bf16[64,512]{1,0:T(8,128)(2,1)S(1)} %fusion.5), channel_id=1, source_target_pairs={{0,4},{4,0},{8,12},{12,8},{1,5},{5,1},{9,13},{13,9},{2,6},{6,2},{1... | collective-permute-start | bytes 196616 | tf_op jit(solution)/shard_map/ppermute | solution.py:485
  89.9 0.9 collective-permute-done.21
  90.9 4.0 %collective-permute-start.22 = (bf16[64,512]{1,0:T(8,128)(2,1)S(1)}, bf16[64,512]{1,0:T(8,128)(2,1)S(1)}, u32[]{:S(2)}, u32[]{:S(2)}) collective-permute-start(bf16[64,512]{1,0:T(8,128)(2,1)S(1)} %fusion.2), channel_id=1, source_target_pairs={{0,8},{4,12},{8,0},{12,4},{1,9},{5,13},{9,1},{13,5},{2,10},{6,14},... | collective-permute-start | bytes 196616 | tf_op jit(solution)/shard_map/ppermute | solution.py:485
  94.9 2.4 %collective-permute-done.22 = bf16[64,512]{1,0:T(8,128)(2,1)S(1)} collective-permute-done((bf16[64,512]{1,0:T(8,128)(2,1)S(1)}, bf16[64,512]{1,0:T(8,128)(2,1)S(1)}, u32[]{:S(2)}, u32[]{:S(2)}) %collective-permute-start.22) | collective-permute-done | bytes 65568 | tf_op jit(solution)/shard_map/ppermute | solution.py:485
  97.4 4.0 %collective-permute-start.23 = (bf16[64,512]{1,0:T(8,128)(2,1)S(1)}, bf16[64,512]{1,0:T(8,128)(2,1)S(1)}, u32[]{:S(2)}, u32[]{:S(2)}) collective-permute-start(bf16[64,512]{1,0:T(8,128)(2,1)S(1)} %get-tuple-element.86), channel_id=1, source_target_pairs={{0,1},{1,0},{2,3},{3,2},{4,5},{5,4},{6,7},{7,6},{8,9},{9,8},{10,11... | collective-permute-start | bytes 196616 | tf_op jit(solution)/shard_map/ppermute | solution.py:485
  101.3 2.2 %collective-permute-done.23 = bf16[64,512]{1,0:T(8,128)(2,1)S(1)} collective-permute-done((bf16[64,512]{1,0:T(8,128)(2,1)S(1)}, bf16[64,512]{1,0:T(8,128)(2,1)S(1)}, u32[]{:S(2)}, u32[]{:S(2)}) %collective-permute-start.23) | collective-permute-done | bytes 65568 | tf_op jit(solution)/shard_map/ppermute | solution.py:485
  103.6 2.3 %collective-permute-start.24 = (bf16[64,512]{1,0:T(8,128)(2,1)S(1)}, bf16[64,512]{1,0:T(8,128)(2,1)S(1)}, u32[]{:S(2)}, u32[]{:S(2)}) collective-permute-start(bf16[64,512]{1,0:T(8,128)(2,1)S(1)} %fusion.3), channel_id=1, source_target_pairs={{0,2},{1,3},{2,0},{3,1},{4,6},{5,7},{6,4},{7,5},{8,10},{9,11},{10,... | collective-permute-start | bytes 196616 | tf_op jit(solution)/shard_map/ppermute | solution.py:485
  105.9 3.0 %collective-permute-done.24 = bf16[64,512]{1,0:T(8,128)(2,1)S(1)} collective-permute-done((bf16[64,512]{1,0:T(8,128)(2,1)S(1)}, bf16[64,512]{1,0:T(8,128)(2,1)S(1)}, u32[]{:S(2)}, u32[]{:S(2)}) %collective-permute-start.24) | collective-permute-done | bytes 65568 | tf_op jit(solution)/shard_map/ppermute | solution.py:485
  108.9 1.9 %second_gradient.1 = (bf16[256,512]{1,0:T(8,128)(2,1)S(1)}, bf16[256,512]{1,0:T(8,128)(2,1)S(1)}, bf16[64,512]{1,0:T(8,128)(2,1)}, f32[1,1]{1,0:T(1,128)}) custom-call(s32[1]{0:T(128)} %bitcast.16.refs_0_, f32[64,512]{1,0:T(8,128)S(1)} %convert_add_fusion.refs_1_, bf16[64,512]{1,0:T(8,128)(2,1)S(1)} %get-tuple-element.56.refs_0_.refs_2_, ...), custom_call_target="tpu_custom_call" | custom-call | flops 1000000000 | bytes 4521984 | tf_op jit(solution)/shard_map/second_gradient/pallas_call | solution.py:58
  111.1 1.8 %collective-permute-start.30 = (bf16[256,512]{1,0:T(8,128)(2,1)S(1)}, bf16[256,512]{1,0:T(8,128)(2,1)S(1)}, u32[]{:S(2)}, u32[]{:S(2)}) collective-permute-start(bf16[256,512]{1,0:T(8,128)(2,1)S(1)} %get-tuple-element.73.refs_1_), channel_id=1, source_target_pairs={{0,16},{16,0},{1,17},{17,1},{2,18},{18,2},{3,19},{19,3},{4,20},{20... | collective-permute-start | bytes 786440 | tf_op jit(solution)/shard_map/ppermute | solution.py:523
  112.8 0.8 copy-done.7
  113.7 1.3 second_fade.1
  115.0 0.8 collective-permute-start.34
  115.8 3.3 %collective-permute-start.33 = (bf16[512,256]{1,0:T(8,128)(2,1)S(1)}, bf16[512,256]{1,0:T(8,128)(2,1)S(1)}, u32[]{:S(2)}, u32[]{:S(2)}) collective-permute-start(bf16[512,256]{1,0:T(8,128)(2,1)S(1)} %get-tuple-element.76), channel_id=1, source_target_pairs={{0,4},{8,12},{4,0},{12,8},{1,5},{9,13},{5,1},{13,9},{2,6},{10,14},... | collective-permute-start | bytes 786440 | tf_op jit(solution)/shard_map/ppermute | solution.py:460
  119.1 1.8 %faded_maps.1.refs_4_.refs_2_ = f32[8,512,64]{2,1,0:T(8,128)S(1)} custom-call(f32[8,512,64]{2,1,0:T(8,128)S(1)} %bitcast.22, f32[64,64]{1,0:T(8,128)S(1)} %get-tuple-element.68.refs_1_), custom_call_target="tpu_custom_call" | custom-call | flops 1000000000 | bytes 1064960 | tf_op jit(solution)/shard_map/faded_maps/pallas_call | solution.py:58
  121.2 1.1 collective-permute-done.30.refs_2_
  122.5 0.7 collective-permute-start.32
  123.2 2.6 %collective-permute-start.31 = (bf16[256,256]{1,0:T(8,128)(2,1)S(1)}, bf16[256,256]{1,0:T(8,128)(2,1)S(1)}, u32[]{:S(2)}, u32[]{:S(2)}) collective-permute-start(bf16[256,256]{1,0:T(8,128)(2,1)S(1)} %get-tuple-element.74), channel_id=1, source_target_pairs={{0,4},{8,12},{4,0},{12,8},{1,5},{9,13},{5,1},{13,9},{2,6},{10,14},... | collective-permute-start | bytes 393224 | tf_op jit(solution)/shard_map/ppermute | solution.py:460
  126.3 0.7 collective-permute-start.27
  127.0 1.3 collective-permute-start.26
  128.9 0.7 filter_lanes.9.refs_8_.refs_3_
  129.9 1.8 %collective-permute-start.35 = (bf16[768,128]{1,0:T(8,128)(2,1)S(1)}, bf16[768,128]{1,0:T(8,128)(2,1)S(1)}, u32[]{:S(2)}, u32[]{:S(2)}) collective-permute-start(bf16[768,128]{1,0:T(8,128)(2,1)S(1)} %get-tuple-element.80), channel_id=1, source_target_pairs={{0,1},{2,3},{1,0},{3,2},{4,5},{6,7},{5,4},{7,6},{8,9},{10,11},{9,8... | collective-permute-start | bytes 589832 | tf_op jit(solution)/shard_map/ppermute | solution.py:460
  131.7 0.7 collective-permute-start.36
  132.8 2.3 %collective-permute-start.28 = (bf16[256,128]{1,0:T(8,128)(2,1)S(1)}, bf16[256,128]{1,0:T(8,128)(2,1)S(1)}, u32[]{:S(2)}, u32[]{:S(2)}) collective-permute-start(bf16[256,128]{1,0:T(8,128)(2,1)S(1)} %get-tuple-element.71), channel_id=1, source_target_pairs={{0,1},{2,3},{1,0},{3,2},{4,5},{6,7},{5,4},{7,6},{8,9},{10,11},{9,8... | collective-permute-start | bytes 196616 | tf_op jit(solution)/shard_map/ppermute | solution.py:460
  135.1 0.7 collective-permute-start.29
  136.6 0.9 collective-permute-done.35.refs_2_.refs_4_
  138.6 12.7 %all_to_all.5.refs_1_ = f32[32,1,128]{2,1,0:T(1,128)S(1)} all-to-all(f32[32,1,128]{2,1,0:T(1,128)S(1)} %get-tuple-element.83), channel_id=1, replica_groups=mesh['gx'=2,'gy'=4,'gz'=4] {'gx','gy','gz'}, dimensions={0} | all-to-all | bytes 32768 | tf_op jit(solution)/shard_map/all_to_all | solution.py:472
  151.4 1.7 %final_maps.1 = f32[8,512,64]{2,1,0:T(8,128)} custom-call(s32[1]{0:T(128)} %bitcast.refs_1_.refs_0_, f32[32,1,128]{2,1,0:T(1,128)S(1)} %all_to_all.5.refs_1_, f32[8,512,64]{2,1,0:T(8,128)S(1)} %faded_maps.1.refs_4_.refs_2_, f32[512,512]{1,0:T(8,128)S(1)} %filter_lanes.9.refs_8_.refs_3_, bf16[768,128]{1,0:T(8,128)(2,1)S(1)} %collective-permute-done.35.refs_2_.refs_4_, ...), custom_call_target="tpu_custom_call" | custom-call | flops 100000000 | bytes 3817472 | tf_op jit(solution)/shard_map/final_maps/pallas_call | solution.py:58
  (84 shorter events, 9.7 us)
Async XLA Ops:
  0.6 1.6 %copy-start.3 = (f32[64,8,16,32]{0,3,2,1:T(8,128)S(1)}, f32[64,8,16,32]{0,3,2,1:T(8,128)}, u32[]{:S(2)}) copy-start(f32[64,8,16,32]{0,3,2,1:T(8,128)} %param.9) | copy-start | bytes 3145732
  2.7 9.3 %collective-permute-start = (bf16[256,512]{1,0:T(8,128)(2,1)S(1)}, bf16[256,512]{1,0:T(8,128)(2,1)S(1)}, u32[]{:S(2)}, u32[]{:S(2)}) collective-permute-start(bf16[256,512]{1,0:T(8,128)(2,1)S(1)} %get-tuple-element.44.refs_1_), channel_id=1, source_target_pairs={{0,16},{16,0},{1,17},{17,1},{2,18},{18,2},{3,19},{19,3},{4,20},{20... | collective-permute-start | bytes 786440 | tf_op jit(solution)/shard_map/ppermute | solution.py:523
  5.8 10.5 %collective-permute-start.6 = (bf16[256,256]{1,0:T(8,128)(2,1)S(1)}, bf16[256,256]{1,0:T(8,128)(2,1)S(1)}, u32[]{:S(2)}, u32[]{:S(2)}) collective-permute-start(bf16[256,256]{1,0:T(8,128)(2,1)S(1)} %cut_face.6), channel_id=1, source_target_pairs={{4,8},{8,4},{5,9},{9,5},{6,10},{10,6},{7,11},{11,7},{20,24},{24,20... | collective-permute-start | bytes 393224 | tf_op jit(solution)/shard_map/ppermute | solution.py:460
  6.5 9.8 %collective-permute-start.5 = (bf16[256,256]{1,0:T(8,128)(2,1)S(1)}, bf16[256,256]{1,0:T(8,128)(2,1)S(1)}, u32[]{:S(2)}, u32[]{:S(2)}) collective-permute-start(bf16[256,256]{1,0:T(8,128)(2,1)S(1)} %get-tuple-element.49), channel_id=1, source_target_pairs={{0,4},{8,12},{4,0},{12,8},{1,5},{9,13},{5,1},{13,9},{2,6},{10,14},... | collective-permute-start | bytes 393224 | tf_op jit(solution)/shard_map/ppermute | solution.py:460
  9.6 6.7 %copy-start.2 = (bf16[1024,256]{1,0:T(8,128)(2,1)S(1)}, bf16[1024,256]{1,0:T(8,128)(2,1)}, u32[]{:S(2)}) copy-start(bf16[1024,256]{1,0:T(8,128)(2,1)} %constant.40.clone.refs_5_) | copy-start | bytes 1572868
  12.3 6.6 %copy-start.1 = (bf16[1024,512]{1,0:T(8,128)(2,1)S(1)}, bf16[1024,512]{1,0:T(8,128)(2,1)}, u32[]{:S(2)}) copy-start(bf16[1024,512]{1,0:T(8,128)(2,1)} %constant.41.clone.refs_4_) | copy-start | bytes 3145732
  12.3 8.6 %copy-start.5 = (bf16[256,512]{1,0:T(8,128)(2,1)S(1)}, bf16[256,512]{1,0:T(8,128)(2,1)}, u32[]{:S(2)}) copy-start(bf16[256,512]{1,0:T(8,128)(2,1)} %constant.42.clone.refs_4_.refs_5_.refs_6_) | copy-start | bytes 786436
  12.4 8.6 %collective-permute-start.2 = (bf16[256,256]{1,0:T(8,128)(2,1)S(1)}, bf16[256,256]{1,0:T(8,128)(2,1)S(1)}, u32[]{:S(2)}, u32[]{:S(2)}) collective-permute-start(bf16[256,256]{1,0:T(8,128)(2,1)S(1)} %cut_face.5), channel_id=1, source_target_pairs={{4,8},{8,4},{5,9},{9,5},{6,10},{10,6},{7,11},{11,7},{20,24},{24,20... | collective-permute-start | bytes 393224 | tf_op jit(solution)/shard_map/ppermute | solution.py:460
  13.2 7.8 %collective-permute-start.1 = (bf16[256,256]{1,0:T(8,128)(2,1)S(1)}, bf16[256,256]{1,0:T(8,128)(2,1)S(1)}, u32[]{:S(2)}, u32[]{:S(2)}) collective-permute-start(bf16[256,256]{1,0:T(8,128)(2,1)S(1)} %get-tuple-element.45), channel_id=1, source_target_pairs={{0,4},{8,12},{4,0},{12,8},{1,5},{9,13},{5,1},{13,9},{2,6},{10,14},... | collective-permute-start | bytes 393224 | tf_op jit(solution)/shard_map/ppermute | solution.py:460
  16.6 4.3 %collective-permute-start.7 = (bf16[256,128]{1,0:T(8,128)(2,1)S(1)}, bf16[256,128]{1,0:T(8,128)(2,1)S(1)}, u32[]{:S(2)}, u32[]{:S(2)}) collective-permute-start(bf16[256,128]{1,0:T(8,128)(2,1)S(1)} %get-tuple-element.51), channel_id=1, source_target_pairs={{0,1},{2,3},{1,0},{3,2},{4,5},{6,7},{5,4},{7,6},{8,9},{10,11},{9,8... | collective-permute-start | bytes 196616 | tf_op jit(solution)/shard_map/ppermute | solution.py:460
  18.3 2.7 %collective-permute-start.8 = (bf16[256,128]{1,0:T(8,128)(2,1)S(1)}, bf16[256,128]{1,0:T(8,128)(2,1)S(1)}, u32[]{:S(2)}, u32[]{:S(2)}) collective-permute-start(bf16[256,128]{1,0:T(8,128)(2,1)S(1)} %get-tuple-element.52), channel_id=1, source_target_pairs={{1,2},{2,1},{5,6},{6,5},{9,10},{10,9},{13,14},{14,13},{17,18},{18,... | collective-permute-start | bytes 196616 | tf_op jit(solution)/shard_map/ppermute | solution.py:460
  21.3 8.6 %collective-permute-start.9 = (bf16[256,512]{1,0:T(8,128)(2,1)S(1)}, bf16[256,512]{1,0:T(8,128)(2,1)S(1)}, u32[]{:S(2)}, u32[]{:S(2)}) collective-permute-start(bf16[256,512]{1,0:T(8,128)(2,1)S(1)} %whole_gradient.1.refs_1_), channel_id=1, source_target_pairs={{0,16},{16,0},{1,17},{17,1},{2,18},{18,2},{3,19},{19,3},{4,20},{20... | collective-permute-start | bytes 786440 | tf_op jit(solution)/shard_map/ppermute | solution.py:523
  22.9 7.2 %copy-start = (bf16[8,16,32,512]{3,2,1,0:T(8,128)(2,1)S(1)}, bf16[8,16,32,512]{3,2,1,0:T(8,128)(2,1)}, u32[]{:S(2)}) copy-start(bf16[8,16,32,512]{3,2,1,0:T(8,128)(2,1)} %param.8) | copy-start | bytes 12582916
  23.2 6.9 %collective-permute-start.3 = (bf16[256,128]{1,0:T(8,128)(2,1)S(1)}, bf16[256,128]{1,0:T(8,128)(2,1)S(1)}, u32[]{:S(2)}, u32[]{:S(2)}) collective-permute-start(bf16[256,128]{1,0:T(8,128)(2,1)S(1)} %get-tuple-element.47), channel_id=1, source_target_pairs={{0,1},{2,3},{1,0},{3,2},{4,5},{6,7},{5,4},{7,6},{8,9},{10,11},{9,8... | collective-permute-start | bytes 196616 | tf_op jit(solution)/shard_map/ppermute | solution.py:460
  27.8 2.3 %collective-permute-start.4 = (bf16[256,128]{1,0:T(8,128)(2,1)S(1)}, bf16[256,128]{1,0:T(8,128)(2,1)S(1)}, u32[]{:S(2)}, u32[]{:S(2)}) collective-permute-start(bf16[256,128]{1,0:T(8,128)(2,1)S(1)} %get-tuple-element.48), channel_id=1, source_target_pairs={{1,2},{2,1},{5,6},{6,5},{9,10},{10,9},{13,14},{14,13},{17,18},{18,... | collective-permute-start | bytes 196616 | tf_op jit(solution)/shard_map/ppermute | solution.py:460
  30.1 41.0 %slice-start = ((s8[6291456]{0:T(1024)(128)(4,1)}), s8[4194304]{0:T(1024)(128)(4,1)S(1)}, s32[]{:S(2)}) async-start(s8[6291456]{0:T(1024)(128)(4,1)} %bitcast.23), calls=%async_computation.1 | async-start | bytes 8388608
  31.9 4.3 %collective-permute-start.10 = (bf16[64,512]{1,0:T(8,128)(2,1)S(1)}, bf16[64,512]{1,0:T(8,128)(2,1)S(1)}, u32[]{:S(2)}, u32[]{:S(2)}) collective-permute-start(bf16[64,512]{1,0:T(8,128)(2,1)S(1)} %reduce-precision_convert_fusion.1), channel_id=1, source_target_pairs={{0,16},{16,0},{1,17},{17,1},{2,18},{18,2},{3,19},{19,3},{4,20},{20... | collective-permute-start | bytes 196616 | tf_op jit(solution)/shard_map/ppermute | solution.py:485
  36.2 1.3 collective-permute-start.11
  37.6 4.3 %collective-permute-start.12 = (bf16[64,512]{1,0:T(8,128)(2,1)S(1)}, bf16[64,512]{1,0:T(8,128)(2,1)S(1)}, u32[]{:S(2)}, u32[]{:S(2)}) collective-permute-start(bf16[64,512]{1,0:T(8,128)(2,1)S(1)} %fusion), channel_id=1, source_target_pairs={{0,8},{4,12},{8,0},{12,4},{1,9},{5,13},{9,1},{13,5},{2,10},{6,14},... | collective-permute-start | bytes 196616 | tf_op jit(solution)/shard_map/ppermute | solution.py:485
  42.0 6.5 %collective-permute-start.13 = (bf16[64,512]{1,0:T(8,128)(2,1)S(1)}, bf16[64,512]{1,0:T(8,128)(2,1)S(1)}, u32[]{:S(2)}, u32[]{:S(2)}) collective-permute-start(bf16[64,512]{1,0:T(8,128)(2,1)S(1)} %get-tuple-element.88), channel_id=1, source_target_pairs={{0,1},{1,0},{2,3},{3,2},{4,5},{5,4},{6,7},{7,6},{8,9},{9,8},{10,11... | collective-permute-start | bytes 196616 | tf_op jit(solution)/shard_map/ppermute | solution.py:485
  48.4 5.8 %collective-permute-start.14 = (bf16[64,512]{1,0:T(8,128)(2,1)S(1)}, bf16[64,512]{1,0:T(8,128)(2,1)S(1)}, u32[]{:S(2)}, u32[]{:S(2)}) collective-permute-start(bf16[64,512]{1,0:T(8,128)(2,1)S(1)} %fusion.1), channel_id=1, source_target_pairs={{0,2},{1,3},{2,0},{3,1},{4,6},{5,7},{6,4},{7,5},{8,10},{9,11},{10,... | collective-permute-start | bytes 196616 | tf_op jit(solution)/shard_map/ppermute | solution.py:485
  54.3 16.8 %slice-start.1 = ((s8[6291456]{0:T(1024)(128)(4,1)}), s8[2097152]{0:T(1024)(128)(4,1)S(1)}, s32[]{:S(2)}) async-start(s8[6291456]{0:T(1024)(128)(4,1)} %bitcast.23), calls=%async_computation.2 | async-start | bytes 4194304
  54.3 16.8 %copy-start.6 = (bf16[4,1024,512]{2,1,0:T(8,128)(2,1)S(1)}, bf16[4,1024,512]{2,1,0:T(8,128)(2,1)}, u32[]{:S(2)}) copy-start(bf16[4,1024,512]{2,1,0:T(8,128)(2,1)} %constant.44.clone.refs_3_) | copy-start | bytes 12582916
  55.7 10.8 %collective-permute-start.15 = (bf16[512,512]{1,0:T(8,128)(2,1)S(1)}, bf16[512,512]{1,0:T(8,128)(2,1)S(1)}, u32[]{:S(2)}, u32[]{:S(2)}) collective-permute-start(bf16[512,512]{1,0:T(8,128)(2,1)S(1)} %get-tuple-element.53.refs_1_), channel_id=1, source_target_pairs={{0,16},{16,0},{1,17},{17,1},{2,18},{18,2},{3,19},{19,3},{4,20},{20... | collective-permute-start | bytes 1572872 | tf_op jit(solution)/shard_map/ppermute | solution.py:523
  67.5 3.8 %collective-permute-start.17 = (bf16[512,512]{1,0:T(8,128)(2,1)S(1)}, bf16[512,512]{1,0:T(8,128)(2,1)S(1)}, u32[]{:S(2)}, u32[]{:S(2)}) collective-permute-start(bf16[512,512]{1,0:T(8,128)(2,1)S(1)} %get-tuple-element.58.refs_3_), channel_id=1, source_target_pairs={{4,8},{8,4},{5,9},{9,5},{6,10},{10,6},{7,11},{11,7},{20,24},{24,20... | collective-permute-start | bytes 1572872 | tf_op jit(solution)/shard_map/ppermute | solution.py:460
  68.2 4.4 %collective-permute-start.16 = (bf16[512,512]{1,0:T(8,128)(2,1)S(1)}, bf16[512,512]{1,0:T(8,128)(2,1)S(1)}, u32[]{:S(2)}, u32[]{:S(2)}) collective-permute-start(bf16[512,512]{1,0:T(8,128)(2,1)S(1)} %get-tuple-element.58.refs_3_), channel_id=1, source_target_pairs={{0,4},{8,12},{4,0},{12,8},{1,5},{9,13},{5,1},{13,9},{2,6},{10,14},... | collective-permute-start | bytes 1572872 | tf_op jit(solution)/shard_map/ppermute | solution.py:460
  73.7 6.4 %collective-permute-start.18 = (bf16[512,256]{1,0:T(8,128)(2,1)S(1)}, bf16[512,256]{1,0:T(8,128)(2,1)S(1)}, u32[]{:S(2)}, u32[]{:S(2)}) collective-permute-start(bf16[512,256]{1,0:T(8,128)(2,1)S(1)} %get-tuple-element.60.refs_1_), channel_id=1, source_target_pairs={{0,1},{2,3},{1,0},{3,2},{4,5},{6,7},{5,4},{7,6},{8,9},{10,11},{9,8... | collective-permute-start | bytes 786440 | tf_op jit(solution)/shard_map/ppermute | solution.py:460
  74.2 5.9 %collective-permute-start.19 = (bf16[512,256]{1,0:T(8,128)(2,1)S(1)}, bf16[512,256]{1,0:T(8,128)(2,1)S(1)}, u32[]{:S(2)}, u32[]{:S(2)}) collective-permute-start(bf16[512,256]{1,0:T(8,128)(2,1)S(1)} %get-tuple-element.61.refs_2_), channel_id=1, source_target_pairs={{1,2},{2,1},{5,6},{6,5},{9,10},{10,9},{13,14},{14,13},{17,18},{18,... | collective-permute-start | bytes 786440 | tf_op jit(solution)/shard_map/ppermute | solution.py:460
  82.3 4.3 %collective-permute-start.20 = (bf16[64,512]{1,0:T(8,128)(2,1)S(1)}, bf16[64,512]{1,0:T(8,128)(2,1)S(1)}, u32[]{:S(2)}, u32[]{:S(2)}) collective-permute-start(bf16[64,512]{1,0:T(8,128)(2,1)S(1)} %reduce-precision_convert_fusion), channel_id=1, source_target_pairs={{0,16},{16,0},{1,17},{17,1},{2,18},{18,2},{3,19},{19,3},{4,20},{20... | collective-permute-start | bytes 196616 | tf_op jit(solution)/shard_map/ppermute | solution.py:485
  86.6 4.2 %collective-permute-start.21 = (bf16[64,512]{1,0:T(8,128)(2,1)S(1)}, bf16[64,512]{1,0:T(8,128)(2,1)S(1)}, u32[]{:S(2)}, u32[]{:S(2)}) collective-permute-start(bf16[64,512]{1,0:T(8,128)(2,1)S(1)} %fusion.5), channel_id=1, source_target_pairs={{0,4},{4,0},{8,12},{12,8},{1,5},{5,1},{9,13},{13,9},{2,6},{6,2},{1... | collective-permute-start | bytes 196616 | tf_op jit(solution)/shard_map/ppermute | solution.py:485
  90.9 6.5 %collective-permute-start.22 = (bf16[64,512]{1,0:T(8,128)(2,1)S(1)}, bf16[64,512]{1,0:T(8,128)(2,1)S(1)}, u32[]{:S(2)}, u32[]{:S(2)}) collective-permute-start(bf16[64,512]{1,0:T(8,128)(2,1)S(1)} %fusion.2), channel_id=1, source_target_pairs={{0,8},{4,12},{8,0},{12,4},{1,9},{5,13},{9,1},{13,5},{2,10},{6,14},... | collective-permute-start | bytes 196616 | tf_op jit(solution)/shard_map/ppermute | solution.py:485
  97.4 6.2 %collective-permute-start.23 = (bf16[64,512]{1,0:T(8,128)(2,1)S(1)}, bf16[64,512]{1,0:T(8,128)(2,1)S(1)}, u32[]{:S(2)}, u32[]{:S(2)}) collective-permute-start(bf16[64,512]{1,0:T(8,128)(2,1)S(1)} %get-tuple-element.86), channel_id=1, source_target_pairs={{0,1},{1,0},{2,3},{3,2},{4,5},{5,4},{6,7},{7,6},{8,9},{9,8},{10,11... | collective-permute-start | bytes 196616 | tf_op jit(solution)/shard_map/ppermute | solution.py:485
  103.6 5.2 %collective-permute-start.24 = (bf16[64,512]{1,0:T(8,128)(2,1)S(1)}, bf16[64,512]{1,0:T(8,128)(2,1)S(1)}, u32[]{:S(2)}, u32[]{:S(2)}) collective-permute-start(bf16[64,512]{1,0:T(8,128)(2,1)S(1)} %fusion.3), channel_id=1, source_target_pairs={{0,2},{1,3},{2,0},{3,1},{4,6},{5,7},{6,4},{7,5},{8,10},{9,11},{10,... | collective-permute-start | bytes 196616 | tf_op jit(solution)/shard_map/ppermute | solution.py:485
  110.8 15.3 %collective-permute-start.25 = (bf16[256,512]{1,0:T(8,128)(2,1)S(1)}, bf16[256,512]{1,0:T(8,128)(2,1)S(1)}, u32[]{:S(2)}, u32[]{:S(2)}) collective-permute-start(bf16[256,512]{1,0:T(8,128)(2,1)S(1)} %get-tuple-element.63.refs_1_), channel_id=1, source_target_pairs={{0,16},{16,0},{1,17},{17,1},{2,18},{18,2},{3,19},{19,3},{4,20},{20... | collective-permute-start | bytes 786440 | tf_op jit(solution)/shard_map/ppermute | solution.py:523
  111.1 11.2 %collective-permute-start.30 = (bf16[256,512]{1,0:T(8,128)(2,1)S(1)}, bf16[256,512]{1,0:T(8,128)(2,1)S(1)}, u32[]{:S(2)}, u32[]{:S(2)}) collective-permute-start(bf16[256,512]{1,0:T(8,128)(2,1)S(1)} %get-tuple-element.73.refs_1_), channel_id=1, source_target_pairs={{0,16},{16,0},{1,17},{17,1},{2,18},{18,2},{3,19},{19,3},{4,20},{20... | collective-permute-start | bytes 786440 | tf_op jit(solution)/shard_map/ppermute | solution.py:523
  112.8 0.8 copy-start.7
  114.9 4.1 %copy-start.4 = (f32[64,8,16,32]{0,3,2,1:T(8,128)S(1)}, f32[64,8,16,32]{0,3,2,1:T(8,128)}, u32[]{:S(2)}) copy-start(f32[64,8,16,32]{0,3,2,1:T(8,128)} %param.9) | copy-start | bytes 3145732
  115.0 12.0 %collective-permute-start.34 = (bf16[512,256]{1,0:T(8,128)(2,1)S(1)}, bf16[512,256]{1,0:T(8,128)(2,1)S(1)}, u32[]{:S(2)}, u32[]{:S(2)}) collective-permute-start(bf16[512,256]{1,0:T(8,128)(2,1)S(1)} %cut_face.9), channel_id=1, source_target_pairs={{4,8},{8,4},{5,9},{9,5},{6,10},{10,6},{7,11},{11,7},{20,24},{24,20... | collective-permute-start | bytes 786440 | tf_op jit(solution)/shard_map/ppermute | solution.py:460
  115.8 12.6 %collective-permute-start.33 = (bf16[512,256]{1,0:T(8,128)(2,1)S(1)}, bf16[512,256]{1,0:T(8,128)(2,1)S(1)}, u32[]{:S(2)}, u32[]{:S(2)}) collective-permute-start(bf16[512,256]{1,0:T(8,128)(2,1)S(1)} %get-tuple-element.76), channel_id=1, source_target_pairs={{0,4},{8,12},{4,0},{12,8},{1,5},{9,13},{5,1},{13,9},{2,6},{10,14},... | collective-permute-start | bytes 786440 | tf_op jit(solution)/shard_map/ppermute | solution.py:460
  122.5 7.1 %collective-permute-start.32 = (bf16[256,256]{1,0:T(8,128)(2,1)S(1)}, bf16[256,256]{1,0:T(8,128)(2,1)S(1)}, u32[]{:S(2)}, u32[]{:S(2)}) collective-permute-start(bf16[256,256]{1,0:T(8,128)(2,1)S(1)} %cut_face.8), channel_id=1, source_target_pairs={{4,8},{8,4},{5,9},{9,5},{6,10},{10,6},{7,11},{11,7},{20,24},{24,20... | collective-permute-start | bytes 393224 | tf_op jit(solution)/shard_map/ppermute | solution.py:460
  123.2 6.4 %collective-permute-start.31 = (bf16[256,256]{1,0:T(8,128)(2,1)S(1)}, bf16[256,256]{1,0:T(8,128)(2,1)S(1)}, u32[]{:S(2)}, u32[]{:S(2)}) collective-permute-start(bf16[256,256]{1,0:T(8,128)(2,1)S(1)} %get-tuple-element.74), channel_id=1, source_target_pairs={{0,4},{8,12},{4,0},{12,8},{1,5},{9,13},{5,1},{13,9},{2,6},{10,14},... | collective-permute-start | bytes 393224 | tf_op jit(solution)/shard_map/ppermute | solution.py:460
  126.3 6.1 %collective-permute-start.27 = (bf16[256,256]{1,0:T(8,128)(2,1)S(1)}, bf16[256,256]{1,0:T(8,128)(2,1)S(1)}, u32[]{:S(2)}, u32[]{:S(2)}) collective-permute-start(bf16[256,256]{1,0:T(8,128)(2,1)S(1)} %cut_face.7), channel_id=1, source_target_pairs={{4,8},{8,4},{5,9},{9,5},{6,10},{10,6},{7,11},{11,7},{20,24},{24,20... | collective-permute-start | bytes 393224 | tf_op jit(solution)/shard_map/ppermute | solution.py:460
  127.0 5.4 %collective-permute-start.26 = (bf16[256,256]{1,0:T(8,128)(2,1)S(1)}, bf16[256,256]{1,0:T(8,128)(2,1)S(1)}, u32[]{:S(2)}, u32[]{:S(2)}) collective-permute-start(bf16[256,256]{1,0:T(8,128)(2,1)S(1)} %get-tuple-element.69), channel_id=1, source_target_pairs={{0,4},{8,12},{4,0},{12,8},{1,5},{9,13},{5,1},{13,9},{2,6},{10,14},... | collective-permute-start | bytes 393224 | tf_op jit(solution)/shard_map/ppermute | solution.py:460
  129.9 7.6 %collective-permute-start.35 = (bf16[768,128]{1,0:T(8,128)(2,1)S(1)}, bf16[768,128]{1,0:T(8,128)(2,1)S(1)}, u32[]{:S(2)}, u32[]{:S(2)}) collective-permute-start(bf16[768,128]{1,0:T(8,128)(2,1)S(1)} %get-tuple-element.80), channel_id=1, source_target_pairs={{0,1},{2,3},{1,0},{3,2},{4,5},{6,7},{5,4},{7,6},{8,9},{10,11},{9,8... | collective-permute-start | bytes 589832 | tf_op jit(solution)/shard_map/ppermute | solution.py:460
  131.7 5.8 %collective-permute-start.36 = (bf16[768,128]{1,0:T(8,128)(2,1)S(1)}, bf16[768,128]{1,0:T(8,128)(2,1)S(1)}, u32[]{:S(2)}, u32[]{:S(2)}) collective-permute-start(bf16[768,128]{1,0:T(8,128)(2,1)S(1)} %get-tuple-element.81), channel_id=1, source_target_pairs={{1,2},{2,1},{5,6},{6,5},{9,10},{10,9},{13,14},{14,13},{17,18},{18,... | collective-permute-start | bytes 589832 | tf_op jit(solution)/shard_map/ppermute | solution.py:460
  132.8 5.5 %collective-permute-start.28 = (bf16[256,128]{1,0:T(8,128)(2,1)S(1)}, bf16[256,128]{1,0:T(8,128)(2,1)S(1)}, u32[]{:S(2)}, u32[]{:S(2)}) collective-permute-start(bf16[256,128]{1,0:T(8,128)(2,1)S(1)} %get-tuple-element.71), channel_id=1, source_target_pairs={{0,1},{2,3},{1,0},{3,2},{4,5},{6,7},{5,4},{7,6},{8,9},{10,11},{9,8... | collective-permute-start | bytes 196616 | tf_op jit(solution)/shard_map/ppermute | solution.py:460
  135.1 3.1 %collective-permute-start.29 = (bf16[256,128]{1,0:T(8,128)(2,1)S(1)}, bf16[256,128]{1,0:T(8,128)(2,1)S(1)}, u32[]{:S(2)}, u32[]{:S(2)}) collective-permute-start(bf16[256,128]{1,0:T(8,128)(2,1)S(1)} %get-tuple-element.72), channel_id=1, source_target_pairs={{1,2},{2,1},{5,6},{6,5},{9,10},{10,9},{13,14},{14,13},{17,18},{18,... | collective-permute-start | bytes 196616 | tf_op jit(solution)/shard_map/ppermute | solution.py:460

commit v12 on v10

--- a/solution.py
+++ b/solution.py
@@ -442,9 +442,16 @@
     )
 
 
+def swap(face, axis, start):
+    pairs = [(i, i + 1) for i in range(start, lax.axis_size(axis) - 1, 2)]
+    return lax.ppermute(face, axis, pairs + [(j, i) for i, j in pairs])
+
+
 def swapped(first, second, axis, inner_first=False):
     peers = lax.axis_size(axis)
     got = {}
+    if axis == "gz":
+        return swap(first, axis, 1), swap(second, axis, 0)
     for start in (1, 0) if inner_first else (0, 1):
         pairs = [(i, i + 1) for i in range(start, peers - 1, 2)]
         pairs += [(j, i) for i, j in pairs]
@@ -484,7 +491,7 @@
     parts_x, parts_y, parts_z = (lax.axis_size(a) for a in AXES)
     peers = parts_x * parts_y * parts_z
     places = [lax.axis_index(a).astype(jnp.int32) for a in AXES]
-    numbers = [*places, places[1] % 2, places[2] % 2, live_blocks]
+    numbers = [*places, places[1] % 2, 1 - places[2] % 2, live_blocks]
     info = [number.reshape(1) for number in numbers]
     bold = bold_data.reshape(size_x * plane, frames)
     voxel_maps = jnp.transpose(spatial_maps, (1, 2, 3, 0)).reshape(size_x, plane, chans)

time: 152 us -> 154 us (1.013)
  starting transfers between devices: 57.9 us -> 60.7 us
    ppermute x0 -> x8, starting transfers between devices: none -> 19.4 us  [swap(): return lax.ppermute(face, axis, pairs + [(j, i) for i, j in pairs])]
    ppermute x18 -> x10, starting transfers between devices: 29.9 us -> 17.8 us  [swapped(): got[start] = lax.ppermute((first, second)[start], axis, pairs)]
    ppermute x0 -> x8, waiting for transfers between devices: none -> 10.9 us  [swap(): return lax.ppermute(face, axis, pairs + [(j, i) for i, j in pairs])]
    ppermute x18 -> x10, waiting for transfers between devices: 11.8 us -> 1.33 us  [swapped(): got[start] = lax.ppermute((first, second)[start], axis, pairs)]
    ppermute x10, starting transfers between devices: 22.6 us -> 17.9 us  [hypercube_sum(): value = value + lax.ppermute(value.astype(BF16), axis, pairs).astype(F32)]
  transfers between devices with their start and end apart: 32 -> 32, of which waited for: 17 -> 18; matrix products, arithmetic and copies ran while one was open for 0% -> 0% of each run, Pallas kernels for 7% -> 7%
where the time goes in v12:
time: 154 us
  starting transfers between devices  60.7 us (39%)
  waiting for transfers between devices  52.2 us (34%)
  Pallas kernels  23.1 us (15%)
  blocking collectives  13.2 us (9%)
  local copies, waits for them, and re-layouts  2.47 us (2%)
  between operations  1.99 us (1%)
    ppermute x10, waiting for transfers between devices, hypercube_sum(): value = value + lax.ppermute(value.astype(BF16), axis, pairs).astype(F32)  26.3 us
    pallas_call x34, Pallas kernels, call(): pl.pallas_call(wrapped, out_shape=shapes, in_specs=[pl.BlockSpec(memory_s...  23.1 us
    ppermute x8, starting transfers between devices, swap(): return lax.ppermute(face, axis, pairs + [(j, i) for i, j in pairs])  19.4 us
    ppermute x10, starting transfers between devices, hypercube_sum(): value = value + lax.ppermute(value.astype(BF16), axis, pairs).astype(F32)  17.9 us
    ppermute x10, starting transfers between devices, swapped(): got[start] = lax.ppermute((first, second)[start], axis, pairs)  17.8 us
    ppermute x4, waiting for transfers between devices, along_x(): got = lax.ppermute(block, 'gx', [(0, 1), (1, 0)])  13.6 us
    all_to_all x1, blocking collectives, exchanged(): return lax.all_to_all(parts, AXES, 0, 0, tiled=True)  13.2 us
    ppermute x8, waiting for transfers between devices, swap(): return lax.ppermute(face, axis, pairs + [(j, i) for i, j in pairs])  10.9 us
  transfers between devices with their start and end apart: 32, of which 18 were waited for; matrix products, arithmetic and copies ran while one was open for 0% of the time, Pallas kernels for 7%

profile of v12, /device:TPU:0, one launch (start us, length us, event | category | flops | bytes accessed | tf_op | source)
XLA Modules:
  0.0 154.0 jit_solution(13001448715336536997)
XLA Ops:
  0.7 1.6 %copy-done.2 = f32[64,8,16,32]{0,3,2,1:T(8,128)S(1)} copy-done((f32[64,8,16,32]{0,3,2,1:T(8,128)S(1)}, f32[64,8,16,32]{0,3,2,1:T(8,128)}, u32[]{:S(2)}) %copy-start.2) | copy-done | bytes 1048600
  2.7 3.0 %collective-permute-start = (bf16[256,512]{1,0:T(8,128)(2,1)S(1)}, bf16[256,512]{1,0:T(8,128)(2,1)S(1)}, u32[]{:S(2)}, u32[]{:S(2)}) collective-permute-start(bf16[256,512]{1,0:T(8,128)(2,1)S(1)} %get-tuple-element.37.refs_1_), channel_id=1, source_target_pairs={{0,16},{16,0},{1,17},{17,1},{2,18},{18,2},{3,19},{19,3},{4,20},{20... | collective-permute-start | bytes 786440 | tf_op jit(solution)/shard_map/ppermute | solution.py:521
  5.8 0.7 collective-permute-start.6
  6.5 2.9 %collective-permute-start.5 = (bf16[256,256]{1,0:T(8,128)(2,1)S(1)}, bf16[256,256]{1,0:T(8,128)(2,1)S(1)}, u32[]{:S(2)}, u32[]{:S(2)}) collective-permute-start(bf16[256,256]{1,0:T(8,128)(2,1)S(1)} %get-tuple-element.42), channel_id=1, source_target_pairs={{0,4},{8,12},{4,0},{12,8},{1,5},{9,13},{5,1},{13,9},{2,6},{10,14},... | collective-permute-start | bytes 393224 | tf_op jit(solution)/shard_map/ppermute | solution.py:458
  9.7 2.4 %collective-permute-done.refs_2_ = bf16[256,512]{1,0:T(8,128)(2,1)S(1)} collective-permute-done((bf16[256,512]{1,0:T(8,128)(2,1)S(1)}, bf16[256,512]{1,0:T(8,128)(2,1)S(1)}, u32[]{:S(2)}, u32[]{:S(2)}) %collective-permute-start) | collective-permute-done | bytes 262176 | tf_op jit(solution)/shard_map/ppermute | solution.py:521
  12.4 0.8 collective-permute-start.2
  13.2 3.1 %collective-permute-start.1 = (bf16[256,256]{1,0:T(8,128)(2,1)S(1)}, bf16[256,256]{1,0:T(8,128)(2,1)S(1)}, u32[]{:S(2)}, u32[]{:S(2)}) collective-permute-start(bf16[256,256]{1,0:T(8,128)(2,1)S(1)} %get-tuple-element.38), channel_id=1, source_target_pairs={{0,4},{8,12},{4,0},{12,8},{1,5},{9,13},{5,1},{13,9},{2,6},{10,14},... | collective-permute-start | bytes 393224 | tf_op jit(solution)/shard_map/ppermute | solution.py:458
  16.6 0.7 collective-permute-start.7
  17.3 4.5 %collective-permute-start.8 = (bf16[256,128]{1,0:T(8,128)(2,1)S(1)}, bf16[256,128]{1,0:T(8,128)(2,1)S(1)}, u32[]{:S(2)}, u32[]{:S(2)}) collective-permute-start(bf16[256,128]{1,0:T(8,128)(2,1)S(1)} %get-tuple-element.45), channel_id=1, source_target_pairs={{0,1},{2,3},{1,0},{3,2},{4,5},{6,7},{5,4},{7,6},{8,9},{10,11},{9,8... | collective-permute-start | bytes 196616 | tf_op jit(solution)/shard_map/ppermute | solution.py:447
  22.2 1.8 %collective-permute-done.8.refs_3_ = bf16[256,128]{1,0:T(8,128)(2,1)S(1)} collective-permute-done((bf16[256,128]{1,0:T(8,128)(2,1)S(1)}, bf16[256,128]{1,0:T(8,128)(2,1)S(1)}, u32[]{:S(2)}, u32[]{:S(2)}) %collective-permute-start.8) | collective-permute-done | bytes 65568 | tf_op jit(solution)/shard_map/ppermute | solution.py:447
  24.3 1.6 %collective-permute-start.9 = (bf16[256,512]{1,0:T(8,128)(2,1)S(1)}, bf16[256,512]{1,0:T(8,128)(2,1)S(1)}, u32[]{:S(2)}, u32[]{:S(2)}) collective-permute-start(bf16[256,512]{1,0:T(8,128)(2,1)S(1)} %whole_gradient.1.refs_1_), channel_id=1, source_target_pairs={{0,16},{16,0},{1,17},{17,1},{2,18},{18,2},{3,19},{19,3},{4,20},{20... | collective-permute-start | bytes 786440 | tf_op jit(solution)/shard_map/ppermute | solution.py:521
  26.2 0.8 collective-permute-start.3
  27.0 3.9 %collective-permute-start.4 = (bf16[256,128]{1,0:T(8,128)(2,1)S(1)}, bf16[256,128]{1,0:T(8,128)(2,1)S(1)}, u32[]{:S(2)}, u32[]{:S(2)}) collective-permute-start(bf16[256,128]{1,0:T(8,128)(2,1)S(1)} %get-tuple-element.41), channel_id=1, source_target_pairs={{0,1},{2,3},{1,0},{3,2},{4,5},{6,7},{5,4},{7,6},{8,9},{10,11},{9,8... | collective-permute-start | bytes 196616 | tf_op jit(solution)/shard_map/ppermute | solution.py:447
  32.5 0.6 collective-permute-done.4.refs_4_
  33.2 1.7 %courses_of.2 = f32[64,512]{1,0:T(8,128)S(1)} custom-call(s32[1]{0:T(128)} %bitcast.13.refs_0_, s32[1]{0:T(128)} %bitcast.refs_1_.refs_0_, f32[256,512]{1,0:T(8,128)S(1)} %filter_lanes.4.refs_2_, bf16[256,128]{1,0:T(8,128)(2,1)S(1)} %collective-permute-done.3.refs_3_, bf16[256,128]{1,0:T(8,128)(2,1)S(1)} %collective-permute-done.4.refs_4_, ...), custom_call_target="tpu_custom_call" | custom-call | flops 1000000000 | bytes 5373952 | tf_op jit(solution)/shard_map/courses_of/pallas_call | solution.py:58
  34.9 0.6 collective-permute-start.10
  35.5 3.7 %collective-permute-done.10 = bf16[64,512]{1,0:T(8,128)(2,1)S(1)} collective-permute-done((bf16[64,512]{1,0:T(8,128)(2,1)S(1)}, bf16[64,512]{1,0:T(8,128)(2,1)S(1)}, u32[]{:S(2)}, u32[]{:S(2)}) %collective-permute-start.10) | collective-permute-done | bytes 65568 | tf_op jit(solution)/shard_map/ppermute | solution.py:483
  39.4 1.2 collective-permute-done.11
  40.7 4.3 %collective-permute-done.12 = bf16[64,512]{1,0:T(8,128)(2,1)S(1)} collective-permute-done((bf16[64,512]{1,0:T(8,128)(2,1)S(1)}, bf16[64,512]{1,0:T(8,128)(2,1)S(1)}, u32[]{:S(2)}, u32[]{:S(2)}) %collective-permute-start.12) | collective-permute-done | bytes 65568 | tf_op jit(solution)/shard_map/ppermute | solution.py:483
  45.0 2.1 %collective-permute-start.13 = (bf16[64,512]{1,0:T(8,128)(2,1)S(1)}, bf16[64,512]{1,0:T(8,128)(2,1)S(1)}, u32[]{:S(2)}, u32[]{:S(2)}) collective-permute-start(bf16[64,512]{1,0:T(8,128)(2,1)S(1)} %get-tuple-element.74), channel_id=1, source_target_pairs={{0,1},{1,0},{2,3},{3,2},{4,5},{5,4},{6,7},{7,6},{8,9},{9,8},{10,11... | collective-permute-start | bytes 196616 | tf_op jit(solution)/shard_map/ppermute | solution.py:483
  47.1 2.2 %collective-permute-done.13 = bf16[64,512]{1,0:T(8,128)(2,1)S(1)} collective-permute-done((bf16[64,512]{1,0:T(8,128)(2,1)S(1)}, bf16[64,512]{1,0:T(8,128)(2,1)S(1)}, u32[]{:S(2)}, u32[]{:S(2)}) %collective-permute-start.13) | collective-permute-done | bytes 65568 | tf_op jit(solution)/shard_map/ppermute | solution.py:483
  49.4 3.1 %collective-permute-start.14 = (bf16[64,512]{1,0:T(8,128)(2,1)S(1)}, bf16[64,512]{1,0:T(8,128)(2,1)S(1)}, u32[]{:S(2)}, u32[]{:S(2)}) collective-permute-start(bf16[64,512]{1,0:T(8,128)(2,1)S(1)} %fusion.1), channel_id=1, source_target_pairs={{0,2},{1,3},{2,0},{3,1},{4,6},{5,7},{6,4},{7,5},{8,10},{9,11},{10,... | collective-permute-start | bytes 196616 | tf_op jit(solution)/shard_map/ppermute | solution.py:483
  52.5 2.2 %collective-permute-done.14 = bf16[64,512]{1,0:T(8,128)(2,1)S(1)} collective-permute-done((bf16[64,512]{1,0:T(8,128)(2,1)S(1)}, bf16[64,512]{1,0:T(8,128)(2,1)S(1)}, u32[]{:S(2)}, u32[]{:S(2)}) %collective-permute-start.14) | collective-permute-done | bytes 65568 | tf_op jit(solution)/shard_map/ppermute | solution.py:483
  54.8 1.4 first_gradient.1
  56.2 0.6 collective-permute-start.15
  56.7 1.0 mix_layers.12
  58.2 8.9 %collective-permute-done.15.refs_1_ = bf16[512,512]{1,0:T(8,128)(2,1)S(1)} collective-permute-done((bf16[512,512]{1,0:T(8,128)(2,1)S(1)}, bf16[512,512]{1,0:T(8,128)(2,1)S(1)}, u32[]{:S(2)}, u32[]{:S(2)}) %collective-permute-start.15) | collective-permute-done | bytes 524320 | tf_op jit(solution)/shard_map/ppermute | solution.py:521
  67.0 1.0 mix_layers.13
  68.0 0.7 collective-permute-start.17
  68.7 2.2 %collective-permute-start.16 = (bf16[512,512]{1,0:T(8,128)(2,1)S(1)}, bf16[512,512]{1,0:T(8,128)(2,1)S(1)}, u32[]{:S(2)}, u32[]{:S(2)}) collective-permute-start(bf16[512,512]{1,0:T(8,128)(2,1)S(1)} %get-tuple-element.51.refs_3_), channel_id=1, source_target_pairs={{0,4},{8,12},{4,0},{12,8},{1,5},{9,13},{5,1},{13,9},{2,6},{10,14},... | collective-permute-start | bytes 1572872 | tf_op jit(solution)/shard_map/ppermute | solution.py:458
  71.2 1.3 collective-permute-done.16.refs_2_
  72.5 1.0 filter_faces.7
  73.5 0.9 collective-permute-start.18
  74.4 4.5 %collective-permute-start.19 = (bf16[512,256]{1,0:T(8,128)(2,1)S(1)}, bf16[512,256]{1,0:T(8,128)(2,1)S(1)}, u32[]{:S(2)}, u32[]{:S(2)}) collective-permute-start(bf16[512,256]{1,0:T(8,128)(2,1)S(1)} %get-tuple-element.54.refs_2_), channel_id=1, source_target_pairs={{0,1},{2,3},{1,0},{3,2},{4,5},{6,7},{5,4},{7,6},{8,9},{10,11},{9,8... | collective-permute-start | bytes 786440 | tf_op jit(solution)/shard_map/ppermute | solution.py:447
  79.3 3.9 %collective-permute-done.19.refs_4_ = bf16[512,256]{1,0:T(8,128)(2,1)S(1)} collective-permute-done((bf16[512,256]{1,0:T(8,128)(2,1)S(1)}, bf16[512,256]{1,0:T(8,128)(2,1)S(1)}, u32[]{:S(2)}, u32[]{:S(2)}) %collective-permute-start.19) | collective-permute-done | bytes 262176 | tf_op jit(solution)/shard_map/ppermute | solution.py:447
  83.2 2.1 %courses_of.3 = f32[64,512]{1,0:T(8,128)S(1)} custom-call(s32[1]{0:T(128)} %bitcast.15.refs_0_, s32[1]{0:T(128)} %bitcast.refs_1_.refs_0_, f32[512,512]{1,0:T(8,128)S(1)} %filter_sent.1.refs_2_, bf16[512,256]{1,0:T(8,128)(2,1)S(1)} %collective-permute-done.18.refs_3_, bf16[512,256]{1,0:T(8,128)(2,1)S(1)} %collective-permute-done.19.refs_4_, ...), custom_call_target="tpu_custom_call" | custom-call | flops 1000000000 | bytes 6815744 | tf_op jit(solution)/shard_map/courses_of/pallas_call | solution.py:58
  85.3 0.6 collective-permute-start.20
  85.9 3.8 %collective-permute-done.20 = bf16[64,512]{1,0:T(8,128)(2,1)S(1)} collective-permute-done((bf16[64,512]{1,0:T(8,128)(2,1)S(1)}, bf16[64,512]{1,0:T(8,128)(2,1)S(1)}, u32[]{:S(2)}, u32[]{:S(2)}) %collective-permute-start.20) | collective-permute-done | bytes 65568 | tf_op jit(solution)/shard_map/ppermute | solution.py:483
  89.7 3.0 %collective-permute-start.21 = (bf16[64,512]{1,0:T(8,128)(2,1)S(1)}, bf16[64,512]{1,0:T(8,128)(2,1)S(1)}, u32[]{:S(2)}, u32[]{:S(2)}) collective-permute-start(bf16[64,512]{1,0:T(8,128)(2,1)S(1)} %fusion.5), channel_id=1, source_target_pairs={{0,4},{4,0},{8,12},{12,8},{1,5},{5,1},{9,13},{13,9},{2,6},{6,2},{1... | collective-permute-start | bytes 196616 | tf_op jit(solution)/shard_map/ppermute | solution.py:483
  92.7 0.9 collective-permute-done.21
  93.6 4.3 %collective-permute-start.22 = (bf16[64,512]{1,0:T(8,128)(2,1)S(1)}, bf16[64,512]{1,0:T(8,128)(2,1)S(1)}, u32[]{:S(2)}, u32[]{:S(2)}) collective-permute-start(bf16[64,512]{1,0:T(8,128)(2,1)S(1)} %fusion.2), channel_id=1, source_target_pairs={{0,8},{4,12},{8,0},{12,4},{1,9},{5,13},{9,1},{13,5},{2,10},{6,14},... | collective-permute-start | bytes 196616 | tf_op jit(solution)/shard_map/ppermute | solution.py:483
  98.0 2.4 %collective-permute-done.22 = bf16[64,512]{1,0:T(8,128)(2,1)S(1)} collective-permute-done((bf16[64,512]{1,0:T(8,128)(2,1)S(1)}, bf16[64,512]{1,0:T(8,128)(2,1)S(1)}, u32[]{:S(2)}, u32[]{:S(2)}) %collective-permute-start.22) | collective-permute-done | bytes 65568 | tf_op jit(solution)/shard_map/ppermute | solution.py:483
  100.4 2.1 %collective-permute-start.23 = (bf16[64,512]{1,0:T(8,128)(2,1)S(1)}, bf16[64,512]{1,0:T(8,128)(2,1)S(1)}, u32[]{:S(2)}, u32[]{:S(2)}) collective-permute-start(bf16[64,512]{1,0:T(8,128)(2,1)S(1)} %get-tuple-element.72), channel_id=1, source_target_pairs={{0,1},{1,0},{2,3},{3,2},{4,5},{5,4},{6,7},{7,6},{8,9},{9,8},{10,11... | collective-permute-start | bytes 196616 | tf_op jit(solution)/shard_map/ppermute | solution.py:483
  102.5 2.2 %collective-permute-done.23 = bf16[64,512]{1,0:T(8,128)(2,1)S(1)} collective-permute-done((bf16[64,512]{1,0:T(8,128)(2,1)S(1)}, bf16[64,512]{1,0:T(8,128)(2,1)S(1)}, u32[]{:S(2)}, u32[]{:S(2)}) %collective-permute-start.23) | collective-permute-done | bytes 65568 | tf_op jit(solution)/shard_map/ppermute | solution.py:483
  104.8 2.0 %collective-permute-start.24 = (bf16[64,512]{1,0:T(8,128)(2,1)S(1)}, bf16[64,512]{1,0:T(8,128)(2,1)S(1)}, u32[]{:S(2)}, u32[]{:S(2)}) collective-permute-start(bf16[64,512]{1,0:T(8,128)(2,1)S(1)} %fusion.3), channel_id=1, source_target_pairs={{0,2},{1,3},{2,0},{3,1},{4,6},{5,7},{6,4},{7,5},{8,10},{9,11},{10,... | collective-permute-start | bytes 196616 | tf_op jit(solution)/shard_map/ppermute | solution.py:483
  106.8 3.3 %collective-permute-done.24 = bf16[64,512]{1,0:T(8,128)(2,1)S(1)} collective-permute-done((bf16[64,512]{1,0:T(8,128)(2,1)S(1)}, bf16[64,512]{1,0:T(8,128)(2,1)S(1)}, u32[]{:S(2)}, u32[]{:S(2)}) %collective-permute-start.24) | collective-permute-done | bytes 65568 | tf_op jit(solution)/shard_map/ppermute | solution.py:483
  110.0 1.9 %second_gradient.1 = (bf16[512,512]{1,0:T(8,128)(2,1)S(1)}, bf16[64,512]{1,0:T(8,128)(2,1)}, f32[1,1]{1,0:T(1,128)}) custom-call(s32[1]{0:T(128)} %bitcast.16.refs_0_, f32[64,512]{1,0:T(8,128)S(1)} %convert_add_fusion.refs_1_, bf16[64,512]{1,0:T(8,128)(2,1)S(1)} %get-tuple-element.49.refs_0_.refs_2_, f32[64,512]{1,0:T(8,128)S(1)} %get-tuple-element.50.refs_4_.refs_3_, ...), custom_call_target="tpu_custom_call" | custom-call | flops 1000000000 | bytes 4521984 | tf_op jit(solution)/shard_map/second_gradient/pallas_call | solution.py:58
  112.5 0.8 copy-done.7
  113.3 1.3 second_fade.1
  114.6 0.8 collective-permute-start.29
  115.5 3.3 %collective-permute-start.28 = (bf16[512,256]{1,0:T(8,128)(2,1)S(1)}, bf16[512,256]{1,0:T(8,128)(2,1)S(1)}, u32[]{:S(2)}, u32[]{:S(2)}) collective-permute-start(bf16[512,256]{1,0:T(8,128)(2,1)S(1)} %get-tuple-element.64), channel_id=1, source_target_pairs={{0,4},{8,12},{4,0},{12,8},{1,5},{9,13},{5,1},{13,9},{2,6},{10,14},... | collective-permute-start | bytes 786440 | tf_op jit(solution)/shard_map/ppermute | solution.py:458
  118.7 0.5 mix_layers.14.refs_3_
  119.3 1.8 %faded_maps.1.refs_4_.refs_2_ = f32[8,512,64]{2,1,0:T(8,128)S(1)} custom-call(f32[8,512,64]{2,1,0:T(8,128)S(1)} %bitcast.22, f32[64,64]{1,0:T(8,128)S(1)} %get-tuple-element.61.refs_1_), custom_call_target="tpu_custom_call" | custom-call | flops 1000000000 | bytes 1064960 | tf_op jit(solution)/shard_map/faded_maps/pallas_call | solution.py:58
  121.1 2.3 %collective-permute-done.25.refs_2_ = bf16[512,512]{1,0:T(8,128)(2,1)S(1)} collective-permute-done((bf16[512,512]{1,0:T(8,128)(2,1)S(1)}, bf16[512,512]{1,0:T(8,128)(2,1)S(1)}, u32[]{:S(2)}, u32[]{:S(2)}) %collective-permute-start.25) | collective-permute-done | bytes 524320 | tf_op jit(solution)/shard_map/ppermute | solution.py:521
  123.9 0.7 collective-permute-start.27
  124.6 2.6 %collective-permute-start.26 = (bf16[512,256]{1,0:T(8,128)(2,1)S(1)}, bf16[512,256]{1,0:T(8,128)(2,1)S(1)}, u32[]{:S(2)}, u32[]{:S(2)}) collective-permute-start(bf16[512,256]{1,0:T(8,128)(2,1)S(1)} %get-tuple-element.62), channel_id=1, source_target_pairs={{0,4},{8,12},{4,0},{12,8},{1,5},{9,13},{5,1},{13,9},{2,6},{10,14},... | collective-permute-start | bytes 786440 | tf_op jit(solution)/shard_map/ppermute | solution.py:458
  127.7 0.7 filter_lanes.7.refs_8_.refs_3_
  128.9 0.7 collective-permute-start.30
  129.6 3.5 %collective-permute-start.31 = (bf16[1024,128]{1,0:T(8,128)(2,1)S(1)}, bf16[1024,128]{1,0:T(8,128)(2,1)S(1)}, u32[]{:S(2)}, u32[]{:S(2)}) collective-permute-start(bf16[1024,128]{1,0:T(8,128)(2,1)S(1)} %get-tuple-element.69), channel_id=1, source_target_pairs={{0,1},{2,3},{1,0},{3,2},{4,5},{6,7},{5,4},{7,6},{8,9},{10,11},{9,8... | collective-permute-start | bytes 786440 | tf_op jit(solution)/shard_map/ppermute | solution.py:447
  133.1 0.7 filter_lanes.6.refs_1_
  133.8 4.6 %collective-permute-done.31.refs_3_.refs_5_ = bf16[1024,128]{1,0:T(8,128)(2,1)S(1)} collective-permute-done((bf16[1024,128]{1,0:T(8,128)(2,1)S(1)}, bf16[1024,128]{1,0:T(8,128)(2,1)S(1)}, u32[]{:S(2)}, u32[]{:S(2)}) %collective-permute-start.31) | collective-permute-done | bytes 262176 | tf_op jit(solution)/shard_map/ppermute | solution.py:447
  138.4 0.5 gradient_energy.1
  138.9 13.2 %all_to_all.5.refs_1_ = f32[32,1,128]{2,1,0:T(1,128)S(1)} all-to-all(f32[32,1,128]{2,1,0:T(1,128)S(1)} %get-tuple-element.70), channel_id=1, replica_groups=mesh['gx'=2,'gy'=4,'gz'=4] {'gx','gy','gz'}, dimensions={0} | all-to-all | bytes 32768 | tf_op jit(solution)/shard_map/all_to_all | solution.py:470
  152.2 1.7 %final_maps.1 = f32[8,512,64]{2,1,0:T(8,128)} custom-call(s32[1]{0:T(128)} %bitcast.refs_1_.refs_0_, f32[32,1,128]{2,1,0:T(1,128)S(1)} %all_to_all.5.refs_1_, f32[8,512,64]{2,1,0:T(8,128)S(1)} %faded_maps.1.refs_4_.refs_2_, f32[512,512]{1,0:T(8,128)S(1)} %filter_lanes.7.refs_8_.refs_3_, bf16[1024,128]{1,0:T(8,128)(2,1)S(1)} %collective-permute-done.30.refs_2_.refs_4_, ...), custom_call_target="tpu_custom_call" | custom-call | flops 100000000 | bytes 3948544 | tf_op jit(solution)/shard_map/final_maps/pallas_call | solution.py:58
  (68 shorter events, 6.8 us)
Async XLA Ops:
  0.6 1.6 %copy-start.2 = (f32[64,8,16,32]{0,3,2,1:T(8,128)S(1)}, f32[64,8,16,32]{0,3,2,1:T(8,128)}, u32[]{:S(2)}) copy-start(f32[64,8,16,32]{0,3,2,1:T(8,128)} %param.9) | copy-start | bytes 3145732
  2.7 9.3 %collective-permute-start = (bf16[256,512]{1,0:T(8,128)(2,1)S(1)}, bf16[256,512]{1,0:T(8,128)(2,1)S(1)}, u32[]{:S(2)}, u32[]{:S(2)}) collective-permute-start(bf16[256,512]{1,0:T(8,128)(2,1)S(1)} %get-tuple-element.37.refs_1_), channel_id=1, source_target_pairs={{0,16},{16,0},{1,17},{17,1},{2,18},{18,2},{3,19},{19,3},{4,20},{20... | collective-permute-start | bytes 786440 | tf_op jit(solution)/shard_map/ppermute | solution.py:521
  5.8 10.5 %collective-permute-start.6 = (bf16[256,256]{1,0:T(8,128)(2,1)S(1)}, bf16[256,256]{1,0:T(8,128)(2,1)S(1)}, u32[]{:S(2)}, u32[]{:S(2)}) collective-permute-start(bf16[256,256]{1,0:T(8,128)(2,1)S(1)} %cut_face.5), channel_id=1, source_target_pairs={{4,8},{8,4},{5,9},{9,5},{6,10},{10,6},{7,11},{11,7},{20,24},{24,20... | collective-permute-start | bytes 393224 | tf_op jit(solution)/shard_map/ppermute | solution.py:458
  6.5 9.8 %collective-permute-start.5 = (bf16[256,256]{1,0:T(8,128)(2,1)S(1)}, bf16[256,256]{1,0:T(8,128)(2,1)S(1)}, u32[]{:S(2)}, u32[]{:S(2)}) collective-permute-start(bf16[256,256]{1,0:T(8,128)(2,1)S(1)} %get-tuple-element.42), channel_id=1, source_target_pairs={{0,4},{8,12},{4,0},{12,8},{1,5},{9,13},{5,1},{13,9},{2,6},{10,14},... | collective-permute-start | bytes 393224 | tf_op jit(solution)/shard_map/ppermute | solution.py:458
  9.6 6.7 %copy-start.4 = (bf16[1024,256]{1,0:T(8,128)(2,1)S(1)}, bf16[1024,256]{1,0:T(8,128)(2,1)}, u32[]{:S(2)}) copy-start(bf16[1024,256]{1,0:T(8,128)(2,1)} %constant.41.clone.refs_5_) | copy-start | bytes 1572868
  12.3 9.5 %copy-start.1 = (bf16[1024,512]{1,0:T(8,128)(2,1)S(1)}, bf16[1024,512]{1,0:T(8,128)(2,1)}, u32[]{:S(2)}) copy-start(bf16[1024,512]{1,0:T(8,128)(2,1)} %constant.42.clone.refs_4_) | copy-start | bytes 3145732
  12.3 11.7 %copy-start.5 = (bf16[256,512]{1,0:T(8,128)(2,1)S(1)}, bf16[256,512]{1,0:T(8,128)(2,1)}, u32[]{:S(2)}) copy-start(bf16[256,512]{1,0:T(8,128)(2,1)} %constant.43.clone.refs_4_.refs_5_.refs_6_) | copy-start | bytes 786436
  12.4 11.7 %collective-permute-start.2 = (bf16[256,256]{1,0:T(8,128)(2,1)S(1)}, bf16[256,256]{1,0:T(8,128)(2,1)S(1)}, u32[]{:S(2)}, u32[]{:S(2)}) collective-permute-start(bf16[256,256]{1,0:T(8,128)(2,1)S(1)} %cut_face.4), channel_id=1, source_target_pairs={{4,8},{8,4},{5,9},{9,5},{6,10},{10,6},{7,11},{11,7},{20,24},{24,20... | collective-permute-start | bytes 393224 | tf_op jit(solution)/shard_map/ppermute | solution.py:458
  13.2 10.9 %collective-permute-start.1 = (bf16[256,256]{1,0:T(8,128)(2,1)S(1)}, bf16[256,256]{1,0:T(8,128)(2,1)S(1)}, u32[]{:S(2)}, u32[]{:S(2)}) collective-permute-start(bf16[256,256]{1,0:T(8,128)(2,1)S(1)} %get-tuple-element.38), channel_id=1, source_target_pairs={{0,4},{8,12},{4,0},{12,8},{1,5},{9,13},{5,1},{13,9},{2,6},{10,14},... | collective-permute-start | bytes 393224 | tf_op jit(solution)/shard_map/ppermute | solution.py:458
  16.6 5.6 %collective-permute-start.7 = (bf16[256,128]{1,0:T(8,128)(2,1)S(1)}, bf16[256,128]{1,0:T(8,128)(2,1)S(1)}, u32[]{:S(2)}, u32[]{:S(2)}) collective-permute-start(bf16[256,128]{1,0:T(8,128)(2,1)S(1)} %get-tuple-element.44), channel_id=1, source_target_pairs={{1,2},{2,1},{5,6},{6,5},{9,10},{10,9},{13,14},{14,13},{17,18},{18,... | collective-permute-start | bytes 196616 | tf_op jit(solution)/shard_map/ppermute | solution.py:447
  17.3 6.7 %collective-permute-start.8 = (bf16[256,128]{1,0:T(8,128)(2,1)S(1)}, bf16[256,128]{1,0:T(8,128)(2,1)S(1)}, u32[]{:S(2)}, u32[]{:S(2)}) collective-permute-start(bf16[256,128]{1,0:T(8,128)(2,1)S(1)} %get-tuple-element.45), channel_id=1, source_target_pairs={{0,1},{2,3},{1,0},{3,2},{4,5},{6,7},{5,4},{7,6},{8,9},{10,11},{9,8... | collective-permute-start | bytes 196616 | tf_op jit(solution)/shard_map/ppermute | solution.py:447
  24.3 8.0 %collective-permute-start.9 = (bf16[256,512]{1,0:T(8,128)(2,1)S(1)}, bf16[256,512]{1,0:T(8,128)(2,1)S(1)}, u32[]{:S(2)}, u32[]{:S(2)}) collective-permute-start(bf16[256,512]{1,0:T(8,128)(2,1)S(1)} %whole_gradient.1.refs_1_), channel_id=1, source_target_pairs={{0,16},{16,0},{1,17},{17,1},{2,18},{18,2},{3,19},{19,3},{4,20},{20... | collective-permute-start | bytes 786440 | tf_op jit(solution)/shard_map/ppermute | solution.py:521
  25.9 7.3 %copy-start = (bf16[8,16,32,512]{3,2,1,0:T(8,128)(2,1)S(1)}, bf16[8,16,32,512]{3,2,1,0:T(8,128)(2,1)}, u32[]{:S(2)}) copy-start(bf16[8,16,32,512]{3,2,1,0:T(8,128)(2,1)} %param.8) | copy-start | bytes 12582916
  26.2 6.3 %collective-permute-start.3 = (bf16[256,128]{1,0:T(8,128)(2,1)S(1)}, bf16[256,128]{1,0:T(8,128)(2,1)S(1)}, u32[]{:S(2)}, u32[]{:S(2)}) collective-permute-start(bf16[256,128]{1,0:T(8,128)(2,1)S(1)} %get-tuple-element.40), channel_id=1, source_target_pairs={{1,2},{2,1},{5,6},{6,5},{9,10},{10,9},{13,14},{14,13},{17,18},{18,... | collective-permute-start | bytes 196616 | tf_op jit(solution)/shard_map/ppermute | solution.py:447
  27.0 6.2 %collective-permute-start.4 = (bf16[256,128]{1,0:T(8,128)(2,1)S(1)}, bf16[256,128]{1,0:T(8,128)(2,1)S(1)}, u32[]{:S(2)}, u32[]{:S(2)}) collective-permute-start(bf16[256,128]{1,0:T(8,128)(2,1)S(1)} %get-tuple-element.41), channel_id=1, source_target_pairs={{0,1},{2,3},{1,0},{3,2},{4,5},{6,7},{5,4},{7,6},{8,9},{10,11},{9,8... | collective-permute-start | bytes 196616 | tf_op jit(solution)/shard_map/ppermute | solution.py:447
  33.2 37.8 %slice-start = ((s8[6291456]{0:T(1024)(128)(4,1)}), s8[4194304]{0:T(1024)(128)(4,1)S(1)}, s32[]{:S(2)}) async-start(s8[6291456]{0:T(1024)(128)(4,1)} %bitcast.23), calls=%async_computation.1 | async-start | bytes 8388608
  34.9 4.3 %collective-permute-start.10 = (bf16[64,512]{1,0:T(8,128)(2,1)S(1)}, bf16[64,512]{1,0:T(8,128)(2,1)S(1)}, u32[]{:S(2)}, u32[]{:S(2)}) collective-permute-start(bf16[64,512]{1,0:T(8,128)(2,1)S(1)} %reduce-precision_convert_fusion.1), channel_id=1, source_target_pairs={{0,16},{16,0},{1,17},{17,1},{2,18},{18,2},{3,19},{19,3},{4,20},{20... | collective-permute-start | bytes 196616 | tf_op jit(solution)/shard_map/ppermute | solution.py:483
  39.3 1.3 collective-permute-start.11
  40.6 4.3 %collective-permute-start.12 = (bf16[64,512]{1,0:T(8,128)(2,1)S(1)}, bf16[64,512]{1,0:T(8,128)(2,1)S(1)}, u32[]{:S(2)}, u32[]{:S(2)}) collective-permute-start(bf16[64,512]{1,0:T(8,128)(2,1)S(1)} %fusion), channel_id=1, source_target_pairs={{0,8},{4,12},{8,0},{12,4},{1,9},{5,13},{9,1},{13,5},{2,10},{6,14},... | collective-permute-start | bytes 196616 | tf_op jit(solution)/shard_map/ppermute | solution.py:483
  45.0 4.3 %collective-permute-start.13 = (bf16[64,512]{1,0:T(8,128)(2,1)S(1)}, bf16[64,512]{1,0:T(8,128)(2,1)S(1)}, u32[]{:S(2)}, u32[]{:S(2)}) collective-permute-start(bf16[64,512]{1,0:T(8,128)(2,1)S(1)} %get-tuple-element.74), channel_id=1, source_target_pairs={{0,1},{1,0},{2,3},{3,2},{4,5},{5,4},{6,7},{7,6},{8,9},{9,8},{10,11... | collective-permute-start | bytes 196616 | tf_op jit(solution)/shard_map/ppermute | solution.py:483
  49.4 5.3 %collective-permute-start.14 = (bf16[64,512]{1,0:T(8,128)(2,1)S(1)}, bf16[64,512]{1,0:T(8,128)(2,1)S(1)}, u32[]{:S(2)}, u32[]{:S(2)}) collective-permute-start(bf16[64,512]{1,0:T(8,128)(2,1)S(1)} %fusion.1), channel_id=1, source_target_pairs={{0,2},{1,3},{2,0},{3,1},{4,6},{5,7},{6,4},{7,5},{8,10},{9,11},{10,... | collective-permute-start | bytes 196616 | tf_op jit(solution)/shard_map/ppermute | solution.py:483
  54.8 16.2 %slice-start.1 = ((s8[6291456]{0:T(1024)(128)(4,1)}), s8[2097152]{0:T(1024)(128)(4,1)S(1)}, s32[]{:S(2)}) async-start(s8[6291456]{0:T(1024)(128)(4,1)} %bitcast.23), calls=%async_computation.2 | async-start | bytes 4194304
  54.8 16.2 %copy-start.6 = (bf16[4,1024,512]{2,1,0:T(8,128)(2,1)S(1)}, bf16[4,1024,512]{2,1,0:T(8,128)(2,1)}, u32[]{:S(2)}) copy-start(bf16[4,1024,512]{2,1,0:T(8,128)(2,1)} %constant.45.clone.refs_3_) | copy-start | bytes 12582916
  56.2 10.9 %collective-permute-start.15 = (bf16[512,512]{1,0:T(8,128)(2,1)S(1)}, bf16[512,512]{1,0:T(8,128)(2,1)S(1)}, u32[]{:S(2)}, u32[]{:S(2)}) collective-permute-start(bf16[512,512]{1,0:T(8,128)(2,1)S(1)} %get-tuple-element.46.refs_1_), channel_id=1, source_target_pairs={{0,16},{16,0},{1,17},{17,1},{2,18},{18,2},{3,19},{19,3},{4,20},{20... | collective-permute-start | bytes 1572872 | tf_op jit(solution)/shard_map/ppermute | solution.py:521
  68.0 3.1 %collective-permute-start.17 = (bf16[512,512]{1,0:T(8,128)(2,1)S(1)}, bf16[512,512]{1,0:T(8,128)(2,1)S(1)}, u32[]{:S(2)}, u32[]{:S(2)}) collective-permute-start(bf16[512,512]{1,0:T(8,128)(2,1)S(1)} %get-tuple-element.51.refs_3_), channel_id=1, source_target_pairs={{4,8},{8,4},{5,9},{9,5},{6,10},{10,6},{7,11},{11,7},{20,24},{24,20... | collective-permute-start | bytes 1572872 | tf_op jit(solution)/shard_map/ppermute | solution.py:458
  68.7 3.7 %collective-permute-start.16 = (bf16[512,512]{1,0:T(8,128)(2,1)S(1)}, bf16[512,512]{1,0:T(8,128)(2,1)S(1)}, u32[]{:S(2)}, u32[]{:S(2)}) collective-permute-start(bf16[512,512]{1,0:T(8,128)(2,1)S(1)} %get-tuple-element.51.refs_3_), channel_id=1, source_target_pairs={{0,4},{8,12},{4,0},{12,8},{1,5},{9,13},{5,1},{13,9},{2,6},{10,14},... | collective-permute-start | bytes 1572872 | tf_op jit(solution)/shard_map/ppermute | solution.py:458
  73.5 5.8 %collective-permute-start.18 = (bf16[512,256]{1,0:T(8,128)(2,1)S(1)}, bf16[512,256]{1,0:T(8,128)(2,1)S(1)}, u32[]{:S(2)}, u32[]{:S(2)}) collective-permute-start(bf16[512,256]{1,0:T(8,128)(2,1)S(1)} %get-tuple-element.53.refs_1_), channel_id=1, source_target_pairs={{1,2},{2,1},{5,6},{6,5},{9,10},{10,9},{13,14},{14,13},{17,18},{18,... | collective-permute-start | bytes 786440 | tf_op jit(solution)/shard_map/ppermute | solution.py:447
  74.4 8.9 %collective-permute-start.19 = (bf16[512,256]{1,0:T(8,128)(2,1)S(1)}, bf16[512,256]{1,0:T(8,128)(2,1)S(1)}, u32[]{:S(2)}, u32[]{:S(2)}) collective-permute-start(bf16[512,256]{1,0:T(8,128)(2,1)S(1)} %get-tuple-element.54.refs_2_), channel_id=1, source_target_pairs={{0,1},{2,3},{1,0},{3,2},{4,5},{6,7},{5,4},{7,6},{8,9},{10,11},{9,8... | collective-permute-start | bytes 786440 | tf_op jit(solution)/shard_map/ppermute | solution.py:447
  85.3 4.3 %collective-permute-start.20 = (bf16[64,512]{1,0:T(8,128)(2,1)S(1)}, bf16[64,512]{1,0:T(8,128)(2,1)S(1)}, u32[]{:S(2)}, u32[]{:S(2)}) collective-permute-start(bf16[64,512]{1,0:T(8,128)(2,1)S(1)} %reduce-precision_convert_fusion), channel_id=1, source_target_pairs={{0,16},{16,0},{1,17},{17,1},{2,18},{18,2},{3,19},{19,3},{4,20},{20... | collective-permute-start | bytes 196616 | tf_op jit(solution)/shard_map/ppermute | solution.py:483
  89.7 3.9 %collective-permute-start.21 = (bf16[64,512]{1,0:T(8,128)(2,1)S(1)}, bf16[64,512]{1,0:T(8,128)(2,1)S(1)}, u32[]{:S(2)}, u32[]{:S(2)}) collective-permute-start(bf16[64,512]{1,0:T(8,128)(2,1)S(1)} %fusion.5), channel_id=1, source_target_pairs={{0,4},{4,0},{8,12},{12,8},{1,5},{5,1},{9,13},{13,9},{2,6},{6,2},{1... | collective-permute-start | bytes 196616 | tf_op jit(solution)/shard_map/ppermute | solution.py:483
  93.6 6.8 %collective-permute-start.22 = (bf16[64,512]{1,0:T(8,128)(2,1)S(1)}, bf16[64,512]{1,0:T(8,128)(2,1)S(1)}, u32[]{:S(2)}, u32[]{:S(2)}) collective-permute-start(bf16[64,512]{1,0:T(8,128)(2,1)S(1)} %fusion.2), channel_id=1, source_target_pairs={{0,8},{4,12},{8,0},{12,4},{1,9},{5,13},{9,1},{13,5},{2,10},{6,14},... | collective-permute-start | bytes 196616 | tf_op jit(solution)/shard_map/ppermute | solution.py:483
  100.4 4.3 %collective-permute-start.23 = (bf16[64,512]{1,0:T(8,128)(2,1)S(1)}, bf16[64,512]{1,0:T(8,128)(2,1)S(1)}, u32[]{:S(2)}, u32[]{:S(2)}) collective-permute-start(bf16[64,512]{1,0:T(8,128)(2,1)S(1)} %get-tuple-element.72), channel_id=1, source_target_pairs={{0,1},{1,0},{2,3},{3,2},{4,5},{5,4},{6,7},{7,6},{8,9},{9,8},{10,11... | collective-permute-start | bytes 196616 | tf_op jit(solution)/shard_map/ppermute | solution.py:483
  104.8 5.2 %collective-permute-start.24 = (bf16[64,512]{1,0:T(8,128)(2,1)S(1)}, bf16[64,512]{1,0:T(8,128)(2,1)S(1)}, u32[]{:S(2)}, u32[]{:S(2)}) collective-permute-start(bf16[64,512]{1,0:T(8,128)(2,1)S(1)} %fusion.3), channel_id=1, source_target_pairs={{0,2},{1,3},{2,0},{3,1},{4,6},{5,7},{6,4},{7,5},{8,10},{9,11},{10,... | collective-permute-start | bytes 196616 | tf_op jit(solution)/shard_map/ppermute | solution.py:483
  112.0 11.4 %collective-permute-start.25 = (bf16[512,512]{1,0:T(8,128)(2,1)S(1)}, bf16[512,512]{1,0:T(8,128)(2,1)S(1)}, u32[]{:S(2)}, u32[]{:S(2)}) collective-permute-start(bf16[512,512]{1,0:T(8,128)(2,1)S(1)} %get-tuple-element.56.refs_1_), channel_id=1, source_target_pairs={{0,16},{16,0},{1,17},{17,1},{2,18},{18,2},{3,19},{19,3},{4,20},{20... | collective-permute-start | bytes 1572872 | tf_op jit(solution)/shard_map/ppermute | solution.py:521
  112.5 0.8 copy-start.7
  114.6 4.6 %copy-start.3 = (f32[64,8,16,32]{0,3,2,1:T(8,128)S(1)}, f32[64,8,16,32]{0,3,2,1:T(8,128)}, u32[]{:S(2)}) copy-start(f32[64,8,16,32]{0,3,2,1:T(8,128)} %param.9) | copy-start | bytes 3145732
  114.6 12.5 %collective-permute-start.29 = (bf16[512,256]{1,0:T(8,128)(2,1)S(1)}, bf16[512,256]{1,0:T(8,128)(2,1)S(1)}, u32[]{:S(2)}, u32[]{:S(2)}) collective-permute-start(bf16[512,256]{1,0:T(8,128)(2,1)S(1)} %cut_face.7), channel_id=1, source_target_pairs={{4,8},{8,4},{5,9},{9,5},{6,10},{10,6},{7,11},{11,7},{20,24},{24,20... | collective-permute-start | bytes 786440 | tf_op jit(solution)/shard_map/ppermute | solution.py:458
  115.5 11.7 %collective-permute-start.28 = (bf16[512,256]{1,0:T(8,128)(2,1)S(1)}, bf16[512,256]{1,0:T(8,128)(2,1)S(1)}, u32[]{:S(2)}, u32[]{:S(2)}) collective-permute-start(bf16[512,256]{1,0:T(8,128)(2,1)S(1)} %get-tuple-element.64), channel_id=1, source_target_pairs={{0,4},{8,12},{4,0},{12,8},{1,5},{9,13},{5,1},{13,9},{2,6},{10,14},... | collective-permute-start | bytes 786440 | tf_op jit(solution)/shard_map/ppermute | solution.py:458
  123.9 4.5 %collective-permute-start.27 = (bf16[512,256]{1,0:T(8,128)(2,1)S(1)}, bf16[512,256]{1,0:T(8,128)(2,1)S(1)}, u32[]{:S(2)}, u32[]{:S(2)}) collective-permute-start(bf16[512,256]{1,0:T(8,128)(2,1)S(1)} %cut_face.6), channel_id=1, source_target_pairs={{4,8},{8,4},{5,9},{9,5},{6,10},{10,6},{7,11},{11,7},{20,24},{24,20... | collective-permute-start | bytes 786440 | tf_op jit(solution)/shard_map/ppermute | solution.py:458
  124.6 3.8 %collective-permute-start.26 = (bf16[512,256]{1,0:T(8,128)(2,1)S(1)}, bf16[512,256]{1,0:T(8,128)(2,1)S(1)}, u32[]{:S(2)}, u32[]{:S(2)}) collective-permute-start(bf16[512,256]{1,0:T(8,128)(2,1)S(1)} %get-tuple-element.62), channel_id=1, source_target_pairs={{0,4},{8,12},{4,0},{12,8},{1,5},{9,13},{5,1},{13,9},{2,6},{10,14},... | collective-permute-start | bytes 786440 | tf_op jit(solution)/shard_map/ppermute | solution.py:458
  128.9 4.9 %collective-permute-start.30 = (bf16[1024,128]{1,0:T(8,128)(2,1)S(1)}, bf16[1024,128]{1,0:T(8,128)(2,1)S(1)}, u32[]{:S(2)}, u32[]{:S(2)}) collective-permute-start(bf16[1024,128]{1,0:T(8,128)(2,1)S(1)} %get-tuple-element.68), channel_id=1, source_target_pairs={{1,2},{2,1},{5,6},{6,5},{9,10},{10,9},{13,14},{14,13},{17,18},{18,... | collective-permute-start | bytes 786440 | tf_op jit(solution)/shard_map/ppermute | solution.py:447
  129.6 8.8 %collective-permute-start.31 = (bf16[1024,128]{1,0:T(8,128)(2,1)S(1)}, bf16[1024,128]{1,0:T(8,128)(2,1)S(1)}, u32[]{:S(2)}, u32[]{:S(2)}) collective-permute-start(bf16[1024,128]{1,0:T(8,128)(2,1)S(1)} %get-tuple-element.69), channel_id=1, source_target_pairs={{0,1},{2,3},{1,0},{3,2},{4,5},{6,7},{5,4},{7,6},{8,9},{10,11},{9,8... | collective-permute-start | bytes 786440 | tf_op jit(solution)/shard_map/ppermute | solution.py:447
